TPU v7x, 32 devices: a whole 2x2x4 slice. The times are simulated.
32 devices in a mesh: dp: 8 (over z, x), mp: 4 (over y, core).
Axes of the slice: x: 2, y: 2, z: 4, core: 2. Of those that a mesh axis runs over, the one named last changes fastest.
Arguments:
- lap_vectors: float32 [8, 1024, 16], P('dp'), may hold values from -3 to 3
- eig_index: int32 [8, 1024, 2], P('dp'), may hold values from 0 to 1023, as said below
- type_ids: int32 [8, 1024], P('dp'), may hold values from 0 to 191
- seg_ids: int32 [8, 1024], P('dp'), may hold values from 0 to 24, as said below
- targets: float32 [8, 24], P('dp'), may hold values from 3 to 7
- layer_weights: float32 [768, 4608], P('dp', 'mp')
- left_stats: float32 [768, 24, 96], P('dp', 'mp')
- right_stats: float32 [8, 24, 192, 192], P('dp', 'mp')
- left_roots: float32 [768, 24, 96], P('dp', 'mp')
- right_roots: float32 [8, 24, 192, 192], P('dp', 'mp')
- tables: float32 [224, 768], replicated, may hold values from -2.4 to 2.4
- tables_m: float32 [224, 768], replicated
- tables_v: float32 [224, 768], replicated
- head_weight: float32 [768, 768], replicated, may hold values from -0.21875 to 0.21875
- head_m: float32 [768, 768], replicated
- head_v: float32 [768, 768], replicated
- vectors: float32 [11, 768], replicated
- vectors_m: float32 [11, 768], replicated
- vectors_v: float32 [11, 768], replicated
Outputs:
- loss_sum: float32 [], replicated
- count: float32 [], replicated
- grad_norm: float32 [], replicated
- layer_grad: float32 [768, 4608], P('dp', 'mp')
- layer_new: float32 [768, 4608], P('dp', 'mp')
- left_new: float32 [768, 24, 96], P('dp', 'mp')
- right_new: float32 [8, 24, 192, 192], P('dp', 'mp')
- tables_m_new: float32 [224, 768], replicated
- tables_v_new: float32 [224, 768], replicated
- tables_new: float32 [224, 768], replicated
- head_m_new: float32 [768, 768], replicated
- head_v_new: float32 [768, 768], replicated
- head_new: float32 [768, 768], replicated
- vectors_m_new: float32 [11, 768], replicated
- vectors_v_new: float32 [11, 768], replicated
- vectors_new: float32 [11, 768], replicated
Inputs may be any that keep to these rules, and one draw needn't show every extreme that they name: `seg_ids`: each row holds 1 to 24 molecules of 16 to 40 positions, laid end to end from position 0 and numbered 0, 1, ... in order, then padding; the last row holds exactly 24 molecules. `eig_index`: both entries equal the position itself except at a molecule's edge positions (those past its first 1 + (length - 1) // 2 positions), where they name node positions of the same molecule.
All inputs are finite; a program needn't handle non-finite values.
Results may differ from a plain program's by a relative error of at most 0.02.
Values may be sent and summed in bfloat16 or wider, within the bound.
No kernel may reach another device: no remote copies, remote signals or barrier semaphores. Data moves between devices by JAX's collectives and lax.ppermute only.
A program may use at most 192 MiB of HBM per device.

v0:
```python
import jax
import jax.numpy as jnp
from jax import lax
from jax.sharding import PartitionSpec as P

HEAD_DIM = 24
TYPES = 192
STEP = 10


HIGHEST_PREC = lax.Precision.HIGHEST
NORM_EPS = 1e-05
CLIP = 0.25
STATS_DECAY = 0.95
RATE_LAYER = 0.15
RATE_TABLES = 0.15
RATE_HEAD = 0.01
RATE_VECTORS = 0.2
BETA_ONE = 0.9
BETA_TWO = 0.99
ADAM_EPS = 1e-08
WEIGHT_DECAY = 0.01
MASKED = -1000000000.0


def split_up(x, dim, peers):
    before, after = (x.shape[:dim], x.shape[dim + 1 :])
    return jnp.moveaxis(x.reshape(*before, peers, -1, *after), dim, 0)


def sum_at_owner(x, axis, dim):
    peers = lax.axis_size(axis)
    pieces = lax.all_to_all(split_up(x, dim, peers), axis, 0, 0, tiled=True)
    return jnp.sum(pieces.astype(jnp.float32), axis=0)


def layer_norm(values, scale_row, shift_row):
    center = values - jnp.mean(values, -1, keepdims=True)
    spread = jnp.mean(center * center, -1, keepdims=True)
    return center * lax.rsqrt(spread + NORM_EPS) * scale_row + shift_row


def matmul(left_side, right_side):
    return jnp.dot(left_side, right_side, preferred_element_type=jnp.float32)


def matmul_nt(left_side, right_side):
    return lax.dot_general(
        left_side, right_side, (((1,), (1,)), ((), ())), preferred_element_type=jnp.float32
    )


def matmul_tn(left_side, right_side):
    return lax.dot_general(
        left_side, right_side, (((0,), (0,)), ((), ())), preferred_element_type=jnp.float32
    )


def block_rows(length):
    return min(512, length)


def masked_scores(query_part, attend_keys, seg_part, segment, scale_factor):
    scores = (
        jnp.einsum("qhe,khe->hqk", query_part, attend_keys, preferred_element_type=jnp.float32)
        * scale_factor
    )
    return jnp.where((seg_part[:, None] == segment[None, :])[None], scores, MASKED)


def attend(queries, attend_keys, values, segment, filled):
    length = queries.shape[0]
    rows_each = block_rows(length)
    pieces = length // rows_each
    scale_factor = queries.shape[2] ** (-0.5)

    def one_block(block_data):
        query_part, seg_part, start = block_data

        def compute(unused):
            scores = masked_scores(query_part, attend_keys, seg_part, segment, scale_factor)
            row_peak = jnp.max(scores, -1, keepdims=True)
            exp_scores = jnp.exp(scores - row_peak)
            row_total = jnp.sum(exp_scores, -1, keepdims=True)
            attn_probs = (exp_scores / row_total).astype(jnp.bfloat16)
            context = jnp.einsum(
                "hqk,khe->qhe", attn_probs, values, preferred_element_type=jnp.float32
            )
            return (context, (row_peak + jnp.log(row_total))[..., 0])

        def skip(unused):
            return (
                jnp.zeros(query_part.shape, jnp.float32),
                jnp.zeros((query_part.shape[1], rows_each), jnp.float32),
            )

        return lax.cond(start < filled, compute, skip, 0)

    shape_blocks = (pieces, rows_each, queries.shape[1], queries.shape[2])
    starts = jnp.arange(pieces, dtype=jnp.int32) * rows_each
    context, log_total = lax.map(
        one_block, (queries.reshape(shape_blocks), segment.reshape(pieces, rows_each), starts)
    )
    return (context.reshape(queries.shape), log_total)


def attend_back(queries, attend_keys, values, segment, filled, log_total, grad_context):
    length = queries.shape[0]
    rows_each = block_rows(length)
    pieces = length // rows_each
    scale_factor = queries.shape[2] ** (-0.5)

    def one_block(accum, block_data):
        query_part, seg_part, total_part, grad_part, start = block_data

        def compute(carried):
            scores = masked_scores(query_part, attend_keys, seg_part, segment, scale_factor)
            attn_probs = jnp.exp(scores - total_part[:, :, None])
            grad_probs = jnp.einsum(
                "qhe,khe->hqk", grad_part, values, preferred_element_type=jnp.float32
            )
            row_inner = jnp.sum(attn_probs * grad_probs, -1, keepdims=True)
            grad_scores = (attn_probs * (grad_probs - row_inner)).astype(jnp.bfloat16)
            grad_queries = (
                jnp.einsum(
                    "hqk,khe->qhe", grad_scores, attend_keys, preferred_element_type=jnp.float32
                )
                * scale_factor
            )
            grad_keys = (
                carried[0]
                + jnp.einsum(
                    "hqk,qhe->khe", grad_scores, query_part, preferred_element_type=jnp.float32
                )
                * scale_factor
            )
            grad_values = carried[1] + jnp.einsum(
                "hqk,qhe->khe",
                attn_probs.astype(jnp.bfloat16),
                grad_part,
                preferred_element_type=jnp.float32,
            )
            return ((grad_keys, grad_values), grad_queries)

        def skip(carried):
            return (carried, jnp.zeros(query_part.shape, jnp.float32))

        return lax.cond(start < filled, compute, skip, accum)

    shape_blocks = (pieces, rows_each, queries.shape[1], queries.shape[2])
    starts = jnp.arange(pieces, dtype=jnp.int32) * rows_each
    zero_init = jnp.zeros(queries.shape, jnp.float32)
    accum, grad_queries = lax.scan(
        one_block,
        (zero_init, zero_init),
        (
            queries.reshape(shape_blocks),
            segment.reshape(pieces, rows_each),
            log_total,
            grad_context.reshape(shape_blocks),
            starts,
        ),
    )
    return (grad_queries.reshape(queries.shape), accum[0], accum[1])


def adam_update(weight, first, second, grad, rate):
    first_new = BETA_ONE * first + (1.0 - BETA_ONE) * grad
    second_new = BETA_TWO * second + (1.0 - BETA_TWO) * grad * grad
    fixed_one = 1.0 - BETA_ONE**STEP
    fixed_two = 1.0 - BETA_TWO**STEP
    update_dir = first_new / fixed_one / (jnp.sqrt(second_new / fixed_two) + ADAM_EPS)
    return (first_new, second_new, weight - rate * (update_dir + WEIGHT_DECAY * weight))


def per_device(
    lap_vectors,
    eig_index,
    type_ids,
    seg_ids,
    targets,
    layer_weights,
    left_stats,
    right_stats,
    left_roots,
    right_roots,
    tables,
    tables_m,
    tables_v,
    head_weight,
    head_m,
    head_v,
    vectors,
    vectors_m,
    vectors_v,
):
    length = seg_ids.shape[1]
    molecules = targets.shape[1]
    slots = 2 * molecules
    model_width = vectors.shape[1]
    group_cols = layer_weights.shape[1] // 6
    group_heads = group_cols // HEAD_DIM
    own_rows = layer_weights.shape[0]
    weights = lax.all_gather(layer_weights.astype(jnp.bfloat16), "dp", axis=0, tiled=True)
    weight_in = weights[:, : 3 * group_cols]
    weight_out = weights[:, 3 * group_cols : 4 * group_cols]
    weight_up = weights[:, 4 * group_cols : 5 * group_cols]
    weight_down = weights[:, 5 * group_cols :]
    own_seg = seg_ids[0]
    own_lap = lap_vectors[0]
    own_goal = targets[0]
    own_eig = eig_index[0]
    own_types = type_ids[0]
    position = jnp.arange(length, dtype=jnp.int32)
    mol_index = jnp.arange(slots, dtype=jnp.int32)
    live = own_seg != molecules
    pairs_flat = jnp.concatenate([own_lap[own_eig[:, 0]], own_lap[own_eig[:, 1]]], 1).astype(
        jnp.bfloat16
    )
    slot_seg = jnp.where(live, own_seg, slots)
    node_mask = (own_eig[:, 0] == own_eig[:, 1])[:, None]
    goals = jnp.concatenate([own_goal, jnp.zeros((molecules,), jnp.float32)])
    filled = jnp.sum(live.astype(jnp.int32))
    previous = jnp.concatenate([jnp.full((1,), -1, jnp.int32), slot_seg[:-1]])
    is_start = (slot_seg != slots) & (slot_seg != previous)
    start_flat = is_start[:, None]
    embedded = jnp.take(tables[:TYPES], own_types, axis=0)
    embedded = embedded + matmul(pairs_flat, tables[TYPES:].astype(jnp.bfloat16))
    embedded = embedded + jnp.where(node_mask, vectors[6], vectors[7])
    resid_zero = jnp.where(start_flat, vectors[8], embedded)
    normed_one, undo_one = jax.vjp(layer_norm, resid_zero, vectors[0], vectors[1])
    normed_one_low = normed_one.astype(jnp.bfloat16)
    projected = matmul(normed_one_low, weight_in).astype(jnp.bfloat16)
    shaped = projected.reshape(length, 3, group_heads, HEAD_DIM)
    queries = shaped[:, 0]
    attend_keys = shaped[:, 1]
    values = shaped[:, 2]
    context, log_total = attend(queries, attend_keys, values, slot_seg, filled)
    context_low = context.reshape(length, group_cols).astype(jnp.bfloat16)
    attn_sum = lax.psum(matmul_nt(context_low, weight_out).astype(jnp.bfloat16), "mp").astype(
        jnp.float32
    )
    resid_one = resid_zero + attn_sum
    normed_two, undo_two = jax.vjp(layer_norm, resid_one, vectors[2], vectors[3])
    normed_two_low = normed_two.astype(jnp.bfloat16)
    hidden = matmul(normed_two_low, weight_up)
    activated, undo_gelu = jax.vjp(jax.nn.gelu, hidden)
    activated_low = activated.astype(jnp.bfloat16)
    ffn_sum = lax.psum(matmul_nt(activated_low, weight_down).astype(jnp.bfloat16), "mp").astype(
        jnp.float32
    )
    resid_two = resid_one + ffn_sum
    select = (slot_seg[None, :] == mol_index[:, None]) & is_start[None, :]
    slot_place = jnp.sum(jnp.where(select, position[None, :], 0), 1)
    present = jnp.any(select, 1)
    graph_rows = resid_two[slot_place]
    head_normed, undo_head = jax.vjp(layer_norm, graph_rows, vectors[4], vectors[5])
    head_low = head_normed.astype(jnp.bfloat16)
    head_weight_low = head_weight.astype(jnp.bfloat16)
    head_mid = matmul(head_low, head_weight_low) + vectors[9]
    head_act, undo_head_gelu = jax.vjp(jax.nn.gelu, head_mid)
    head_act_low = head_act.astype(jnp.bfloat16)
    readout_low = vectors[10].astype(jnp.bfloat16)
    predicted = matmul(head_act_low, readout_low)
    pred_error = predicted - goals
    loss_terms = jnp.where(present, jnp.sqrt(pred_error * pred_error + 1.0) - 1.0, 0.0)
    loss_sum, count = lax.psum((jnp.sum(loss_terms), jnp.sum(present.astype(jnp.float32))), "dp")
    grad_pred = (
        jnp.where(present, pred_error / jnp.sqrt(pred_error * pred_error + 1.0), 0.0) / count
    )
    grad_readout = jnp.sum(grad_pred[:, None] * head_act_low.astype(jnp.float32), 0)
    grad_act = grad_pred[:, None] * readout_low.astype(jnp.float32)[None, :]
    grad_mid = undo_head_gelu(grad_act)[0].astype(jnp.bfloat16)
    grad_head_bias = jnp.sum(grad_mid.astype(jnp.float32), 0)
    grad_head_weight = matmul_tn(head_low, grad_mid)
    grad_rows, grad_gain_out, grad_shift_out = undo_head(matmul_nt(grad_mid, head_weight_low))
    grad_two = jnp.zeros((length, model_width), jnp.float32).at[slot_place].add(grad_rows)
    grad_two_low = grad_two.astype(jnp.bfloat16)
    grad_hidden = undo_gelu(matmul(grad_two_low, weight_down))[0].astype(jnp.bfloat16)
    grad_normed_two = lax.psum(matmul_nt(grad_hidden, weight_up).astype(jnp.bfloat16), "mp").astype(
        jnp.float32
    )
    back_two = undo_two(grad_normed_two)
    grad_one = grad_two + back_two[0]
    grad_one_low = grad_one.astype(jnp.bfloat16)
    grad_context = (
        matmul(grad_one_low, weight_out).astype(jnp.bfloat16).reshape(length, group_heads, HEAD_DIM)
    )
    grad_queries, grad_keys, grad_values = attend_back(
        queries, attend_keys, values, slot_seg, filled, log_total, grad_context
    )
    grad_proj = (
        jnp.stack([grad_queries, grad_keys, grad_values], 1)
        .reshape(length, 3 * group_cols)
        .astype(jnp.bfloat16)
    )
    grad_normed_one = lax.psum(matmul_nt(grad_proj, weight_in).astype(jnp.bfloat16), "mp").astype(
        jnp.float32
    )
    back_one = undo_one(grad_normed_one)
    grad_zero_low = (grad_one + back_one[0]).astype(jnp.bfloat16)
    embed_grad = jnp.where(start_flat, jnp.zeros((), jnp.bfloat16), grad_zero_low)
    embed_float = embed_grad.astype(jnp.float32)
    grad_graph = jnp.sum(jnp.where(start_flat, grad_zero_low.astype(jnp.float32), 0.0), 0)
    type_onehot = (own_types[:, None] == jnp.arange(TYPES, dtype=jnp.int32)[None, :]).astype(
        jnp.bfloat16
    )
    grad_types = matmul_tn(type_onehot, embed_grad)
    grad_lap = matmul_tn(pairs_flat, embed_grad)
    grad_node = jnp.sum(jnp.where(node_mask, embed_float, 0.0), 0)
    grad_edge = jnp.sum(jnp.where(node_mask, 0.0, embed_float), 0)
    layer_grad = sum_at_owner(
        jnp.concatenate(
            [
                matmul_tn(normed_one_low, grad_proj),
                matmul_tn(grad_one_low, context_low),
                matmul_tn(normed_two_low, grad_hidden),
                matmul_tn(grad_two_low, activated_low),
            ],
            1,
        ).astype(jnp.bfloat16),
        "dp",
        0,
    )
    grad_tables = jnp.concatenate([grad_types, grad_lap], 0)
    grad_vectors = jnp.stack(
        [
            back_one[1],
            back_one[2],
            back_two[1],
            back_two[2],
            grad_gain_out,
            grad_shift_out,
            grad_node,
            grad_edge,
            grad_graph,
            grad_head_bias,
            grad_readout,
        ],
        0,
    )
    layer_square = jnp.sum(layer_grad * layer_grad)
    grad_tables, grad_head, grad_vectors = lax.psum(
        (grad_tables, grad_head_weight, grad_vectors), "dp"
    )
    layer_total = lax.psum(layer_square, ("dp", "mp"))
    grand_total = (
        layer_total
        + jnp.sum(grad_tables * grad_tables)
        + jnp.sum(grad_head * grad_head)
        + jnp.sum(grad_vectors * grad_vectors)
    )
    grad_norm = jnp.sqrt(grand_total)
    factor = CLIP / jnp.maximum(grad_norm, CLIP)
    clipped = layer_grad * factor
    grad_blocks = clipped.reshape(own_rows, 6, group_cols)
    current = layer_weights.reshape(own_rows, 6, group_cols)
    left_new = STATS_DECAY * left_stats + (1.0 - STATS_DECAY) * jnp.einsum(
        "ijc,kjc->ijk", grad_blocks, grad_blocks, precision=HIGHEST_PREC
    )
    right_new = (
        STATS_DECAY * right_stats
        + (1.0 - STATS_DECAY)
        * jnp.einsum("ijc,ijd->jcd", grad_blocks, grad_blocks, precision=HIGHEST_PREC)[None]
    )
    preconditioned = jnp.einsum("ijk,kjc->ijc", left_roots, grad_blocks, precision=HIGHEST_PREC)
    preconditioned = jnp.einsum(
        "ijc,jcd->ijd", preconditioned, right_roots[0], precision=HIGHEST_PREC
    )
    layer_new = (current - RATE_LAYER * (preconditioned + WEIGHT_DECAY * current)).reshape(
        own_rows, 6 * group_cols
    )
    tables_m_new, tables_v_new, tables_new = adam_update(
        tables, tables_m, tables_v, grad_tables * factor, RATE_TABLES
    )
    head_m_new, head_v_new, head_new = adam_update(
        head_weight, head_m, head_v, grad_head * factor, RATE_HEAD
    )
    vectors_m_new, vectors_v_new, vectors_new = adam_update(
        vectors, vectors_m, vectors_v, grad_vectors * factor, RATE_VECTORS
    )
    return (
        loss_sum,
        count,
        grad_norm,
        clipped,
        layer_new,
        left_new,
        right_new,
        tables_m_new,
        tables_v_new,
        tables_new,
        head_m_new,
        head_v_new,
        head_new,
        vectors_m_new,
        vectors_v_new,
        vectors_new,
    )


def solution(mesh):
    placed = (
        P("dp", None, None),
        P("dp", None, None),
        P("dp", None),
        P("dp", None),
        P("dp", None),
        P("dp", "mp"),
        P("dp", "mp", None),
        P("dp", "mp", None, None),
        P("dp", "mp", None),
        P("dp", "mp", None, None),
        P(),
        P(),
        P(),
        P(),
        P(),
        P(),
        P(),
        P(),
        P(),
    )
    return jax.shard_map(
        per_device,
        mesh=mesh,
        in_specs=placed,
        out_specs=(
            P(),
            P(),
            P(),
            P("dp", "mp"),
            P("dp", "mp"),
            P("dp", "mp", None),
            P("dp", "mp", None, None),
            P(),
            P(),
            P(),
            P(),
            P(),
            P(),
            P(),
            P(),
            P(),
        ),
        check_vma=False,
    )
```

profile of v0, /device:TPU:0, one launch (start us, length us, event | category | flops | bytes accessed | tf_op | source)
XLA Modules:
  0.0 664.6 jit_solution(8613638754775313551)
XLA Ops:
  13.4 3.2 gather_fusion.2
  16.8 3.2 gather_fusion.1
  20.1 5.2 gather_fusion
  25.4 3.6 copy.141
  30.5 4.5 fusion.138
  37.1 22.2 %all-gather.2.cloned.1.call-done = bf16[768,1152]{1,0:T(8,128)(2,1)} async-done(((bf16[96,1152]{1,0:T(8,128)(2,1)}), bf16[768,1152]{1,0:T(8,128)(2,1)}) %all-gather.2.cloned.1.call-update) | async-done | bytes 1769488 | tf_op jit(solution)/shard_map/all_gather | solution.py:204
  59.4 3.4 fusion.58
  64.0 17.8 %while.26 = (s32[]{:T(128)}, bf16[2,512,8,24]{1,3,2,0:T(8,128)(2,1)S(1)}, f32[2,8,512]{2,1,0:T(8,128)S(1)}, s32[2]{0:T(128)S(1)}, s32[]{:T(128)}, /*index=5*/s32...) while((s32[]{:T(128)}, ...), condition=%wide.region_9.10_spmd, body=%wide.region_4.9_spmd.sunk | while | flops 453505024 | bytes 54176472 | solution.py:101
  65.8 13.9 %conditional.4 = (bf16[1,512,8,24]{1,3,2,0:T(8,128)(2,1)S(1)}, f32[1,8,512]{2,1,0:T(8,128)S(1)}) conditional(s32[]{:T(128)} %convert_element_type.294, () %tuple.124, (s32[2,512]{1,0:T(2,128)S(1)}, s32[]{:T(128)}, s32[1024]{0:T(1024)S(1)}, bf16[2,512,8,24]{1,3,2,0:T(8,128)(2,1)}, bf16[1024,8,24]{0,2,1:T(8,128)(2,1)S(1)}, ...), branch_computations={%region_5.5_spmd, %region_6.8_spmd} | conditional | flops 453505024 | bytes 53750292 | solution.py:97
  66.2 4.2 fusion
  70.5 4.4 fusion.1
  74.8 4.8 fusion.3
  83.0 2.8 convolution_convert_fusion.3
  86.3 55.4 %all-reduce.9.cloned.1.call-done = bf16[1024,768]{0,1:T(8,128)(2,1)} async-done(((bf16[1024,768]{0,1:T(8,128)(2,1)}), bf16[1024,768]{0,1:T(8,128)(2,1)}) %all-reduce.9.cloned.1.call-update) | async-done | bytes 1572880 | tf_op jit(solution)/shard_map/psum | solution.py:240
  141.7 3.0 fusion.137
  148.9 2.8 convolution_convert_fusion.2
  152.3 42.6 %all-reduce.11.cloned.1.call-done = bf16[1024,768]{0,1:T(8,128)(2,1)} async-done(((bf16[1024,768]{0,1:T(8,128)(2,1)}), bf16[1024,768]{0,1:T(8,128)(2,1)}) %all-reduce.11.cloned.1.call-update) | async-done | bytes 1572880 | tf_op jit(solution)/shard_map/psum | solution.py:249
  194.9 4.8 convert_add_fusion
  199.7 3.6 copy.149
  203.3 2.6 gather_fusion.3
  206.3 2.7 multiply_convert_fusion.2
  209.8 22.0 %psum.73 = f32[]{:T(128)} all-reduce(f32[]{:T(128)} %get-tuple-element.512), channel_id=1, replica_groups=mesh['dp'=8,'mp'=4] {'dp'}, use_global_device_ids=true, to_apply=%region_20.21 | all-reduce | flops 1 | bytes 8 | tf_op jit(solution)/shard_map/psum | solution.py:267
  234.2 2.8 multiply_reduce_fusion.7
  239.1 3.2 scatter_custom_fusion
  242.4 3.4 fusion.80
  246.5 2.7 convolution_convert_fusion.1
  249.4 3.4 fusion.49
  252.9 2.0 reshape.378
  254.9 3.6 copy.152
  258.4 2.4 convolution_convert_fusion.8
  262.7 2.8 convolution_convert_fusion.7
  266.4 22.2 %all-reduce.13.cloned.1.call-done = bf16[1024,768]{0,1:T(8,128)(2,1)} async-done(((bf16[1024,768]{0,1:T(8,128)(2,1)}), bf16[1024,768]{0,1:T(8,128)(2,1)}) %all-reduce.13.cloned.1.call-update) | async-done | bytes 1572880 | tf_op jit(solution)/shard_map/psum | solution.py:280
  288.6 4.1 convert_reduce_fusion.1
  292.7 2.2 fusion.42
  300.2 80.2 %while.27 = (s32[]{:T(128)}, f32[1024,8,24]{0,2,1:T(8,128)S(1)}, f32[1024,8,24]{0,2,1:T(8,128)S(1)}, bf16[2,512,8,24]{1,0,3,2:T(2,128)(2,1)}, s32[2]{0:T(128)S(1...) while((s32[]{:T(128)}, f32[1024,8,24]{0,2,1:T(8,128)S(1)}, ...), condition=%wide.region_31.32_spmd, body=%wide.region_27.31_spmd.sunk | while | flops 1045688320 | bytes 168980368 | solution.py:153
  302.3 53.0 %conditional.5 = (f32[1024,8,24]{0,2,1:T(8,128)S(1)}, f32[1024,8,24]{0,2,1:T(8,128)S(1)}, bf16[1,512,8,24]{1,3,2,0:T(8,128)(2,1)S(1)}) conditional(s32[]{:T(128)} %convert_element_type.295, (f32[1024,8,24]{0,2,1:T(8,128)S(1)}, f32[1024,8,24]{0,2,1:T(8,128)S(1)}) %tuple.127, (s32[2,512]{1,0:T(2,128)S(1)}, s32[]{:T(128)}, s32[1024]{0:T(1024)S(1)}, ...), branch_computations={%region_28.28_spmd, %region_29.30_spmd} | conditional | flops 1045688320 | bytes 167407200 | solution.py:148
  303.4 9.2 %fusion.22 = f32[8,512,1024]{2,1,0:T(8,128)} fusion(bf16[1024,8,24]{0,2,1:T(8,128)(2,1)} %get-tuple-element.258, bf16[2,512,8,24]{1,3,2,0:T(8,128)(2,1)} %get-tuple-element.257, s32[]{:T(128)} %get-tuple-element.252), kind=kOutput, calls=%fused_computation.37 | convolution fusion | flops 201326592 | bytes 17367552 | tf_op jit(solution)/shard_map/while/body/eval_jaxpr/cond/branch_1_fun/qhe,khe->hqk/dot_general | solution.py:119
  312.7 12.7 %multiply_reduce_fusion = (f32[8,512]{1,0:T(8,128)S(1)}, f32[8,512,1024]{2,1,0:T(8,128)}) fusion(f32[8,512,1024]{2,1,0:T(8,128)} %fusion.22, f32[8,512]{1,0:T(8,128)S(1)} %dynamic-slice_bitcast_fusion, bf16[1024,8,24]{0,2,1:T(8,128)(2,1)S(1)} %get-tuple-element.255, bf16[2,512,8,24]{1,3,2,0:T(8,128)(2,1)} %get-tuple-element.254, s32[]{:T(128)} %get-tuple-element.252, ...), kind=kOutput, calls=%fused_computation.24 | convolution fusion | flops 222294016 | bytes 34701824 | tf_op jit(solution)/shard_map/while/body/eval_jaxpr/cond/branch_1_fun/qhe,khe->hqk/dot_general | solution.py:65
  325.3 14.9 %multiply_convert_fusion = bf16[8,512,1024]{2,1,0:T(8,128)(2,1)} fusion(f32[8,512,1024]{2,1,0:T(8,128)} %get-tuple-element.585, f32[8,512,1024]{2,1,0:T(8,128)} %fusion.22, f32[8,512]{1,0:T(8,128)S(1)} %get-tuple-element.584), kind=kLoop, calls=%fused_computation.23 | loop fusion | flops 12582912 | bytes 41959424 | tf_op jit(solution)/shard_map/while/body/eval_jaxpr/cond/branch_1_fun/convert_element_type | solution.py:123
  340.2 7.0 %fusion.17 = f32[1024,8,24]{0,2,1:T(8,128)S(1)} fusion(f32[1024,8,24]{0,2,1:T(8,128)S(1)} %get-tuple-element.259, f32[8,512,1024]{2,1,0:T(8,128)} %get-tuple-element.585, bf16[2,512,8,24]{1,3,2,0:T(8,128)(2,1)S(1)} %copy-done.15, s32[]{:T(128)} %get-tuple-element.252), kind=kOutput, calls=%fused_computation.32 | convolution fusion | flops 205717504 | bytes 18546692 | tf_op jit(solution)/shard_map/while/body/eval_jaxpr/cond/branch_1_fun/hqk,qhe->khe/dot_general | solution.py:137
  347.2 5.8 fusion.20
  353.1 2.2 fusion.16
  357.3 9.6 %dynamic_update_slice.18 = bf16[2,512,8,24]{1,0,3,2:T(2,128)(2,1)} dynamic-update-slice(bf16[2,512,8,24]{1,0,3,2:T(2,128)(2,1)} %get-tuple-element.814, bf16[1,512,8,24]{1,0,3,2:T(2,128)(2,1)S(1)} %copy.214, s32[]{:T(128)} %copy.244, s32[]{:T(128)} %constant.185.clone.1..sunk, s32[]{:T(128)} %constant.185.clone.1..sunk, s32[]{:T(128)} %constant.185.clone.1..sunk) | dynamic-update-slice | bytes 393220 | tf_op jit(solution)/shard_map/while/body/jit(dynamic_update_index_in_dim)/dynamic_update_slice | solution.py:101
  370.7 9.6 %dynamic_update_slice.18 = bf16[2,512,8,24]{1,0,3,2:T(2,128)(2,1)} dynamic-update-slice(bf16[2,512,8,24]{1,0,3,2:T(2,128)(2,1)} %get-tuple-element.814, bf16[1,512,8,24]{1,0,3,2:T(2,128)(2,1)S(1)} %copy.214, s32[]{:T(128)} %copy.244, s32[]{:T(128)} %constant.185.clone.1..sunk, s32[]{:T(128)} %constant.185.clone.1..sunk, s32[]{:T(128)} %constant.185.clone.1..sunk) | dynamic-update-slice | bytes 393220 | tf_op jit(solution)/shard_map/while/body/jit(dynamic_update_index_in_dim)/dynamic_update_slice | solution.py:101
  383.7 2.5 convolution_convert_fusion
  386.3 2.0 fusion.130
  388.3 2.7 convolution_convert_fusion.5
  391.0 2.4 convolution_convert_fusion.4
  393.4 4.0 concatenate.38
  397.4 58.6 %all-to-all-start = ((bf16[8,96,1152]{2,1,0:T(8,128)(2,1)}), bf16[8,96,1152]{2,1,0:T(8,128)(2,1)}, u32[]{:S(2)}, u32[]{:S(2)}) async-start(bf16[8,96,1152]{2,1,0:T(8,128)(2,1)} %concatenate.38), calls=%async_computation | async-start | bytes 3538944 | tf_op jit(solution)/shard_map/all_to_all | solution.py:33
  456.1 26.2 %all-reduce.15.cloned.1.call-done = bf16[1024,768]{0,1:T(8,128)(2,1)} async-done(((bf16[1024,768]{0,1:T(8,128)(2,1)}), bf16[1024,768]{0,1:T(8,128)(2,1)}) %all-reduce.15.cloned.1.call-update) | async-done | bytes 1572880 | tf_op jit(solution)/shard_map/psum | solution.py:297
  482.2 3.5 convert_reduce_fusion
  485.8 3.1 fusion.43
  489.1 4.6 fusion.41
  497.8 40.3 %all-reduce.1 = (f32[]{:T(128)}, f32[11,768]{1,0:T(8,128)S(1)}) all-reduce(f32[]{:T(128)} %get-tuple-element.513, f32[11,768]{1,0:T(8,128)S(1)} %stack.41), channel_id=1, replica_groups=mesh['dp'=8,'mp'=4] {'dp'}, use_global_device_ids=true, to_apply=%region_18.19 | all-reduce | flops 8449 | bytes 67592 | tf_op jit(solution)/shard_map/psum | solution.py:267
  541.2 37.7 %psum.75 = f32[]{:T(128)} all-reduce(f32[]{:T(128)} %multiply_reduce_fusion.5), channel_id=1, replica_groups=mesh['dp'=8,'mp'=4] {'dp','mp'}, use_global_device_ids=true, to_apply=%region_34.35 | all-reduce | flops 1 | bytes 8 | tf_op jit(solution)/shard_map/psum | solution.py:346
  578.8 45.8 %all-reduce.17.cloned.1.call-done = (f32[224,768]{1,0:T(8,128)}, f32[768,768]{1,0:T(8,128)}) async-done(((f32[224,768]{1,0:T(8,128)}, f32[768,768]{1,0:T(8,128)}), (f32[224,768]{1,0:T(8,128)}, f32[768,768]{1,0:T(8,128)})) %all-reduce.17.cloned.1.call-update) | async-done | bytes 3047440 | tf_op jit(solution)/shard_map/psum | solution.py:343
  624.6 2.9 multiply_reduce_fusion.3
  632.3 2.2 fusion.67
  637.1 2.1 fusion.63
  639.2 2.2 copy.164
  641.5 2.1 copy.169
  643.5 3.7 fusion.60
  650.4 5.8 multiply_subtract_fusion
  (353 shorter events, 57.7 us)
Async XLA Ops:
  7.2 629.9 %copy-start = (f32[1,6,192,192]{3,2,1,0:T(8,128)S(1)}, f32[1,6,192,192]{3,2,1,0:T(8,128)}, u32[]{:S(2)}) copy-start(f32[1,6,192,192]{3,2,1,0:T(8,128)} %param.36) | copy-start | bytes 2654212
  7.2 52.2 %all-gather.2.cloned.1.call-start = ((), (), s32[]{:S(2)}) async-start(), calls=%async_computation.1 | async-start | bytes 1990656 | tf_op jit(solution)/shard_map/all_gather | solution.py:204
  9.1 132.6 %all-reduce.9.cloned.1.call-start = ((), (), s32[]{:S(2)}) async-start(), calls=%async_computation.2 | async-start | bytes 3145728 | tf_op jit(solution)/shard_map/psum | solution.py:240
  13.4 6.7 %copy-start.100 = (s32[1,1024]{1,0:T(1,128)S(1)}, s32[1,1024]{1,0:T(1,128)}, u32[]{:S(2)}) copy-start(s32[1,1024]{1,0:T(1,128)} %param.29) | copy-start | bytes 12292
  13.4 6.7 %slice-start = ((f32[224,768]{1,0:T(8,128)}), f32[192,768]{1,0:T(8,128)S(1)}, s32[]{:S(2)}) async-start(f32[224,768]{1,0:T(8,128)} %param.37), calls=%async_computation.7 | async-start | bytes 1179648 | tf_op jit(solution)/shard_map/slice | solution.py:227
  16.7 13.7 %copy-start.50 = (bf16[1024,16]{0,1:T(8,128)(2,1)}, bf16[1024,16]{0,1:T(8,128)(2,1)S(1)}, u32[]{:S(2)}) copy-start(bf16[1024,16]{0,1:T(8,128)(2,1)S(1)} %copy.144) | copy-start | bytes 98308
  20.1 10.4 %copy-start.52 = (bf16[1024,16]{0,1:T(8,128)(2,1)}, bf16[1024,16]{0,1:T(8,128)(2,1)S(1)}, u32[]{:S(2)}) copy-start(bf16[1024,16]{0,1:T(8,128)(2,1)S(1)} %copy.143) | copy-start | bytes 98308
  25.4 4.3 copy-start.66
  25.4 5.1 copy-start.2
  29.1 5.9 copy-start.84
  29.7 5.3 copy-start.72
  29.7 5.3 copy-start.74
  29.7 5.3 copy-start.76
  29.7 29.6 %copy-start.54 = (f32[768]{0:T(1024)}, f32[768]{0:T(1024)S(1)}, u32[]{:S(2)}) copy-start(f32[768]{0:T(1024)S(1)} %get-tuple-element.508) | copy-start | bytes 9220
  29.7 29.6 %copy-start.90 = (f32[768]{0:T(1024)}, f32[768]{0:T(1024)S(1)}, u32[]{:S(2)}) copy-start(f32[768]{0:T(1024)S(1)} %get-tuple-element.507) | copy-start | bytes 9220
  30.5 4.6 copy-start.87
  35.1 27.7 %copy-start.47 = (f32[1024]{0:T(1024)}, f32[1024]{0:T(1024)S(1)}, u32[]{:S(2)}) copy-start(f32[1024]{0:T(1024)S(1)} %broadcast_multiply_fusion.2) | copy-start | bytes 12292
  37.1 25.7 %copy-start.80 = (f32[1024]{0:T(1024)}, f32[1024]{0:T(1024)S(1)}, u32[]{:S(2)}) copy-start(f32[1024]{0:T(1024)S(1)} %multiply_reduce_fusion.2) | copy-start | bytes 12292
  37.1 25.7 %copy-start.63 = (f32[1024]{0:T(1024)}, f32[1024]{0:T(1024)S(1)}, u32[]{:S(2)}) copy-start(f32[1024]{0:T(1024)S(1)} %fusion.119) | copy-start | bytes 12292
  81.8 63.0 %copy-start.16 = (bf16[1024,8,24]{0,2,1:T(8,128)(2,1)}, bf16[1024,8,24]{0,2,1:T(8,128)(2,1)S(1)}, u32[]{:S(2)}) copy-start(bf16[1024,8,24]{0,2,1:T(8,128)(2,1)S(1)} %get-tuple-element.853) | copy-start | bytes 1179652
  81.8 62.9 %copy-start.42 = (f32[2,8,512]{2,1,0:T(8,128)}, f32[2,8,512]{2,1,0:T(8,128)S(1)}, u32[]{:S(2)}) copy-start(f32[2,8,512]{2,1,0:T(8,128)S(1)} %get-tuple-element.806) | copy-start | bytes 98308
  81.8 62.9 %copy-start.109 = (s32[2]{0:T(128)}, s32[2]{0:T(128)S(1)}, u32[]{:S(2)}) copy-start(s32[2]{0:T(128)S(1)} %get-tuple-element.877) | copy-start | bytes 28
  85.9 109.0 %all-reduce.11.cloned.1.call-start = ((), (), s32[]{:S(2)}) async-start(), calls=%async_computation.3 | async-start | bytes 3145728 | tf_op jit(solution)/shard_map/psum | solution.py:249
  144.8 150.2 %copy-start.43 = (f32[1024]{0:T(1024)}, f32[1024]{0:T(1024)S(1)}, u32[]{:S(2)}) copy-start(f32[1024]{0:T(1024)S(1)} %broadcast_multiply_fusion.1) | copy-start | bytes 12292
  145.2 149.8 %copy-start.59 = (f32[1024]{0:T(1024)}, f32[1024]{0:T(1024)S(1)}, u32[]{:S(2)}) copy-start(f32[1024]{0:T(1024)S(1)} %fusion.120) | copy-start | bytes 12292
  146.5 5.3 copy-start.40
  146.5 5.4 copy-start.67
  146.5 5.5 copy-start.82
  151.8 136.9 %all-reduce.13.cloned.1.call-start = ((), (), s32[]{:S(2)}) async-start(), calls=%async_computation.4 | async-start | bytes 3145728 | tf_op jit(solution)/shard_map/psum | solution.py:280
  152.1 42.7 %copy-start.108 = (s32[48]{0:T(128)}, s32[48]{0:T(128)S(1)}, u32[]{:S(2)}) copy-start(s32[48]{0:T(128)S(1)} %fusion.124) | copy-start | bytes 580
  199.7 6.6 copy-start.57
  199.7 6.6 copy-start.70
  199.7 6.6 copy-start.92
  203.3 5.7 copy-start.106
  205.9 33.2 %copy-start.18 = (f32[48,768]{1,0:T(8,128)}, f32[48,768]{1,0:T(8,128)S(1)}, u32[]{:S(2)}) copy-start(f32[48,768]{1,0:T(8,128)S(1)} %gather_fusion.3) | copy-start | bytes 442372
  206.0 33.1 %copy-start.102 = (f32[48]{0:T(128)}, f32[48]{0:T(128)S(1)}, u32[]{:S(2)}) copy-start(f32[48]{0:T(128)S(1)} %broadcast_multiply_fusion.3) | copy-start | bytes 580
  206.2 27.9 %copy-start.107 = (f32[48]{0:T(128)}, f32[48]{0:T(128)S(1)}, u32[]{:S(2)}) copy-start(f32[48]{0:T(128)S(1)} %multiply_reduce_fusion.9) | copy-start | bytes 580
  206.2 26.2 %copy-start.104 = (f32[48]{0:T(128)}, f32[48]{0:T(128)S(1)}, u32[]{:S(2)}) copy-start(f32[48]{0:T(128)S(1)} %fusion.125) | copy-start | bytes 580
  234.2 8.2 %copy-start.34 = (bf16[48,768]{1,0:T(8,128)(2,1)}, bf16[48,768]{1,0:T(8,128)(2,1)S(1)}, u32[]{:S(2)}) copy-start(bf16[48,768]{1,0:T(8,128)(2,1)S(1)} %get-tuple-element.574) | copy-start | bytes 221188
  249.3 233.0 %all-reduce.15.cloned.1.call-start = ((), (), s32[]{:S(2)}) async-start(), calls=%async_computation.5 | async-start | bytes 3145728 | tf_op jit(solution)/shard_map/psum | solution.py:297
  325.3 14.9 %copy-start.15 = (bf16[2,512,8,24]{1,3,2,0:T(8,128)(2,1)S(1)}, bf16[2,512,8,24]{1,3,2,0:T(8,128)(2,1)}, u32[]{:S(2)}) copy-start(bf16[2,512,8,24]{1,3,2,0:T(8,128)(2,1)} %get-tuple-element.257) | copy-start | bytes 1179652 | tf_op jit(solution)/shard_map/while/body/eval_jaxpr/cond
  347.2 5.9 copy-start.1
  386.2 4.8 copy-start.26
  386.3 4.7 copy-start.30
  393.4 88.8 %copy-start.49 = (f32[1024]{0:T(1024)S(1)}, f32[1024]{0:T(1024)}, u32[]{:S(2)}) copy-start(f32[1024]{0:T(1024)} %copy-done.47) | copy-start | bytes 12292
  393.4 88.8 %copy-start.56 = (f32[768]{0:T(1024)S(1)}, f32[768]{0:T(1024)}, u32[]{:S(2)}) copy-start(f32[768]{0:T(1024)} %copy-done.54) | copy-start | bytes 9220
  397.4 91.5 %copy-start.12 = (bf16[1024,768]{0,1:T(8,128)(2,1)S(1)}, bf16[1024,768]{0,1:T(8,128)(2,1)}, u32[]{:S(2)}) copy-start(bf16[1024,768]{0,1:T(8,128)(2,1)} %all-reduce.13.cloned.1.call-done) | copy-start | bytes 4718596
  397.4 140.7 %all-to-all-start = ((bf16[8,96,1152]{2,1,0:T(8,128)(2,1)}), bf16[8,96,1152]{2,1,0:T(8,128)(2,1)}, u32[]{:S(2)}, u32[]{:S(2)}) async-start(bf16[8,96,1152]{2,1,0:T(8,128)(2,1)} %concatenate.38), calls=%async_computation | async-start | bytes 3538944 | tf_op jit(solution)/shard_map/all_to_all | solution.py:33
  456.0 29.8 %copy-start.81 = (f32[1024]{0:T(1024)S(1)}, f32[1024]{0:T(1024)}, u32[]{:S(2)}) copy-start(f32[1024]{0:T(1024)} %copy-done.80) | copy-start | bytes 12292
  456.0 29.8 %copy-start.65 = (f32[1024]{0:T(1024)S(1)}, f32[1024]{0:T(1024)}, u32[]{:S(2)}) copy-start(f32[1024]{0:T(1024)} %copy-done.63) | copy-start | bytes 12292
  456.0 168.6 %all-reduce.17.cloned.1.call-start = ((), (), s32[]{:S(2)}) async-start(), calls=%async_computation.6 | async-start | bytes 6094848 | tf_op jit(solution)/shard_map/psum | solution.py:343
  482.2 6.7 %copy-start.10 = (f32[1024,768]{0,1:T(8,128)S(1)}, f32[1024,768]{0,1:T(8,128)}, u32[]{:S(2)}) copy-start(f32[1024,768]{0,1:T(8,128)} %copy.152) | copy-start | bytes 9437188
  489.0 4.7 copy-start.51
  489.0 4.6 copy-start.53
  489.1 5.2 copy-start.101
  632.1 5.0 copy-start.24
  639.2 8.0 %copy-start.41 = (f32[11,768]{1,0:T(8,128)S(1)}, f32[11,768]{1,0:T(8,128)}, u32[]{:S(2)}) copy-start(f32[11,768]{1,0:T(8,128)} %param.43) | copy-start | bytes 101380
  639.2 8.0 %copy-start.68 = (f32[11,768]{1,0:T(8,128)S(1)}, f32[11,768]{1,0:T(8,128)}, u32[]{:S(2)}) copy-start(f32[11,768]{1,0:T(8,128)} %param.45) | copy-start | bytes 101380
  639.2 8.0 %copy-start.69 = (f32[11,768]{1,0:T(8,128)S(1)}, f32[11,768]{1,0:T(8,128)}, u32[]{:S(2)}) copy-start(f32[11,768]{1,0:T(8,128)} %param.44) | copy-start | bytes 101380
  639.2 8.7 %copy-start.3 = (f32[224,768]{1,0:T(8,128)S(1)}, f32[224,768]{1,0:T(8,128)}, u32[]{:S(2)}) copy-start(f32[224,768]{1,0:T(8,128)} %param.37) | copy-start | bytes 2064388
  639.2 8.7 %copy-start.22 = (f32[224,768]{1,0:T(8,128)S(1)}, f32[224,768]{1,0:T(8,128)}, u32[]{:S(2)}) copy-start(f32[224,768]{1,0:T(8,128)} %get-tuple-element.562) | copy-start | bytes 2064388
  643.5 4.4 copy-start.32
  643.5 4.4 copy-start.33
  643.5 6.0 copy-start.23
  (56 other events, 130.8 us)
Sparse Core Ops, SparseCore 0:
  10.8 48.5 all-gather.1
  86.0 55.6 all-reduce.8
  151.9 42.9 all-reduce.10
  249.4 39.1 all-reduce.12
  386.4 95.8 all-reduce.14
  496.2 128.3 all-reduce.16
where the time goes:
time: 677 us; the launch traced here: 665 us
  waiting for transfers between devices  214 us (32%)
  matrix products  101 us (15%)
  blocking collectives  100 us (15%)
  local copies, waits for them, and re-layouts  82.2 us (12%)
  other arithmetic  81.9 us (12%)
  starting transfers between devices  59.2 us (9%)
  between operations  19.9 us (3%)
    psum x2, blocking collectives, per_device(): lax.psum((jnp.sum(loss_terms), jnp.sum(present.astype(jnp.float32))), 'dp')  62.3 us
    all_to_all x1, starting transfers between devices, sum_at_owner(): pieces = lax.all_to_all(split_up(x, dim, peers), axis, 0, 0, tiled=True)  58.6 us
    psum x1, waiting for transfers between devices, per_device(): lax.psum(matmul_nt(context_low, weight_out).astype(jnp.bfloat16), 'mp')  55.4 us
    psum x1, waiting for transfers between devices, per_device(): lax.psum((grad_tables, grad_head_weight, grad_vectors), 'dp')  45.8 us
    psum x1, waiting for transfers between devices, per_device(): lax.psum(matmul_nt(activated_low, weight_down).astype(jnp.bfloat16), 'mp')  42.6 us
    psum x1, blocking collectives, per_device(): layer_total = lax.psum(layer_square, ('dp', 'mp'))  37.7 us
    psum x1, waiting for transfers between devices, per_device(): lax.psum(matmul_nt(grad_proj, weight_in).astype(jnp.bfloat16), 'mp')  26.2 us
    all_gather x1, waiting for transfers between devices, per_device(): lax.all_gather(layer_weights.astype(jnp.bfloat16), 'dp', axis=0, tiled=True)  22.2 us
  transfers between devices with their start and end apart: 7, of which 6 were waited for; matrix products, arithmetic and copies ran while one was open for 11% of the time, Pallas kernels for 0%

commit v1 on v0

v1 whole, which is shorter than its diff:
```python
import functools

import jax
import jax.numpy as jnp
from jax import lax
from jax.experimental import pallas as pl
from jax.experimental.pallas import tpu as pltpu
from jax.sharding import PartitionSpec as P

HEAD_DIM = 24
TYPES = 192
STEP = 10
NORM_EPS = 1e-05
CLIP = 0.25
STATS_DECAY = 0.95
RATE_LAYER = 0.15
RATE_TABLES = 0.15
RATE_HEAD = 0.01
RATE_VECTORS = 0.2
BETA_ONE = 0.9
BETA_TWO = 0.99
ADAM_EPS = 1e-08
WEIGHT_DECAY = 0.01
MASKED = -1000000000.0
GELU_C = 0.7978845608028654
GELU_A = 0.044715

BF = jnp.bfloat16
F32 = jnp.float32
I32 = jnp.int32
HIGHEST = lax.Precision.HIGHEST
NN = ((1,), (0,))
NT = ((1,), (1,))
TN = ((0,), (0,))
BLOCK = 256
FEATS = 256
MIB = 1024 * 1024


def dot(a, b, dims=NN, precision=None):
    return lax.dot_general(a, b, (dims, ((), ())), preferred_element_type=F32, precision=precision)


def iota(shape, dim):
    return lax.broadcasted_iota(I32, shape, dim)


def call(kernel, outs, ins, scratch=(), flops=0, vmem=40, in_specs=None, aliases=None):
    moved = sum(x.size * x.dtype.itemsize for x in list(ins) + list(outs))
    full = pl.BlockSpec(memory_space=pltpu.VMEM)
    return pl.pallas_call(
        kernel,
        out_shape=tuple(outs),
        in_specs=in_specs or [full] * len(ins),
        out_specs=tuple([full] * len(outs)),
        scratch_shapes=list(scratch),
        compiler_params=pltpu.CompilerParams(vmem_limit_bytes=vmem * MIB),
        cost_estimate=pl.CostEstimate(flops=flops, bytes_accessed=moved, transcendentals=0),
    )(*ins)


def sds(shape, dtype):
    return jax.ShapeDtypeStruct(shape, dtype)


def norm_parts(values):
    center = values - jnp.mean(values, -1, keepdims=True)
    spread = jnp.mean(center * center, -1, keepdims=True)
    inverse = lax.rsqrt(spread + NORM_EPS)
    return center * inverse, inverse


def norm_back(grad, hat, inverse, gain):
    scaled = grad * gain
    mean_one = jnp.mean(scaled, -1, keepdims=True)
    mean_two = jnp.mean(scaled * hat, -1, keepdims=True)
    return inverse * (scaled - mean_one - hat * mean_two)


def gelu_pair(x):
    t = jnp.tanh(GELU_C * (x + GELU_A * x * x * x))
    value = 0.5 * x * (1.0 + t)
    slope = 0.5 * (1.0 + t) + 0.5 * x * (1.0 - t * t) * (GELU_C * (1.0 + 3.0 * GELU_A * x * x))
    return value, slope


def tree(refs):
    parts = [r[...].astype(F32) for r in refs]
    while len(parts) > 1:
        parts = [parts[i] + parts[i + 1] for i in range(0, len(parts), 2)]
    return parts[0]


def three(x):
    high = x.astype(BF).astype(F32)
    mid = (x - high).astype(BF).astype(F32)
    return high, mid, x - high - mid


def assemble(pieces, whole, first_owner):
    rows = pieces[0].shape[0]
    if len(pieces) == 1:
        whole[...] = pieces[0][...]
        return
    for k, piece in enumerate(pieces):
        start = pl.multiple_of((first_owner ^ k) * rows, 16)
        whole[pl.ds(start, rows), :] = piece[...]


def embed_kernel(mols, lap, eig, kinds, seg, tables, vectors, at, normed, hats, invs, high, low, prev):
    length = seg.shape[1]
    width = vectors.shape[1]
    rows = tables.shape[0]
    tab = tables[...]
    tab_high = tab.astype(BF)
    high[0:rows, :] = tab_high
    rest = jnp.where(iota(tab.shape, 0) < TYPES, tab - tab_high.astype(F32), 0.0)
    low[0:rows, :] = rest.astype(BF)
    r = iota((FEATS - rows, width), 0)
    extra = jnp.where(r == 0, vectors[6:7, :], jnp.where(r == 1, vectors[7:8, :], jnp.where(r == 2, vectors[8:9, :], 0.0)))
    extra_high = extra.astype(BF)
    high[rows:FEATS, :] = extra_high
    low[rows:FEATS, :] = (extra - extra_high.astype(F32)).astype(BF)
    seg_row = seg[...]
    before = pltpu.roll(jnp.broadcast_to(seg_row, (8, length)), 1, 1)
    before = jnp.where(iota((8, length), 1) == 0, -1, before)
    prev[...] = before
    filled = jnp.sum((seg_row != mols).astype(F32)).astype(I32)
    normed[...] = jnp.zeros(normed.shape, BF)
    gain = vectors[0:1, :]
    shift = vectors[1:2, :]
    window = 2 * BLOCK

    def one_block(b, unused):
        start = pl.multiple_of(b * BLOCK, BLOCK)
        here = pl.ds(start, BLOCK)
        first = pl.multiple_of(jnp.clip(start - 128, 0, length - window), 128)
        source = iota((window, BLOCK), 0) + first
        one = eig[0:1, here]
        two = eig[1:2, here]
        near = lap[:, pl.ds(first, window)].astype(BF)
        pair_one = dot(near, (source == one).astype(F32).astype(BF))
        pair_two = dot(near, (source == two).astype(F32).astype(BF))
        seg_here = seg[0:1, here]
        begins = (seg_here != mols) & (seg_here != prev[0:1, here])
        kind = jnp.where(begins, -1, kinds[0:1, here])
        keep = jnp.where(begins, 0.0, 1.0)
        at[0:TYPES, here] = (iota((TYPES, BLOCK), 0) == kind).astype(F32).astype(BF)
        half = pair_one.shape[0]
        at[TYPES : TYPES + half, here] = (pair_one * keep).astype(BF)
        at[TYPES + half : rows, here] = (pair_two * keep).astype(BF)
        which = jnp.where(begins, 2, jnp.where(one == two, 0, 1))
        at[rows:FEATS, here] = (iota((FEATS - rows, BLOCK), 0) == which).astype(F32).astype(BF)
        picks = at[:, here]
        resid = dot(picks, high[...], TN) + dot(picks, low[...], TN)
        hat, inverse = norm_parts(resid)
        normed[here, :] = (hat * gain + shift).astype(BF)
        hats[here, :] = hat.astype(BF)
        invs[here, :] = jnp.broadcast_to(inverse, (BLOCK, 128))
        return 0

    lax.fori_loop(0, (filled + BLOCK - 1) // BLOCK, one_block, 0)


def attn_kernel(npiece, mols, heads, scale, *refs):
    normed, seg, vectors = refs[:3]
    ones = refs[3 : 3 + npiece]
    twos = refs[3 + npiece : 3 + 2 * npiece]
    part, probs, values, ctx_out, keyed, query_out, w1, w2 = refs[3 + 2 * npiece :]
    me = lax.axis_index("dp")
    assemble(ones, w1, me)
    assemble(twos, w2, me)
    width = vectors.shape[1]
    cols = heads * HEAD_DIM
    hat, _ = norm_parts(vectors[8:9, :])
    start_row = (hat * vectors[0:1, :] + vectors[1:2, :]).astype(BF)
    q = dot(jnp.broadcast_to(start_row, (16, width)), w1[:, 0:256])
    q = q.astype(BF).astype(F32)
    q = jnp.where(iota((16, 256), 1) < cols, q, 0.0)
    r = iota((16, 256), 0)
    head_of = iota((16, 256), 1) // HEAD_DIM
    query_out[...] = jnp.where(r == head_of, q, 0.0)[0:8, :]
    shifted = pltpu.roll(q, 64, 1)[0:1, :]
    r = iota((128, 256), 0)
    lane = iota((128, 256), 1) - 64
    pick = (lane >= 0) & ((r & 7) == lane // HEAD_DIM) & (r >= 64) & (r < 80)
    q_keys = jnp.where(pick, shifted, 0.0).astype(BF)
    u = dot(w1[:, 128:384], q_keys, NT)
    u_high = u.astype(BF)
    lane = iota(u.shape, 1)
    u_both = jnp.where(lane < 72, u_high.astype(F32), u - u_high.astype(F32))
    last = w1[:, 512:640].astype(F32)
    side = jnp.where(lane < 64, last, u_both).astype(BF)
    keyed[:, 0:128] = w1[:, 384:512]
    keyed[:, 128:256] = jnp.where(lane < 64, last, jnp.where(lane < 72, u * scale, 0.0)).astype(BF)
    normed_all = normed[...]
    values[:, 0:128] = dot(normed_all, w1[:, 384:512]).astype(BF)
    second = dot(normed_all, side)
    values[:, 128:256] = jnp.where(iota(second.shape, 1) < 64, second, 0.0).astype(BF)
    turned = second.T
    scores = (turned[64:72, :] + turned[72:80, :]) * scale
    seg_row = seg[...]
    length = seg_row.shape[1]
    mine = iota((mols, 1, length), 0) == seg_row[None]
    masked = jnp.where(mine, scores[None], MASKED)
    peak = jnp.max(masked, -1, keepdims=True)
    grown = jnp.where(mine, jnp.exp(masked - peak), 0.0)
    total = jnp.sum(grown, -1, keepdims=True)
    total = jnp.where(total > 0.0, total, 1.0)
    prob = (grown / total).reshape(mols * heads, length).astype(BF)
    probs[...] = prob
    wide = dot(prob, values[...])
    r = iota(wide.shape, 0) & (heads - 1)
    wide = jnp.where(r == iota(wide.shape, 1) // HEAD_DIM, wide, 0.0)
    ctx = jnp.sum(wide.reshape(mols, heads, 256), 1)
    ctx_out[...] = ctx.astype(BF)
    low = ctx.astype(BF)
    tail = pltpu.roll(ctx[:, 128:256], 64, 1)
    tail = jnp.where(iota(tail.shape, 1) >= 64, tail, 0.0).astype(BF)
    out = dot(low[:, 0:128], w2[:, 0:128], NT) + dot(tail, w1[:, 512:640], NT)
    part[...] = out.astype(BF)


def ffn_kernel(npiece, nmp, cols, *refs):
    terms = refs[:nmp]
    vectors = refs[nmp]
    twos = refs[nmp + 1 : nmp + 1 + npiece]
    part, resid_out, normed_out, hidden_out, act_out, w2 = refs[nmp + 1 + npiece :]
    assemble(twos, w2, lax.axis_index("dp"))
    resid = vectors[8:9, :] + tree(terms)
    resid_out[...] = resid
    hat, _ = norm_parts(resid)
    low = (hat * vectors[2:3, :] + vectors[3:4, :]).astype(BF)
    normed_out[...] = low
    hidden = dot(low, w2[:, 128:384])
    hidden = jnp.where(iota(hidden.shape, 1) < cols, hidden, 0.0)
    hidden_out[...] = hidden
    act, _ = gelu_pair(hidden)
    act_out[...] = act.astype(BF)
    turned = pltpu.roll(act, 64, 1).astype(BF)
    part[...] = dot(turned, w2[:, 256:512], NT).astype(BF)


def head_kernel(npiece, nmp, cols, *refs):
    terms = refs[:nmp]
    resid_one, vectors, head, targets, seg, normed_two, ctx, hidden, act = refs[nmp : nmp + 9]
    twos = refs[nmp + 9 : nmp + 9 + npiece]
    part, pack, grad_out, rows_out, w2, head_low = refs[nmp + 9 + npiece :]
    assemble(twos, w2, lax.axis_index("dp"))
    width = vectors.shape[1]
    mols = targets.shape[1]
    head_low[...] = head[...].astype(BF)
    resid = resid_one[...] + tree(terms)
    hat, inverse = norm_parts(resid)
    gain = vectors[4:5, :]
    low = (hat * gain + vectors[5:6, :]).astype(BF)
    mid = dot(low, head_low[...]) + vectors[9:10, :]
    act_head, slope = gelu_pair(mid)
    act_head = act_head.astype(BF).astype(F32)
    readout = vectors[10:11, :].astype(BF).astype(F32)
    predicted = jnp.sum(act_head * readout, -1, keepdims=True)
    spot = iota((mols, mols), 0) == iota((mols, mols), 1)
    goal = jnp.sum(jnp.where(spot, targets[...], 0.0), -1, keepdims=True)
    seg_row = seg[...]
    there = iota((mols, seg_row.shape[1]), 0) == seg_row
    present = jnp.max(there.astype(F32), -1, keepdims=True)
    error = predicted - goal
    root = jnp.sqrt(error * error + 1.0)
    loss = jnp.sum(present * (root - 1.0), 0, keepdims=True)
    count = jnp.sum(present, 0, keepdims=True)
    grad_pred = present * error / root
    grad_readout = jnp.sum(grad_pred * act_head, 0, keepdims=True)
    grad_mid = (grad_pred * readout * slope).astype(BF)
    grad_bias = jnp.sum(grad_mid.astype(F32), 0, keepdims=True)
    grad_rows = dot(grad_mid, head_low[...], NT)
    grad_gain = jnp.sum(grad_rows * hat, 0, keepdims=True)
    grad_shift = jnp.sum(grad_rows, 0, keepdims=True)
    grad_two = norm_back(grad_rows, hat, inverse, gain)
    grad_out[...] = grad_two
    grad_low = grad_two.astype(BF)
    grad_act = dot(grad_low, w2[:, 256:512])
    grad_act = pltpu.roll(grad_act, 192, 1)
    _, slope_hidden = gelu_pair(hidden[...])
    grad_hidden = jnp.where(iota(grad_act.shape, 1) < cols, grad_act * slope_hidden, 0.0).astype(BF)
    part[...] = dot(grad_hidden, w2[:, 128:384], NT).astype(BF)
    pack[:, 0:width] = low
    pack[:, width : 2 * width] = grad_mid
    pack[:, 2 * width : 3 * width] = normed_two[...]
    pack[:, 3 * width : 4 * width] = grad_low
    pack[:, 4 * width : 4 * width + 256] = ctx[...]
    pack[:, 4 * width + 256 : 4 * width + 512] = act[...]
    pack[:, 4 * width + 512 : 4 * width + 768] = grad_hidden
    r = iota((8, width), 0)
    lane = iota((8, width), 1)
    scalars = jnp.where(lane == 0, loss, jnp.where(lane == 1, count, 0.0))
    rows_out[...] = jnp.where(
        r == 0,
        grad_gain,
        jnp.where(r == 1, grad_shift, jnp.where(r == 2, grad_bias, jnp.where(r == 3, grad_readout, jnp.where(r == 4, scalars, 0.0)))),
    )


def back_kernel(npiece, nmp, mols, heads, scale, *refs):
    terms = refs[:nmp]
    resid_one, grad_two, head_rows, vectors, keyed, probs, values, normed, hats, invs, at, seg = refs[nmp : nmp + 12]
    ones = refs[nmp + 12 : nmp + 12 + npiece]
    twos = refs[nmp + 12 + npiece : nmp + 12 + 2 * npiece]
    rest = refs[nmp + 12 + 2 * npiece :]
    outs = rest[:nmp]
    layer, query_grad, w1, w2, sides, comb, total, gains = rest[nmp:]
    assemble(ones, w1, lax.axis_index("dp"))
    assemble(twos, w2, lax.axis_index("dp"))
    group = lax.axis_index("mp")
    width = vectors.shape[1]
    length = seg.shape[1]
    cols = heads * HEAD_DIM
    filled = jnp.sum((seg[...] != mols).astype(F32)).astype(I32)
    grad_normed = tree(terms)
    hat, inverse = norm_parts(resid_one[...])
    grad_gain = jnp.sum(grad_normed * hat, 0, keepdims=True)
    grad_shift = jnp.sum(grad_normed, 0, keepdims=True)
    grad_one = grad_two[...] + norm_back(grad_normed, hat, inverse, vectors[2:3, :])
    low = grad_one.astype(BF)
    grad_start = jnp.sum(low.astype(F32), 0, keepdims=True)
    ctx_one = dot(low, w2[:, 0:128])
    ctx_two = dot(low, w1[:, 512:640])
    ctx_two = pltpu.roll(ctx_two, 64, 1)
    grad_ctx = jnp.concatenate([ctx_one, ctx_two], 1).astype(BF).astype(F32)
    spread = jnp.broadcast_to(grad_ctx[:, None, :], (mols, heads, 256)).reshape(mols * heads, 256)
    r = iota(spread.shape, 0) & (heads - 1)
    spread = jnp.where(r == iota(spread.shape, 1) // HEAD_DIM, spread, 0.0).astype(BF)
    grad_probs = dot(spread, values[...], NT)
    prob = probs[...].astype(F32)
    inner = jnp.sum(prob * grad_probs, -1, keepdims=True)
    grad_scores = (prob * (grad_probs - inner)).astype(BF).astype(F32)
    grad_scores = jnp.sum(grad_scores.reshape(mols, heads, length), 0)
    grad_values = dot(spread, probs[...], TN)
    sides[0:cols, :] = grad_values[0:cols, :].astype(BF)
    sides[cols:256, :] = jnp.concatenate([grad_scores, jnp.zeros((256 - cols - heads, length), F32)], 0).astype(BF)
    sums = dot(sides[...], normed[...])
    comb[...] = keyed[...].astype(F32).T.astype(BF)
    total[...] = jnp.zeros(total.shape, F32)
    gains[...] = jnp.zeros(gains.shape, F32)
    gain = vectors[0:1, :]

    def one_block(b, unused):
        here = pl.ds(pl.multiple_of(b * BLOCK, BLOCK), BLOCK)
        grad = dot(sides[:, here], comb[...], TN)
        hat_here = hats[here, :].astype(F32)
        low_grad = norm_back(grad, hat_here, invs[here, 0:1], gain).astype(BF)
        total[...] += dot(at[:, here], low_grad)
        gains[0:8, :] += jnp.sum((grad * hat_here).reshape(BLOCK // 8, 8, width), 0)
        gains[8:16, :] += jnp.sum(grad.reshape(BLOCK // 8, 8, width), 0)
        return 0

    lax.fori_loop(0, (filled + BLOCK - 1) // BLOCK, one_block, 0)
    grad_keys = sums[cols : cols + heads, :]
    turned = dot(grad_keys.astype(BF), w1[:, 128:384])
    lane = iota(turned.shape, 1) - 64
    picked = jnp.where((lane >= 0) & (lane // HEAD_DIM == iota(turned.shape, 0)), turned, 0.0)
    grad_query = jnp.sum(pltpu.roll(picked, 192, 1), 0, keepdims=True) * scale
    query_grad[...] = jnp.broadcast_to(grad_query, query_grad.shape)
    grad_query = jnp.broadcast_to(grad_query.astype(BF), (16, 256))
    grad_row = dot(grad_query, w1[:, 0:256], NT)[0:1, :]
    hat_start, inverse_start = norm_parts(vectors[8:9, :])
    start_row = (hat_start * gain + vectors[1:2, :]).astype(BF).astype(F32)
    first = jnp.where(group == 0, 1.0, 0.0)
    row_graph = norm_back(grad_row, hat_start, inverse_start, gain) + first * grad_start
    row_gain = jnp.sum(gains[0:8, :], 0, keepdims=True) + grad_row * hat_start
    row_shift = jnp.sum(gains[8:16, :], 0, keepdims=True) + grad_row
    base = TYPES + 32
    r = iota((FEATS - base, width), 0)
    extra = jnp.where(r == 2, row_graph, 0.0)
    extra = jnp.where(r == 3, row_gain, extra)
    extra = jnp.where(r == 4, row_shift, extra)
    extra = jnp.where(r == 5, first * grad_gain, extra)
    extra = jnp.where(r == 6, first * grad_shift, extra)
    for i in range(4):
        extra = jnp.where(r == 7 + i, first * head_rows[i : i + 1, :], extra)
    total[base:FEATS, :] += extra
    each = FEATS // nmp
    for k in range(nmp):
        start = pl.multiple_of((group ^ k) * each, 16)
        outs[k][...] = total[pl.ds(start, each), :].astype(BF)
    lay = jnp.concatenate(
        [
            sums[0:cols, :],
            grad_one,
            jnp.zeros((32 - mols, width), F32),
            grad_keys,
            jnp.broadcast_to(start_row, (8, width)),
            jnp.zeros((256 - cols - 48, width), F32),
        ],
        0,
    )
    layer[...] = lay.T.astype(BF)


def packet_kernel(nmp, owners, *refs):
    terms = refs[:nmp]
    layer, head_rows, query_grad, out = refs[nmp:]
    dp, deep = layer.shape[0], layer.shape[1]
    half = terms[0].shape[1] // 2
    summed = tree(terms)
    scal = head_rows[4:5, 0:128]
    loss, count = scal[:, 0:1], scal[:, 1:2]
    a, b, c = three(loss)
    lane = iota((16, 128), 1)
    first = jnp.where(lane == 0, a, jnp.where(lane == 1, b, jnp.where(lane == 2, c, jnp.where(lane == 3, count, 0.0))))
    r = iota((16, 128), 0)
    side = jnp.where(r == 0, first, jnp.where(r == 1, query_grad[0:1, 0:128], jnp.where(r == 2, query_grad[0:1, 128:256], 0.0)))
    for p in range(dp):
        if p < owners:
            each = summed[p * 8 : p * 8 + 8, :]
        else:
            each = jnp.zeros((8, 2 * half), F32)
        each = jnp.concatenate([each[:, 0:half], each[:, half:]], 0)
        out[p, 0:deep, :] = layer[p]
        out[p, deep : deep + 16, :] = each[:, 0:256].astype(BF)
        out[p, deep + 16 : deep + 32, :] = jnp.concatenate([each[:, 256:384], side], 1).astype(BF)


def outer_kernel(own, head_in, grad_mid, normed, grad_low, act, grad_hidden, head_grad, up_grad, down_grad, squares, full):
    me = lax.axis_index("dp")
    grad = dot(head_in[...], grad_mid[...], TN)
    head_grad[...] = grad
    squares[...] = jnp.broadcast_to(jnp.sum(jnp.sum(grad * grad, 0, keepdims=True), 1, keepdims=True), squares.shape)
    kept = up_grad.shape[0]
    start = 0 if kept == full.shape[0] else pl.multiple_of(me * own, 8)
    full[...] = dot(normed[...], grad_hidden[...], TN)
    up_grad[...] = full[pl.ds(start, kept), :]
    full[...] = dot(grad_low[...], act[...], TN)
    down_grad[...] = full[pl.ds(start, kept), :]


def owner_kernel(own, mols, cols, scale, packets, ctx, query, up_grad, down_grad, layer, send, scalars):
    dp = packets.shape[0]
    deep = packets.shape[1] - 32
    acc = jnp.zeros((deep, 256), F32)
    table = jnp.zeros((16, 256), F32)
    rest = jnp.zeros((16, 256), F32)
    out_grad = jnp.zeros((deep, 256), F32)
    for p in range(dp):
        piece = packets[p, 0:deep, :]
        acc += piece.astype(F32)
        table += packets[p, deep : deep + 16, :].astype(F32)
        rest += packets[p, deep + 16 : deep + 32, :].astype(F32)
        rows = ctx[p * mols : (p + 1) * mols, :].astype(F32)
        rows = jnp.concatenate([jnp.zeros((64, 256), F32), rows, jnp.zeros((64 - mols, 256), F32)], 0).astype(BF)
        out_grad += dot(piece[:, 128:256], rows)
    keys = jnp.concatenate([jnp.zeros((96, 256), F32), query[...], jnp.zeros((24, 256), F32)], 0)
    key_grad = dot(acc[:, 128:256], keys, precision=HIGHEST) * scale
    start_col = packets[0, 0:deep, 128:256].astype(F32)[:, 104:105]
    side = rest[:, 128:256]
    query_row = jnp.concatenate([side[1:2, :], side[2:3, :]], 1)
    grads = [start_col * query_row, key_grad, acc, out_grad]
    square = jnp.zeros((1, 1), F32)

    def add(value):
        return jnp.sum(jnp.sum(value * value, 0, keepdims=True), 1, keepdims=True)

    for j in range(6):
        g = grads[j][0:own, 0:cols] if j < 4 else (up_grad if j == 4 else down_grad)[:, 0:cols]
        layer[j] = g
        square += add(g)
    third = rest[:, 0:128]
    square += add(table) + add(third)
    a, b, c = three(square)
    lane = iota((16, 128), 1)
    r = iota((16, 128), 0)
    tail = jnp.where(r == 0, jnp.where(lane == 0, a, jnp.where(lane == 1, b, jnp.where(lane == 2, c, 0.0))), 0.0)
    packet = jnp.concatenate([table, third, tail], 1).astype(BF)
    for p in range(dp):
        send[p] = packet
    loss = side[0:1, 0:1] + side[0:1, 1:2] + side[0:1, 2:3]
    count = side[0:1, 3:4]
    lane = iota((8, 128), 1)
    scalars[...] = jnp.where(lane == 0, loss, jnp.where(lane == 1, count, 0.0))


def stats_kernel(layer, left_roots, right_roots, left, right, shaped):
    for j in range(6):
        g = layer[j]
        left[j] = dot(g, g, NT, HIGHEST)
        right[j] = dot(g, g, TN, HIGHEST)
        shaped[j] = dot(dot(left_roots[j], g, NN, HIGHEST), right_roots[j], NN, HIGHEST)


def adam(weight, first, second, grad, rate):
    first_new = BETA_ONE * first + (1.0 - BETA_ONE) * grad
    second_new = BETA_TWO * second + (1.0 - BETA_TWO) * grad * grad
    fixed_one = 1.0 - BETA_ONE**STEP
    fixed_two = 1.0 - BETA_TWO**STEP
    update = first_new / fixed_one / (jnp.sqrt(second_new / fixed_two) + ADAM_EPS)
    return first_new, second_new, weight - rate * (update + WEIGHT_DECAY * weight)


def update_kernel(nmp, owners, cols, *refs):
    packets = refs[:nmp]
    (
        squares, scalars, layer, left_add, right_add, shaped, weights, left, right,
        tables, tables_m, tables_v, head, head_m, head_v, head_grad, vectors, vectors_m, vectors_v,
        loss_out, layer_out, weights_out, left_out, right_out,
        tm_out, tv_out, t_out, hm_out, hv_out, h_out, vm_out, vv_out, v_out, factors, grads,
    ) = refs[nmp:]
    step = pl.program_id(0)

    @pl.when(step == 0)
    def _():
        parts = []
        for ref in packets:
            s = jnp.zeros((1, 1), F32)
            for p in range(ref.shape[0]):
                tail = ref[p, :, 384:512].astype(F32)
                s += tail[0:1, 0:1] + tail[0:1, 1:2] + tail[0:1, 2:3]
            parts.append(s)
        while len(parts) > 1:
            parts = [parts[i] + parts[i + 1] for i in range(0, len(parts), 2)]
        square = parts[0] + squares[0:1, 0:1]
        loss, count = scalars[0:1, 0:1], scalars[0:1, 1:2]
        norm = jnp.sqrt(square) / count
        factor = CLIP / jnp.maximum(norm, CLIP) / count
        lane = iota((8, 128), 1)
        loss_out[...] = jnp.where(lane == 0, loss, jnp.where(lane == 1, count, norm))
        factors[...] = jnp.broadcast_to(factor, (8, 128))
        group = lax.axis_index("mp")
        each = FEATS // nmp
        half = 384
        for k in range(nmp):
            start = pl.multiple_of((group ^ k) * each, 8)
            for p in range(owners):
                piece = packets[k][p, :, 0:half].astype(F32)
                piece = jnp.concatenate([piece[0:8, :], piece[8:16, :]], 1) * factor
                grads[pl.ds(pl.multiple_of(start + p * 8, 8), 8), :] = piece
        rows = tables.shape[0]
        tm_out[...], tv_out[...], t_out[...] = adam(tables[...], tables_m[...], tables_v[...], grads[0:rows, :], RATE_TABLES)
        order = (3, 4, 5, 6, 7, 8, 0, 1, 2, 9, 10)
        r = iota((16, vectors.shape[1]), 0)
        tail = jnp.zeros(r.shape, F32)
        for i, o in enumerate(order):
            tail = jnp.where(r == i, grads[rows + o : rows + o + 1, :], tail)
        nrows = vectors.shape[0]
        vm_out[...], vv_out[...], v_out[...] = adam(vectors[...], vectors_m[...], vectors_v[...], tail[0:nrows, :], RATE_VECTORS)
        for j in range(6):
            span = slice(j * cols, (j + 1) * cols)
            layer_out[:, span] = layer[j] * factor
            weights_out[:, span] = weights[:, span] - RATE_LAYER * (shaped[j] * factor + WEIGHT_DECAY * weights[:, span])

    factor = factors[0:1, 0:1]
    hm_out[...], hv_out[...], h_out[...] = adam(head[...], head_m[...], head_v[...], head_grad[...] * factor, RATE_HEAD)
    scale = (1.0 - STATS_DECAY) * factor * factor
    left_out[...] = STATS_DECAY * left[...] + scale[None] * left_add[...]
    right_out[...] = STATS_DECAY * right[...] + scale[None] * right_add[...]


def exchange(x, axis):
    n = lax.axis_size(axis)
    return [x] + [lax.ppermute(x, axis, [(i, i ^ k) for i in range(n)]) for k in range(1, n)]


def gather_rows(x):
    if lax.axis_size("dp") == 8 and x.shape[0] % 16 == 0:
        return exchange(x, "dp")
    return [lax.all_gather(x, "dp", axis=0, tiled=True)]


def per_device(
    lap_vectors,
    eig_index,
    type_ids,
    seg_ids,
    targets,
    layer_weights,
    left_stats,
    right_stats,
    left_roots,
    right_roots,
    tables,
    tables_m,
    tables_v,
    head_weight,
    head_m,
    head_v,
    vectors,
    vectors_m,
    vectors_v,
):
    dp = lax.axis_size("dp")
    nmp = lax.axis_size("mp")
    length = seg_ids.shape[1]
    mols = targets.shape[1]
    width = vectors.shape[1]
    own, group_cols = layer_weights.shape[0], layer_weights.shape[1]
    cols = group_cols // 6
    heads = cols // HEAD_DIM
    scale = HEAD_DIM ** (-0.5)
    owners = FEATS // nmp // 8

    split = 3 * cols + 128
    w = layer_weights.astype(BF)
    ones = gather_rows(jnp.concatenate([w[:, : 3 * cols], w[:, split : 4 * cols]], 1))
    twos = gather_rows(jnp.concatenate([w[:, 3 * cols : split], w[:, 4 * cols :]], 1))
    np_ = len(ones)

    at, normed, hats, invs = call(
        functools.partial(embed_kernel, mols),
        [sds((FEATS, length), BF), sds((length, width), BF), sds((length, width), BF), sds((length, 128), F32)],
        [lap_vectors[0].T, eig_index[0].T, type_ids, seg_ids, tables, vectors],
        [pltpu.VMEM((FEATS, width), BF), pltpu.VMEM((FEATS, width), BF), pltpu.VMEM((8, length), I32)],
        flops=4 * length * FEATS * width,
    )
    wbuf = [pltpu.VMEM((width, 640), BF), pltpu.VMEM((width, 512), BF)]
    part, probs, values, ctx, keyed, query = call(
        functools.partial(attn_kernel, np_, mols, heads, scale),
        [
            sds((mols, width), BF),
            sds((mols * heads, length), BF),
            sds((length, 256), BF),
            sds((mols, 256), BF),
            sds((width, 256), BF),
            sds((8, 256), F32),
        ],
        [normed, seg_ids, vectors, *ones, *twos],
        wbuf,
        flops=4 * length * 256 * width,
    )
    part, resid_one, normed_two, hidden, act = call(
        functools.partial(ffn_kernel, np_, nmp, cols),
        [sds((mols, width), BF), sds((mols, width), F32), sds((mols, width), BF), sds((mols, 256), F32), sds((mols, 256), BF)],
        [*exchange(part, "mp"), vectors, *twos],
        wbuf[1:],
        flops=4 * mols * width * 256,
    )
    part, pack, grad_two, head_rows = call(
        functools.partial(head_kernel, np_, nmp, cols),
        [sds((mols, width), BF), sds((mols, 4 * width + 768), BF), sds((mols, width), F32), sds((8, width), F32)],
        [*exchange(part, "mp"), resid_one, vectors, head_weight, targets, seg_ids, normed_two, ctx, hidden, act, *twos],
        [wbuf[1], pltpu.VMEM((width, width), BF)],
        flops=4 * width * width * mols,
    )
    packs = lax.all_gather(pack, "dp", axis=0, tiled=True)
    back = call(
        functools.partial(back_kernel, np_, nmp, mols, heads, scale),
        [sds((FEATS // nmp, width), BF) for _ in range(nmp)] + [sds((width, 256), BF), sds((8, 256), F32)],
        [
            *exchange(part, "mp"), resid_one, grad_two, head_rows, vectors, keyed, probs, values, normed, hats, invs, at,
            seg_ids, *ones, *twos,
        ],
        [
            *wbuf,
            pltpu.VMEM((256, length), BF),
            pltpu.VMEM((256, width), BF),
            pltpu.VMEM((FEATS, width), F32),
            pltpu.VMEM((16, width), F32),
        ],
        flops=8 * length * 256 * width,
    )
    shares, layer_part, query_grad = back[:nmp], back[nmp], back[nmp + 1]
    moved = [shares[0]] + [lax.ppermute(shares[k], "mp", [(i, i ^ k) for i in range(nmp)]) for k in range(1, nmp)]
    deep = (own + 15) // 16 * 16
    layer_part = layer_part.reshape(dp, own, 256)
    if deep != own:
        layer_part = jnp.pad(layer_part, ((0, 0), (0, deep - own), (0, 0)))
    (packet,) = call(
        functools.partial(packet_kernel, nmp, owners),
        [sds((dp, deep + 32, 256), BF)],
        [*moved, layer_part, head_rows, query_grad],
    )
    packets = lax.all_to_all(packet, "dp", 0, 0, tiled=True)
    total = dp * mols

    def lanes(first, size):
        return pl.BlockSpec((total, size), lambda *unused: (0, first // size))

    kept = width if own % 8 else own
    head_grad, up_grad, down_grad, squares = pl.pallas_call(
        functools.partial(outer_kernel, own),
        out_shape=(sds((width, width), F32), sds((kept, 256), F32), sds((kept, 256), F32), sds((8, 128), F32)),
        grid=(1,),
        in_specs=[
            lanes(0, width),
            lanes(width, width),
            lanes(2 * width, width),
            lanes(3 * width, width),
            lanes(4 * width + 256, 256),
            lanes(4 * width + 512, 256),
        ],
        out_specs=(
            pl.BlockSpec((width, width), lambda i: (0, 0)),
            pl.BlockSpec((kept, 256), lambda i: (0, 0)),
            pl.BlockSpec((kept, 256), lambda i: (0, 0)),
            pl.BlockSpec((8, 128), lambda i: (0, 0)),
        ),
        scratch_shapes=[pltpu.VMEM((width, 256), F32)],
        compiler_params=pltpu.CompilerParams(vmem_limit_bytes=40 * MIB),
        cost_estimate=pl.CostEstimate(flops=2 * total * width * (width + 512), bytes_accessed=4 * width * width, transcendentals=0),
    )(*[packs] * 6)
    if kept != own:
        up_grad, down_grad = [lax.dynamic_slice_in_dim(x, lax.axis_index("dp") * own, own) for x in (up_grad, down_grad)]
    layer, send, scalars = pl.pallas_call(
        functools.partial(owner_kernel, own, mols, cols, scale),
        out_shape=(sds((6, own, cols), F32), sds((dp, 16, 512), BF), sds((8, 128), F32)),
        grid=(1,),
        in_specs=[
            pl.BlockSpec((dp, deep + 32, 256), lambda i: (0, 0, 0)),
            lanes(4 * width, 256),
            pl.BlockSpec((8, 256), lambda i: (0, 0)),
            pl.BlockSpec((own, 256), lambda i: (0, 0)),
            pl.BlockSpec((own, 256), lambda i: (0, 0)),
        ],
        out_specs=(
            pl.BlockSpec((6, own, cols), lambda i: (0, 0, 0)),
            pl.BlockSpec((dp, 16, 512), lambda i: (0, 0, 0)),
            pl.BlockSpec((8, 128), lambda i: (0, 0)),
        ),
        compiler_params=pltpu.CompilerParams(vmem_limit_bytes=40 * MIB),
        cost_estimate=pl.CostEstimate(flops=2 * own * 256 * 1024, bytes_accessed=1 << 20, transcendentals=0),
    )(packets, packs, query, up_grad, down_grad)
    sums = exchange(lax.all_to_all(send, "dp", 0, 0, tiled=True), "mp")
    left_add, right_add, shaped = call(
        stats_kernel,
        [sds((6, own, own), F32), sds((6, cols, cols), F32), sds((6, own, cols), F32)],
        [layer, jnp.swapaxes(left_roots, 0, 1), right_roots[0]],
        flops=12 * 6 * own * cols * (2 * own + 2 * cols),
    )
    steps = 6
    rows_each = width // steps

    def fixed(shape):
        return pl.BlockSpec(shape, lambda i: (0,) * len(shape))

    head_spec = pl.BlockSpec((rows_each, width), lambda i: (i, 0))
    left_spec = pl.BlockSpec((1, own, own), lambda i: (i, 0, 0))
    right_spec = pl.BlockSpec((1, cols, cols), lambda i: (i, 0, 0))
    layer_spec = fixed((own, group_cols))
    table_spec = fixed(tables.shape)
    vector_spec = fixed(vectors.shape)
    outs = pl.pallas_call(
        functools.partial(update_kernel, nmp, owners, cols),
        out_shape=(
            sds((8, 128), F32),
            sds((own, group_cols), F32),
            sds((own, group_cols), F32),
            sds((6, own, own), F32),
            sds((6, cols, cols), F32),
            *[sds(tables.shape, F32)] * 3,
            *[sds(head_weight.shape, F32)] * 3,
            *[sds(vectors.shape, F32)] * 3,
        ),
        grid=(steps,),
        in_specs=[fixed((dp, 16, 512))] * nmp
        + [fixed((8, 128)), fixed((8, 128)), fixed((6, own, cols)), left_spec, right_spec, fixed((6, own, cols))]
        + [layer_spec, left_spec, right_spec]
        + [table_spec] * 3
        + [head_spec] * 4
        + [vector_spec] * 3,
        out_specs=(
            fixed((8, 128)),
            layer_spec,
            layer_spec,
            left_spec,
            right_spec,
            *[table_spec] * 3,
            *[head_spec] * 3,
            *[vector_spec] * 3,
        ),
        scratch_shapes=[pltpu.VMEM((8, 128), F32), pltpu.VMEM((FEATS, width), F32)],
        compiler_params=pltpu.CompilerParams(vmem_limit_bytes=48 * MIB),
        cost_estimate=pl.CostEstimate(flops=20 * width * width, bytes_accessed=28 * width * width, transcendentals=0),
    )(
        *sums, squares, scalars, layer, left_add, right_add, shaped, layer_weights, jnp.swapaxes(left_stats, 0, 1), right_stats[0],
        tables, tables_m, tables_v, head_weight, head_m, head_v, head_grad, vectors, vectors_m, vectors_v,
    )
    facts, layer_grad, layer_new, left_new, right_new, tm, tv, tn, hm, hv, hn, vm, vv, vn = outs
    return (
        facts[0, 0],
        facts[0, 1],
        facts[0, 2],
        layer_grad,
        layer_new,
        jnp.swapaxes(left_new, 0, 1),
        right_new[None],
        tm,
        tv,
        tn,
        hm,
        hv,
        hn,
        vm,
        vv,
        vn,
    )


def solution(mesh):
    placed = (
        P("dp", None, None),
        P("dp", None, None),
        P("dp", None),
        P("dp", None),
        P("dp", None),
        P("dp", "mp"),
        P("dp", "mp", None),
        P("dp", "mp", None, None),
        P("dp", "mp", None),
        P("dp", "mp", None, None),
        *[P()] * 9,
    )
    return jax.shard_map(
        per_device,
        mesh=mesh,
        in_specs=placed,
        out_specs=(
            P(),
            P(),
            P(),
            P("dp", "mp"),
            P("dp", "mp"),
            P("dp", "mp", None),
            P("dp", "mp", None, None),
            *[P()] * 9,
        ),
        check_vma=False,
    )
```

time: 677 us -> 168 us (0.25); the launches traced: 665 us -> 167 us
  waiting for transfers between devices: 214 us -> 38.3 us
  matrix products: 101 us -> 0 us
  blocking collectives: 100 us -> 10.2 us
  other arithmetic: 81.9 us -> 1.14 us
  local copies, waits for them, and re-layouts: 82.2 us -> 26 us
  Pallas kernels: 0 us -> 26.6 us
  starting transfers between devices: 59.2 us -> 50.1 us
    psum x5 -> x0, waiting for transfers between devices: 192 us -> none  [the longest x1 55.4 us: per_device(): lax.psum(matmul_nt(context_low, weight_out).astype(jnp.bfloat16), 'mp')]
    dot_general x30 -> x0, matrix products: 101 us -> none  [the longest x7 18.1 us: matmul(): return jnp.dot(left_side, right_side, preferred_element_type=jnp.float32)]
    psum x3 -> x0, blocking collectives: 100 us -> none  [the longest x2 62.3 us: per_device(): lax.psum((jnp.sum(loss_terms), jnp.sum(present.astype(jnp.float32))), 'dp')]
    all_to_all x1, starting transfers between devices: 58.6 us -> 6.91 us  [per_device(): packets = lax.all_to_all(packet, 'dp', 0, 0, tiled=True)]
    ppermute x0 -> x29, starting transfers between devices: none -> 43.2 us  [the longest x26 41.2 us: exchange(): lax.ppermute(x, axis, [(i, i ^ k) for i in range(n)])]
    reduce_sum x20 -> x0, other arithmetic: 37.7 us -> none  [the longest x4 12.8 us: layer_norm(): return center * lax.rsqrt(spread + NORM_EPS) * scale_row + shift_row]
    pallas_call x0 -> x10, Pallas kernels: none -> 26.6 us  [the longest x7 13.2 us: call(): pl.pallas_call(kernel, out_shape=tuple(outs), in_specs=in_specs or [full]...]
    dynamic_update_slice x8 -> x0, local copies, waits for them, and re-layouts: 21.7 us -> none  [attend(): lax.map(one_block, (queries.reshape(shape_blocks), segment.reshape(pieces...]
  transfers between devices with their start and end apart: 7 -> 31, of which waited for: 6 -> 16; matrix products, arithmetic and copies ran while one was open for 11% -> 0% of each run, Pallas kernels for 0% -> 5%
where the time goes in v1:
time: 168 us; the launch traced here: 167 us
  starting transfers between devices  50.1 us (30%)
  waiting for transfers between devices  38.3 us (23%)
  Pallas kernels  26.6 us (16%)
  local copies, waits for them, and re-layouts  26 us (15%)
  between operations  14.4 us (9%)
  blocking collectives  10.2 us (6%)
    ppermute x26, starting transfers between devices, exchange(): lax.ppermute(x, axis, [(i, i ^ k) for i in range(n)])  41.2 us
    unnamed x98, local copies, waits for them, and re-layouts  25.2 us
    ppermute x26, waiting for transfers between devices, exchange(): lax.ppermute(x, axis, [(i, i ^ k) for i in range(n)])  16.5 us
    all_gather x1, waiting for transfers between devices, per_device(): packs = lax.all_gather(pack, 'dp', axis=0, tiled=True)  13.9 us
    pallas_call x7, Pallas kernels, call(): pl.pallas_call(kernel, out_shape=tuple(outs), in_specs=in_specs or [full]...  13.2 us
    pallas_call x1, Pallas kernels, per_device(): pl.pallas_call(functools.partial(update_kernel, nmp, owners, cols), out_s...  12.2 us
    all_to_all x1, blocking collectives, per_device(): sums = exchange(lax.all_to_all(send, 'dp', 0, 0, tiled=True), 'mp')  10.2 us
    all_to_all x1, starting transfers between devices, per_device(): packets = lax.all_to_all(packet, 'dp', 0, 0, tiled=True)  6.91 us
  transfers between devices with their start and end apart: 31, of which 16 were waited for; matrix products, arithmetic and copies ran while one was open for 0% of the time, Pallas kernels for 5%

profile of v1, /device:TPU:0, one launch (start us, length us, event | category | flops | bytes accessed | tf_op | source)
XLA Modules:
  0.0 166.6 jit_solution(14405036367421850003)
XLA Ops:
  7.2 1.0 convert_element_type.3
  8.4 6.0 %collective-permute-start.13 = (bf16[96,512]{1,0:T(8,128)(2,1)S(1)}, bf16[96,512]{1,0:T(8,128)(2,1)S(1)}, u32[]{:S(2)}, u32[]{:S(2)}) collective-permute-start(bf16[96,512]{1,0:T(8,128)(2,1)S(1)} %pad_maximum_fusion.1.refs_11_.refs_5_.refs_13_.refs_24_), channel_id=1, source_target_pairs={{0,28},{4,24},{8,20},{12,16},{16,12},{20,8},{24,4},{28,0},{1,29},{... | collective-permute-start | bytes 294920 | tf_op jit(solution)/shard_map/ppermute | solution.py:558
  14.7 0.8 collective-permute-start.11
  15.4 2.0 %collective-permute-start.10 = (bf16[96,512]{1,0:T(8,128)(2,1)S(1)}, bf16[96,512]{1,0:T(8,128)(2,1)S(1)}, u32[]{:S(2)}, u32[]{:S(2)}) collective-permute-start(bf16[96,512]{1,0:T(8,128)(2,1)S(1)} %pad_maximum_fusion.1.refs_11_.refs_5_.refs_13_.refs_24_), channel_id=1, source_target_pairs={{0,16},{4,20},{8,24},{12,28},{16,0},{20,4},{24,8},{28,12},{1,17},{... | collective-permute-start | bytes 294920 | tf_op jit(solution)/shard_map/ppermute | solution.py:558
  17.6 4.7 %collective-permute-start.6 = (bf16[96,640]{1,0:T(8,128)(2,1)S(1)}, bf16[96,640]{1,0:T(8,128)(2,1)S(1)}, u32[]{:S(2)}, u32[]{:S(2)}) collective-permute-start(bf16[96,640]{1,0:T(8,128)(2,1)S(1)} %pad_maximum_fusion.refs_3_.refs_16_), channel_id=1, source_target_pairs={{0,28},{4,24},{8,20},{12,16},{16,12},{20,8},{24,4},{28,0},{1,29},{... | collective-permute-start | bytes 368648 | tf_op jit(solution)/shard_map/ppermute | solution.py:558
  22.5 11.7 %collective-permute-start.9 = (bf16[96,512]{1,0:T(8,128)(2,1)S(1)}, bf16[96,512]{1,0:T(8,128)(2,1)S(1)}, u32[]{:S(2)}, u32[]{:S(2)}) collective-permute-start(bf16[96,512]{1,0:T(8,128)(2,1)S(1)} %pad_maximum_fusion.1.refs_11_.refs_5_.refs_13_.refs_24_), channel_id=1, source_target_pairs={{0,12},{4,8},{8,4},{12,0},{16,28},{20,24},{24,20},{28,16},{1,13},{... | collective-permute-start | bytes 294920 | tf_op jit(solution)/shard_map/ppermute | solution.py:558
  34.3 1.1 collective-permute-done.11.refs_16_.refs_10_.refs_18_.refs_29_
  35.4 2.0 %collective-permute-done.10.refs_15_.refs_9_.refs_17_.refs_28_ = bf16[96,512]{1,0:T(8,128)(2,1)S(1)} collective-permute-done((bf16[96,512]{1,0:T(8,128)(2,1)S(1)}, bf16[96,512]{1,0:T(8,128)(2,1)S(1)}, u32[]{:S(2)}, u32[]{:S(2)}) %collective-permute-start.10) | collective-permute-done | bytes 98336 | tf_op jit(solution)/shard_map/ppermute | solution.py:558
  38.0 0.8 collective-permute-done.9.refs_14_.refs_8_.refs_16_.refs_27_
  38.8 2.5 %collective-permute-start.4 = (bf16[96,640]{1,0:T(8,128)(2,1)S(1)}, bf16[96,640]{1,0:T(8,128)(2,1)S(1)}, u32[]{:S(2)}, u32[]{:S(2)}) collective-permute-start(bf16[96,640]{1,0:T(8,128)(2,1)S(1)} %pad_maximum_fusion.refs_3_.refs_16_), channel_id=1, source_target_pairs={{0,20},{4,16},{8,28},{12,24},{16,4},{20,0},{24,12},{28,8},{1,21},{... | collective-permute-start | bytes 368648 | tf_op jit(solution)/shard_map/ppermute | solution.py:558
  41.2 1.2 collective-permute-start.3
  42.4 2.5 %collective-permute-start.2 = (bf16[96,640]{1,0:T(8,128)(2,1)S(1)}, bf16[96,640]{1,0:T(8,128)(2,1)S(1)}, u32[]{:S(2)}, u32[]{:S(2)}) collective-permute-start(bf16[96,640]{1,0:T(8,128)(2,1)S(1)} %pad_maximum_fusion.refs_3_.refs_16_), channel_id=1, source_target_pairs={{0,12},{4,8},{8,4},{12,0},{16,28},{20,24},{24,20},{28,16},{1,13},{... | collective-permute-start | bytes 368648 | tf_op jit(solution)/shard_map/ppermute | solution.py:558
  45.0 0.9 collective-permute-start
  45.9 0.8 copy-done.7
  46.7 1.1 copy-done.9
  47.8 0.7 copy-done.39
  48.5 0.8 copy-done.46
  49.4 0.7 copy-done.47
  50.7 1.1 shard_map.306
  51.9 1.1 copy-done.5
  53.0 0.8 copy-done.13
  54.1 2.7 %shard_map.307 = (bf16[24,768]{1,0:T(8,128)(2,1)S(1)}, bf16[192,1024]{1,0:T(8,128)(2,1)S(1)}, bf16[1024,256]{1,0:T(8,128)(2,1)S(1)}, bf16[24,256]{1,0:T(8,128)(2...) custom-call(bf16[1024,768]{1,0:T(8,128)(2,1)S(1)} %get-tuple-element.65.refs_0_.refs_11_, ...), custom_call_target="tpu_custom_call" | custom-call | flops 805306368 | bytes 4748288 | tf_op jit(solution)/shard_map/pallas_call | solution.py:51
  56.8 0.8 copy-done.15
  57.6 0.7 copy-done.23
  58.4 0.7 collective-permute-start.16
  59.1 0.9 collective-permute-start.15
  60.2 1.8 %collective-permute-done.16.refs_3_ = bf16[24,768]{1,0:T(8,128)(2,1)S(1)} collective-permute-done((bf16[24,768]{1,0:T(8,128)(2,1)S(1)}, bf16[24,768]{1,0:T(8,128)(2,1)S(1)}, u32[]{:S(2)}, u32[]{:S(2)}) %collective-permute-start.16) | collective-permute-done | bytes 36896 | tf_op jit(solution)/shard_map/ppermute | solution.py:558
  62.1 1.3 collective-permute-done.15.refs_2_
  64.6 1.1 collective-permute-start.18
  65.9 1.7 %collective-permute-done.19.refs_3_ = bf16[24,768]{1,0:T(8,128)(2,1)S(1)} collective-permute-done((bf16[24,768]{1,0:T(8,128)(2,1)S(1)}, bf16[24,768]{1,0:T(8,128)(2,1)S(1)}, u32[]{:S(2)}, u32[]{:S(2)}) %collective-permute-start.19) | collective-permute-done | bytes 36896 | tf_op jit(solution)/shard_map/ppermute | solution.py:558
  67.6 1.0 collective-permute-done.18.refs_2_
  68.7 1.6 shard_map.309
  73.0 1.4 collective-permute-start.21
  74.8 2.1 %collective-permute-done.22.refs_3_ = bf16[24,768]{1,0:T(8,128)(2,1)S(1)} collective-permute-done((bf16[24,768]{1,0:T(8,128)(2,1)}, bf16[24,768]{1,0:T(8,128)(2,1)S(1)}, u32[]{:S(2)}, u32[]{:S(2)}) %collective-permute-start.22) | collective-permute-done | bytes 36896 | tf_op jit(solution)/shard_map/ppermute | solution.py:558
  76.9 0.7 collective-permute-done.21.refs_2_
  77.7 1.4 copy-done.6
  79.1 1.0 copy-done.14
  80.1 1.1 copy-done.16
  81.2 0.9 copy-done.18
  82.1 0.9 copy-done.20
  83.0 0.9 copy-done.22
  83.9 1.0 copy-done.24
  84.9 1.0 copy-done.26
  85.9 0.9 copy-done.28
  86.8 0.7 copy-done.32
  87.5 0.9 copy-done.34
  88.4 0.8 copy-done.38
  89.2 3.3 %shard_map.310 = (bf16[64,768]{1,0:T(8,128)(2,1)S(1)}, bf16[64,768]{1,0:T(8,128)(2,1)S(1)}, bf16[64,768]{1,0:T(8,128)(2,1)S(1)}, bf16[64,768]{1,0:T(8,128)(2,1)S...) custom-call(bf16[24,768]{1,0:T(8,128)(2,1)S(1)} %copy-done.38, ...), custom_call_target="tpu_custom_call" | custom-call | flops 1610612736 | bytes 8426496 | tf_op jit(solution)/shard_map/pallas_call | solution.py:51
  92.7 0.9 collective-permute-start.24
  93.7 0.8 collective-permute-start.25
  94.5 3.9 %collective-permute-done.24.refs_2_ = bf16[64,768]{1,0:T(8,128)(2,1)S(1)} collective-permute-done((bf16[64,768]{1,0:T(8,128)(2,1)S(1)}, bf16[64,768]{1,0:T(8,128)(2,1)S(1)}, u32[]{:S(2)}, u32[]{:S(2)}) %collective-permute-start.24) | collective-permute-done | bytes 98336 | tf_op jit(solution)/shard_map/ppermute | solution.py:659
  98.4 1.0 collective-permute-done.25.refs_3_
  99.4 0.9 shard_map.311
  100.3 6.9 %all-to-all-start = ((bf16[8,128,256]{2,1,0:T(8,128)(2,1)}), bf16[8,128,256]{2,1,0:T(8,128)(2,1)S(1)}, u32[]{:S(2)}, u32[]{:S(2)}) async-start(bf16[8,128,256]{2,1,0:T(8,128)(2,1)} %shard_map.311), calls=%async_computation | async-start | bytes 1048576 | tf_op jit(solution)/shard_map/all_to_all | solution.py:669
  107.2 13.9 %all-gather.2.cloned.1.call-done.head_in.grad_mid.normed.grad_low.act.grad_hidden.ctx = bf16[192,3840]{1,0:T(8,128)(2,1)} async-done(((bf16[24,3840]{1,0:T(8,128)(2,1)}), bf16[192,3840]{1,0:T(8,128)(2,1)}) %all-gather.2.cloned.1.call-update) | async-done | bytes 1474576 | tf_op jit(solution)/shard_map/all_gather | solution.py:641
  121.0 1.4 copy-done
  122.4 0.8 shard_map.312
  123.2 1.4 copy-done.3
  124.6 3.1 %all-to-all-done.packets = bf16[8,128,256]{2,1,0:T(8,128)(2,1)S(1)} async-done(((bf16[8,128,256]{2,1,0:T(8,128)(2,1)}), bf16[8,128,256]{2,1,0:T(8,128)(2,1)S(1)}, u32[]{:S(2)}, u32[]{:S(2)}) %all-to-all-start) | async-done | bytes 524320 | tf_op jit(solution)/shard_map/all_to_all | solution.py:669
  128.2 10.2 %all_to_all.10.refs_0_ = bf16[8,16,512]{2,1,0:T(8,128)(2,1)S(1)} all-to-all(bf16[8,16,512]{2,1,0:T(8,128)(2,1)S(1)} %get-tuple-element.92), channel_id=1, replica_groups=mesh['dp'=8,'mp'=4] {'dp'}, dimensions={0} | all-to-all | bytes 262144 | tf_op jit(solution)/shard_map/all_to_all | solution.py:719
  138.3 2.0 %collective-permute-start.27 = (bf16[8,16,512]{2,1,0:T(8,128)(2,1)S(1)}, bf16[8,16,512]{2,1,0:T(8,128)(2,1)S(1)}, u32[]{:S(2)}, u32[]{:S(2)}) collective-permute-start(bf16[8,16,512]{2,1,0:T(8,128)(2,1)S(1)} %all_to_all.10.refs_0_), channel_id=1, source_target_pairs={{0,2},{1,3},{2,0},{3,1},{4,6},{5,7},{6,4},{7,5},{8,10},{9,11},{10,... | collective-permute-start | bytes 393224 | tf_op jit(solution)/shard_map/ppermute | solution.py:558
  140.4 3.0 %shard_map.314 = (f32[6,96,96]{2,1,0:T(8,128)S(1)}, f32[6,192,192]{2,1,0:T(8,128)S(1)}, f32[6,96,192]{2,1,0:T(8,128)S(1)}) custom-call(f32[6,96,192]{2,1,0:T(8,128)S(1)} %get-tuple-element.95.layer.refs_6_, f32[6,96,96]{2,1,0:T(8,128)S(1)} %bitcast.19, f32[6,192,192]{2,1,0:T(8,128)S(1)} %bitcast.18), custom_call_target="tpu_custom_call" | custom-call | flops 764411904 | bytes 3096576 | tf_op jit(solution)/shard_map/pallas_call | solution.py:51
  143.7 3.3 %collective-permute-done.27.refs_2_ = bf16[8,16,512]{2,1,0:T(8,128)(2,1)S(1)} collective-permute-done((bf16[8,16,512]{2,1,0:T(8,128)(2,1)S(1)}, bf16[8,16,512]{2,1,0:T(8,128)(2,1)S(1)}, u32[]{:S(2)}, u32[]{:S(2)}) %collective-permute-start.27) | collective-permute-done | bytes 131104 | tf_op jit(solution)/shard_map/ppermute | solution.py:558
  147.0 12.2 %shard_map.315 = (f32[8,128]{1,0:T(8,128)S(1)}, f32[96,1152]{1,0:T(8,128)}, f32[96,1152]{1,0:T(8,128)}, f32[6,96,96]{2,1,0:T(8,128)}, f32[6,192,192]{2,1,0:T(8,1...) custom-call(bf16[8,16,512]{2,1,0:T(8,128)(2,1)S(1)} %all_to_all.10.r, ...), custom_call_target="tpu_custom_call" | custom-call | flops 11796480 | bytes 16515072 | tf_op jit(solution)/shard_map/pallas_call | solution.py:738
  (116 shorter events, 8.9 us)
Async XLA Ops:
  7.2 46.9 %copy-start.40 = (s32[1,1024]{1,0:T(1,128)S(1)}, s32[1,1024]{1,0:T(1,128)}, u32[]{:S(2)}) copy-start(s32[1,1024]{1,0:T(1,128)} %refs_15_.2) | copy-start | bytes 12292
  7.2 113.8 %all-gather.2.cloned.1.call-start = ((), (), s32[]{:S(2)}) async-start(), calls=%async_computation.2 | async-start | bytes 1658880 | tf_op jit(solution)/shard_map/all_gather | solution.py:641
  8.4 13.9 %collective-permute-start.13 = (bf16[96,512]{1,0:T(8,128)(2,1)S(1)}, bf16[96,512]{1,0:T(8,128)(2,1)S(1)}, u32[]{:S(2)}, u32[]{:S(2)}) collective-permute-start(bf16[96,512]{1,0:T(8,128)(2,1)S(1)} %pad_maximum_fusion.1.refs_11_.refs_5_.refs_13_.refs_24_), channel_id=1, source_target_pairs={{0,28},{4,24},{8,20},{12,16},{16,12},{20,8},{24,4},{28,0},{1,29},{... | collective-permute-start | bytes 294920 | tf_op jit(solution)/shard_map/ppermute | solution.py:558
  14.4 8.1 %collective-permute-start.12 = (bf16[96,512]{1,0:T(8,128)(2,1)S(1)}, bf16[96,512]{1,0:T(8,128)(2,1)S(1)}, u32[]{:S(2)}, u32[]{:S(2)}) collective-permute-start(bf16[96,512]{1,0:T(8,128)(2,1)S(1)} %pad_maximum_fusion.1.refs_11_.refs_5_.refs_13_.refs_24_), channel_id=1, source_target_pairs={{0,24},{4,28},{8,16},{12,20},{16,8},{20,12},{24,0},{28,4},{1,25},{... | collective-permute-start | bytes 294920 | tf_op jit(solution)/shard_map/ppermute | solution.py:558
  14.7 20.7 %collective-permute-start.11 = (bf16[96,512]{1,0:T(8,128)(2,1)S(1)}, bf16[96,512]{1,0:T(8,128)(2,1)S(1)}, u32[]{:S(2)}, u32[]{:S(2)}) collective-permute-start(bf16[96,512]{1,0:T(8,128)(2,1)S(1)} %pad_maximum_fusion.1.refs_11_.refs_5_.refs_13_.refs_24_), channel_id=1, source_target_pairs={{0,20},{4,16},{8,28},{12,24},{16,4},{20,0},{24,12},{28,8},{1,21},{... | collective-permute-start | bytes 294920 | tf_op jit(solution)/shard_map/ppermute | solution.py:558
  15.4 21.9 %collective-permute-start.10 = (bf16[96,512]{1,0:T(8,128)(2,1)S(1)}, bf16[96,512]{1,0:T(8,128)(2,1)S(1)}, u32[]{:S(2)}, u32[]{:S(2)}) collective-permute-start(bf16[96,512]{1,0:T(8,128)(2,1)S(1)} %pad_maximum_fusion.1.refs_11_.refs_5_.refs_13_.refs_24_), channel_id=1, source_target_pairs={{0,16},{4,20},{8,24},{12,28},{16,0},{20,4},{24,8},{28,12},{1,17},{... | collective-permute-start | bytes 294920 | tf_op jit(solution)/shard_map/ppermute | solution.py:558
  17.6 27.4 %collective-permute-start.6 = (bf16[96,640]{1,0:T(8,128)(2,1)S(1)}, bf16[96,640]{1,0:T(8,128)(2,1)S(1)}, u32[]{:S(2)}, u32[]{:S(2)}) collective-permute-start(bf16[96,640]{1,0:T(8,128)(2,1)S(1)} %pad_maximum_fusion.refs_3_.refs_16_), channel_id=1, source_target_pairs={{0,28},{4,24},{8,20},{12,16},{16,12},{20,8},{24,4},{28,0},{1,29},{... | collective-permute-start | bytes 368648 | tf_op jit(solution)/shard_map/ppermute | solution.py:558
  22.3 22.7 %collective-permute-start.5 = (bf16[96,640]{1,0:T(8,128)(2,1)S(1)}, bf16[96,640]{1,0:T(8,128)(2,1)S(1)}, u32[]{:S(2)}, u32[]{:S(2)}) collective-permute-start(bf16[96,640]{1,0:T(8,128)(2,1)S(1)} %pad_maximum_fusion.refs_3_.refs_16_), channel_id=1, source_target_pairs={{0,24},{4,28},{8,16},{12,20},{16,8},{20,12},{24,0},{28,4},{1,25},{... | collective-permute-start | bytes 368648 | tf_op jit(solution)/shard_map/ppermute | solution.py:558
  22.5 16.2 %collective-permute-start.9 = (bf16[96,512]{1,0:T(8,128)(2,1)S(1)}, bf16[96,512]{1,0:T(8,128)(2,1)S(1)}, u32[]{:S(2)}, u32[]{:S(2)}) collective-permute-start(bf16[96,512]{1,0:T(8,128)(2,1)S(1)} %pad_maximum_fusion.1.refs_11_.refs_5_.refs_13_.refs_24_), channel_id=1, source_target_pairs={{0,12},{4,8},{8,4},{12,0},{16,28},{20,24},{24,20},{28,16},{1,13},{... | collective-permute-start | bytes 294920 | tf_op jit(solution)/shard_map/ppermute | solution.py:558
  35.4 5.9 %collective-permute-start.8 = (bf16[96,512]{1,0:T(8,128)(2,1)S(1)}, bf16[96,512]{1,0:T(8,128)(2,1)S(1)}, u32[]{:S(2)}, u32[]{:S(2)}) collective-permute-start(bf16[96,512]{1,0:T(8,128)(2,1)S(1)} %pad_maximum_fusion.1.refs_11_.refs_5_.refs_13_.refs_24_), channel_id=1, source_target_pairs={{0,8},{4,12},{8,0},{12,4},{16,24},{20,28},{24,16},{28,20},{1,9},{5... | collective-permute-start | bytes 294920 | tf_op jit(solution)/shard_map/ppermute | solution.py:558
  37.3 5.1 %collective-permute-start.7 = (bf16[96,512]{1,0:T(8,128)(2,1)S(1)}, bf16[96,512]{1,0:T(8,128)(2,1)S(1)}, u32[]{:S(2)}, u32[]{:S(2)}) collective-permute-start(bf16[96,512]{1,0:T(8,128)(2,1)S(1)} %pad_maximum_fusion.1.refs_11_.refs_5_.refs_13_.refs_24_), channel_id=1, source_target_pairs={{0,4},{4,0},{8,12},{12,8},{16,20},{20,16},{24,28},{28,24},{1,5},{5... | collective-permute-start | bytes 294920 | tf_op jit(solution)/shard_map/ppermute | solution.py:558
  38.8 15.0 %collective-permute-start.4 = (bf16[96,640]{1,0:T(8,128)(2,1)S(1)}, bf16[96,640]{1,0:T(8,128)(2,1)S(1)}, u32[]{:S(2)}, u32[]{:S(2)}) collective-permute-start(bf16[96,640]{1,0:T(8,128)(2,1)S(1)} %pad_maximum_fusion.refs_3_.refs_16_), channel_id=1, source_target_pairs={{0,20},{4,16},{8,28},{12,24},{16,4},{20,0},{24,12},{28,8},{1,21},{... | collective-permute-start | bytes 368648 | tf_op jit(solution)/shard_map/ppermute | solution.py:558
  41.2 12.6 %collective-permute-start.3 = (bf16[96,640]{1,0:T(8,128)(2,1)S(1)}, bf16[96,640]{1,0:T(8,128)(2,1)S(1)}, u32[]{:S(2)}, u32[]{:S(2)}) collective-permute-start(bf16[96,640]{1,0:T(8,128)(2,1)S(1)} %pad_maximum_fusion.refs_3_.refs_16_), channel_id=1, source_target_pairs={{0,16},{4,20},{8,24},{12,28},{16,0},{20,4},{24,8},{28,12},{1,17},{... | collective-permute-start | bytes 368648 | tf_op jit(solution)/shard_map/ppermute | solution.py:558
  42.4 11.4 %collective-permute-start.2 = (bf16[96,640]{1,0:T(8,128)(2,1)S(1)}, bf16[96,640]{1,0:T(8,128)(2,1)S(1)}, u32[]{:S(2)}, u32[]{:S(2)}) collective-permute-start(bf16[96,640]{1,0:T(8,128)(2,1)S(1)} %pad_maximum_fusion.refs_3_.refs_16_), channel_id=1, source_target_pairs={{0,12},{4,8},{8,4},{12,0},{16,28},{20,24},{24,20},{28,16},{1,13},{... | collective-permute-start | bytes 368648 | tf_op jit(solution)/shard_map/ppermute | solution.py:558
  45.0 9.1 %collective-permute-start.1 = (bf16[96,640]{1,0:T(8,128)(2,1)S(1)}, bf16[96,640]{1,0:T(8,128)(2,1)S(1)}, u32[]{:S(2)}, u32[]{:S(2)}) collective-permute-start(bf16[96,640]{1,0:T(8,128)(2,1)S(1)} %pad_maximum_fusion.refs_3_.refs_16_), channel_id=1, source_target_pairs={{0,8},{4,12},{8,0},{12,4},{16,24},{20,28},{24,16},{28,20},{1,9},{5... | collective-permute-start | bytes 368648 | tf_op jit(solution)/shard_map/ppermute | solution.py:558
  45.0 9.1 %collective-permute-start = (bf16[96,640]{1,0:T(8,128)(2,1)S(1)}, bf16[96,640]{1,0:T(8,128)(2,1)S(1)}, u32[]{:S(2)}, u32[]{:S(2)}) collective-permute-start(bf16[96,640]{1,0:T(8,128)(2,1)S(1)} %pad_maximum_fusion.refs_3_.refs_16_), channel_id=1, source_target_pairs={{0,4},{4,0},{8,12},{12,8},{16,20},{20,16},{24,28},{28,24},{1,5},{5... | collective-permute-start | bytes 368648 | tf_op jit(solution)/shard_map/ppermute | solution.py:558
  46.7 1.1 copy-start.9
  51.8 1.1 copy-start.5
  53.8 14.9 %copy-start.2 = (f32[768,768]{1,0:T(8,128)S(1)}, f32[768,768]{1,0:T(8,128)}, u32[]{:S(2)}) copy-start(f32[768,768]{1,0:T(8,128)} %refs_16_.1) | copy-start | bytes 7077892
  53.8 14.9 %copy-start.43 = (f32[1,24]{1,0:T(1,128)S(1)}, f32[1,24]{1,0:T(1,128)}, u32[]{:S(2)}) copy-start(f32[1,24]{1,0:T(1,128)} %refs_7_.2) | copy-start | bytes 292
  53.8 16.4 %copy-start.17 = (bf16[96,640]{1,0:T(8,128)(2,1)}, bf16[96,640]{1,0:T(8,128)(2,1)S(1)}, u32[]{:S(2)}) copy-start(bf16[96,640]{1,0:T(8,128)(2,1)S(1)} %collective-permute-done.2.refs_6_.refs_19_) | copy-start | bytes 368644
  54.1 16.2 %copy-start.19 = (bf16[96,640]{1,0:T(8,128)(2,1)}, bf16[96,640]{1,0:T(8,128)(2,1)S(1)}, u32[]{:S(2)}) copy-start(bf16[96,640]{1,0:T(8,128)(2,1)S(1)} %collective-permute-done.1.refs_5_.refs_18_) | copy-start | bytes 368644
  54.1 16.2 %copy-start.21 = (bf16[96,640]{1,0:T(8,128)(2,1)}, bf16[96,640]{1,0:T(8,128)(2,1)S(1)}, u32[]{:S(2)}) copy-start(bf16[96,640]{1,0:T(8,128)(2,1)S(1)} %collective-permute-done.refs_4_.refs_17_) | copy-start | bytes 368644
  58.4 12.0 %copy-start.25 = (bf16[768,256]{1,0:T(8,128)(2,1)}, bf16[768,256]{1,0:T(8,128)(2,1)S(1)}, u32[]{:S(2)}) copy-start(bf16[768,256]{1,0:T(8,128)(2,1)S(1)} %get-tuple-element.76.refs_8_) | copy-start | bytes 1179652
  58.4 12.0 %copy-start.41 = (f32[8,256]{1,0:T(8,128)}, f32[8,256]{1,0:T(8,128)S(1)}, u32[]{:S(2)}) copy-start(f32[8,256]{1,0:T(8,128)S(1)} %get-tuple-element.89.query) | copy-start | bytes 24580
  58.4 19.3 %copy-start.8 = (f32[11,768]{1,0:T(8,128)S(1)}, f32[11,768]{1,0:T(8,128)}, u32[]{:S(2)}) copy-start(f32[11,768]{1,0:T(8,128)} %refs_20_.1) | copy-start | bytes 101380
  58.4 3.7 %collective-permute-start.16 = (bf16[24,768]{1,0:T(8,128)(2,1)S(1)}, bf16[24,768]{1,0:T(8,128)(2,1)S(1)}, u32[]{:S(2)}, u32[]{:S(2)}) collective-permute-start(bf16[24,768]{1,0:T(8,128)(2,1)S(1)} %get-tuple-element.66.refs_0_), channel_id=1, source_target_pairs={{0,3},{1,2},{2,1},{3,0},{4,7},{5,6},{6,5},{7,4},{8,11},{9,10},{10,... | collective-permute-start | bytes 110600 | tf_op jit(solution)/shard_map/ppermute | solution.py:558
  59.1 4.3 %collective-permute-start.15 = (bf16[24,768]{1,0:T(8,128)(2,1)S(1)}, bf16[24,768]{1,0:T(8,128)(2,1)S(1)}, u32[]{:S(2)}, u32[]{:S(2)}) collective-permute-start(bf16[24,768]{1,0:T(8,128)(2,1)S(1)} %get-tuple-element.66.refs_0_), channel_id=1, source_target_pairs={{0,2},{1,3},{2,0},{3,1},{4,6},{5,7},{6,4},{7,5},{8,10},{9,11},{10,... | collective-permute-start | bytes 110600 | tf_op jit(solution)/shard_map/ppermute | solution.py:558
  60.0 3.4 %collective-permute-start.14 = (bf16[24,768]{1,0:T(8,128)(2,1)S(1)}, bf16[24,768]{1,0:T(8,128)(2,1)S(1)}, u32[]{:S(2)}, u32[]{:S(2)}) collective-permute-start(bf16[24,768]{1,0:T(8,128)(2,1)S(1)} %get-tuple-element.66.refs_0_), channel_id=1, source_target_pairs={{0,1},{1,0},{2,3},{3,2},{4,5},{5,4},{6,7},{7,6},{8,9},{9,8},{10,11... | collective-permute-start | bytes 110600 | tf_op jit(solution)/shard_map/ppermute | solution.py:558
  64.0 6.3 %copy-start.27 = (f32[24,768]{1,0:T(8,128)}, f32[24,768]{1,0:T(8,128)S(1)}, u32[]{:S(2)}) copy-start(f32[24,768]{1,0:T(8,128)S(1)} %get-tuple-element.68.refs_4_) | copy-start | bytes 221188
  64.0 3.6 %collective-permute-start.19 = (bf16[24,768]{1,0:T(8,128)(2,1)S(1)}, bf16[24,768]{1,0:T(8,128)(2,1)S(1)}, u32[]{:S(2)}, u32[]{:S(2)}) collective-permute-start(bf16[24,768]{1,0:T(8,128)(2,1)S(1)} %get-tuple-element.67.refs_0_), channel_id=1, source_target_pairs={{0,3},{1,2},{2,1},{3,0},{4,7},{5,6},{6,5},{7,4},{8,11},{9,10},{10,... | collective-permute-start | bytes 110600 | tf_op jit(solution)/shard_map/ppermute | solution.py:558
  64.6 4.0 %collective-permute-start.18 = (bf16[24,768]{1,0:T(8,128)(2,1)S(1)}, bf16[24,768]{1,0:T(8,128)(2,1)S(1)}, u32[]{:S(2)}, u32[]{:S(2)}) collective-permute-start(bf16[24,768]{1,0:T(8,128)(2,1)S(1)} %get-tuple-element.67.refs_0_), channel_id=1, source_target_pairs={{0,2},{1,3},{2,0},{3,1},{4,6},{5,7},{6,4},{7,5},{8,10},{9,11},{10,... | collective-permute-start | bytes 110600 | tf_op jit(solution)/shard_map/ppermute | solution.py:558
  65.7 2.9 %collective-permute-start.17 = (bf16[24,768]{1,0:T(8,128)(2,1)S(1)}, bf16[24,768]{1,0:T(8,128)(2,1)S(1)}, u32[]{:S(2)}, u32[]{:S(2)}) collective-permute-start(bf16[24,768]{1,0:T(8,128)(2,1)S(1)} %get-tuple-element.67.refs_0_), channel_id=1, source_target_pairs={{0,1},{1,0},{2,3},{3,2},{4,5},{5,4},{6,7},{7,6},{8,9},{9,8},{10,11... | collective-permute-start | bytes 110600 | tf_op jit(solution)/shard_map/ppermute | solution.py:558
  72.9 4.1 %collective-permute-start.22 = (bf16[24,768]{1,0:T(8,128)(2,1)}, bf16[24,768]{1,0:T(8,128)(2,1)S(1)}, u32[]{:S(2)}, u32[]{:S(2)}) collective-permute-start(bf16[24,768]{1,0:T(8,128)(2,1)} %copy-done.37), channel_id=1, source_target_pairs={{0,3},{1,2},{2,1},{3,0},{4,7},{5,6},{6,5},{7,4},{8,11},{9,10},{10,... | collective-permute-start | bytes 110600 | tf_op jit(solution)/shard_map/ppermute | solution.py:558
  73.0 4.7 %collective-permute-start.21 = (bf16[24,768]{1,0:T(8,128)(2,1)}, bf16[24,768]{1,0:T(8,128)(2,1)S(1)}, u32[]{:S(2)}, u32[]{:S(2)}) collective-permute-start(bf16[24,768]{1,0:T(8,128)(2,1)} %copy-done.37), channel_id=1, source_target_pairs={{0,2},{1,3},{2,0},{3,1},{4,6},{5,7},{6,4},{7,5},{8,10},{9,11},{10,... | collective-permute-start | bytes 110600 | tf_op jit(solution)/shard_map/ppermute | solution.py:558
  74.4 3.3 %collective-permute-start.20 = (bf16[24,768]{1,0:T(8,128)(2,1)}, bf16[24,768]{1,0:T(8,128)(2,1)S(1)}, u32[]{:S(2)}, u32[]{:S(2)}) collective-permute-start(bf16[24,768]{1,0:T(8,128)(2,1)} %copy-done.37), channel_id=1, source_target_pairs={{0,1},{1,0},{2,3},{3,2},{4,5},{5,4},{6,7},{7,6},{8,9},{9,8},{10,11... | collective-permute-start | bytes 110600 | tf_op jit(solution)/shard_map/ppermute | solution.py:558
  77.7 1.4 copy-start.6
  79.1 1.0 copy-start.14
  80.1 1.1 copy-start.16
  81.2 0.9 copy-start.18
  82.1 0.9 copy-start.20
  83.0 0.9 copy-start.22
  83.9 1.0 copy-start.24
  84.9 1.0 copy-start.26
  92.5 1.9 %collective-permute-start.23 = (bf16[64,768]{1,0:T(8,128)(2,1)S(1)}, bf16[64,768]{1,0:T(8,128)(2,1)S(1)}, u32[]{:S(2)}, u32[]{:S(2)}) collective-permute-start(bf16[64,768]{1,0:T(8,128)(2,1)S(1)} %get-tuple-element.83), channel_id=1, source_target_pairs={{0,1},{1,0},{2,3},{3,2},{4,5},{5,4},{6,7},{7,6},{8,9},{9,8},{10,11... | collective-permute-start | bytes 294920 | tf_op jit(solution)/shard_map/ppermute | solution.py:659
  92.7 5.6 %collective-permute-start.24 = (bf16[64,768]{1,0:T(8,128)(2,1)S(1)}, bf16[64,768]{1,0:T(8,128)(2,1)S(1)}, u32[]{:S(2)}, u32[]{:S(2)}) collective-permute-start(bf16[64,768]{1,0:T(8,128)(2,1)S(1)} %get-tuple-element.84), channel_id=1, source_target_pairs={{0,2},{1,3},{2,0},{3,1},{4,6},{5,7},{6,4},{7,5},{8,10},{9,11},{10,... | collective-permute-start | bytes 294920 | tf_op jit(solution)/shard_map/ppermute | solution.py:659
  93.7 5.7 %collective-permute-start.25 = (bf16[64,768]{1,0:T(8,128)(2,1)S(1)}, bf16[64,768]{1,0:T(8,128)(2,1)S(1)}, u32[]{:S(2)}, u32[]{:S(2)}) collective-permute-start(bf16[64,768]{1,0:T(8,128)(2,1)S(1)} %get-tuple-element.85), channel_id=1, source_target_pairs={{0,3},{1,2},{2,1},{3,0},{4,7},{5,6},{6,5},{7,4},{8,11},{9,10},{10,... | collective-permute-start | bytes 294920 | tf_op jit(solution)/shard_map/ppermute | solution.py:659
  100.3 27.4 %all-to-all-start = ((bf16[8,128,256]{2,1,0:T(8,128)(2,1)}), bf16[8,128,256]{2,1,0:T(8,128)(2,1)S(1)}, u32[]{:S(2)}, u32[]{:S(2)}) async-start(bf16[8,128,256]{2,1,0:T(8,128)(2,1)} %shard_map.311), calls=%async_computation | async-start | bytes 1048576 | tf_op jit(solution)/shard_map/all_to_all | solution.py:669
  121.0 1.4 copy-start
  122.4 5.2 %copy-start.1 = (bf16[192,3840]{1,0:T(8,128)(2,1)S(1)}, bf16[192,3840]{1,0:T(8,128)(2,1)}, u32[]{:S(2)}) copy-start(bf16[192,3840]{1,0:T(8,128)(2,1)} %all-gather.2.cloned.1.call-done.head_in.grad_mid.normed.grad_low.act.grad_hidden.ctx) | copy-start | bytes 4423684
  122.4 5.2 %copy-start.42 = (f32[8,256]{1,0:T(8,128)S(1)}, f32[8,256]{1,0:T(8,128)}, u32[]{:S(2)}) copy-start(f32[8,256]{1,0:T(8,128)} %copy-done.41) | copy-start | bytes 24580
  123.2 1.4 copy-start.3
  127.6 12.8 %copy-start.44 = (f32[1,6,192,192]{3,2,1,0:T(8,128)S(1)}, f32[1,6,192,192]{3,2,1,0:T(8,128)}, u32[]{:S(2)}) copy-start(f32[1,6,192,192]{3,2,1,0:T(8,128)} %param.28) | copy-start | bytes 2654212
  127.6 12.8 %copy-start.45 = (f32[96,6,96]{2,0,1:T(8,128)S(1)}, f32[96,6,96]{2,0,1:T(8,128)}, u32[]{:S(2)}) copy-start(f32[96,6,96]{2,0,1:T(8,128)} %param.27) | copy-start | bytes 663556
  127.6 19.3 %copy-start.4 = (f32[96,1152]{1,0:T(8,128)S(1)}, f32[96,1152]{1,0:T(8,128)}, u32[]{:S(2)}) copy-start(f32[96,1152]{1,0:T(8,128)} %refs_10_.1) | copy-start | bytes 1327108
  127.6 19.3 %copy-start.10 = (f32[224,768]{1,0:T(8,128)S(1)}, f32[224,768]{1,0:T(8,128)}, u32[]{:S(2)}) copy-start(f32[224,768]{1,0:T(8,128)} %refs_13_.1) | copy-start | bytes 2064388
  127.7 19.3 %copy-start.11 = (f32[224,768]{1,0:T(8,128)S(1)}, f32[224,768]{1,0:T(8,128)}, u32[]{:S(2)}) copy-start(f32[224,768]{1,0:T(8,128)} %refs_14_.1) | copy-start | bytes 2064388
  127.7 19.3 %copy-start.12 = (f32[224,768]{1,0:T(8,128)S(1)}, f32[224,768]{1,0:T(8,128)}, u32[]{:S(2)}) copy-start(f32[224,768]{1,0:T(8,128)} %refs_15_.3) | copy-start | bytes 2064388
  127.7 19.3 %copy-start.29 = (f32[96,6,96]{2,0,1:T(8,128)S(1)}, f32[96,6,96]{2,0,1:T(8,128)}, u32[]{:S(2)}) copy-start(f32[96,6,96]{2,0,1:T(8,128)} %param.25) | copy-start | bytes 663556
  127.7 19.3 %copy-start.35 = (f32[11,768]{1,0:T(8,128)S(1)}, f32[11,768]{1,0:T(8,128)}, u32[]{:S(2)}) copy-start(f32[11,768]{1,0:T(8,128)} %refs_21_.1) | copy-start | bytes 101380
  127.7 19.3 %copy-start.36 = (f32[11,768]{1,0:T(8,128)S(1)}, f32[11,768]{1,0:T(8,128)}, u32[]{:S(2)}) copy-start(f32[11,768]{1,0:T(8,128)} %refs_22_.1) | copy-start | bytes 101380
  138.3 5.4 %collective-permute-start.28 = (bf16[8,16,512]{2,1,0:T(8,128)(2,1)S(1)}, bf16[8,16,512]{2,1,0:T(8,128)(2,1)S(1)}, u32[]{:S(2)}, u32[]{:S(2)}) collective-permute-start(bf16[8,16,512]{2,1,0:T(8,128)(2,1)S(1)} %all_to_all.10.refs_0_), channel_id=1, source_target_pairs={{0,3},{1,2},{2,1},{3,0},{4,7},{5,6},{6,5},{7,4},{8,11},{9,10},{10,... | collective-permute-start | bytes 393224 | tf_op jit(solution)/shard_map/ppermute | solution.py:558
  138.3 8.6 %collective-permute-start.27 = (bf16[8,16,512]{2,1,0:T(8,128)(2,1)S(1)}, bf16[8,16,512]{2,1,0:T(8,128)(2,1)S(1)}, u32[]{:S(2)}, u32[]{:S(2)}) collective-permute-start(bf16[8,16,512]{2,1,0:T(8,128)(2,1)S(1)} %all_to_all.10.refs_0_), channel_id=1, source_target_pairs={{0,2},{1,3},{2,0},{3,1},{4,6},{5,7},{6,4},{7,5},{8,10},{9,11},{10,... | collective-permute-start | bytes 393224 | tf_op jit(solution)/shard_map/ppermute | solution.py:558
  140.3 6.6 %collective-permute-start.26 = (bf16[8,16,512]{2,1,0:T(8,128)(2,1)S(1)}, bf16[8,16,512]{2,1,0:T(8,128)(2,1)S(1)}, u32[]{:S(2)}, u32[]{:S(2)}) collective-permute-start(bf16[8,16,512]{2,1,0:T(8,128)(2,1)S(1)} %all_to_all.10.refs_0_), channel_id=1, source_target_pairs={{0,1},{1,0},{2,3},{3,2},{4,5},{5,4},{6,7},{7,6},{8,9},{9,8},{10,11... | collective-permute-start | bytes 393224 | tf_op jit(solution)/shard_map/ppermute | solution.py:558
  (16 other events, 11.9 us)
Sparse Core Ops, SparseCore 0:
  73.0 47.9 all-gather.1

commit v2 on v1

v2 whole, which is shorter than its diff:
```python
import functools

import jax
import jax.numpy as jnp
from jax import lax
from jax.experimental import pallas as pl
from jax.experimental.pallas import tpu as pltpu
from jax.sharding import PartitionSpec as P

HEAD_DIM = 24
TYPES = 192
STEP = 10
NORM_EPS = 1e-05
CLIP = 0.25
STATS_DECAY = 0.95
RATE_LAYER = 0.15
RATE_TABLES = 0.15
RATE_HEAD = 0.01
RATE_VECTORS = 0.2
BETA_ONE = 0.9
BETA_TWO = 0.99
ADAM_EPS = 1e-08
WEIGHT_DECAY = 0.01
MASKED = -1000000000.0
GELU_C = 0.7978845608028654
GELU_A = 0.044715

BF = jnp.bfloat16
F32 = jnp.float32
I32 = jnp.int32
HIGHEST = lax.Precision.HIGHEST
NN = ((1,), (0,))
NT = ((1,), (1,))
TN = ((0,), (0,))
BLOCK = 256
FEATS = 256
MIB = 1024 * 1024


def dot(a, b, dims=NN, precision=None):
    return lax.dot_general(a, b, (dims, ((), ())), preferred_element_type=F32, precision=precision)


def iota(shape, dim):
    return lax.broadcasted_iota(I32, shape, dim)


IN_VMEM = pl.BlockSpec(memory_space=pltpu.VMEM)
IN_PLACE = pl.BlockSpec(memory_space=pl.ANY)


def call(kernel, outs, ins, scratch=(), flops=0, vmem=16, in_specs=None, out_specs=None):
    moved = sum(x.size * x.dtype.itemsize for x in list(ins) + list(outs))
    return pl.pallas_call(
        kernel,
        out_shape=tuple(outs),
        in_specs=in_specs or [IN_VMEM] * len(ins),
        out_specs=tuple(out_specs or [IN_VMEM] * len(outs)),
        scratch_shapes=list(scratch),
        compiler_params=pltpu.CompilerParams(vmem_limit_bytes=vmem * MIB),
        cost_estimate=pl.CostEstimate(flops=flops, bytes_accessed=moved, transcendentals=0),
    )(*ins)


def sds(shape, dtype):
    return jax.ShapeDtypeStruct(shape, dtype)


def norm_parts(values):
    center = values - jnp.mean(values, -1, keepdims=True)
    spread = jnp.mean(center * center, -1, keepdims=True)
    inverse = lax.rsqrt(spread + NORM_EPS)
    return center * inverse, inverse


def norm_back(grad, hat, inverse, gain):
    scaled = grad * gain
    mean_one = jnp.mean(scaled, -1, keepdims=True)
    mean_two = jnp.mean(scaled * hat, -1, keepdims=True)
    return inverse * (scaled - mean_one - hat * mean_two)


def gelu_pair(x):
    t = jnp.tanh(GELU_C * (x + GELU_A * x * x * x))
    value = 0.5 * x * (1.0 + t)
    slope = 0.5 * (1.0 + t) + 0.5 * x * (1.0 - t * t) * (GELU_C * (1.0 + 3.0 * GELU_A * x * x))
    return value, slope


def tree(refs):
    parts = [r[...].astype(F32) for r in refs]
    while len(parts) > 1:
        parts = [parts[i] + parts[i + 1] for i in range(0, len(parts), 2)]
    return parts[0]


def three(x):
    high = x.astype(BF).astype(F32)
    mid = (x - high).astype(BF).astype(F32)
    return high, mid, x - high - mid


def assemble(pieces, whole, first_owner):
    rows = pieces[0].shape[0]
    if len(pieces) == 1:
        whole[...] = pieces[0][...]
        return
    for k, piece in enumerate(pieces):
        start = pl.multiple_of((first_owner ^ k) * rows, 16)
        whole[pl.ds(start, rows), :] = piece[...]


def embed_kernel(mols, *refs):
    sources, (at, normed, hats, invs), held, (high, low, prev, sems) = refs[:6], refs[6:10], refs[10:16], refs[16:]
    copies = [pltpu.make_async_copy(a, b, sems.at[i]) for i, (a, b) in enumerate(zip(sources, held))]
    for copy in copies:
        copy.start()
    normed[...] = jnp.zeros(normed.shape, BF)
    for copy in copies:
        copy.wait()
    lap, eig, kinds, seg, tables, vectors = held
    length = seg.shape[1]
    width = vectors.shape[1]
    rows = tables.shape[0]
    tab = tables[...]
    tab_high = tab.astype(BF)
    high[0:rows, :] = tab_high
    rest = jnp.where(iota(tab.shape, 0) < TYPES, tab - tab_high.astype(F32), 0.0)
    low[0:rows, :] = rest.astype(BF)
    r = iota((FEATS - rows, width), 0)
    extra = jnp.where(r == 0, vectors[6:7, :], jnp.where(r == 1, vectors[7:8, :], jnp.where(r == 2, vectors[8:9, :], 0.0)))
    extra_high = extra.astype(BF)
    high[rows:FEATS, :] = extra_high
    low[rows:FEATS, :] = (extra - extra_high.astype(F32)).astype(BF)
    seg_row = seg[...]
    before = pltpu.roll(jnp.broadcast_to(seg_row, (8, length)), 1, 1)
    before = jnp.where(iota((8, length), 1) == 0, -1, before)
    prev[...] = before
    filled = jnp.sum((seg_row != mols).astype(F32)).astype(I32)
    gain = vectors[0:1, :]
    shift = vectors[1:2, :]
    window = 2 * BLOCK

    def one_block(b, unused):
        start = pl.multiple_of(b * BLOCK, BLOCK)
        here = pl.ds(start, BLOCK)
        first = pl.multiple_of(jnp.clip(start - 128, 0, length - window), 128)
        source = iota((window, BLOCK), 0) + first
        one = eig[0:1, here]
        two = eig[1:2, here]
        near = lap[:, pl.ds(first, window)].astype(BF)
        pair_one = dot(near, (source == one).astype(F32).astype(BF))
        pair_two = dot(near, (source == two).astype(F32).astype(BF))
        seg_here = seg[0:1, here]
        begins = (seg_here != mols) & (seg_here != prev[0:1, here])
        kind = jnp.where(begins, -1, kinds[0:1, here])
        keep = jnp.where(begins, 0.0, 1.0)
        at[0:TYPES, here] = (iota((TYPES, BLOCK), 0) == kind).astype(F32).astype(BF)
        half = pair_one.shape[0]
        at[TYPES : TYPES + half, here] = (pair_one * keep).astype(BF)
        at[TYPES + half : rows, here] = (pair_two * keep).astype(BF)
        which = jnp.where(begins, 2, jnp.where(one == two, 0, 1))
        at[rows:FEATS, here] = (iota((FEATS - rows, BLOCK), 0) == which).astype(F32).astype(BF)
        picks = at[:, here]
        resid = dot(picks, high[...], TN) + dot(picks, low[...], TN)
        hat, inverse = norm_parts(resid)
        normed[here, :] = (hat * gain + shift).astype(BF)
        hats[here, :] = hat.astype(BF)
        invs[here, :] = jnp.broadcast_to(inverse, (BLOCK, 128))
        return 0

    lax.fori_loop(0, (filled + BLOCK - 1) // BLOCK, one_block, 0)


def attn_kernel(npiece, mols, heads, scale, *refs):
    normed, seg, vectors = refs[:3]
    ones = refs[3 : 3 + npiece]
    part, probs, values, ctx_out, keyed, query_out, w1 = refs[3 + npiece :]
    assemble(ones, w1, lax.axis_index("dp"))
    width = vectors.shape[1]
    cols = heads * HEAD_DIM
    hat, _ = norm_parts(vectors[8:9, :])
    start_row = (hat * vectors[0:1, :] + vectors[1:2, :]).astype(BF)
    q = dot(jnp.broadcast_to(start_row, (16, width)), w1[:, 0:256])
    q = q.astype(BF).astype(F32)
    q = jnp.where(iota((16, 256), 1) < cols, q, 0.0)
    r = iota((16, 256), 0)
    head_of = iota((16, 256), 1) // HEAD_DIM
    query_out[...] = jnp.where(r == head_of, q, 0.0)[0:8, :]
    shifted = pltpu.roll(q, 64, 1)[0:1, :]
    r = iota((128, 256), 0)
    lane = iota((128, 256), 1) - 64
    pick = (lane >= 0) & ((r & 7) == lane // HEAD_DIM) & (r >= 64) & (r < 80)
    q_keys = jnp.where(pick, shifted, 0.0).astype(BF)
    u = dot(w1[:, 128:384], q_keys, NT)
    u_high = u.astype(BF)
    lane = iota(u.shape, 1)
    u_both = jnp.where(lane < 72, u_high.astype(F32), u - u_high.astype(F32))
    last = w1[:, 512:640].astype(F32)
    side = jnp.where(lane < 64, last, u_both).astype(BF)
    keyed[:, 0:128] = w1[:, 384:512]
    keyed[:, 128:256] = jnp.where(lane < 64, last, jnp.where(lane < 72, u * scale, 0.0)).astype(BF)
    normed_all = normed[...]
    values[:, 0:128] = dot(normed_all, w1[:, 384:512]).astype(BF)
    second = dot(normed_all, side)
    values[:, 128:256] = jnp.where(iota(second.shape, 1) < 64, second, 0.0).astype(BF)
    turned = second.T
    scores = (turned[64:72, :] + turned[72:80, :]) * scale
    seg_row = seg[...]
    length = seg_row.shape[1]
    mine = iota((mols, 1, length), 0) == seg_row[None]
    masked = jnp.where(mine, scores[None], MASKED)
    peak = jnp.max(masked, -1, keepdims=True)
    grown = jnp.where(mine, jnp.exp(masked - peak), 0.0)
    total = jnp.sum(grown, -1, keepdims=True)
    total = jnp.where(total > 0.0, total, 1.0)
    prob = (grown / total).reshape(mols * heads, length).astype(BF)
    probs[...] = prob
    wide = dot(prob, values[...])
    r = iota(wide.shape, 0) & (heads - 1)
    wide = jnp.where(r == iota(wide.shape, 1) // HEAD_DIM, wide, 0.0)
    ctx = jnp.sum(wide.reshape(mols, heads, 256), 1)
    ctx_out[...] = ctx.astype(BF)
    turned_ctx = pltpu.roll(ctx, 64, 1).astype(BF)
    part[...] = dot(turned_ctx, w1[:, 512:768], NT).astype(BF)


def ffn_kernel(npiece, nmp, cols, *refs):
    terms = refs[:nmp]
    vectors = refs[nmp]
    twos = refs[nmp + 1 : nmp + 1 + npiece]
    part, resid_out, normed_out, hidden_out, act_out, w2 = refs[nmp + 1 + npiece :]
    assemble(twos, w2, lax.axis_index("dp"))
    resid = vectors[8:9, :] + tree(terms)
    resid_out[...] = resid
    hat, _ = norm_parts(resid)
    low = (hat * vectors[2:3, :] + vectors[3:4, :]).astype(BF)
    normed_out[...] = low
    hidden = dot(low, w2[:, 0:256])
    hidden = jnp.where(iota(hidden.shape, 1) < cols, hidden, 0.0)
    hidden_out[...] = hidden
    act, _ = gelu_pair(hidden)
    act_out[...] = act.astype(BF)
    turned = pltpu.roll(act, 64, 1).astype(BF)
    part[...] = dot(turned, w2[:, 128:384], NT).astype(BF)


def head_kernel(nmp, cols, *refs):
    terms = refs[:nmp]
    resid_one, vectors, head, targets, seg, normed_two, ctx, hidden, act, w2 = refs[nmp : nmp + 10]
    part, pack, grad_out, rows_out, head_low = refs[nmp + 10 :]
    width = vectors.shape[1]
    mols = targets.shape[1]
    head_low[...] = head[...].astype(BF)
    resid = resid_one[...] + tree(terms)
    hat, inverse = norm_parts(resid)
    gain = vectors[4:5, :]
    low = (hat * gain + vectors[5:6, :]).astype(BF)
    mid = dot(low, head_low[...]) + vectors[9:10, :]
    act_head, slope = gelu_pair(mid)
    act_head = act_head.astype(BF).astype(F32)
    readout = vectors[10:11, :].astype(BF).astype(F32)
    predicted = jnp.sum(act_head * readout, -1, keepdims=True)
    spot = iota((mols, mols), 0) == iota((mols, mols), 1)
    goal = jnp.sum(jnp.where(spot, targets[...], 0.0), -1, keepdims=True)
    seg_row = seg[...]
    there = iota((mols, seg_row.shape[1]), 0) == seg_row
    present = jnp.max(there.astype(F32), -1, keepdims=True)
    error = predicted - goal
    root = jnp.sqrt(error * error + 1.0)
    loss = jnp.sum(present * (root - 1.0), 0, keepdims=True)
    count = jnp.sum(present, 0, keepdims=True)
    grad_pred = present * error / root
    grad_readout = jnp.sum(grad_pred * act_head, 0, keepdims=True)
    grad_mid = (grad_pred * readout * slope).astype(BF)
    grad_bias = jnp.sum(grad_mid.astype(F32), 0, keepdims=True)
    grad_rows = dot(grad_mid, head_low[...], NT)
    grad_gain = jnp.sum(grad_rows * hat, 0, keepdims=True)
    grad_shift = jnp.sum(grad_rows, 0, keepdims=True)
    grad_two = norm_back(grad_rows, hat, inverse, gain)
    grad_out[...] = grad_two
    grad_low = grad_two.astype(BF)
    grad_act = dot(grad_low, w2[:, 128:384])
    grad_act = pltpu.roll(grad_act, 192, 1)
    _, slope_hidden = gelu_pair(hidden[...])
    grad_hidden = jnp.where(iota(grad_act.shape, 1) < cols, grad_act * slope_hidden, 0.0).astype(BF)
    part[...] = dot(grad_hidden, w2[:, 0:256], NT).astype(BF)
    pack[:, 0:width] = low
    pack[:, width : 2 * width] = grad_mid
    pack[:, 2 * width : 3 * width] = normed_two[...]
    pack[:, 3 * width : 4 * width] = grad_low
    pack[:, 4 * width : 4 * width + 256] = ctx[...]
    pack[:, 4 * width + 256 : 4 * width + 512] = act[...]
    pack[:, 4 * width + 512 : 4 * width + 768] = grad_hidden
    r = iota((8, width), 0)
    lane = iota((8, width), 1)
    scalars = jnp.where(lane == 0, loss, jnp.where(lane == 1, count, 0.0))
    rows_out[...] = jnp.where(
        r == 0,
        grad_gain,
        jnp.where(r == 1, grad_shift, jnp.where(r == 2, grad_bias, jnp.where(r == 3, grad_readout, jnp.where(r == 4, scalars, 0.0)))),
    )


def back_kernel(nmp, nlayer, mols, heads, scale, *refs):
    terms = refs[:nmp]
    resid_one, grad_two, head_rows, vectors, keyed, probs, values, normed, hats, invs, at, seg, w1 = refs[nmp : nmp + 13]
    rest = refs[nmp + 13 :]
    outs = rest[:nmp]
    layer_outs = rest[nmp : nmp + nlayer]
    side, sides, comb, total, gains = rest[nmp + nlayer : nmp + nlayer + 5]
    group = lax.axis_index("mp")
    width = vectors.shape[1]
    length = seg.shape[1]
    cols = heads * HEAD_DIM
    filled = jnp.sum((seg[...] != mols).astype(F32)).astype(I32)
    grad_normed = tree(terms)
    hat, inverse = norm_parts(resid_one[...])
    grad_gain = jnp.sum(grad_normed * hat, 0, keepdims=True)
    grad_shift = jnp.sum(grad_normed, 0, keepdims=True)
    grad_one = grad_two[...] + norm_back(grad_normed, hat, inverse, vectors[2:3, :])
    low = grad_one.astype(BF)
    grad_start = jnp.sum(low.astype(F32), 0, keepdims=True)
    grad_ctx = pltpu.roll(dot(low, w1[:, 512:768]), 192, 1).astype(BF).astype(F32)
    spread = jnp.broadcast_to(grad_ctx[:, None, :], (mols, heads, 256)).reshape(mols * heads, 256)
    r = iota(spread.shape, 0) & (heads - 1)
    spread = jnp.where(r == iota(spread.shape, 1) // HEAD_DIM, spread, 0.0).astype(BF)
    grad_probs = dot(spread, values[...], NT)
    prob = probs[...].astype(F32)
    inner = jnp.sum(prob * grad_probs, -1, keepdims=True)
    grad_scores = (prob * (grad_probs - inner)).astype(BF).astype(F32)
    grad_scores = jnp.sum(grad_scores.reshape(mols, heads, length), 0)
    grad_values = dot(spread, probs[...], TN)
    sides[0:cols, :] = grad_values[0:cols, :].astype(BF)
    sides[cols:256, :] = jnp.concatenate([grad_scores, jnp.zeros((256 - cols - heads, length), F32)], 0).astype(BF)
    sums = dot(sides[...], normed[...])
    comb[...] = keyed[...].astype(F32).T.astype(BF)
    total[...] = jnp.zeros(total.shape, F32)
    gains[...] = jnp.zeros(gains.shape, F32)
    gain = vectors[0:1, :]

    def one_block(b, unused):
        here = pl.ds(pl.multiple_of(b * BLOCK, BLOCK), BLOCK)
        grad = dot(sides[:, here], comb[...], TN)
        hat_here = hats[here, :].astype(F32)
        low_grad = norm_back(grad, hat_here, invs[here, 0:1], gain).astype(BF)
        total[...] += dot(at[:, here], low_grad)
        gains[0:8, :] += jnp.sum((grad * hat_here).reshape(BLOCK // 8, 8, width), 0)
        gains[8:16, :] += jnp.sum(grad.reshape(BLOCK // 8, 8, width), 0)
        return 0

    lax.fori_loop(0, (filled + BLOCK - 1) // BLOCK, one_block, 0)
    grad_keys = sums[cols : cols + heads, :]
    turned = dot(grad_keys.astype(BF), w1[:, 128:384])
    lane = iota(turned.shape, 1) - 64
    picked = jnp.where((lane >= 0) & (lane // HEAD_DIM == iota(turned.shape, 0)), turned, 0.0)
    grad_query = jnp.sum(pltpu.roll(picked, 192, 1), 0, keepdims=True) * scale
    r = iota(side.shape, 0)
    side[...] = jnp.where(r == 0, grad_query, jnp.where(r == 1, head_rows[4:5, 0:256], 0.0))
    grad_query = jnp.broadcast_to(grad_query.astype(BF), (16, 256))
    grad_row = dot(grad_query, w1[:, 0:256], NT)[0:1, :]
    hat_start, inverse_start = norm_parts(vectors[8:9, :])
    start_row = (hat_start * gain + vectors[1:2, :]).astype(BF).astype(F32)
    first = jnp.where(group == 0, 1.0, 0.0)
    row_graph = norm_back(grad_row, hat_start, inverse_start, gain) + first * grad_start
    row_gain = jnp.sum(gains[0:8, :], 0, keepdims=True) + grad_row * hat_start
    row_shift = jnp.sum(gains[8:16, :], 0, keepdims=True) + grad_row
    base = TYPES + 32
    r = iota((FEATS - base, width), 0)
    extra = jnp.where(r == 2, row_graph, 0.0)
    extra = jnp.where(r == 3, row_gain, extra)
    extra = jnp.where(r == 4, row_shift, extra)
    extra = jnp.where(r == 5, first * grad_gain, extra)
    extra = jnp.where(r == 6, first * grad_shift, extra)
    for i in range(4):
        extra = jnp.where(r == 7 + i, first * head_rows[i : i + 1, :], extra)
    total[base:FEATS, :] += extra
    each = FEATS // nmp
    for k in range(nmp):
        start = pl.multiple_of((group ^ k) * each, 16)
        outs[k][...] = total[pl.ds(start, each), :].astype(BF)
    odd = lax.axis_index("dp") & 1
    even_share = jnp.where(odd == 0, 1.0, 0.0)
    lay = jnp.concatenate(
        [
            sums[0:cols, :],
            grad_one * even_share,
            grad_one * (1.0 - even_share),
            grad_keys,
            jnp.zeros((256 - cols - 2 * mols - heads, width), F32),
        ],
        0,
    )
    lay = lay.T.astype(BF)
    if nlayer == 1:
        layer_outs[0][...] = lay
    else:
        turned_lay = rest[nmp + nlayer + 5]
        turned_lay[...] = lay
        keep, send = layer_outs
        high, own = keep.shape[0], keep.shape[1]
        for z in range(high):
            keep[z] = turned_lay[pl.ds(pl.multiple_of((2 * z + odd) * own, 16), own), :]
            send[z] = turned_lay[pl.ds(pl.multiple_of((2 * z + 1 - odd) * own, 16), own), :]


def merge_kernel(nmp, owners, *refs):
    terms = refs[:nmp]
    layer_keep, layer_came, side_keep, side_came = refs[nmp : nmp + 4]
    high, deep = layer_keep.shape[0], layer_keep.shape[1]
    table_keep, table_send, side = refs[nmp + 4 : nmp + 7]
    outs = refs[nmp + 7 : nmp + 7 + high]
    layer_sum, table_sum = refs[nmp + 7 + high :]
    me = lax.axis_index("dp")
    odd, mine = me & 1, me >> 1
    for z in range(high):
        layer_sum[z] = (layer_keep[z].astype(F32) + layer_came[z].astype(F32)).astype(BF)
    for k in range(high):
        outs[k][...] = layer_sum[mine ^ k]
    side[...] = side_keep[...] + side_came[...]
    table_sum[...] = tree(terms)
    width = table_sum.shape[1]
    for z in range(0, high, 2):
        kept, sent = [], []
        for y in (z, z + 1):
            if 2 * y + 1 < owners:
                kept.append(table_sum[pl.ds(pl.multiple_of((2 * y + odd) * 8, 8), 8), :])
                sent.append(table_sum[pl.ds(pl.multiple_of((2 * y + 1 - odd) * 8, 8), 8), :])
            else:
                kept.append(jnp.zeros((8, width), F32))
                sent.append(jnp.zeros((8, width), F32))
        table_keep[z * 8 : z * 8 + 16, :] = jnp.concatenate(kept, 0)
        table_send[z * 8 : z * 8 + 16, :] = jnp.concatenate(sent, 0).astype(BF)


def table_kernel(keep, came, side, *outs):
    mine = lax.axis_index("dp") >> 1
    high = keep.shape[0] // 8
    width = keep.shape[1]
    summed = outs[high]
    summed[...] = keep[...] + came[...].astype(F32)
    for k in range(high):
        outs[k][:, 0:width] = summed[pl.ds(pl.multiple_of((mine ^ k) * 8, 8), 8), :]
        outs[k][:, width:] = side[...]


def sum_squares(value):
    return jnp.sum(jnp.sum(value * value, 0, keepdims=True), 1, keepdims=True)


def outer_kernel(own, dp, *refs):
    pieces = refs[:-6]
    head_grad, up_grad, down_grad, squares, packs, full = refs[-6:]
    me = lax.axis_index("dp")
    width = head_grad.shape[0]
    if len(pieces) == 1:
        packs[...] = pieces[0][...]
    mols = pieces[0].shape[0]
    slot = packs.shape[0] // dp
    for k, piece in enumerate(pieces[: dp if len(pieces) > 1 else 0]):
        rows = piece[...].astype(F32)
        rows = jnp.concatenate([rows, jnp.zeros((slot - mols, rows.shape[1]), F32)], 0).astype(BF)
        packs[pl.ds(pl.multiple_of((me ^ k) * slot, 16), slot), :] = rows
    grad = dot(packs[:, 0:width], packs[:, width : 2 * width], TN)
    head_grad[...] = grad
    head_square = sum_squares(grad)
    kept = up_grad.shape[0]
    start = 0 if kept == full.shape[0] else pl.multiple_of(me * own, 8)
    first = 4 * width
    grad = dot(packs[:, 2 * width : 3 * width], packs[:, first + 512 : first + 768], TN)
    square = sum_squares(grad)
    full[...] = grad
    up_grad[...] = full[pl.ds(start, kept), :]
    grad = dot(packs[:, 3 * width : 4 * width], packs[:, first + 256 : first + 512], TN)
    square += sum_squares(grad)
    full[...] = grad
    down_grad[...] = full[pl.ds(start, kept), :]
    squares[...] = jnp.where(iota((8, 128), 1) == 0, square, head_square)


def owner_kernel(own, cols, scale, dp, *refs):
    high = dp // 2
    table_parts, layer_parts, packs = refs[:high], refs[high : 2 * high], refs[2 * high : 2 * high + dp]
    query, vectors, layer, send, scalars = refs[2 * high + dp :]
    deep = layer_parts[0].shape[0]
    me = lax.axis_index("dp")
    even = (me & 1) == 0
    mols = packs[0].shape[0]
    width = vectors.shape[1]
    first = packs[0].shape[1] - 3 * 256
    acc = tree(layer_parts)
    summed = tree(table_parts)
    out_grad = jnp.zeros((deep, 256), F32)
    for j in range(high):
        near = packs[2 * j][:, first : first + 256].astype(F32)
        far = packs[2 * j + 1][:, first : first + 256].astype(F32)
        rows = [jnp.where(even, near, far), jnp.where(even, far, near)]
        rows = jnp.concatenate([jnp.zeros((64, 256), F32), *rows, jnp.zeros((64 - 2 * mols, 256), F32)], 0)
        out_grad += dot(layer_parts[j][:, 128:256], rows.astype(BF))
    keys = jnp.concatenate([jnp.zeros((64 + 2 * mols, 256), F32), query[...], jnp.zeros((56 - 2 * mols, 256), F32)], 0)
    key_grad = dot(acc[:, 128:256], keys, precision=HIGHEST) * scale
    hat, _ = norm_parts(vectors[8:9, :])
    start_row = (hat * vectors[0:1, :] + vectors[1:2, :]).astype(BF).astype(F32)
    here = iota((deep, width), 1) == iota((deep, width), 0) + me * own
    start_col = jnp.sum(jnp.where(here, start_row, 0.0), -1, keepdims=True)
    table, side = summed[:, 0:width], summed[:, width:]
    square = jnp.zeros((1, 1), F32)
    for j, grad in enumerate([start_col * side[0:1, :], key_grad, acc, out_grad]):
        grad = grad[0:own, 0:cols]
        layer[j] = grad
        square += sum_squares(grad)
    square += sum_squares(table)
    a, b, c = three(square)
    lane = iota((16, 128), 1)
    r = iota((16, 128), 0)
    tail = jnp.where(r == 0, jnp.where(lane == 0, a, jnp.where(lane == 1, b, jnp.where(lane == 2, c, 0.0))), 0.0)
    half = width // 2
    table = jnp.concatenate([table[:, 0:half], table[:, half:]], 0)
    packet = jnp.concatenate([table, tail], 1).astype(BF)
    for p in range(dp):
        send[p] = packet
    scalars[...] = jnp.broadcast_to(side[1:2, 0:128], scalars.shape)


def stats_kernel(cols, layer, up_grad, down_grad, left_roots, right_roots, left, right, shaped):
    for j in range(6):
        g = layer[j] if j < 4 else (up_grad if j == 4 else down_grad)[:, 0:cols]
        left[j] = dot(g, g, NT, HIGHEST)
        right[j] = dot(g, g, TN, HIGHEST)
        shaped[j] = dot(dot(left_roots[j], g, NN, HIGHEST), right_roots[j], NN, HIGHEST)


def adam(weight, first, second, grad, rate):
    first_new = BETA_ONE * first + (1.0 - BETA_ONE) * grad
    second_new = BETA_TWO * second + (1.0 - BETA_TWO) * grad * grad
    fixed_one = 1.0 - BETA_ONE**STEP
    fixed_two = 1.0 - BETA_TWO**STEP
    update = first_new * (1.0 / fixed_one) / (jnp.sqrt(second_new * (1.0 / fixed_two)) + ADAM_EPS)
    return first_new, second_new, weight - rate * (update + WEIGHT_DECAY * weight)


def update_kernel(nmp, owners, cols, *refs):
    packets, squares = refs[:nmp], refs[nmp : 2 * nmp]
    (
        scalars, layer, up_grad, down_grad, left_add, right_add, shaped, weights, left, right,
        tables, tables_m, tables_v, head, head_m, head_v, head_grad, vectors, vectors_m, vectors_v,
    ) = refs[2 * nmp : 2 * nmp + 20]
    loss_out, count_out, norm_out = refs[2 * nmp + 20 : 2 * nmp + 23]
    outs = refs[2 * nmp + 23 : 2 * nmp + 36]
    held = refs[2 * nmp + 36 : 2 * nmp + 49]
    grads, sems = refs[2 * nmp + 49 :]
    layer_out, weights_out, left_out, right_out, tm_out, tv_out, t_out, hm_out, hv_out, h_out, vm_out, vv_out, v_out = held
    started = []

    def send(i, rows=None):
        src, dst = held[i], outs[i]
        if rows is not None:
            src, dst = src.at[rows], dst.at[rows]
        copy = pltpu.make_async_copy(src, dst, sems.at[len(started)])
        copy.start()
        started.append(copy)

    parts = []
    for packet, ref in zip(packets, squares):
        s = ref[0:1, 0:1]
        for p in range(packet.shape[0]):
            tail = packet[p, :, 384:512].astype(F32)
            s += tail[0:1, 0:1] + tail[0:1, 1:2] + tail[0:1, 2:3]
        parts.append(s)
    while len(parts) > 1:
        parts = [parts[i] + parts[i + 1] for i in range(0, len(parts), 2)]
    square = parts[0] + squares[0][0:1, 1:2]
    loss, count = scalars[0:1, 0:1], scalars[0:1, 1:2]
    norm = jnp.sqrt(square) / count
    factor = CLIP / jnp.maximum(norm, CLIP) / count
    loss_out[...] = loss
    count_out[...] = count
    norm_out[...] = norm
    width = head.shape[0]
    each = width // 4
    for i in range(4):
        rows = slice(i * each, (i + 1) * each)
        hm_out[rows, :], hv_out[rows, :], h_out[rows, :] = adam(
            head[rows, :], head_m[rows, :], head_v[rows, :], head_grad[rows, :] * factor, RATE_HEAD
        )
        for k in (7, 8, 9):
            send(k, pl.ds(i * each, each))
    scale = (1.0 - STATS_DECAY) * factor * factor
    right_out[...] = STATS_DECAY * right[...] + scale[None] * right_add[...]
    send(3)
    left_out[...] = STATS_DECAY * left[...] + scale[None] * left_add[...]
    send(2)
    for j in range(6):
        span = slice(j * cols, (j + 1) * cols)
        g = layer[j] if j < 4 else (up_grad if j == 4 else down_grad)[:, 0:cols]
        layer_out[:, span] = g * factor
        weights_out[:, span] = weights[:, span] - RATE_LAYER * (shaped[j] * factor + WEIGHT_DECAY * weights[:, span])
    send(0)
    send(1)
    group = lax.axis_index("mp")
    share = FEATS // nmp
    half = 384
    for k in range(nmp):
        start = pl.multiple_of((group ^ k) * share, 8)
        for p in range(owners):
            piece = packets[k][p, :, 0:half].astype(F32)
            piece = jnp.concatenate([piece[0:8, :], piece[8:16, :]], 1) * factor
            grads[pl.ds(pl.multiple_of(start + p * 8, 8), 8), :] = piece
    rows = tables.shape[0]
    tm_out[...], tv_out[...], t_out[...] = adam(tables[...], tables_m[...], tables_v[...], grads[0:rows, :], RATE_TABLES)
    for k in (4, 5, 6):
        send(k)
    order = (3, 4, 5, 6, 7, 8, 0, 1, 2, 9, 10)
    r = iota((16, vectors.shape[1]), 0)
    tail = jnp.zeros(r.shape, F32)
    for i, o in enumerate(order):
        tail = jnp.where(r == i, grads[rows + o : rows + o + 1, :], tail)
    nrows = vectors.shape[0]
    vm_out[...], vv_out[...], v_out[...] = adam(vectors[...], vectors_m[...], vectors_v[...], tail[0:nrows, :], RATE_VECTORS)
    for k in (10, 11, 12):
        send(k)
    for copy in started:
        copy.wait()


def exchange(x, axis):
    n = lax.axis_size(axis)
    return [x] + [lax.ppermute(x, axis, [(i, i ^ k) for i in range(n)]) for k in range(1, n)]


def flip(x, k):
    n = lax.axis_size("dp")
    return lax.ppermute(x, "dp", [(i, i ^ k) for i in range(n)])


def after(values, *others):
    return lax.optimization_barrier((tuple(values), tuple(others)))[0]


def gather_rows(x):
    if lax.axis_size("dp") != 8 or x.shape[0] % 16:
        return [lax.all_gather(x, "dp", axis=0, tiled=True)]
    return spread(x, (), ())


def spread(x, second, third):
    four, one, two = after([flip(x, 4), flip(x, 1), flip(x, 2)], *second)
    far = after([flip(one, 2), flip(four, 2), flip(four, 1)], *third)
    return [x, one, two, far[0], four, far[2], far[1], flip(far[1], 1)]


def per_device(
    lap_vectors,
    eig_index,
    type_ids,
    seg_ids,
    targets,
    layer_weights,
    left_stats,
    right_stats,
    left_roots,
    right_roots,
    tables,
    tables_m,
    tables_v,
    head_weight,
    head_m,
    head_v,
    vectors,
    vectors_m,
    vectors_v,
):
    dp = lax.axis_size("dp")
    nmp = lax.axis_size("mp")
    length = seg_ids.shape[1]
    mols = targets.shape[1]
    width = vectors.shape[1]
    own, group_cols = layer_weights.shape[0], layer_weights.shape[1]
    cols = group_cols // 6
    heads = cols // HEAD_DIM
    scale = HEAD_DIM ** (-0.5)
    owners = FEATS // nmp // 8

    w = layer_weights.astype(BF)
    ones = gather_rows(w[:, : 4 * cols])
    twos = gather_rows(w[:, 4 * cols :])
    np_ = len(ones)

    sources = [lap_vectors[0].T, eig_index[0].T, type_ids, seg_ids, tables, vectors]
    at, normed, hats, invs = call(
        functools.partial(embed_kernel, mols),
        [sds((FEATS, length), BF), sds((length, width), BF), sds((length, width), BF), sds((length, 128), F32)],
        sources,
        [pltpu.VMEM(x.shape, x.dtype) for x in sources]
        + [pltpu.VMEM((FEATS, width), BF), pltpu.VMEM((FEATS, width), BF), pltpu.VMEM((8, length), I32), pltpu.SemaphoreType.DMA((6,))],
        flops=4 * length * FEATS * width,
        in_specs=[IN_PLACE] * 6,
    )
    part, probs, values, ctx, keyed, query, w1 = call(
        functools.partial(attn_kernel, np_, mols, heads, scale),
        [
            sds((mols, width), BF),
            sds((mols * heads, length), BF),
            sds((length, 256), BF),
            sds((mols, 256), BF),
            sds((width, 256), BF),
            sds((8, 256), F32),
            sds((width, 4 * cols), BF),
        ],
        [normed, seg_ids, vectors, *ones],
        flops=4 * length * 256 * width,
    )
    part, resid_one, normed_two, hidden, act, w2 = call(
        functools.partial(ffn_kernel, np_, nmp, cols),
        [
            sds((mols, width), BF),
            sds((mols, width), F32),
            sds((mols, width), BF),
            sds((mols, 256), F32),
            sds((mols, 256), BF),
            sds((width, 2 * cols), BF),
        ],
        [*exchange(part, "mp"), vectors, *twos],
        flops=4 * mols * width * 256,
    )
    part, pack, grad_two, head_rows = call(
        functools.partial(head_kernel, nmp, cols),
        [sds((mols, width), BF), sds((mols, 4 * width + 768), BF), sds((mols, width), F32), sds((8, width), F32)],
        [*exchange(part, "mp"), resid_one, vectors, head_weight, targets, seg_ids, normed_two, ctx, hidden, act, w2],
        [pltpu.VMEM((width, width), BF)],
        flops=4 * width * width * mols,
    )
    odd = lax.axis_index("dp") & 1
    high = dp // 2
    deep = (own + 15) // 16 * 16
    simple = own == deep
    layer_shape = [sds((high, own, 256), BF)] * 2 if simple else [sds((width, 256), BF)]
    nlayer = len(layer_shape)
    back = call(
        functools.partial(back_kernel, nmp, nlayer, mols, heads, scale),
        [sds((FEATS // nmp, width), BF) for _ in range(nmp)] + layer_shape + [sds((8, 256), F32)],
        [
            *exchange(part, "mp"), resid_one, grad_two, head_rows, vectors, keyed, probs, values, normed, hats, invs, at,
            seg_ids, w1,
        ],
        [
            pltpu.VMEM((256, length), BF),
            pltpu.VMEM((256, width), BF),
            pltpu.VMEM((FEATS, width), F32),
            pltpu.VMEM((16, width), F32),
            pltpu.VMEM((width, 256), BF),
        ],
        flops=8 * length * 256 * width,
    )
    shares, side = back[:nmp], back[nmp + nlayer]
    if simple:
        layer_keep, layer_send = back[nmp], back[nmp + 1]
    else:
        both = back[nmp].reshape(high, 2, own, 256)
        both = jnp.pad(both, ((0, 0), (0, 0), (0, deep - own), (0, 0)))
        layer_keep, layer_send = [lax.dynamic_index_in_dim(both, i, 1, False) for i in (odd, 1 - odd)]
    moved = [shares[0]] + [lax.ppermute(shares[k], "mp", [(i, i ^ k) for i in range(nmp)]) for k in range(1, nmp)]
    merged = call(
        functools.partial(merge_kernel, nmp, owners),
        [sds((high * 8, width), F32), sds((high * 8, width), BF), sds((8, 256), F32)] + [sds((deep, 256), BF)] * high,
        [*moved, layer_keep, flip(layer_send, 1), side, flip(side, 1)],
        [pltpu.VMEM((high, deep, 256), BF), pltpu.VMEM((FEATS // nmp, width), F32)],
    )
    table_keep, table_send, side, *layer_parts = merged
    if dp == 8:
        packs = spread(pack, (shares[0],), (table_keep,))
        contexts = packs
    else:
        packs = lax.all_gather(pack, "dp", axis=0)
        near = packs[:, :, 4 * width :]
        contexts = [lax.dynamic_index_in_dim(near, lax.axis_index("dp") ^ k, 0, False) for k in range(dp)]
        packs = [jnp.pad(packs, ((0, 0), (0, 32 - mols), (0, 0))).reshape(dp * 32, -1)]
    layer_parts = [layer_parts[0]] + [flip(layer_parts[k], 2 * k) for k in range(1, high)]
    table_parts = call(
        table_kernel,
        [sds((8, width + 256), F32)] * high,
        [table_keep, flip(table_send, 1), side],
        [pltpu.VMEM((high * 8, width), F32)],
    )
    table_parts = [table_parts[0]] + [flip(table_parts[k], 2 * k) for k in range(1, high)]
    layer, send, scalars = call(
        functools.partial(owner_kernel, own, cols, scale, dp),
        [sds((4, own, cols), F32), sds((dp, 16, 512), BF), sds((8, 128), F32)],
        [*table_parts, *layer_parts, *contexts, query, vectors],
        flops=2 * own * 256 * 1024,
    )
    sums = lax.all_to_all(send, "dp", 0, 0, tiled=True)
    kept = width if own % 8 else own
    head_grad, up_grad, down_grad, squares = call(
        functools.partial(outer_kernel, own, dp),
        [sds((width, width), F32), sds((kept, 256), F32), sds((kept, 256), F32), sds((8, 128), F32)],
        packs,
        [pltpu.VMEM((dp * 32, pack.shape[1]), BF), pltpu.VMEM((width, 256), F32)],
        vmem=16 + dp // 4,
        flops=2 * dp * mols * width * (width + 512),
    )
    sums = exchange(sums, "mp")
    squares = exchange(squares, "mp")
    if kept != own:
        up_grad, down_grad = [lax.dynamic_slice_in_dim(x, lax.axis_index("dp") * own, own) for x in (up_grad, down_grad)]
    left_add, right_add, shaped = call(
        functools.partial(stats_kernel, cols),
        [sds((6, own, own), F32), sds((6, cols, cols), F32), sds((6, own, cols), F32)],
        [layer, up_grad, down_grad, jnp.swapaxes(left_roots, 0, 1), right_roots[0]],
        flops=12 * 6 * own * cols * (2 * own + 2 * cols),
    )
    results = [
        sds((own, group_cols), F32),
        sds((own, group_cols), F32),
        sds((6, own, own), F32),
        sds((6, cols, cols), F32),
        *[sds(tables.shape, F32)] * 3,
        *[sds(head_weight.shape, F32)] * 3,
        *[sds(vectors.shape, F32)] * 3,
    ]
    outs = call(
        functools.partial(update_kernel, nmp, owners, cols),
        [sds((1, 1), F32)] * 3 + results,
        [
            *sums, *squares, scalars, layer, up_grad, down_grad, left_add, right_add, shaped, layer_weights,
            jnp.swapaxes(left_stats, 0, 1), right_stats[0], tables, tables_m, tables_v, head_weight, head_m, head_v, head_grad,
            vectors, vectors_m, vectors_v,
        ],
        [pltpu.VMEM(x.shape, x.dtype) for x in results] + [pltpu.VMEM((FEATS, width), F32), pltpu.SemaphoreType.DMA((22,))],
        flops=20 * width * width,
        vmem=24,
        out_specs=[IN_VMEM] * 3 + [IN_PLACE] * 13,
    )
    loss, count, norm, layer_grad, layer_new, left_new, right_new, tm, tv, tn, hm, hv, hn, vm, vv, vn = outs
    return (
        loss.reshape(()),
        count.reshape(()),
        norm.reshape(()),
        layer_grad,
        layer_new,
        jnp.swapaxes(left_new, 0, 1),
        right_new[None],
        tm,
        tv,
        tn,
        hm,
        hv,
        hn,
        vm,
        vv,
        vn,
    )


def solution(mesh):
    placed = (
        P("dp", None, None),
        P("dp", None, None),
        P("dp", None),
        P("dp", None),
        P("dp", None),
        P("dp", "mp"),
        P("dp", "mp", None),
        P("dp", "mp", None, None),
        P("dp", "mp", None),
        P("dp", "mp", None, None),
        *[P()] * 9,
    )
    return jax.shard_map(
        per_device,
        mesh=mesh,
        in_specs=placed,
        out_specs=(
            P(),
            P(),
            P(),
            P("dp", "mp"),
            P("dp", "mp"),
            P("dp", "mp", None),
            P("dp", "mp", None, None),
            *[P()] * 9,
        ),
        check_vma=False,
    )
```

time: 168 us -> 126 us (0.75)
  local copies, waits for them, and re-layouts: 26 us -> 4.91 us
  between operations: 14.4 us -> 1.2 us
  starting transfers between devices: 50.1 us -> 44.6 us
  Pallas kernels: 26.6 us -> 22.3 us
  waiting for transfers between devices: 38.3 us -> 41.5 us
    ppermute x0 -> x30, starting transfers between devices: none -> 34.1 us  [flip(): return lax.ppermute(x, 'dp', [(i, i ^ k) for i in range(n)])]
    ppermute x26 -> x15, starting transfers between devices: 41.2 us -> 9.26 us  [exchange(): lax.ppermute(x, axis, [(i, i ^ k) for i in range(n)])]
    ppermute x0 -> x30, waiting for transfers between devices: none -> 26.5 us  [flip(): return lax.ppermute(x, 'dp', [(i, i ^ k) for i in range(n)])]
    unnamed x98 -> x44, local copies, waits for them, and re-layouts: 25.2 us -> 4.89 us
    all_gather x1 -> x0, waiting for transfers between devices: 13.9 us -> none  [per_device(): packs = lax.all_gather(pack, 'dp', axis=0, tiled=True)]
    all_to_all x1 -> x0, starting transfers between devices: 6.91 us -> none  [per_device(): packets = lax.all_to_all(packet, 'dp', 0, 0, tiled=True)]
    ppermute x26 -> x15, waiting for transfers between devices: 16.5 us -> 10.4 us  [exchange(): lax.ppermute(x, axis, [(i, i ^ k) for i in range(n)])]
    pallas_call x10 -> x11, Pallas kernels: 26.6 us -> 22.3 us  [call(): pl.pallas_call(kernel, out_shape=tuple(outs), in_specs=in_specs or [IN_VM...]
  transfers between devices with their start and end apart: 31 -> 48, of which waited for: 16 -> 21; matrix products, arithmetic and copies ran while one was open for 0% -> 0% of each run, Pallas kernels for 5% -> 9%
where the time goes in v2:
time: 126 us
  starting transfers between devices  44.6 us (35%)
  waiting for transfers between devices  41.5 us (33%)
  Pallas kernels  22.3 us (18%)
  blocking collectives  10.3 us (8%)
  local copies, waits for them, and re-layouts  4.91 us (4%)
    ppermute x30, starting transfers between devices, flip(): return lax.ppermute(x, 'dp', [(i, i ^ k) for i in range(n)])  34.1 us
    ppermute x30, waiting for transfers between devices, flip(): return lax.ppermute(x, 'dp', [(i, i ^ k) for i in range(n)])  26.5 us
    pallas_call x11, Pallas kernels, call(): pl.pallas_call(kernel, out_shape=tuple(outs), in_specs=in_specs or [IN_VM...  22.3 us
    ppermute x15, waiting for transfers between devices, exchange(): lax.ppermute(x, axis, [(i, i ^ k) for i in range(n)])  10.4 us
    all_to_all x1, blocking collectives, per_device(): sums = lax.all_to_all(send, 'dp', 0, 0, tiled=True)  10.3 us
    ppermute x15, starting transfers between devices, exchange(): lax.ppermute(x, axis, [(i, i ^ k) for i in range(n)])  9.26 us
    unnamed x44, local copies, waits for them, and re-layouts  4.89 us
    ppermute x3, waiting for transfers between devices, per_device(): lax.ppermute(shares[k], 'mp', [(i, i ^ k) for i in range(nmp)])  4.67 us
  transfers between devices with their start and end apart: 48, of which 21 were waited for; matrix products, arithmetic and copies ran while one was open for 0% of the time, Pallas kernels for 9%

profile of v2, /device:TPU:0, one launch (start us, length us, event | category | flops | bytes accessed | tf_op | source)
XLA Modules:
  0.0 125.9 jit_solution(8882769289277462768)
XLA Ops:
  0.6 1.0 convert_element_type.3
  1.7 3.1 %collective-permute-start.2 = (bf16[96,768]{1,0:T(8,128)(2,1)S(1)}, bf16[96,768]{1,0:T(8,128)(2,1)S(1)}, u32[]{:S(2)}, u32[]{:S(2)}) collective-permute-start(bf16[96,768]{1,0:T(8,128)(2,1)S(1)} %slice.8.refs_3_), channel_id=1, source_target_pairs={{0,8},{4,12},{8,0},{12,4},{16,24},{20,28},{24,16},{28,20},{1,9},{5... | collective-permute-start | bytes 442376 | tf_op jit(solution)/shard_map/ppermute | solution.py:633
  4.8 1.5 %collective-permute-start.1 = (bf16[96,768]{1,0:T(8,128)(2,1)S(1)}, bf16[96,768]{1,0:T(8,128)(2,1)S(1)}, u32[]{:S(2)}, u32[]{:S(2)}) collective-permute-start(bf16[96,768]{1,0:T(8,128)(2,1)S(1)} %slice.8.refs_3_), channel_id=1, source_target_pairs={{0,4},{4,0},{8,12},{12,8},{16,20},{20,16},{24,28},{28,24},{1,5},{5... | collective-permute-start | bytes 442376 | tf_op jit(solution)/shard_map/ppermute | solution.py:633
  6.3 2.6 %collective-permute-start = (bf16[96,768]{1,0:T(8,128)(2,1)S(1)}, bf16[96,768]{1,0:T(8,128)(2,1)S(1)}, u32[]{:S(2)}, u32[]{:S(2)}) collective-permute-start(bf16[96,768]{1,0:T(8,128)(2,1)S(1)} %slice.8.refs_3_), channel_id=1, source_target_pairs={{0,16},{4,20},{8,24},{12,28},{16,0},{20,4},{24,8},{28,12},{1,17},{... | collective-permute-start | bytes 442376 | tf_op jit(solution)/shard_map/ppermute | solution.py:633
  8.9 1.2 collective-permute-done.1.refs_4_
  10.1 5.3 %collective-permute-done.refs_7_ = bf16[96,768]{1,0:T(8,128)(2,1)S(1)} collective-permute-done((bf16[96,768]{1,0:T(8,128)(2,1)S(1)}, bf16[96,768]{1,0:T(8,128)(2,1)S(1)}, u32[]{:S(2)}, u32[]{:S(2)}) %collective-permute-start) | collective-permute-done | bytes 147488 | tf_op jit(solution)/shard_map/ppermute | solution.py:633
  15.4 0.8 collective-permute-start.5
  16.2 1.9 %collective-permute-start.4 = (bf16[96,768]{1,0:T(8,128)(2,1)S(1)}, bf16[96,768]{1,0:T(8,128)(2,1)S(1)}, u32[]{:S(2)}, u32[]{:S(2)}) collective-permute-start(bf16[96,768]{1,0:T(8,128)(2,1)S(1)} %collective-permute-done.refs_7_), channel_id=1, source_target_pairs={{0,8},{4,12},{8,0},{12,4},{16,24},{20,28},{24,16},{28,20},{1,9},{5... | collective-permute-start | bytes 442376 | tf_op jit(solution)/shard_map/ppermute | solution.py:633
  18.3 1.3 %collective-permute-start.11 = (bf16[96,384]{1,0:T(8,128)(2,1)S(1)}, bf16[96,384]{1,0:T(8,128)(2,1)S(1)}, u32[]{:S(2)}, u32[]{:S(2)}) collective-permute-start(bf16[96,384]{1,0:T(8,128)(2,1)S(1)} %slice.9.refs_5_), channel_id=1, source_target_pairs={{0,4},{4,0},{8,12},{12,8},{16,20},{20,16},{24,28},{28,24},{1,5},{5... | collective-permute-start | bytes 221192 | tf_op jit(solution)/shard_map/ppermute | solution.py:633
  19.6 3.4 %collective-permute-done.3.refs_6_ = bf16[96,768]{1,0:T(8,128)(2,1)S(1)} collective-permute-done((bf16[96,768]{1,0:T(8,128)(2,1)S(1)}, bf16[96,768]{1,0:T(8,128)(2,1)S(1)}, u32[]{:S(2)}, u32[]{:S(2)}) %collective-permute-start.3) | collective-permute-done | bytes 147488 | tf_op jit(solution)/shard_map/ppermute | solution.py:633
  23.2 1.5 %collective-permute-done.4.refs_9_ = bf16[96,768]{1,0:T(8,128)(2,1)S(1)} collective-permute-done((bf16[96,768]{1,0:T(8,128)(2,1)S(1)}, bf16[96,768]{1,0:T(8,128)(2,1)S(1)}, u32[]{:S(2)}, u32[]{:S(2)}) %collective-permute-start.4) | collective-permute-done | bytes 147488 | tf_op jit(solution)/shard_map/ppermute | solution.py:633
  24.9 0.6 collective-permute-done.12.refs_7_
  25.5 3.1 %collective-permute-done.10.refs_9_ = bf16[96,384]{1,0:T(8,128)(2,1)S(1)} collective-permute-done((bf16[96,384]{1,0:T(8,128)(2,1)S(1)}, bf16[96,384]{1,0:T(8,128)(2,1)S(1)}, u32[]{:S(2)}, u32[]{:S(2)}) %collective-permute-start.10) | collective-permute-done | bytes 73760 | tf_op jit(solution)/shard_map/ppermute | solution.py:633
  28.6 0.6 collective-permute-start.15
  29.2 2.0 %collective-permute-start.13 = (bf16[96,384]{1,0:T(8,128)(2,1)S(1)}, bf16[96,384]{1,0:T(8,128)(2,1)S(1)}, u32[]{:S(2)}, u32[]{:S(2)}) collective-permute-start(bf16[96,384]{1,0:T(8,128)(2,1)S(1)} %collective-permute-done.11.refs_6_), channel_id=1, source_target_pairs={{0,8},{4,12},{8,0},{12,4},{16,24},{20,28},{24,16},{28,20},{1,9},{5... | collective-permute-start | bytes 221192 | tf_op jit(solution)/shard_map/ppermute | solution.py:633
  31.2 0.8 copy-done.4
  32.0 1.1 copy-done.7
  33.1 0.7 copy-done.14
  33.8 0.8 copy-done.19
  34.7 0.7 copy-done.20
  35.4 0.7 copy-done.21
  36.0 1.6 %shard_map.306 = (bf16[256,1024]{1,0:T(8,128)(2,1)S(1)}, bf16[1024,768]{1,0:T(8,128)(2,1)S(1)}, bf16[1024,768]{1,0:T(8,128)(2,1)S(1)}, f32[1024,128]{1,0:T(8,128)S(1)}) custom-call(f32[16,1024]{1,0:T(8,128)S(1)} %bitcast.19, s32[2,1024]{1,0:T(2,128)S(1)} %bitcast.20, s32[1,1024]{1,0:T(1,128)S(1)} %copy-done.21, s32[1,1024]{1,0:T(1,128)S(1)} %copy-done.14, ...), custom_call_target="tpu_custom_call" | custom-call | flops 805306368 | bytes 4998144 | tf_op jit(solution)/shard_map/pallas_call | solution.py:54
  37.7 1.5 %collective-permute-start.16 = (bf16[96,384]{1,0:T(8,128)(2,1)S(1)}, bf16[96,384]{1,0:T(8,128)(2,1)S(1)}, u32[]{:S(2)}, u32[]{:S(2)}) collective-permute-start(bf16[96,384]{1,0:T(8,128)(2,1)S(1)} %collective-permute-done.14.refs_11_), channel_id=1, source_target_pairs={{0,4},{4,0},{8,12},{12,8},{16,20},{20,16},{24,28},{28,24},{1,5},{5... | collective-permute-start | bytes 221192 | tf_op jit(solution)/shard_map/ppermute | solution.py:633
  39.2 2.5 %shard_map.307 = (bf16[24,768]{1,0:T(8,128)(2,1)S(1)}, bf16[192,1024]{1,0:T(8,128)(2,1)S(1)}, bf16[1024,256]{1,0:T(8,128)(2,1)S(1)}, bf16[24,256]{1,0:T(8,128)(2...) custom-call(bf16[1024,768]{1,0:T(8,128)(2,1)S(1)} %get-tuple-element.99.refs_0_.refs_11_, ...), custom_call_target="tpu_custom_call" | custom-call | flops 805306368 | bytes 5338112 | tf_op jit(solution)/shard_map/pallas_call | solution.py:54
  41.8 1.6 %collective-permute-start.8 = (bf16[24,768]{1,0:T(8,128)(2,1)S(1)}, bf16[24,768]{1,0:T(8,128)(2,1)S(1)}, u32[]{:S(2)}, u32[]{:S(2)}) collective-permute-start(bf16[24,768]{1,0:T(8,128)(2,1)S(1)} %get-tuple-element.106.refs_0_), channel_id=1, source_target_pairs={{0,2},{1,3},{2,0},{3,1},{4,6},{5,7},{6,4},{7,5},{8,10},{9,11},{10,... | collective-permute-start | bytes 110600 | tf_op jit(solution)/shard_map/ppermute | solution.py:628
  43.7 1.8 %collective-permute-done.9.refs_3_ = bf16[24,768]{1,0:T(8,128)(2,1)S(1)} collective-permute-done((bf16[24,768]{1,0:T(8,128)(2,1)S(1)}, bf16[24,768]{1,0:T(8,128)(2,1)S(1)}, u32[]{:S(2)}, u32[]{:S(2)}) %collective-permute-start.9) | collective-permute-done | bytes 36896 | tf_op jit(solution)/shard_map/ppermute | solution.py:628
  46.0 0.6 shard_map.308
  46.6 1.1 collective-permute-start.19
  47.7 0.9 collective-permute-start.18
  48.6 1.5 %collective-permute-done.19.refs_3_ = bf16[24,768]{1,0:T(8,128)(2,1)S(1)} collective-permute-done((bf16[24,768]{1,0:T(8,128)(2,1)S(1)}, bf16[24,768]{1,0:T(8,128)(2,1)S(1)}, u32[]{:S(2)}, u32[]{:S(2)}) %collective-permute-start.19) | collective-permute-done | bytes 36896 | tf_op jit(solution)/shard_map/ppermute | solution.py:628
  50.1 1.6 %collective-permute-done.18.refs_2_ = bf16[24,768]{1,0:T(8,128)(2,1)S(1)} collective-permute-done((bf16[24,768]{1,0:T(8,128)(2,1)S(1)}, bf16[24,768]{1,0:T(8,128)(2,1)S(1)}, u32[]{:S(2)}, u32[]{:S(2)}) %collective-permute-start.18) | collective-permute-done | bytes 36896 | tf_op jit(solution)/shard_map/ppermute | solution.py:628
  51.7 1.6 %shard_map.309 = (bf16[24,768]{1,0:T(8,128)(2,1)S(1)}, bf16[24,3840]{1,0:T(8,128)(2,1)S(1)}, f32[24,768]{1,0:T(8,128)S(1)}, f32[8,768]{1,0:T(8,128)S(1)}) custom-call(bf16[24,768]{1,0:T(8,128)(2,1)S(1)} %get-tuple-element.113.refs_0_, bf16[24,768]{1,0:T(8,128)(2,1)S(1)} %collective-permute-done.17.refs_1_, ...), custom_call_target="tpu_custom_call" | custom-call | flops 56623104 | bytes 3613792 | tf_op jit(solution)/shard_map/pallas_call | solution.py:54
  53.3 0.7 collective-permute-start.22
  54.0 0.9 collective-permute-start.21
  55.2 0.6 collective-permute-start.36
  55.8 1.3 %collective-permute-done.22.refs_3_ = bf16[24,768]{1,0:T(8,128)(2,1)S(1)} collective-permute-done((bf16[24,768]{1,0:T(8,128)(2,1)S(1)}, bf16[24,768]{1,0:T(8,128)(2,1)S(1)}, u32[]{:S(2)}, u32[]{:S(2)}) %collective-permute-start.22) | collective-permute-done | bytes 36896 | tf_op jit(solution)/shard_map/ppermute | solution.py:628
  57.1 2.5 %collective-permute-start.35 = (bf16[24,3840]{1,0:T(8,128)(2,1)S(1)}, bf16[24,3840]{1,0:T(8,128)(2,1)S(1)}, u32[]{:S(2)}, u32[]{:S(2)}) collective-permute-start(bf16[24,3840]{1,0:T(8,128)(2,1)S(1)} %get-tuple-element.148.refs_8_.refs_0_), channel_id=1, source_target_pairs={{0,16},{4,20},{8,24},{12,28},{16,0},{20,4},{24,8},{28,12},{1,17},{... | collective-permute-start | bytes 552968 | tf_op jit(solution)/shard_map/ppermute | solution.py:633
  59.6 3.3 %shard_map.310 = (bf16[64,768]{1,0:T(8,128)(2,1)S(1)}, bf16[64,768]{1,0:T(8,128)(2,1)S(1)}, bf16[64,768]{1,0:T(8,128)(2,1)S(1)}, bf16[64,768]{1,0:T(8,128)(2,1)S...) custom-call(bf16[24,768]{1,0:T(8,128)(2,1)S(1)} %get-tuple-element.120.refs_0_, ...), custom_call_target="tpu_custom_call" | custom-call | flops 1610612736 | bytes 7836672 | tf_op jit(solution)/shard_map/pallas_call | solution.py:54
  63.0 1.1 collective-permute-start.24
  64.2 1.0 collective-permute-done.37.refs_10_.refs_2_
  65.1 1.0 collective-permute-start.26
  66.2 1.0 collective-permute-start.27
  67.2 1.5 %collective-permute-done.35.refs_12_.refs_4_ = bf16[24,3840]{1,0:T(8,128)(2,1)S(1)} collective-permute-done((bf16[24,3840]{1,0:T(8,128)(2,1)S(1)}, bf16[24,3840]{1,0:T(8,128)(2,1)S(1)}, u32[]{:S(2)}, u32[]{:S(2)}) %collective-permute-start.35) | collective-permute-done | bytes 184352 | tf_op jit(solution)/shard_map/ppermute | solution.py:633
  69.0 2.5 %collective-permute-done.27.refs_7_ = f32[8,256]{1,0:T(8,128)S(1)} collective-permute-done((f32[8,256]{1,0:T(8,128)S(1)}, f32[8,256]{1,0:T(8,128)S(1)}, u32[]{:S(2)}, u32[]{:S(2)}) %collective-permute-start.27) | collective-permute-done | bytes 8224 | tf_op jit(solution)/shard_map/ppermute | solution.py:633
  71.6 1.7 %collective-permute-start.40 = (bf16[24,3840]{1,0:T(8,128)(2,1)S(1)}, bf16[24,3840]{1,0:T(8,128)(2,1)S(1)}, u32[]{:S(2)}, u32[]{:S(2)}) collective-permute-start(bf16[24,3840]{1,0:T(8,128)(2,1)S(1)} %collective-permute-done.35.refs_12_.refs_4_), channel_id=1, source_target_pairs={{0,4},{4,0},{8,12},{12,8},{16,20},{20,16},{24,28},{28,24},{1,5},{5... | collective-permute-start | bytes 552968 | tf_op jit(solution)/shard_map/ppermute | solution.py:633
  73.4 4.7 %collective-permute-done.25.refs_3_ = bf16[64,768]{1,0:T(8,128)(2,1)S(1)} collective-permute-done((bf16[64,768]{1,0:T(8,128)(2,1)S(1)}, bf16[64,768]{1,0:T(8,128)(2,1)S(1)}, u32[]{:S(2)}, u32[]{:S(2)}) %collective-permute-start.25) | collective-permute-done | bytes 98336 | tf_op jit(solution)/shard_map/ppermute | solution.py:762
  78.3 0.7 collective-permute-done.39.refs_14_.refs_6_
  78.9 1.1 collective-permute-start.41
  80.1 0.9 collective-permute-start.28
  81.0 1.3 %collective-permute-start.32 = (bf16[96,256]{1,0:T(8,128)(2,1)S(1)}, bf16[96,256]{1,0:T(8,128)(2,1)S(1)}, u32[]{:S(2)}, u32[]{:S(2)}) collective-permute-start(bf16[96,256]{1,0:T(8,128)(2,1)S(1)} %get-tuple-element.145), channel_id=1, source_target_pairs={{0,8},{4,12},{8,0},{12,4},{16,24},{20,28},{24,16},{28,20},{1,9},{5... | collective-permute-start | bytes 147464 | tf_op jit(solution)/shard_map/ppermute | solution.py:633
  82.3 2.7 %collective-permute-start.33 = (bf16[96,256]{1,0:T(8,128)(2,1)S(1)}, bf16[96,256]{1,0:T(8,128)(2,1)S(1)}, u32[]{:S(2)}, u32[]{:S(2)}) collective-permute-start(bf16[96,256]{1,0:T(8,128)(2,1)S(1)} %get-tuple-element.146), channel_id=1, source_target_pairs={{0,16},{4,20},{8,24},{12,28},{16,0},{20,4},{24,8},{28,12},{1,17},{... | collective-permute-start | bytes 147464 | tf_op jit(solution)/shard_map/ppermute | solution.py:633
  85.8 1.8 %collective-permute-start.29 = (f32[8,1024]{1,0:T(8,128)S(1)}, f32[8,1024]{1,0:T(8,128)S(1)}, u32[]{:S(2)}, u32[]{:S(2)}) collective-permute-start(f32[8,1024]{1,0:T(8,128)S(1)} %get-tuple-element.141), channel_id=1, source_target_pairs={{0,8},{4,12},{8,0},{12,4},{16,24},{20,28},{24,16},{28,20},{1,9},{5... | collective-permute-start | bytes 98312 | tf_op jit(solution)/shard_map/ppermute | solution.py:633
  87.6 2.2 %collective-permute-start.30 = (f32[8,1024]{1,0:T(8,128)S(1)}, f32[8,1024]{1,0:T(8,128)S(1)}, u32[]{:S(2)}, u32[]{:S(2)}) collective-permute-start(f32[8,1024]{1,0:T(8,128)S(1)} %get-tuple-element.142), channel_id=1, source_target_pairs={{0,16},{4,20},{8,24},{12,28},{16,0},{20,4},{24,8},{28,12},{1,17},{... | collective-permute-start | bytes 98312 | tf_op jit(solution)/shard_map/ppermute | solution.py:633
  90.2 0.7 collective-permute-done.34.refs_7_
  90.9 1.9 %collective-permute-done.30.refs_2_ = f32[8,1024]{1,0:T(8,128)S(1)} collective-permute-done((f32[8,1024]{1,0:T(8,128)S(1)}, f32[8,1024]{1,0:T(8,128)S(1)}, u32[]{:S(2)}, u32[]{:S(2)}) %collective-permute-start.30) | collective-permute-done | bytes 32800 | tf_op jit(solution)/shard_map/ppermute | solution.py:633
  92.8 2.7 %collective-permute-done.31.refs_3_ = f32[8,1024]{1,0:T(8,128)S(1)} collective-permute-done((f32[8,1024]{1,0:T(8,128)S(1)}, f32[8,1024]{1,0:T(8,128)S(1)}, u32[]{:S(2)}, u32[]{:S(2)}) %collective-permute-start.31) | collective-permute-done | bytes 32800 | tf_op jit(solution)/shard_map/ppermute | solution.py:633
  96.0 10.3 %all_to_all.5.refs_0_ = bf16[8,16,512]{2,1,0:T(8,128)(2,1)S(1)} all-to-all(bf16[8,16,512]{2,1,0:T(8,128)(2,1)S(1)} %get-tuple-element.156), channel_id=1, replica_groups=mesh['dp'=8,'mp'=4] {'dp'}, dimensions={0} | all-to-all | bytes 262144 | tf_op jit(solution)/shard_map/all_to_all | solution.py:792
  106.3 0.9 collective-permute-start.43
  107.2 0.9 collective-permute-start.42
  108.2 1.0 shard_map.314
  109.7 1.1 collective-permute-start.46
  110.8 3.7 %collective-permute-done.47.refs_7_ = f32[8,128]{1,0:T(8,128)S(1)} collective-permute-done((f32[8,128]{1,0:T(8,128)S(1)}, f32[8,128]{1,0:T(8,128)S(1)}, u32[]{:S(2)}, u32[]{:S(2)}) %collective-permute-start.47) | collective-permute-done | bytes 4128 | tf_op jit(solution)/shard_map/ppermute | solution.py:628
  114.5 3.0 %shard_map.315 = (f32[6,96,96]{2,1,0:T(8,128)S(1)}, f32[6,192,192]{2,1,0:T(8,128)S(1)}, f32[6,96,192]{2,1,0:T(8,128)S(1)}) custom-call(f32[4,96,192]{2,1,0:T(8,128)S(1)} %get-tuple-element.159.layer.refs_9_, f32[96,256]{1,0:T(8,128)S(1)} %get-tuple-element.160.up_grad.refs_10_, f32[96,256]{1,0:T(8,128)S(1)} %get-tuple-element.161.down_grad.refs_11_, ...), custom_call_target="tpu_custom_call" | custom-call | flops 764411904 | bytes 3145728 | tf_op jit(solution)/shard_map/pallas_call | solution.py:54
  117.7 8.1 %shard_map.316 = (f32[1,1]{1,0:T(1,128)}, f32[1,1]{1,0:T(1,128)}, f32[1,1]{1,0:T(1,128)}, f32[96,1152]{1,0:T(8,128)}, f32[96,1152]{1,0:T(8,128)}, /*index=5*/f32...) custom-call(bf16[8,16,512]{2,1,0:T(8,128)(2,1)S(1)} %all_to_all.5.re, ...), custom_call_target="tpu_custom_call" | custom-call | flops 11796480 | bytes 26970124 | tf_op jit(solution)/shard_map/pallas_call | solution.py:54
  (91 shorter events, 4.9 us)
Async XLA Ops:
  1.7 7.2 %collective-permute-start.2 = (bf16[96,768]{1,0:T(8,128)(2,1)S(1)}, bf16[96,768]{1,0:T(8,128)(2,1)S(1)}, u32[]{:S(2)}, u32[]{:S(2)}) collective-permute-start(bf16[96,768]{1,0:T(8,128)(2,1)S(1)} %slice.8.refs_3_), channel_id=1, source_target_pairs={{0,8},{4,12},{8,0},{12,4},{16,24},{20,28},{24,16},{28,20},{1,9},{5... | collective-permute-start | bytes 442376 | tf_op jit(solution)/shard_map/ppermute | solution.py:633
  4.8 5.3 %collective-permute-start.1 = (bf16[96,768]{1,0:T(8,128)(2,1)S(1)}, bf16[96,768]{1,0:T(8,128)(2,1)S(1)}, u32[]{:S(2)}, u32[]{:S(2)}) collective-permute-start(bf16[96,768]{1,0:T(8,128)(2,1)S(1)} %slice.8.refs_3_), channel_id=1, source_target_pairs={{0,4},{4,0},{8,12},{12,8},{16,20},{20,16},{24,28},{28,24},{1,5},{5... | collective-permute-start | bytes 442376 | tf_op jit(solution)/shard_map/ppermute | solution.py:633
  6.3 9.1 %collective-permute-start = (bf16[96,768]{1,0:T(8,128)(2,1)S(1)}, bf16[96,768]{1,0:T(8,128)(2,1)S(1)}, u32[]{:S(2)}, u32[]{:S(2)}) collective-permute-start(bf16[96,768]{1,0:T(8,128)(2,1)S(1)} %slice.8.refs_3_), channel_id=1, source_target_pairs={{0,16},{4,20},{8,24},{12,28},{16,0},{20,4},{24,8},{28,12},{1,17},{... | collective-permute-start | bytes 442376 | tf_op jit(solution)/shard_map/ppermute | solution.py:633
  15.4 7.6 %collective-permute-start.3 = (bf16[96,768]{1,0:T(8,128)(2,1)S(1)}, bf16[96,768]{1,0:T(8,128)(2,1)S(1)}, u32[]{:S(2)}, u32[]{:S(2)}) collective-permute-start(bf16[96,768]{1,0:T(8,128)(2,1)S(1)} %collective-permute-done.1.refs_4_), channel_id=1, source_target_pairs={{0,8},{4,12},{8,0},{12,4},{16,24},{20,28},{24,16},{28,20},{1,9},{5... | collective-permute-start | bytes 442376 | tf_op jit(solution)/shard_map/ppermute | solution.py:633
  15.4 7.8 %collective-permute-start.5 = (bf16[96,768]{1,0:T(8,128)(2,1)S(1)}, bf16[96,768]{1,0:T(8,128)(2,1)S(1)}, u32[]{:S(2)}, u32[]{:S(2)}) collective-permute-start(bf16[96,768]{1,0:T(8,128)(2,1)S(1)} %collective-permute-done.refs_7_), channel_id=1, source_target_pairs={{0,4},{4,0},{8,12},{12,8},{16,20},{20,16},{24,28},{28,24},{1,5},{5... | collective-permute-start | bytes 442376 | tf_op jit(solution)/shard_map/ppermute | solution.py:633
  16.2 8.6 %collective-permute-start.4 = (bf16[96,768]{1,0:T(8,128)(2,1)S(1)}, bf16[96,768]{1,0:T(8,128)(2,1)S(1)}, u32[]{:S(2)}, u32[]{:S(2)}) collective-permute-start(bf16[96,768]{1,0:T(8,128)(2,1)S(1)} %collective-permute-done.refs_7_), channel_id=1, source_target_pairs={{0,8},{4,12},{8,0},{12,4},{16,24},{20,28},{24,16},{28,20},{1,9},{5... | collective-permute-start | bytes 442376 | tf_op jit(solution)/shard_map/ppermute | solution.py:633
  18.0 7.5 %collective-permute-start.12 = (bf16[96,384]{1,0:T(8,128)(2,1)S(1)}, bf16[96,384]{1,0:T(8,128)(2,1)S(1)}, u32[]{:S(2)}, u32[]{:S(2)}) collective-permute-start(bf16[96,384]{1,0:T(8,128)(2,1)S(1)} %slice.9.refs_5_), channel_id=1, source_target_pairs={{0,8},{4,12},{8,0},{12,4},{16,24},{20,28},{24,16},{28,20},{1,9},{5... | collective-permute-start | bytes 221192 | tf_op jit(solution)/shard_map/ppermute | solution.py:633
  18.3 7.3 %collective-permute-start.11 = (bf16[96,384]{1,0:T(8,128)(2,1)S(1)}, bf16[96,384]{1,0:T(8,128)(2,1)S(1)}, u32[]{:S(2)}, u32[]{:S(2)}) collective-permute-start(bf16[96,384]{1,0:T(8,128)(2,1)S(1)} %slice.9.refs_5_), channel_id=1, source_target_pairs={{0,4},{4,0},{8,12},{12,8},{16,20},{20,16},{24,28},{28,24},{1,5},{5... | collective-permute-start | bytes 221192 | tf_op jit(solution)/shard_map/ppermute | solution.py:633
  23.0 5.7 %collective-permute-start.10 = (bf16[96,384]{1,0:T(8,128)(2,1)S(1)}, bf16[96,384]{1,0:T(8,128)(2,1)S(1)}, u32[]{:S(2)}, u32[]{:S(2)}) collective-permute-start(bf16[96,384]{1,0:T(8,128)(2,1)S(1)} %slice.9.refs_5_), channel_id=1, source_target_pairs={{0,16},{4,20},{8,24},{12,28},{16,0},{20,4},{24,8},{28,12},{1,17},{... | collective-permute-start | bytes 221192 | tf_op jit(solution)/shard_map/ppermute | solution.py:633
  24.8 14.5 %collective-permute-start.6 = (bf16[96,768]{1,0:T(8,128)(2,1)S(1)}, bf16[96,768]{1,0:T(8,128)(2,1)S(1)}, u32[]{:S(2)}, u32[]{:S(2)}) collective-permute-start(bf16[96,768]{1,0:T(8,128)(2,1)S(1)} %collective-permute-done.4.refs_9_), channel_id=1, source_target_pairs={{0,4},{4,0},{8,12},{12,8},{16,20},{20,16},{24,28},{28,24},{1,5},{5... | collective-permute-start | bytes 442376 | tf_op jit(solution)/shard_map/ppermute | solution.py:633
  28.6 9.1 %collective-permute-start.15 = (bf16[96,384]{1,0:T(8,128)(2,1)S(1)}, bf16[96,384]{1,0:T(8,128)(2,1)S(1)}, u32[]{:S(2)}, u32[]{:S(2)}) collective-permute-start(bf16[96,384]{1,0:T(8,128)(2,1)S(1)} %collective-permute-done.10.refs_9_), channel_id=1, source_target_pairs={{0,4},{4,0},{8,12},{12,8},{16,20},{20,16},{24,28},{28,24},{1,5},{5... | collective-permute-start | bytes 221192 | tf_op jit(solution)/shard_map/ppermute | solution.py:633
  29.2 8.5 %collective-permute-start.14 = (bf16[96,384]{1,0:T(8,128)(2,1)S(1)}, bf16[96,384]{1,0:T(8,128)(2,1)S(1)}, u32[]{:S(2)}, u32[]{:S(2)}) collective-permute-start(bf16[96,384]{1,0:T(8,128)(2,1)S(1)} %collective-permute-done.10.refs_9_), channel_id=1, source_target_pairs={{0,8},{4,12},{8,0},{12,4},{16,24},{20,28},{24,16},{28,20},{1,9},{5... | collective-permute-start | bytes 221192 | tf_op jit(solution)/shard_map/ppermute | solution.py:633
  29.2 8.5 %collective-permute-start.13 = (bf16[96,384]{1,0:T(8,128)(2,1)S(1)}, bf16[96,384]{1,0:T(8,128)(2,1)S(1)}, u32[]{:S(2)}, u32[]{:S(2)}) collective-permute-start(bf16[96,384]{1,0:T(8,128)(2,1)S(1)} %collective-permute-done.11.refs_6_), channel_id=1, source_target_pairs={{0,8},{4,12},{8,0},{12,4},{16,24},{20,28},{24,16},{28,20},{1,9},{5... | collective-permute-start | bytes 221192 | tf_op jit(solution)/shard_map/ppermute | solution.py:633
  36.0 10.0 %copy-start.5 = (f32[11,768]{1,0:T(8,128)S(1)}, f32[11,768]{1,0:T(8,128)}, u32[]{:S(2)}) copy-start(f32[11,768]{1,0:T(8,128)} %refs_25_.1) | copy-start | bytes 101380
  37.7 14.0 %copy-start = (f32[768,768]{1,0:T(8,128)S(1)}, f32[768,768]{1,0:T(8,128)}, u32[]{:S(2)}) copy-start(f32[768,768]{1,0:T(8,128)} %refs_21_.1) | copy-start | bytes 7077892
  37.7 14.0 %copy-start.15 = (s32[1,1024]{1,0:T(1,128)S(1)}, s32[1,1024]{1,0:T(1,128)}, u32[]{:S(2)}) copy-start(s32[1,1024]{1,0:T(1,128)} %refs_15_.2) | copy-start | bytes 12292
  37.7 14.0 %copy-start.16 = (f32[1,24]{1,0:T(1,128)S(1)}, f32[1,24]{1,0:T(1,128)}, u32[]{:S(2)}) copy-start(f32[1,24]{1,0:T(1,128)} %refs_7_.2) | copy-start | bytes 292
  37.7 6.0 %collective-permute-start.16 = (bf16[96,384]{1,0:T(8,128)(2,1)S(1)}, bf16[96,384]{1,0:T(8,128)(2,1)S(1)}, u32[]{:S(2)}, u32[]{:S(2)}) collective-permute-start(bf16[96,384]{1,0:T(8,128)(2,1)S(1)} %collective-permute-done.14.refs_11_), channel_id=1, source_target_pairs={{0,4},{4,0},{8,12},{12,8},{16,20},{20,16},{24,28},{28,24},{1,5},{5... | collective-permute-start | bytes 221192 | tf_op jit(solution)/shard_map/ppermute | solution.py:633
  41.8 3.8 %collective-permute-start.9 = (bf16[24,768]{1,0:T(8,128)(2,1)S(1)}, bf16[24,768]{1,0:T(8,128)(2,1)S(1)}, u32[]{:S(2)}, u32[]{:S(2)}) collective-permute-start(bf16[24,768]{1,0:T(8,128)(2,1)S(1)} %get-tuple-element.106.refs_0_), channel_id=1, source_target_pairs={{0,3},{1,2},{2,1},{3,0},{4,7},{5,6},{6,5},{7,4},{8,11},{9,10},{10,... | collective-permute-start | bytes 110600 | tf_op jit(solution)/shard_map/ppermute | solution.py:628
  41.8 4.2 %collective-permute-start.8 = (bf16[24,768]{1,0:T(8,128)(2,1)S(1)}, bf16[24,768]{1,0:T(8,128)(2,1)S(1)}, u32[]{:S(2)}, u32[]{:S(2)}) collective-permute-start(bf16[24,768]{1,0:T(8,128)(2,1)S(1)} %get-tuple-element.106.refs_0_), channel_id=1, source_target_pairs={{0,2},{1,3},{2,0},{3,1},{4,6},{5,7},{6,4},{7,5},{8,10},{9,11},{10,... | collective-permute-start | bytes 110600 | tf_op jit(solution)/shard_map/ppermute | solution.py:628
  43.4 2.6 %collective-permute-start.7 = (bf16[24,768]{1,0:T(8,128)(2,1)S(1)}, bf16[24,768]{1,0:T(8,128)(2,1)S(1)}, u32[]{:S(2)}, u32[]{:S(2)}) collective-permute-start(bf16[24,768]{1,0:T(8,128)(2,1)S(1)} %get-tuple-element.106.refs_0_), channel_id=1, source_target_pairs={{0,1},{1,0},{2,3},{3,2},{4,5},{5,4},{6,7},{7,6},{8,9},{9,8},{10,11... | collective-permute-start | bytes 110600 | tf_op jit(solution)/shard_map/ppermute | solution.py:628
  46.6 3.4 %collective-permute-start.19 = (bf16[24,768]{1,0:T(8,128)(2,1)S(1)}, bf16[24,768]{1,0:T(8,128)(2,1)S(1)}, u32[]{:S(2)}, u32[]{:S(2)}) collective-permute-start(bf16[24,768]{1,0:T(8,128)(2,1)S(1)} %get-tuple-element.113.refs_0_), channel_id=1, source_target_pairs={{0,3},{1,2},{2,1},{3,0},{4,7},{5,6},{6,5},{7,4},{8,11},{9,10},{10,... | collective-permute-start | bytes 110600 | tf_op jit(solution)/shard_map/ppermute | solution.py:628
  47.7 4.0 %collective-permute-start.18 = (bf16[24,768]{1,0:T(8,128)(2,1)S(1)}, bf16[24,768]{1,0:T(8,128)(2,1)S(1)}, u32[]{:S(2)}, u32[]{:S(2)}) collective-permute-start(bf16[24,768]{1,0:T(8,128)(2,1)S(1)} %get-tuple-element.113.refs_0_), channel_id=1, source_target_pairs={{0,2},{1,3},{2,0},{3,1},{4,6},{5,7},{6,4},{7,5},{8,10},{9,11},{10,... | collective-permute-start | bytes 110600 | tf_op jit(solution)/shard_map/ppermute | solution.py:628
  48.6 3.1 %collective-permute-start.17 = (bf16[24,768]{1,0:T(8,128)(2,1)S(1)}, bf16[24,768]{1,0:T(8,128)(2,1)S(1)}, u32[]{:S(2)}, u32[]{:S(2)}) collective-permute-start(bf16[24,768]{1,0:T(8,128)(2,1)S(1)} %get-tuple-element.113.refs_0_), channel_id=1, source_target_pairs={{0,1},{1,0},{2,3},{3,2},{4,5},{5,4},{6,7},{7,6},{8,9},{9,8},{10,11... | collective-permute-start | bytes 110600 | tf_op jit(solution)/shard_map/ppermute | solution.py:628
  53.3 3.8 %collective-permute-start.22 = (bf16[24,768]{1,0:T(8,128)(2,1)S(1)}, bf16[24,768]{1,0:T(8,128)(2,1)S(1)}, u32[]{:S(2)}, u32[]{:S(2)}) collective-permute-start(bf16[24,768]{1,0:T(8,128)(2,1)S(1)} %get-tuple-element.120.refs_0_), channel_id=1, source_target_pairs={{0,3},{1,2},{2,1},{3,0},{4,7},{5,6},{6,5},{7,4},{8,11},{9,10},{10,... | collective-permute-start | bytes 110600 | tf_op jit(solution)/shard_map/ppermute | solution.py:628
  54.0 5.6 %collective-permute-start.21 = (bf16[24,768]{1,0:T(8,128)(2,1)S(1)}, bf16[24,768]{1,0:T(8,128)(2,1)S(1)}, u32[]{:S(2)}, u32[]{:S(2)}) collective-permute-start(bf16[24,768]{1,0:T(8,128)(2,1)S(1)} %get-tuple-element.120.refs_0_), channel_id=1, source_target_pairs={{0,2},{1,3},{2,0},{3,1},{4,6},{5,7},{6,4},{7,5},{8,10},{9,11},{10,... | collective-permute-start | bytes 110600 | tf_op jit(solution)/shard_map/ppermute | solution.py:628
  54.8 4.8 %collective-permute-start.20 = (bf16[24,768]{1,0:T(8,128)(2,1)S(1)}, bf16[24,768]{1,0:T(8,128)(2,1)S(1)}, u32[]{:S(2)}, u32[]{:S(2)}) collective-permute-start(bf16[24,768]{1,0:T(8,128)(2,1)S(1)} %get-tuple-element.120.refs_0_), channel_id=1, source_target_pairs={{0,1},{1,0},{2,3},{3,2},{4,5},{5,4},{6,7},{7,6},{8,9},{9,8},{10,11... | collective-permute-start | bytes 110600 | tf_op jit(solution)/shard_map/ppermute | solution.py:628
  55.2 9.9 %collective-permute-start.37 = (bf16[24,3840]{1,0:T(8,128)(2,1)S(1)}, bf16[24,3840]{1,0:T(8,128)(2,1)S(1)}, u32[]{:S(2)}, u32[]{:S(2)}) collective-permute-start(bf16[24,3840]{1,0:T(8,128)(2,1)S(1)} %get-tuple-element.148.refs_8_.refs_0_), channel_id=1, source_target_pairs={{0,8},{4,12},{8,0},{12,4},{16,24},{20,28},{24,16},{28,20},{1,9},{5... | collective-permute-start | bytes 552968 | tf_op jit(solution)/shard_map/ppermute | solution.py:633
  55.2 10.9 %collective-permute-start.36 = (bf16[24,3840]{1,0:T(8,128)(2,1)S(1)}, bf16[24,3840]{1,0:T(8,128)(2,1)S(1)}, u32[]{:S(2)}, u32[]{:S(2)}) collective-permute-start(bf16[24,3840]{1,0:T(8,128)(2,1)S(1)} %get-tuple-element.148.refs_8_.refs_0_), channel_id=1, source_target_pairs={{0,4},{4,0},{8,12},{12,8},{16,20},{20,16},{24,28},{28,24},{1,5},{5... | collective-permute-start | bytes 552968 | tf_op jit(solution)/shard_map/ppermute | solution.py:633
  57.1 11.6 %collective-permute-start.35 = (bf16[24,3840]{1,0:T(8,128)(2,1)S(1)}, bf16[24,3840]{1,0:T(8,128)(2,1)S(1)}, u32[]{:S(2)}, u32[]{:S(2)}) collective-permute-start(bf16[24,3840]{1,0:T(8,128)(2,1)S(1)} %get-tuple-element.148.refs_8_.refs_0_), channel_id=1, source_target_pairs={{0,16},{4,20},{8,24},{12,28},{16,0},{20,4},{24,8},{28,12},{1,17},{... | collective-permute-start | bytes 552968 | tf_op jit(solution)/shard_map/ppermute | solution.py:633
  59.6 54.9 %copy-start.17 = (f32[1,6,192,192]{3,2,1,0:T(8,128)S(1)}, f32[1,6,192,192]{3,2,1,0:T(8,128)}, u32[]{:S(2)}) copy-start(f32[1,6,192,192]{3,2,1,0:T(8,128)} %param.28) | copy-start | bytes 2654212
  59.6 54.9 %copy-start.18 = (f32[96,6,96]{2,0,1:T(8,128)S(1)}, f32[96,6,96]{2,0,1:T(8,128)}, u32[]{:S(2)}) copy-start(f32[96,6,96]{2,0,1:T(8,128)} %param.27) | copy-start | bytes 663556
  59.6 58.0 %copy-start.9 = (f32[224,768]{1,0:T(8,128)S(1)}, f32[224,768]{1,0:T(8,128)}, u32[]{:S(2)}) copy-start(f32[224,768]{1,0:T(8,128)} %refs_19_.1) | copy-start | bytes 2064388
  59.6 58.0 %copy-start.10 = (f32[224,768]{1,0:T(8,128)S(1)}, f32[224,768]{1,0:T(8,128)}, u32[]{:S(2)}) copy-start(f32[224,768]{1,0:T(8,128)} %refs_20_.1) | copy-start | bytes 2064388
  63.0 10.4 %collective-permute-start.23 = (bf16[64,768]{1,0:T(8,128)(2,1)S(1)}, bf16[64,768]{1,0:T(8,128)(2,1)S(1)}, u32[]{:S(2)}, u32[]{:S(2)}) collective-permute-start(bf16[64,768]{1,0:T(8,128)(2,1)S(1)} %get-tuple-element.131), channel_id=1, source_target_pairs={{0,1},{1,0},{2,3},{3,2},{4,5},{5,4},{6,7},{7,6},{8,9},{9,8},{10,11... | collective-permute-start | bytes 294920 | tf_op jit(solution)/shard_map/ppermute | solution.py:762
  63.0 10.3 %collective-permute-start.24 = (bf16[64,768]{1,0:T(8,128)(2,1)S(1)}, bf16[64,768]{1,0:T(8,128)(2,1)S(1)}, u32[]{:S(2)}, u32[]{:S(2)}) collective-permute-start(bf16[64,768]{1,0:T(8,128)(2,1)S(1)} %get-tuple-element.132), channel_id=1, source_target_pairs={{0,2},{1,3},{2,0},{3,1},{4,6},{5,7},{6,4},{7,5},{8,10},{9,11},{10,... | collective-permute-start | bytes 294920 | tf_op jit(solution)/shard_map/ppermute | solution.py:762
  65.1 12.9 %collective-permute-start.26 = (bf16[4,96,256]{2,1,0:T(8,128)(2,1)S(1)}, bf16[4,96,256]{2,1,0:T(8,128)(2,1)S(1)}, u32[]{:S(2)}, u32[]{:S(2)}) collective-permute-start(bf16[4,96,256]{2,1,0:T(8,128)(2,1)S(1)} %get-tuple-element.135), channel_id=1, source_target_pairs={{0,4},{4,0},{8,12},{12,8},{16,20},{20,16},{24,28},{28,24},{1,5},{5... | collective-permute-start | bytes 589832 | tf_op jit(solution)/shard_map/ppermute | solution.py:633
  66.2 5.4 %collective-permute-start.27 = (f32[8,256]{1,0:T(8,128)S(1)}, f32[8,256]{1,0:T(8,128)S(1)}, u32[]{:S(2)}, u32[]{:S(2)}) collective-permute-start(f32[8,256]{1,0:T(8,128)S(1)} %get-tuple-element.136.refs_6_), channel_id=1, source_target_pairs={{0,4},{4,0},{8,12},{12,8},{16,20},{20,16},{24,28},{28,24},{1,5},{5... | collective-permute-start | bytes 24584 | tf_op jit(solution)/shard_map/ppermute | solution.py:633
  68.7 9.6 %collective-permute-start.38 = (bf16[24,3840]{1,0:T(8,128)(2,1)S(1)}, bf16[24,3840]{1,0:T(8,128)(2,1)S(1)}, u32[]{:S(2)}, u32[]{:S(2)}) collective-permute-start(bf16[24,3840]{1,0:T(8,128)(2,1)S(1)} %collective-permute-done.36.refs_9_.refs_1_), channel_id=1, source_target_pairs={{0,8},{4,12},{8,0},{12,4},{16,24},{20,28},{24,16},{28,20},{1,9},{5... | collective-permute-start | bytes 552968 | tf_op jit(solution)/shard_map/ppermute | solution.py:633
  71.6 6.7 %collective-permute-start.40 = (bf16[24,3840]{1,0:T(8,128)(2,1)S(1)}, bf16[24,3840]{1,0:T(8,128)(2,1)S(1)}, u32[]{:S(2)}, u32[]{:S(2)}) collective-permute-start(bf16[24,3840]{1,0:T(8,128)(2,1)S(1)} %collective-permute-done.35.refs_12_.refs_4_), channel_id=1, source_target_pairs={{0,4},{4,0},{8,12},{12,8},{16,20},{20,16},{24,28},{28,24},{1,5},{5... | collective-permute-start | bytes 552968 | tf_op jit(solution)/shard_map/ppermute | solution.py:633
  73.3 5.6 %collective-permute-start.39 = (bf16[24,3840]{1,0:T(8,128)(2,1)S(1)}, bf16[24,3840]{1,0:T(8,128)(2,1)S(1)}, u32[]{:S(2)}, u32[]{:S(2)}) collective-permute-start(bf16[24,3840]{1,0:T(8,128)(2,1)S(1)} %collective-permute-done.35.refs_12_.refs_4_), channel_id=1, source_target_pairs={{0,8},{4,12},{8,0},{12,4},{16,24},{20,28},{24,16},{28,20},{1,9},{5... | collective-permute-start | bytes 552968 | tf_op jit(solution)/shard_map/ppermute | solution.py:633
  73.4 4.7 %collective-permute-start.25 = (bf16[64,768]{1,0:T(8,128)(2,1)S(1)}, bf16[64,768]{1,0:T(8,128)(2,1)S(1)}, u32[]{:S(2)}, u32[]{:S(2)}) collective-permute-start(bf16[64,768]{1,0:T(8,128)(2,1)S(1)} %get-tuple-element.133), channel_id=1, source_target_pairs={{0,3},{1,2},{2,1},{3,0},{4,7},{5,6},{6,5},{7,4},{8,11},{9,10},{10,... | collective-permute-start | bytes 294920 | tf_op jit(solution)/shard_map/ppermute | solution.py:762
  78.1 39.5 %copy-start.8 = (f32[224,768]{1,0:T(8,128)S(1)}, f32[224,768]{1,0:T(8,128)}, u32[]{:S(2)}) copy-start(f32[224,768]{1,0:T(8,128)} %refs_18_.1) | copy-start | bytes 2064388
  78.1 39.5 %copy-start.11 = (f32[96,6,96]{2,0,1:T(8,128)S(1)}, f32[96,6,96]{2,0,1:T(8,128)}, u32[]{:S(2)}) copy-start(f32[96,6,96]{2,0,1:T(8,128)} %param.25) | copy-start | bytes 663556
  78.9 16.6 %collective-permute-start.41 = (bf16[24,3840]{1,0:T(8,128)(2,1)S(1)}, bf16[24,3840]{1,0:T(8,128)(2,1)S(1)}, u32[]{:S(2)}, u32[]{:S(2)}) collective-permute-start(bf16[24,3840]{1,0:T(8,128)(2,1)S(1)} %collective-permute-done.39.refs_14_.refs_6_), channel_id=1, source_target_pairs={{0,4},{4,0},{8,12},{12,8},{16,20},{20,16},{24,28},{28,24},{1,5},{5... | collective-permute-start | bytes 552968 | tf_op jit(solution)/shard_map/ppermute | solution.py:633
  80.1 5.7 %collective-permute-start.28 = (bf16[32,768]{1,0:T(8,128)(2,1)S(1)}, bf16[32,768]{1,0:T(8,128)(2,1)S(1)}, u32[]{:S(2)}, u32[]{:S(2)}) collective-permute-start(bf16[32,768]{1,0:T(8,128)(2,1)S(1)} %get-tuple-element.138), channel_id=1, source_target_pairs={{0,4},{4,0},{8,12},{12,8},{16,20},{20,16},{24,28},{28,24},{1,5},{5... | collective-permute-start | bytes 147464 | tf_op jit(solution)/shard_map/ppermute | solution.py:633
  81.0 6.6 %collective-permute-start.32 = (bf16[96,256]{1,0:T(8,128)(2,1)S(1)}, bf16[96,256]{1,0:T(8,128)(2,1)S(1)}, u32[]{:S(2)}, u32[]{:S(2)}) collective-permute-start(bf16[96,256]{1,0:T(8,128)(2,1)S(1)} %get-tuple-element.145), channel_id=1, source_target_pairs={{0,8},{4,12},{8,0},{12,4},{16,24},{20,28},{24,16},{28,20},{1,9},{5... | collective-permute-start | bytes 147464 | tf_op jit(solution)/shard_map/ppermute | solution.py:633
  82.3 7.6 %collective-permute-start.33 = (bf16[96,256]{1,0:T(8,128)(2,1)S(1)}, bf16[96,256]{1,0:T(8,128)(2,1)S(1)}, u32[]{:S(2)}, u32[]{:S(2)}) collective-permute-start(bf16[96,256]{1,0:T(8,128)(2,1)S(1)} %get-tuple-element.146), channel_id=1, source_target_pairs={{0,16},{4,20},{8,24},{12,28},{16,0},{20,4},{24,8},{28,12},{1,17},{... | collective-permute-start | bytes 147464 | tf_op jit(solution)/shard_map/ppermute | solution.py:633
  85.0 5.9 %collective-permute-start.34 = (bf16[96,256]{1,0:T(8,128)(2,1)S(1)}, bf16[96,256]{1,0:T(8,128)(2,1)S(1)}, u32[]{:S(2)}, u32[]{:S(2)}) collective-permute-start(bf16[96,256]{1,0:T(8,128)(2,1)S(1)} %get-tuple-element.147), channel_id=1, source_target_pairs={{0,24},{4,28},{8,16},{12,20},{16,8},{20,12},{24,0},{28,4},{1,25},{... | collective-permute-start | bytes 147464 | tf_op jit(solution)/shard_map/ppermute | solution.py:633
  85.8 5.1 %collective-permute-start.29 = (f32[8,1024]{1,0:T(8,128)S(1)}, f32[8,1024]{1,0:T(8,128)S(1)}, u32[]{:S(2)}, u32[]{:S(2)}) collective-permute-start(f32[8,1024]{1,0:T(8,128)S(1)} %get-tuple-element.141), channel_id=1, source_target_pairs={{0,8},{4,12},{8,0},{12,4},{16,24},{20,28},{24,16},{28,20},{1,9},{5... | collective-permute-start | bytes 98312 | tf_op jit(solution)/shard_map/ppermute | solution.py:633
  87.6 5.2 %collective-permute-start.30 = (f32[8,1024]{1,0:T(8,128)S(1)}, f32[8,1024]{1,0:T(8,128)S(1)}, u32[]{:S(2)}, u32[]{:S(2)}) collective-permute-start(f32[8,1024]{1,0:T(8,128)S(1)} %get-tuple-element.142), channel_id=1, source_target_pairs={{0,16},{4,20},{8,24},{12,28},{16,0},{20,4},{24,8},{28,12},{1,17},{... | collective-permute-start | bytes 98312 | tf_op jit(solution)/shard_map/ppermute | solution.py:633
  89.8 5.7 %collective-permute-start.31 = (f32[8,1024]{1,0:T(8,128)S(1)}, f32[8,1024]{1,0:T(8,128)S(1)}, u32[]{:S(2)}, u32[]{:S(2)}) collective-permute-start(f32[8,1024]{1,0:T(8,128)S(1)} %get-tuple-element.143), channel_id=1, source_target_pairs={{0,24},{4,28},{8,16},{12,20},{16,8},{20,12},{24,0},{28,4},{1,25},{... | collective-permute-start | bytes 98312 | tf_op jit(solution)/shard_map/ppermute | solution.py:633
  95.5 22.1 %copy-start.2 = (f32[768,768]{1,0:T(8,128)S(1)}, f32[768,768]{1,0:T(8,128)}, u32[]{:S(2)}) copy-start(f32[768,768]{1,0:T(8,128)} %refs_23_.1) | copy-start | bytes 7077892
  96.0 21.6 %copy-start.1 = (f32[768,768]{1,0:T(8,128)S(1)}, f32[768,768]{1,0:T(8,128)}, u32[]{:S(2)}) copy-start(f32[768,768]{1,0:T(8,128)} %refs_22_.1) | copy-start | bytes 7077892
  96.0 21.6 %copy-start.3 = (f32[96,1152]{1,0:T(8,128)S(1)}, f32[96,1152]{1,0:T(8,128)}, u32[]{:S(2)}) copy-start(f32[96,1152]{1,0:T(8,128)} %refs_15_.3) | copy-start | bytes 1327108
  96.0 21.6 %copy-start.6 = (f32[1,6,192,192]{3,2,1,0:T(8,128)S(1)}, f32[1,6,192,192]{3,2,1,0:T(8,128)}, u32[]{:S(2)}) copy-start(f32[1,6,192,192]{3,2,1,0:T(8,128)} %param.26) | copy-start | bytes 2654212
  96.0 21.6 %copy-start.12 = (f32[11,768]{1,0:T(8,128)S(1)}, f32[11,768]{1,0:T(8,128)}, u32[]{:S(2)}) copy-start(f32[11,768]{1,0:T(8,128)} %refs_26_.1) | copy-start | bytes 101380
  96.0 21.6 %copy-start.13 = (f32[11,768]{1,0:T(8,128)S(1)}, f32[11,768]{1,0:T(8,128)}, u32[]{:S(2)}) copy-start(f32[11,768]{1,0:T(8,128)} %refs_27_.1) | copy-start | bytes 101380
  106.3 11.2 %collective-permute-start.44 = (bf16[8,16,512]{2,1,0:T(8,128)(2,1)S(1)}, bf16[8,16,512]{2,1,0:T(8,128)(2,1)S(1)}, u32[]{:S(2)}, u32[]{:S(2)}) collective-permute-start(bf16[8,16,512]{2,1,0:T(8,128)(2,1)S(1)} %all_to_all.5.refs_0_), channel_id=1, source_target_pairs={{0,3},{1,2},{2,1},{3,0},{4,7},{5,6},{6,5},{7,4},{8,11},{9,10},{10,... | collective-permute-start | bytes 393224 | tf_op jit(solution)/shard_map/ppermute | solution.py:628
  106.3 11.2 %collective-permute-start.43 = (bf16[8,16,512]{2,1,0:T(8,128)(2,1)S(1)}, bf16[8,16,512]{2,1,0:T(8,128)(2,1)S(1)}, u32[]{:S(2)}, u32[]{:S(2)}) collective-permute-start(bf16[8,16,512]{2,1,0:T(8,128)(2,1)S(1)} %all_to_all.5.refs_0_), channel_id=1, source_target_pairs={{0,2},{1,3},{2,0},{3,1},{4,6},{5,7},{6,4},{7,5},{8,10},{9,11},{10,... | collective-permute-start | bytes 393224 | tf_op jit(solution)/shard_map/ppermute | solution.py:628
  107.2 10.3 %collective-permute-start.42 = (bf16[8,16,512]{2,1,0:T(8,128)(2,1)S(1)}, bf16[8,16,512]{2,1,0:T(8,128)(2,1)S(1)}, u32[]{:S(2)}, u32[]{:S(2)}) collective-permute-start(bf16[8,16,512]{2,1,0:T(8,128)(2,1)S(1)} %all_to_all.5.refs_0_), channel_id=1, source_target_pairs={{0,1},{1,0},{2,3},{3,2},{4,5},{5,4},{6,7},{7,6},{8,9},{9,8},{10,11... | collective-permute-start | bytes 393224 | tf_op jit(solution)/shard_map/ppermute | solution.py:628
  109.2 5.3 %collective-permute-start.47 = (f32[8,128]{1,0:T(8,128)S(1)}, f32[8,128]{1,0:T(8,128)S(1)}, u32[]{:S(2)}, u32[]{:S(2)}) collective-permute-start(f32[8,128]{1,0:T(8,128)S(1)} %get-tuple-element.157.refs_4_), channel_id=1, source_target_pairs={{0,3},{1,2},{2,1},{3,0},{4,7},{5,6},{6,5},{7,4},{8,11},{9,10},{10,... | collective-permute-start | bytes 12296 | tf_op jit(solution)/shard_map/ppermute | solution.py:628
  109.7 7.8 %collective-permute-start.46 = (f32[8,128]{1,0:T(8,128)S(1)}, f32[8,128]{1,0:T(8,128)S(1)}, u32[]{:S(2)}, u32[]{:S(2)}) collective-permute-start(f32[8,128]{1,0:T(8,128)S(1)} %get-tuple-element.157.refs_4_), channel_id=1, source_target_pairs={{0,2},{1,3},{2,0},{3,1},{4,6},{5,7},{6,4},{7,5},{8,10},{9,11},{10,... | collective-permute-start | bytes 12296 | tf_op jit(solution)/shard_map/ppermute | solution.py:628
  114.5 3.0 %collective-permute-start.45 = (f32[8,128]{1,0:T(8,128)S(1)}, f32[8,128]{1,0:T(8,128)S(1)}, u32[]{:S(2)}, u32[]{:S(2)}) collective-permute-start(f32[8,128]{1,0:T(8,128)S(1)} %get-tuple-element.157.refs_4_), channel_id=1, source_target_pairs={{0,1},{1,0},{2,3},{3,2},{4,5},{5,4},{6,7},{7,6},{8,9},{9,8},{10,11... | collective-permute-start | bytes 12296 | tf_op jit(solution)/shard_map/ppermute | solution.py:628
  (6 other events, 4.8 us)

commit v3 on v2

v3 whole, which is shorter than its diff:
```python
import functools
import math

import jax
import jax.numpy as jnp
from jax import lax
from jax.experimental import pallas as pl
from jax.experimental.pallas import tpu as pltpu
from jax.sharding import PartitionSpec as P

HEAD_DIM = 24
TYPES = 192
STEP = 10
NORM_EPS = 1e-05
CLIP = 0.25
STATS_DECAY = 0.95
RATE_LAYER = 0.15
RATE_TABLES = 0.15
RATE_HEAD = 0.01
RATE_VECTORS = 0.2
BETA_ONE = 0.9
BETA_TWO = 0.99
ADAM_EPS = 1e-08
WEIGHT_DECAY = 0.01
MASKED = -1000000000.0
GELU_C = 0.7978845608028654
GELU_A = 0.044715

BF = jnp.bfloat16
F32 = jnp.float32
I32 = jnp.int32
HIGHEST = lax.Precision.HIGHEST
NN = ((1,), (0,))
NT = ((1,), (1,))
TN = ((0,), (0,))
BLOCK = 256
FEATS = 256
MIB = 1024 * 1024


def dot(a, b, dims=NN, precision=None):
    return lax.dot_general(a, b, (dims, ((), ())), preferred_element_type=F32, precision=precision)


def iota(shape, dim):
    return lax.broadcasted_iota(I32, shape, dim)


IN_VMEM = pl.BlockSpec(memory_space=pltpu.VMEM)
IN_PLACE = pl.BlockSpec(memory_space=pltpu.HBM)


def call(kernel, outs, ins, scratch=(), flops=0, vmem=16, in_specs=None, out_specs=None):
    moved = sum(math.prod(x.shape) * x.dtype.itemsize for x in list(ins) + list(outs))
    return pl.pallas_call(
        kernel,
        out_shape=tuple(outs),
        in_specs=in_specs or [IN_VMEM] * len(ins),
        out_specs=tuple(out_specs or [IN_VMEM] * len(outs)),
        scratch_shapes=list(scratch),
        compiler_params=pltpu.CompilerParams(vmem_limit_bytes=vmem * MIB),
        cost_estimate=pl.CostEstimate(flops=flops, bytes_accessed=moved, transcendentals=0),
    )(*ins)


def in_hbm(x):
    return pltpu.with_memory_space_constraint(x, pltpu.HBM)


def in_vmem(x):
    return pltpu.with_memory_space_constraint(x, pltpu.VMEM)


def sds(shape, dtype):
    return jax.ShapeDtypeStruct(shape, dtype)


def norm_parts(values):
    center = values - jnp.mean(values, -1, keepdims=True)
    spread = jnp.mean(center * center, -1, keepdims=True)
    inverse = lax.rsqrt(spread + NORM_EPS)
    return center * inverse, inverse


def norm_back(grad, hat, inverse, gain):
    scaled = grad * gain
    mean_one = jnp.mean(scaled, -1, keepdims=True)
    mean_two = jnp.mean(scaled * hat, -1, keepdims=True)
    return inverse * (scaled - mean_one - hat * mean_two)


def gelu_pair(x):
    t = jnp.tanh(GELU_C * (x + GELU_A * x * x * x))
    value = 0.5 * x * (1.0 + t)
    slope = 0.5 * (1.0 + t) + 0.5 * x * (1.0 - t * t) * (GELU_C * (1.0 + 3.0 * GELU_A * x * x))
    return value, slope


def tree(refs):
    parts = [r[...].astype(F32) for r in refs]
    while len(parts) > 1:
        parts = [parts[i] + parts[i + 1] for i in range(0, len(parts), 2)]
    return parts[0]


def three(x):
    high = x.astype(BF).astype(F32)
    mid = (x - high).astype(BF).astype(F32)
    return high, mid, x - high - mid


def assemble(pieces, first, second, owner):
    rows = pieces[0].shape[0]
    split = first.shape[1]
    for k, piece in enumerate(pieces):
        here = pl.ds(0 if len(pieces) == 1 else pl.multiple_of((owner ^ k) * rows, 16), rows)
        first[here, :] = piece[:, 0:split]
        second[here, :] = piece[:, split:]


def embed_kernel(mols, *refs):
    sources, (at, normed, hats, invs), held, (high, low, prev, sems) = refs[:6], refs[6:10], refs[10:16], refs[16:]
    copies = [pltpu.make_async_copy(a, b, sems.at[i]) for i, (a, b) in enumerate(zip(sources, held))]
    for copy in copies:
        copy.start()
    normed[...] = jnp.zeros(normed.shape, BF)
    for copy in copies:
        copy.wait()
    lap, eig, kinds, seg, tables, vectors = held
    length = seg.shape[1]
    width = vectors.shape[1]
    rows = tables.shape[0]
    tab = tables[...]
    tab_high = tab.astype(BF)
    high[0:rows, :] = tab_high
    rest = jnp.where(iota(tab.shape, 0) < TYPES, tab - tab_high.astype(F32), 0.0)
    low[0:rows, :] = rest.astype(BF)
    r = iota((FEATS - rows, width), 0)
    extra = jnp.where(r == 0, vectors[6:7, :], jnp.where(r == 1, vectors[7:8, :], jnp.where(r == 2, vectors[8:9, :], 0.0)))
    extra_high = extra.astype(BF)
    high[rows:FEATS, :] = extra_high
    low[rows:FEATS, :] = (extra - extra_high.astype(F32)).astype(BF)
    seg_row = seg[...]
    before = pltpu.roll(jnp.broadcast_to(seg_row, (8, length)), 1, 1)
    before = jnp.where(iota((8, length), 1) == 0, -1, before)
    prev[...] = before
    filled = jnp.sum((seg_row != mols).astype(F32)).astype(I32)
    gain = vectors[0:1, :]
    shift = vectors[1:2, :]
    window = 2 * BLOCK

    def one_block(b, unused):
        start = pl.multiple_of(b * BLOCK, BLOCK)
        here = pl.ds(start, BLOCK)
        first = pl.multiple_of(jnp.clip(start - 128, 0, length - window), 128)
        source = iota((window, BLOCK), 0) + first
        one = eig[0:1, here]
        two = eig[1:2, here]
        near = lap[:, pl.ds(first, window)].astype(BF)
        pair_one = dot(near, (source == one).astype(F32).astype(BF))
        pair_two = dot(near, (source == two).astype(F32).astype(BF))
        seg_here = seg[0:1, here]
        begins = (seg_here != mols) & (seg_here != prev[0:1, here])
        kind = jnp.where(begins, -1, kinds[0:1, here])
        keep = jnp.where(begins, 0.0, 1.0)
        at[0:TYPES, here] = (iota((TYPES, BLOCK), 0) == kind).astype(F32).astype(BF)
        half = pair_one.shape[0]
        at[TYPES : TYPES + half, here] = (pair_one * keep).astype(BF)
        at[TYPES + half : rows, here] = (pair_two * keep).astype(BF)
        which = jnp.where(begins, 2, jnp.where(one == two, 0, 1))
        at[rows:FEATS, here] = (iota((FEATS - rows, BLOCK), 0) == which).astype(F32).astype(BF)
        picks = at[:, here]
        resid = dot(picks, high[...], TN) + dot(picks, low[...], TN)
        hat, inverse = norm_parts(resid)
        normed[here, :] = (hat * gain + shift).astype(BF)
        hats[here, :] = hat.astype(BF)
        invs[here, :] = jnp.broadcast_to(inverse, (BLOCK, 128))
        return 0

    lax.fori_loop(0, (filled + BLOCK - 1) // BLOCK, one_block, 0)


def attn_kernel(npiece, mols, heads, scale, *refs):
    normed, seg, vectors = refs[:3]
    ones = refs[3 : 3 + npiece]
    part, probs, values, ctx_out, keyed, query_out, w1, w2 = refs[3 + npiece :]
    assemble(ones, w1, w2, lax.axis_index("dp"))
    width = vectors.shape[1]
    cols = heads * HEAD_DIM
    hat, _ = norm_parts(vectors[8:9, :])
    start_row = (hat * vectors[0:1, :] + vectors[1:2, :]).astype(BF)
    q = dot(jnp.broadcast_to(start_row, (16, width)), w1[:, 0:256])
    q = q.astype(BF).astype(F32)
    q = jnp.where(iota((16, 256), 1) < cols, q, 0.0)
    r = iota((16, 256), 0)
    head_of = iota((16, 256), 1) // HEAD_DIM
    query_out[...] = jnp.where(r == head_of, q, 0.0)[0:8, :]
    shifted = pltpu.roll(q, 64, 1)[0:1, :]
    r = iota((128, 256), 0)
    lane = iota((128, 256), 1) - 64
    pick = (lane >= 0) & ((r & 7) == lane // HEAD_DIM) & (r >= 64) & (r < 80)
    q_keys = jnp.where(pick, shifted, 0.0).astype(BF)
    u = dot(w1[:, 128:384], q_keys, NT)
    u_high = u.astype(BF)
    lane = iota(u.shape, 1)
    u_both = jnp.where(lane < 72, u_high.astype(F32), u - u_high.astype(F32))
    last = w1[:, 512:640].astype(F32)
    side = jnp.where(lane < 64, last, u_both).astype(BF)
    keyed[:, 0:128] = w1[:, 384:512]
    keyed[:, 128:256] = jnp.where(lane < 64, last, jnp.where(lane < 72, u * scale, 0.0)).astype(BF)
    normed_all = normed[...]
    values[:, 0:128] = dot(normed_all, w1[:, 384:512]).astype(BF)
    second = dot(normed_all, side)
    values[:, 128:256] = jnp.where(iota(second.shape, 1) < 64, second, 0.0).astype(BF)
    turned = second.T
    scores = (turned[64:72, :] + turned[72:80, :]) * scale
    seg_row = seg[...]
    length = seg_row.shape[1]
    mine = iota((mols, 1, length), 0) == seg_row[None]
    masked = jnp.where(mine, scores[None], MASKED)
    peak = jnp.max(masked, -1, keepdims=True)
    grown = jnp.where(mine, jnp.exp(masked - peak), 0.0)
    total = jnp.sum(grown, -1, keepdims=True)
    total = jnp.where(total > 0.0, total, 1.0)
    prob = (grown / total).reshape(mols * heads, length).astype(BF)
    probs[...] = prob
    wide = dot(prob, values[...])
    r = iota(wide.shape, 0) & (heads - 1)
    wide = jnp.where(r == iota(wide.shape, 1) // HEAD_DIM, wide, 0.0)
    ctx = jnp.sum(wide.reshape(mols, heads, 256), 1)
    ctx_out[...] = ctx.astype(BF)
    turned_ctx = pltpu.roll(ctx, 64, 1).astype(BF)
    part[...] = dot(turned_ctx, w1[:, 512:768], NT).astype(BF)


def ffn_kernel(nmp, cols, *refs):
    terms = refs[:nmp]
    vectors, w2, part, resid_out, normed_out, hidden_out, act_out = refs[nmp:]
    resid = vectors[8:9, :] + tree(terms)
    resid_out[...] = resid
    hat, _ = norm_parts(resid)
    low = (hat * vectors[2:3, :] + vectors[3:4, :]).astype(BF)
    normed_out[...] = low
    hidden = dot(low, w2[:, 0:256])
    hidden = jnp.where(iota(hidden.shape, 1) < cols, hidden, 0.0)
    hidden_out[...] = hidden
    act, _ = gelu_pair(hidden)
    act_out[...] = act.astype(BF)
    turned = pltpu.roll(act, 64, 1).astype(BF)
    part[...] = dot(turned, w2[:, 128:384], NT).astype(BF)


def head_kernel(nmp, cols, *refs):
    terms = refs[:nmp]
    resid_one, vectors, head, targets, seg, hidden, w2 = refs[nmp : nmp + 7]
    part, pack, grad_out, low_out, hidden_out, rows_out, head_low = refs[nmp + 7 :]
    width = vectors.shape[1]
    mols = targets.shape[1]
    head_low[...] = head[...].astype(BF)
    resid = resid_one[...] + tree(terms)
    hat, inverse = norm_parts(resid)
    gain = vectors[4:5, :]
    low = (hat * gain + vectors[5:6, :]).astype(BF)
    mid = dot(low, head_low[...]) + vectors[9:10, :]
    act_head, slope = gelu_pair(mid)
    act_head = act_head.astype(BF).astype(F32)
    readout = vectors[10:11, :].astype(BF).astype(F32)
    predicted = jnp.sum(act_head * readout, -1, keepdims=True)
    spot = iota((mols, mols), 0) == iota((mols, mols), 1)
    goal = jnp.sum(jnp.where(spot, targets[...], 0.0), -1, keepdims=True)
    seg_row = seg[...]
    there = iota((mols, seg_row.shape[1]), 0) == seg_row
    present = jnp.max(there.astype(F32), -1, keepdims=True)
    error = predicted - goal
    root = jnp.sqrt(error * error + 1.0)
    loss = jnp.sum(present * (root - 1.0), 0, keepdims=True)
    count = jnp.sum(present, 0, keepdims=True)
    grad_pred = present * error / root
    grad_readout = jnp.sum(grad_pred * act_head, 0, keepdims=True)
    grad_mid = (grad_pred * readout * slope).astype(BF)
    grad_bias = jnp.sum(grad_mid.astype(F32), 0, keepdims=True)
    grad_rows = dot(grad_mid, head_low[...], NT)
    grad_gain = jnp.sum(grad_rows * hat, 0, keepdims=True)
    grad_shift = jnp.sum(grad_rows, 0, keepdims=True)
    grad_two = norm_back(grad_rows, hat, inverse, gain)
    grad_out[...] = grad_two
    grad_low = grad_two.astype(BF)
    grad_act = dot(grad_low, w2[:, 128:384])
    grad_act = pltpu.roll(grad_act, 192, 1)
    _, slope_hidden = gelu_pair(hidden[...])
    grad_hidden = jnp.where(iota(grad_act.shape, 1) < cols, grad_act * slope_hidden, 0.0).astype(BF)
    part[...] = dot(grad_hidden, w2[:, 0:256], NT).astype(BF)
    pack[:, 0:width] = low
    pack[:, width : 2 * width] = grad_mid
    low_out[...] = grad_low
    hidden_out[...] = grad_hidden
    r = iota((8, width), 0)
    lane = iota((8, width), 1)
    scalars = jnp.where(lane == 0, loss, jnp.where(lane == 1, count, 0.0))
    rows_out[...] = jnp.where(
        r == 0,
        grad_gain,
        jnp.where(r == 1, grad_shift, jnp.where(r == 2, grad_bias, jnp.where(r == 3, grad_readout, jnp.where(r == 4, scalars, 0.0)))),
    )


def parts_for(rows, keep, send, each, odd, high, number=1):
    for z in range(high):
        for i in range(number):
            keep[z * number + i] = rows[pl.ds(pl.multiple_of(((2 * z + odd) * number + i) * each, 16), each), :]
            send[z * number + i] = rows[pl.ds(pl.multiple_of(((2 * z + 1 - odd) * number + i) * each, 16), each), :]


def ffn_grad_kernel(nlayer, high, normed, grad_hidden, grad_low, act, pack, keyed, *refs):
    outs, (comb, rows) = refs[:nlayer], refs[nlayer:]
    comb[...] = keyed[...].astype(F32).T.astype(BF)
    up = dot(normed[...], grad_hidden[...], TN)
    turned = pltpu.roll(act[...].astype(F32), 64, 1).astype(BF)
    down = dot(grad_low[...], turned, TN)
    target = rows if nlayer == 2 else outs[0]
    target[:, 0:128] = up[:, 0:128].astype(BF)
    target[:, 128:256] = (up[:, 128:256] + down[:, 0:128]).astype(BF)
    target[:, 256:384] = down[:, 128:256].astype(BF)
    if nlayer == 2:
        half = outs[0].shape[1]
        parts_for(rows, *outs, half, lax.axis_index("dp") & 1, high, 2)
        if outs[0].shape[0] > 2 * high:
            width = pack.shape[1] // 2
            lanes = pack[...].astype(F32)
            lanes = jnp.where((lax.axis_index("mp") & 1) == 0, lanes[:, 0:width], lanes[:, width:])
            lanes = jnp.concatenate([lanes[:, 0:384], lanes[:, 384:768]], 0).astype(BF)
            outs[0][2 * high] = lanes
            outs[1][2 * high] = lanes


def attn_back_kernel(nmp, nlayer, high, mols, heads, scale, *refs):
    terms = refs[:nmp]
    resid_one, grad_two, head_rows, vectors, probs, values, normed, w1, ctx = refs[nmp : nmp + 9]
    layer_outs = refs[nmp + 9 : nmp + 9 + nlayer]
    side, key_rows, sides, extras, turned_lay = refs[nmp + 9 + nlayer :]
    group = lax.axis_index("mp")
    width = vectors.shape[1]
    length = probs.shape[1]
    cols = heads * HEAD_DIM
    grad_normed = tree(terms)
    hat, inverse = norm_parts(resid_one[...])
    grad_gain = jnp.sum(grad_normed * hat, 0, keepdims=True)
    grad_shift = jnp.sum(grad_normed, 0, keepdims=True)
    grad_one = grad_two[...] + norm_back(grad_normed, hat, inverse, vectors[2:3, :])
    low = grad_one.astype(BF)
    grad_start = jnp.sum(low.astype(F32), 0, keepdims=True)
    grad_ctx = pltpu.roll(dot(low, w1[:, 512:768]), 192, 1).astype(BF).astype(F32)
    spread_ctx = jnp.broadcast_to(grad_ctx[:, None, :], (mols, heads, 256)).reshape(mols * heads, 256)
    r = iota(spread_ctx.shape, 0) & (heads - 1)
    spread_ctx = jnp.where(r == iota(spread_ctx.shape, 1) // HEAD_DIM, spread_ctx, 0.0).astype(BF)
    grad_probs = dot(spread_ctx, values[...], NT)
    prob = probs[...].astype(F32)
    inner = jnp.sum(prob * grad_probs, -1, keepdims=True)
    grad_scores = (prob * (grad_probs - inner)).astype(BF).astype(F32)
    grad_scores = jnp.sum(grad_scores.reshape(mols, heads, length), 0)
    grad_values = dot(spread_ctx, probs[...], TN)
    sides[0:cols, :] = grad_values[0:cols, :].astype(BF)
    sides[cols:256, :] = jnp.concatenate([grad_scores, jnp.zeros((256 - cols - heads, length), F32)], 0).astype(BF)
    sums = dot(sides[...], normed[...])
    turned_ctx = pltpu.roll(ctx[...].astype(F32), 64, 1).astype(BF)
    out_grad = dot(low, turned_ctx, TN)
    r = iota(sums.shape, 0)
    value_grad = jnp.where(r < cols, sums, 0.0).T
    lay = layer_outs[0] if nlayer == 1 else turned_lay
    lay[:, 0:128] = value_grad[:, 0:128].astype(BF)
    lay[:, 128:256] = (value_grad[:, 128:256] + out_grad[:, 0:128]).astype(BF)
    lay[:, 256:384] = out_grad[:, 128:256].astype(BF)
    if nlayer == 2:
        parts_for(lay, *layer_outs, layer_outs[0].shape[1], lax.axis_index("dp") & 1, high)
    gain = vectors[0:1, :]
    grad_keys = sums[cols : cols + heads, :]
    key_rows[...] = grad_keys
    turned = dot(grad_keys.astype(BF), w1[:, 128:384])
    lane = iota(turned.shape, 1) - 64
    picked = jnp.where((lane >= 0) & (lane // HEAD_DIM == iota(turned.shape, 0)), turned, 0.0)
    grad_query = jnp.sum(pltpu.roll(picked, 192, 1), 0, keepdims=True) * scale
    r = iota(side.shape, 0)
    side[...] = jnp.where(r == 0, grad_query, jnp.where(r == 1, head_rows[4:5, 0:256], 0.0))
    grad_query = jnp.broadcast_to(grad_query.astype(BF), (16, 256))
    grad_row = dot(grad_query, w1[:, 0:256], NT)[0:1, :]
    hat_start, inverse_start = norm_parts(vectors[8:9, :])
    first = jnp.where(group == 0, 1.0, 0.0)
    row_graph = norm_back(grad_row, hat_start, inverse_start, gain) + first * grad_start
    r = iota(extras.shape, 0)
    extra = jnp.where(r == 2, row_graph, 0.0)
    extra = jnp.where(r == 3, grad_row * hat_start, extra)
    extra = jnp.where(r == 4, grad_row, extra)
    extra = jnp.where(r == 5, first * grad_gain, extra)
    extra = jnp.where(r == 6, first * grad_shift, extra)
    for i in range(4):
        extra = jnp.where(r == 7 + i, first * head_rows[i : i + 1, :], extra)
    extras[...] = extra


def embed_back_kernel(nmp, mols, *refs):
    sides, comb, extras, vectors, hats, invs, at, seg = refs[:8]
    outs, (total, gains) = refs[8 : 8 + nmp], refs[8 + nmp :]
    width = vectors.shape[1]
    filled = jnp.sum((seg[...] != mols).astype(F32)).astype(I32)
    total[...] = jnp.zeros(total.shape, F32)
    gains[...] = jnp.zeros(gains.shape, F32)
    gain = vectors[0:1, :]

    def one_block(b, unused):
        here = pl.ds(pl.multiple_of(b * BLOCK, BLOCK), BLOCK)
        grad = dot(sides[:, here], comb[...], TN)
        hat_here = hats[here, :].astype(F32)
        low_grad = norm_back(grad, hat_here, invs[here, 0:1], gain).astype(BF)
        total[...] += dot(at[:, here], low_grad)
        gains[0:8, :] += jnp.sum((grad * hat_here).reshape(BLOCK // 8, 8, width), 0)
        gains[8:16, :] += jnp.sum(grad.reshape(BLOCK // 8, 8, width), 0)
        return 0

    lax.fori_loop(0, (filled + BLOCK - 1) // BLOCK, one_block, 0)
    base = FEATS - extras.shape[0]
    r = iota(extras.shape, 0)
    extra = extras[...] + jnp.where(r == 3, jnp.sum(gains[0:8, :], 0, keepdims=True), 0.0)
    extra += jnp.where(r == 4, jnp.sum(gains[8:16, :], 0, keepdims=True), 0.0)
    total[base:FEATS, :] += extra
    group = lax.axis_index("mp")
    each = FEATS // nmp
    for k in range(nmp):
        start = pl.multiple_of((group ^ k) * each, 16)
        outs[k][...] = total[pl.ds(start, each), :].astype(BF)


def loss_row(value, count, lanes):
    a, b, c = three(value)
    lane = iota((1, lanes), 1)
    return jnp.where(lane == 0, a, jnp.where(lane == 1, b, jnp.where(lane == 2, c, jnp.where(lane == 3, count, 0.0))))


def merge_table_kernel(nmp, owners, own, high, *refs):
    terms = refs[:nmp]
    side, key_rows, table_keep, table_send, table_sum, key_sum = refs[nmp:]
    odd = lax.axis_index("dp") & 1
    table_sum[...] = tree(terms)
    half = table_sum.shape[1] // 2
    query = jnp.concatenate([side[0:1, :], jnp.zeros((1, 128), F32)], 1)
    scal = loss_row(side[1:2, 0:1], side[1:2, 1:2], 384)
    r = iota((8, 384), 0)
    scal = jnp.where(r == 0, query, jnp.where(r == 1, scal, 0.0))
    fill = jnp.zeros((8, 384 - own), F32)
    for p in range(2 * high):
        key_sum[p] = jnp.concatenate([key_rows[:, p * own : (p + 1) * own], fill], 1)
    for z in range(high):
        for out, x in ((table_keep, odd), (table_send, 1 - odd)):
            p = 2 * z + x
            if 2 * z < owners:
                each = table_sum[pl.ds(pl.multiple_of(p * 8, 8), 8), :]
            else:
                each = jnp.zeros((8, 2 * half), F32)
            out[z] = jnp.concatenate([each[:, 0:half], each[:, half:], key_sum[p], scal], 0).astype(BF)


def merge_kernel(layer_keep, layer_came, table_keep, table_came, *outs):
    deep = layer_keep.shape[1]
    mine = lax.axis_index("dp") >> 1
    r = iota((16, 384), 0)
    for k, out in enumerate(outs):
        z = mine ^ k
        out[0:deep, :] = (layer_keep[z].astype(F32) + layer_came[z].astype(F32)).astype(BF)
        out[deep : deep + 16, :] = (table_keep[z, 0:16].astype(F32) + table_came[z, 0:16].astype(F32)).astype(BF)
        both = table_keep[z, 16:32].astype(F32) + table_came[z, 16:32].astype(F32)
        loss = both[9:10, 0:1] + both[9:10, 1:2] + both[9:10, 2:3]
        out[deep + 16 :, :] = jnp.where(r == 9, loss_row(loss, both[9:10, 3:4], 384), both).astype(BF)


def ffn_all_kernel(keep, came, *outs):
    mine = lax.axis_index("dp") >> 1
    for k, out in enumerate(outs):
        out[...] = (keep[mine ^ k].astype(F32) + came[mine ^ k].astype(F32)).astype(BF)


def ffn_x_kernel(keep, came, near_keep, near_send, pair):
    me = lax.axis_index("dp")
    odd, side = me & 1, (me >> 1) & 1
    for out, s in ((near_keep, side), (near_send, 1 - side)):
        for h in range(2):
            for i in range(2):
                p = (2 * h + s) * 2 + i
                out[h, i * 48 : (i + 1) * 48, :] = (keep[p].astype(F32) + came[p].astype(F32)).astype(BF)
    last = keep.shape[0] - 1
    pair[odd] = keep[last]
    pair[1 - odd] = came[last]


def ffn_z_kernel(keep, came, far_keep, far_send):
    side = lax.axis_index("dp") >> 2
    for out, h in ((far_keep, side), (far_send, 1 - side)):
        out[...] = (keep[h].astype(F32) + came[h].astype(F32)).astype(BF)


def sum_squares(value):
    return jnp.sum(jnp.sum(value * value, 0, keepdims=True), 1, keepdims=True)


def rows_kernel(*refs):
    pieces, out = refs[:-1], refs[-1]
    mine = lax.axis_index("dp") >> 1
    slot = out.shape[0] // (2 * len(pieces))
    for k, piece in enumerate(pieces):
        for x in range(2):
            rows = piece[x].astype(F32)
            mols = rows.shape[0] // 2
            rows = jnp.concatenate([rows[0:mols, :], rows[mols:, :]], 1)
            rows = jnp.concatenate([rows, jnp.zeros((slot - mols, rows.shape[1]), F32)], 0).astype(BF)
            out[pl.ds(pl.multiple_of(((mine ^ k) * 2 + x) * slot, 16), slot), :] = rows


def outer_kernel(keep, came, head_grad, square):
    first = (lax.axis_index("mp") & 1) == 0
    mine, other = keep[...].astype(F32), came[...].astype(F32)
    head_in = jnp.where(first, mine, other).astype(BF)
    grad_mid = jnp.where(first, other, mine).astype(BF)
    grad = dot(head_in, grad_mid, TN)
    head_grad[...] = grad
    square[...] = jnp.broadcast_to(sum_squares(grad), square.shape)


def owner_kernel(own, cols, scale, dp, *refs):
    parts, ffn_parts, (query, vectors, layer, send, scalars) = refs[: dp // 2], refs[dp // 2 : -5], refs[-5:]
    width = vectors.shape[1]
    summed = tree(parts)
    ffn = tree(ffn_parts)
    deep = ffn.shape[0]
    acc, summed = summed[0:deep, :], summed[deep:, :]
    table, keys, side = summed[0:16, :], summed[16:24, 0:128], summed[24:32, :]
    key_grad = dot(keys, query[...], TN, HIGHEST) * scale
    hat, _ = norm_parts(vectors[8:9, :])
    start_row = (hat * vectors[0:1, :] + vectors[1:2, :]).astype(BF).astype(F32)
    here = iota((deep, width), 1) == iota((deep, width), 0) + lax.axis_index("dp") * own
    start_col = jnp.sum(jnp.where(here, start_row, 0.0), -1, keepdims=True)
    square = sum_squares(table)
    grads = [start_col * side[0:1, 0:256], key_grad, acc[:, 0:256], acc[:, 192:384], ffn[:, 0:256], ffn[:, 192:384]]
    for j, grad in enumerate(grads):
        grad = grad[0:own, 0:cols]
        layer[j] = grad
        square += sum_squares(grad)
    a, b, c = three(square)
    lane = iota((16, 128), 1)
    r = iota((16, 128), 0)
    tail = jnp.where(r == 0, jnp.where(lane == 0, a, jnp.where(lane == 1, b, jnp.where(lane == 2, c, 0.0))), 0.0)
    packet = jnp.concatenate([table, tail], 1).astype(BF)
    for p in range(dp):
        send[p] = packet
    loss = side[1:2, 0:1] + side[1:2, 1:2] + side[1:2, 2:3]
    scalars[...] = jnp.where(iota(scalars.shape, 1) == 0, loss, side[1:2, 3:4])


def stats_kernel(nkept, layer, left_source, right_source, *refs):
    sources, (left, right, shaped), kept = refs[:nkept], refs[nkept : nkept + 3], refs[nkept + 3 : 2 * nkept + 3]
    left_roots, right_roots, sems = refs[2 * nkept + 3 :]
    pairs = [(left_source, left_roots), (right_source, right_roots), *zip(sources, kept)]
    copies = [pltpu.make_async_copy(a, b, sems.at[i]) for i, (a, b) in enumerate(pairs)]
    for copy in copies:
        copy.start()
    for j in range(6):
        low = layer[j].astype(BF)
        left[j] = dot(low, low, NT)
        right[j] = dot(low, low, TN)
    copies[0].wait()
    copies[1].wait()
    for j in range(6):
        near = dot(left_roots[j].astype(BF), layer[j].astype(BF))
        shaped[j] = dot(near.astype(BF), right_roots[j].astype(BF))
    for copy in copies[2:]:
        copy.wait()


def adam(weight, first, second, grad, rate):
    first_new = BETA_ONE * first + (1.0 - BETA_ONE) * grad
    second_new = BETA_TWO * second + (1.0 - BETA_TWO) * grad * grad
    fixed_one = 1.0 - BETA_ONE**STEP
    fixed_two = 1.0 - BETA_TWO**STEP
    update = first_new * (1.0 / fixed_one) / (jnp.sqrt(second_new * (1.0 / fixed_two)) + ADAM_EPS)
    return first_new, second_new, weight - rate * (update + WEIGHT_DECAY * weight)


def update_kernel(nmp, owners, cols, *refs):
    packets = refs[:nmp]
    (
        head_square, scalars, layer, left_add, right_add, shaped, weights, left, right,
        tables, tables_m, tables_v, head, head_m, head_v, head_grad, vectors, vectors_m, vectors_v,
    ) = refs[nmp : nmp + 19]
    loss_out, count_out, norm_out = refs[nmp + 19 : nmp + 22]
    outs = refs[nmp + 22 : nmp + 35]
    held = refs[nmp + 35 : nmp + 48]
    grads, sems = refs[nmp + 48 :]
    layer_out, weights_out, left_out, right_out, tm_out, tv_out, t_out, hm_out, hv_out, h_out, vm_out, vv_out, v_out = held
    started = []

    def send(i, rows=None):
        src, dst = held[i], outs[i]
        if rows is not None:
            src, dst = src.at[rows], dst.at[rows]
        copy = pltpu.make_async_copy(src, dst, sems.at[len(started)])
        copy.start()
        started.append(copy)

    parts = []
    for packet in packets:
        s = jnp.zeros((1, 1), F32)
        for p in range(packet.shape[0]):
            tail = packet[p, :, 384:512].astype(F32)
            s += tail[0:1, 0:1] + tail[0:1, 1:2] + tail[0:1, 2:3]
        parts.append(s)
    while len(parts) > 1:
        parts = [parts[i] + parts[i + 1] for i in range(0, len(parts), 2)]
    square = parts[0] + head_square[0:1, 0:1]
    loss, count = scalars[0:1, 0:1], scalars[0:1, 1:2]
    norm = jnp.sqrt(square) / count
    factor = CLIP / jnp.maximum(norm, CLIP) / count
    loss_out[...] = loss
    count_out[...] = count
    norm_out[...] = norm
    width = head.shape[0]
    parts = 8
    each = width // parts
    for i in range(parts):

        def some_rows(t, unused, i=i):
            rows = pl.ds(pl.multiple_of(i * each + t * 8, 8), 8)
            hm_out[rows, :], hv_out[rows, :], h_out[rows, :] = adam(
                head[rows, :], head_m[rows, :], head_v[rows, :], head_grad[rows, :] * factor, RATE_HEAD
            )
            return 0

        lax.fori_loop(0, each // 8, some_rows, 0, unroll=4)
        for k in (7, 8, 9):
            send(k, pl.ds(i * each, each))
    scale = (1.0 - STATS_DECAY) * factor * factor
    right_out[...] = STATS_DECAY * right[...] + scale[None] * right_add[...]
    send(3)
    left_out[...] = STATS_DECAY * left[...] + scale[None] * left_add[...]
    send(2)
    for j in range(6):
        span = slice(j * cols, (j + 1) * cols)
        layer_out[:, span] = layer[j] * factor
        weights_out[:, span] = weights[:, span] - RATE_LAYER * (shaped[j] * factor + WEIGHT_DECAY * weights[:, span])
    send(0)
    send(1)
    group = lax.axis_index("mp")
    share = FEATS // nmp
    half = 384
    for k in range(nmp):
        start = pl.multiple_of((group ^ k) * share, 8)
        for p in range(owners):
            piece = packets[k][p, :, 0:half].astype(F32)
            piece = jnp.concatenate([piece[0:8, :], piece[8:16, :]], 1) * factor
            grads[pl.ds(pl.multiple_of(start + p * 8, 8), 8), :] = piece
    rows = tables.shape[0]

    def table_rows(t, unused):
        r = pl.ds(pl.multiple_of(t * 8, 8), 8)
        tm_out[r, :], tv_out[r, :], t_out[r, :] = adam(tables[r, :], tables_m[r, :], tables_v[r, :], grads[r, :], RATE_TABLES)
        return 0

    lax.fori_loop(0, rows // 8, table_rows, 0, unroll=4)
    for k in (4, 5, 6):
        send(k)
    order = (3, 4, 5, 6, 7, 8, 0, 1, 2, 9, 10)
    r = iota((16, vectors.shape[1]), 0)
    tail = jnp.zeros(r.shape, F32)
    for i, o in enumerate(order):
        tail = jnp.where(r == i, grads[rows + o : rows + o + 1, :], tail)
    nrows = vectors.shape[0]
    vm_out[...], vv_out[...], v_out[...] = adam(vectors[...], vectors_m[...], vectors_v[...], tail[0:nrows, :], RATE_VECTORS)
    for k in (10, 11, 12):
        send(k)
    for copy in started:
        copy.wait()


def exchange(x, axis):
    n = lax.axis_size(axis)
    return [x] + [lax.ppermute(x, axis, [(i, i ^ k) for i in range(n)]) for k in range(1, n)]


def flip(x, k):
    n = lax.axis_size("dp")
    return lax.ppermute(x, "dp", [(i, i ^ k) for i in range(n)])


def after(values, *others):
    return lax.optimization_barrier((tuple(values), tuple(others)))[0]


def spread(x, second=()):
    four, one, two = after([flip(x, 4), flip(x, 1), flip(x, 2)], *second)
    return [x, one, two, flip(two, 1), four, flip(four, 1), flip(four, 2), flip(one, 6)]


def per_device(
    lap_vectors,
    eig_index,
    type_ids,
    seg_ids,
    targets,
    layer_weights,
    left_stats,
    right_stats,
    left_roots,
    right_roots,
    tables,
    tables_m,
    tables_v,
    head_weight,
    head_m,
    head_v,
    vectors,
    vectors_m,
    vectors_v,
):
    dp = lax.axis_size("dp")
    nmp = lax.axis_size("mp")
    length = seg_ids.shape[1]
    mols = targets.shape[1]
    width = vectors.shape[1]
    own, group_cols = layer_weights.shape[0], layer_weights.shape[1]
    cols = group_cols // 6
    heads = cols // HEAD_DIM
    scale = HEAD_DIM ** (-0.5)
    owners = FEATS // nmp // 8

    w = layer_weights.astype(BF)
    sources = [in_hbm(x) for x in (lap_vectors[0].T, eig_index[0].T, type_ids, seg_ids, tables, vectors)]
    at, normed, hats, invs = call(
        functools.partial(embed_kernel, mols),
        [sds((FEATS, length), BF), sds((length, width), BF), sds((length, width), BF), sds((length, 128), F32)],
        sources,
        [pltpu.VMEM(x.shape, x.dtype) for x in sources]
        + [pltpu.VMEM((FEATS, width), BF), pltpu.VMEM((FEATS, width), BF), pltpu.VMEM((8, length), I32), pltpu.SemaphoreType.DMA((6,))],
        flops=4 * length * FEATS * width,
        in_specs=[IN_PLACE] * 6,
    )
    direct = dp == 8 and own == 4 * mols and own % 16 == 0
    if direct:
        ones = spread(w, (normed,))
    else:
        ones = [lax.all_gather(w, "dp", axis=0, tiled=True)]
    np_ = len(ones)
    part, probs, values, ctx, keyed, query, w1, w2 = call(
        functools.partial(attn_kernel, np_, mols, heads, scale),
        [
            sds((mols, width), BF),
            sds((mols * heads, length), BF),
            sds((length, 256), BF),
            sds((mols, 256), BF),
            sds((width, 256), BF),
            sds((8, 256), F32),
            sds((width, 4 * cols), BF),
            sds((width, 2 * cols), BF),
        ],
        [normed, seg_ids, vectors, *ones],
        flops=4 * length * 256 * width,
    )
    part, resid_one, normed_two, hidden, act = call(
        functools.partial(ffn_kernel, nmp, cols),
        [
            sds((mols, width), BF),
            sds((mols, width), F32),
            sds((mols, width), BF),
            sds((mols, 256), F32),
            sds((mols, 256), BF),
        ],
        [*exchange(part, "mp"), vectors, w2],
        flops=4 * mols * width * 256,
    )
    part, pack, grad_two, grad_low, grad_hidden, head_rows = call(
        functools.partial(head_kernel, nmp, cols),
        [
            sds((mols, width), BF),
            sds((mols, 2 * width), BF),
            sds((mols, width), F32),
            sds((mols, width), BF),
            sds((mols, 256), BF),
            sds((8, width), F32),
        ],
        [*exchange(part, "mp"), resid_one, vectors, head_weight, targets, seg_ids, hidden, w2],
        [pltpu.VMEM((width, width), BF)],
        flops=4 * width * width * mols,
    )
    odd = lax.axis_index("dp") & 1
    high = dp // 2
    deep = (own + 15) // 16 * 16
    nlayer = 2 if own == deep else 1

    def halves(parts):
        if nlayer == 2:
            return parts
        both = parts[0].reshape(high, 2, own, -1)
        both = jnp.pad(both, ((0, 0), (0, 0), (0, deep - own), (0, 0)))
        return [lax.dynamic_index_in_dim(both, i, 1, False) for i in (odd, 1 - odd)]

    def half_shapes(lanes, number=1, more=0):
        return [sds((high * number + more, own // number, lanes), BF)] * 2 if nlayer == 2 else [sds((width, lanes), BF)]

    number = 2 if direct else 1
    *ffn_parts, comb = call(
        functools.partial(ffn_grad_kernel, nlayer, high),
        half_shapes(384, number, number - 1) + [sds((256, width), BF)],
        [normed_two, grad_hidden, grad_low, act, pack, keyed],
        [pltpu.VMEM((width, 384), BF)],
        flops=4 * mols * width * 256,
    )
    ffn_keep, ffn_send = halves(ffn_parts)
    ffn_came = flip(ffn_send, 1)
    if direct:
        near_keep, near_send, pair = call(
            ffn_x_kernel,
            [sds((2, own, 384), BF)] * 2 + [sds((2, 2 * mols, width // 2), BF)],
            [ffn_keep, ffn_came],
        )
        far_keep, far_send = call(ffn_z_kernel, [sds((own, 384), BF)] * 2, [near_keep, flip(near_send, 2)])
        ffn_parts = [far_keep, flip(far_send, 4)]
    else:
        ffn_parts = call(ffn_all_kernel, [sds((deep, 384), BF)] * high, [ffn_keep, ffn_came])
        ffn_parts = [ffn_parts[0]] + [flip(ffn_parts[k], 2 * k) for k in range(1, high)]
    *layer_halves, side, key_rows, sides, extras = call(
        functools.partial(attn_back_kernel, nmp, nlayer, high, mols, heads, scale),
        half_shapes(384)
        + [sds((8, 256), F32), sds((8, width), F32), sds((256, length), BF), sds((FEATS - TYPES - 32, width), F32)],
        [*exchange(part, "mp"), resid_one, grad_two, head_rows, vectors, probs, values, normed, w1, ctx],
        [pltpu.VMEM((width, 384), BF)],
        flops=4 * length * 256 * width,
    )
    layer_keep, layer_send = halves(layer_halves)
    layer_came = flip(layer_send, 1)
    shares = call(
        functools.partial(embed_back_kernel, nmp, mols),
        [sds((FEATS // nmp, width), BF) for _ in range(nmp)],
        [sides, comb, extras, vectors, hats, invs, at, seg_ids],
        [pltpu.VMEM((FEATS, width), F32), pltpu.VMEM((16, width), F32)],
        flops=4 * length * 256 * width,
    )
    moved = [shares[0]] + [lax.ppermute(shares[k], "mp", [(i, i ^ k) for i in range(nmp)]) for k in range(1, nmp)]
    table_keep, table_send = call(
        functools.partial(merge_table_kernel, nmp, owners, own, high),
        [sds((high, 32, 384), BF)] * 2,
        [*moved, side, key_rows],
        [pltpu.VMEM((FEATS // nmp, width), F32), pltpu.VMEM((dp, 8, 384), F32)],
    )
    merged = call(
        merge_kernel,
        [sds((deep + 32, 384), BF)] * high,
        [layer_keep, layer_came, table_keep, flip(table_send, 1)],
    )
    merged = [merged[0]] + [flip(merged[k], 2 * k) for k in range(1, high)]
    if direct:
        two, four = flip(pair, 2), flip(pair, 4)
        merged = after(merged, two, four)
    layer, send, scalars = call(
        functools.partial(owner_kernel, own, cols, scale, dp),
        [sds((6, own, cols), F32), sds((dp, 16, 512), BF), sds((8, 128), F32)],
        [*merged, *ffn_parts, query, vectors],
        flops=2 * own * 256 * 1024,
    )
    sums = lax.all_to_all(send, "dp", 0, 0, tiled=True)
    swap = [(i, i ^ 1) for i in range(nmp)]
    if direct:
        (later,) = after([four], scalars)
        (six,) = after([flip(later, 2)], sums)
        (mine,) = call(rows_kernel, [sds((dp * 32, width), BF)], [pair, two, four, six])
        other = lax.ppermute(mine, "mp", swap)
    else:
        packs = lax.all_gather(pack, "dp", axis=0)
        packs = jnp.pad(packs, ((0, 0), (0, 32 - mols), (0, 0))).reshape(dp * 32, -1)
        first = (lax.axis_index("mp") & 1) == 0
        mine = jnp.where(first, packs[:, :width], packs[:, width:])
        other = jnp.where(first, packs[:, width:], packs[:, :width])
    sums = exchange(sums, "mp")
    head_grad, head_square = call(
        outer_kernel,
        [sds((width, width), F32), sds((8, 128), F32)],
        [mine, other],
        flops=2 * dp * mols * width * width,
        vmem=16 + dp // 4,
    )
    left_roots, right_roots = jnp.swapaxes(left_roots, 0, 1), right_roots[0]
    kept = [
        layer_weights, jnp.swapaxes(left_stats, 0, 1), right_stats[0],
        tables, tables_m, tables_v, head_weight, head_m, head_v, vectors, vectors_m, vectors_v,
    ]
    left_add, right_add, shaped, *kept = call(
        functools.partial(stats_kernel, len(kept)),
        [sds((6, own, own), F32), sds((6, cols, cols), F32), sds((6, own, cols), F32)] + [pltpu.VMEM(x.shape, F32) for x in kept],
        [layer, *[in_hbm(x) for x in (left_roots, right_roots, *kept)]],
        [pltpu.VMEM(left_roots.shape, F32), pltpu.VMEM(right_roots.shape, F32), pltpu.SemaphoreType.DMA((14,))],
        flops=12 * 6 * own * cols * (2 * own + 2 * cols),
        in_specs=[IN_VMEM] + [IN_PLACE] * 14,
    )
    kept = [in_vmem(x) for x in kept]
    results = [
        sds((own, group_cols), F32),
        sds((own, group_cols), F32),
        sds((6, own, own), F32),
        sds((6, cols, cols), F32),
        *[sds(tables.shape, F32)] * 3,
        *[sds(head_weight.shape, F32)] * 3,
        *[sds(vectors.shape, F32)] * 3,
    ]
    outs = call(
        functools.partial(update_kernel, nmp, owners, cols),
        [sds((1, 1), F32)] * 3 + results,
        [
            *sums, head_square, scalars, layer, left_add, right_add, shaped, *kept[:9], head_grad, *kept[9:],
        ],
        [pltpu.VMEM(x.shape, x.dtype) for x in results] + [pltpu.VMEM((FEATS, width), F32), pltpu.SemaphoreType.DMA((34,))],
        flops=20 * width * width,
        vmem=24,
        out_specs=[IN_VMEM] * 3 + [IN_PLACE] * 13,
    )
    loss, count, norm, layer_grad, layer_new, left_new, right_new, tm, tv, tn, hm, hv, hn, vm, vv, vn = outs
    return (
        loss.reshape(()),
        count.reshape(()),
        norm.reshape(()),
        layer_grad,
        layer_new,
        jnp.swapaxes(left_new, 0, 1),
        right_new[None],
        tm,
        tv,
        tn,
        hm,
        hv,
        hn,
        vm,
        vv,
        vn,
    )


def solution(mesh):
    placed = (
        P("dp", None, None),
        P("dp", None, None),
        P("dp", None),
        P("dp", None),
        P("dp", None),
        P("dp", "mp"),
        P("dp", "mp", None),
        P("dp", "mp", None, None),
        P("dp", "mp", None),
        P("dp", "mp", None, None),
        *[P()] * 9,
    )
    return jax.shard_map(
        per_device,
        mesh=mesh,
        in_specs=placed,
        out_specs=(
            P(),
            P(),
            P(),
            P("dp", "mp"),
            P("dp", "mp"),
            P("dp", "mp", None),
            P("dp", "mp", None, None),
            *[P()] * 9,
        ),
        check_vma=False,
    )
```

time: 126 us -> 111 us (0.88)
  blocking collectives: 10.3 us -> 0 us
  starting transfers between devices: 44.6 us -> 38.2 us
  local copies, waits for them, and re-layouts: 4.91 us -> 0.03 us
  waiting for transfers between devices: 41.5 us -> 46.3 us
  Pallas kernels: 22.3 us -> 24.3 us
    all_to_all x1 -> x0, blocking collectives: 10.3 us -> none  [per_device(): sums = lax.all_to_all(send, 'dp', 0, 0, tiled=True)]
    ppermute x30 -> x18, starting transfers between devices: 34.1 us -> 24.8 us  [flip(): return lax.ppermute(x, 'dp', [(i, i ^ k) for i in range(n)])]
    unnamed x44 -> x8, local copies, waits for them, and re-layouts: 4.89 us -> 0.03 us
    ppermute x30 -> x18, waiting for transfers between devices: 26.5 us -> 30.3 us  [flip(): return lax.ppermute(x, 'dp', [(i, i ^ k) for i in range(n)])]
    all_to_all x0 -> x1, starting transfers between devices: none -> 3.55 us  [per_device(): sums = lax.all_to_all(send, 'dp', 0, 0, tiled=True)]
    all_to_all x0 -> x1, waiting for transfers between devices: none -> 2.39 us  [per_device(): sums = lax.all_to_all(send, 'dp', 0, 0, tiled=True)]
    pallas_call x11 -> x16, Pallas kernels: 22.3 us -> 24.3 us  [call(): pl.pallas_call(kernel, out_shape=tuple(outs), in_specs=in_specs or [IN_VM...]
    ppermute x15 -> x12, starting transfers between devices: 9.26 us -> 7.85 us  [exchange(): lax.ppermute(x, axis, [(i, i ^ k) for i in range(n)])]
  transfers between devices with their start and end apart: 48 -> 35, of which waited for: 21 -> 21; matrix products, arithmetic and copies ran while one was open for 0% -> 0% of each run, Pallas kernels for 9% -> 11%
where the time goes in v3:
time: 111 us
  waiting for transfers between devices  46.3 us (42%)
  starting transfers between devices  38.2 us (34%)
  Pallas kernels  24.3 us (22%)
    ppermute x18, waiting for transfers between devices, flip(): return lax.ppermute(x, 'dp', [(i, i ^ k) for i in range(n)])  30.3 us
    ppermute x18, starting transfers between devices, flip(): return lax.ppermute(x, 'dp', [(i, i ^ k) for i in range(n)])  24.8 us
    pallas_call x16, Pallas kernels, call(): pl.pallas_call(kernel, out_shape=tuple(outs), in_specs=in_specs or [IN_VM...  24.3 us
    ppermute x12, waiting for transfers between devices, exchange(): lax.ppermute(x, axis, [(i, i ^ k) for i in range(n)])  9.07 us
    ppermute x12, starting transfers between devices, exchange(): lax.ppermute(x, axis, [(i, i ^ k) for i in range(n)])  7.85 us
    ppermute x3, waiting for transfers between devices, per_device(): lax.ppermute(shares[k], 'mp', [(i, i ^ k) for i in range(nmp)])  4.51 us
    all_to_all x1, starting transfers between devices, per_device(): sums = lax.all_to_all(send, 'dp', 0, 0, tiled=True)  3.55 us
    all_to_all x1, waiting for transfers between devices, per_device(): sums = lax.all_to_all(send, 'dp', 0, 0, tiled=True)  2.39 us
  transfers between devices with their start and end apart: 35, of which 21 were waited for; matrix products, arithmetic and copies ran while one was open for 0% of the time, Pallas kernels for 11%

profile of v3, /device:TPU:0, one launch (start us, length us, event | category | flops | bytes accessed | tf_op | source)
XLA Modules:
  0.0 110.9 jit_solution(3300076536569295868)
XLA Ops:
  0.7 1.1 convert_element_type.3.refs_3_
  1.7 3.1 %collective-permute-start.2 = (bf16[96,1152]{1,0:T(8,128)(2,1)S(1)}, bf16[96,1152]{1,0:T(8,128)(2,1)S(1)}, u32[]{:S(2)}, u32[]{:S(2)}) collective-permute-start(bf16[96,1152]{1,0:T(8,128)(2,1)S(1)} %convert_element_type.3.refs_3_), channel_id=1, source_target_pairs={{0,8},{4,12},{8,0},{12,4},{16,24},{20,28},{24,16},{28,20},{1,9},{5... | collective-permute-start | bytes 663560 | tf_op jit(solution)/shard_map/ppermute | solution.py:687
  4.8 1.5 %collective-permute-start.1 = (bf16[96,1152]{1,0:T(8,128)(2,1)S(1)}, bf16[96,1152]{1,0:T(8,128)(2,1)S(1)}, u32[]{:S(2)}, u32[]{:S(2)}) collective-permute-start(bf16[96,1152]{1,0:T(8,128)(2,1)S(1)} %convert_element_type.3.refs_3_), channel_id=1, source_target_pairs={{0,4},{4,0},{8,12},{12,8},{16,20},{20,16},{24,28},{28,24},{1,5},{5... | collective-permute-start | bytes 663560 | tf_op jit(solution)/shard_map/ppermute | solution.py:687
  6.3 2.6 %collective-permute-start = (bf16[96,1152]{1,0:T(8,128)(2,1)S(1)}, bf16[96,1152]{1,0:T(8,128)(2,1)S(1)}, u32[]{:S(2)}, u32[]{:S(2)}) collective-permute-start(bf16[96,1152]{1,0:T(8,128)(2,1)S(1)} %convert_element_type.3.refs_3_), channel_id=1, source_target_pairs={{0,16},{4,20},{8,24},{12,28},{16,0},{20,4},{24,8},{28,12},{1,17},{... | collective-permute-start | bytes 663560 | tf_op jit(solution)/shard_map/ppermute | solution.py:687
  8.9 2.3 %shard_map.306 = (bf16[256,1024]{1,0:T(8,128)(2,1)S(1)}, bf16[1024,768]{1,0:T(8,128)(2,1)S(1)}, bf16[1024,768]{1,0:T(8,128)(2,1)S(1)}, f32[1024,128]{1,0:T(8,128)S(1)}) custom-call(f32[16,1024]{1,0:T(8,128)} %bitcast.21, s32[2,1024]{1,0:T(2,128)} %bitcast.22, s32[1,1024]{1,0:T(1,128)} %refs_2_.2, s32[1,1024]{1,0:T(1,128)} %refs_7_.7, f32[224,768]{1,0:T(8,128)} %refs_3_.5, ...), custom_call_target="tpu_custom_call" | custom-call | flops 805306368 | bytes 4998144 | tf_op jit(solution)/shard_map/pallas_call | solution.py:55
  11.2 2.3 %collective-permute-done.2.refs_5_ = bf16[96,1152]{1,0:T(8,128)(2,1)S(1)} collective-permute-done((bf16[96,1152]{1,0:T(8,128)(2,1)S(1)}, bf16[96,1152]{1,0:T(8,128)(2,1)S(1)}, u32[]{:S(2)}, u32[]{:S(2)}) %collective-permute-start.2) | collective-permute-done | bytes 221216 | tf_op jit(solution)/shard_map/ppermute | solution.py:687
  13.5 5.1 %collective-permute-done.refs_7_ = bf16[96,1152]{1,0:T(8,128)(2,1)S(1)} collective-permute-done((bf16[96,1152]{1,0:T(8,128)(2,1)S(1)}, bf16[96,1152]{1,0:T(8,128)(2,1)S(1)}, u32[]{:S(2)}, u32[]{:S(2)}) %collective-permute-start) | collective-permute-done | bytes 221216 | tf_op jit(solution)/shard_map/ppermute | solution.py:687
  18.6 3.3 %collective-permute-start.6 = (bf16[96,1152]{1,0:T(8,128)(2,1)S(1)}, bf16[96,1152]{1,0:T(8,128)(2,1)S(1)}, u32[]{:S(2)}, u32[]{:S(2)}) collective-permute-start(bf16[96,1152]{1,0:T(8,128)(2,1)S(1)} %collective-permute-done.1.refs_4_), channel_id=1, source_target_pairs={{0,24},{4,28},{8,16},{12,20},{16,8},{20,12},{24,0},{28,4},{1,25},{... | collective-permute-start | bytes 663560 | tf_op jit(solution)/shard_map/ppermute | solution.py:687
  21.9 2.0 %collective-permute-start.4 = (bf16[96,1152]{1,0:T(8,128)(2,1)S(1)}, bf16[96,1152]{1,0:T(8,128)(2,1)S(1)}, u32[]{:S(2)}, u32[]{:S(2)}) collective-permute-start(bf16[96,1152]{1,0:T(8,128)(2,1)S(1)} %collective-permute-done.refs_7_), channel_id=1, source_target_pairs={{0,4},{4,0},{8,12},{12,8},{16,20},{20,16},{24,28},{28,24},{1,5},{5... | collective-permute-start | bytes 663560 | tf_op jit(solution)/shard_map/ppermute | solution.py:687
  23.9 4.0 %collective-permute-done.6.refs_10_ = bf16[96,1152]{1,0:T(8,128)(2,1)S(1)} collective-permute-done((bf16[96,1152]{1,0:T(8,128)(2,1)S(1)}, bf16[96,1152]{1,0:T(8,128)(2,1)S(1)}, u32[]{:S(2)}, u32[]{:S(2)}) %collective-permute-start.6) | collective-permute-done | bytes 221216 | tf_op jit(solution)/shard_map/ppermute | solution.py:687
  27.9 1.3 %collective-permute-done.3.refs_6_ = bf16[96,1152]{1,0:T(8,128)(2,1)S(1)} collective-permute-done((bf16[96,1152]{1,0:T(8,128)(2,1)S(1)}, bf16[96,1152]{1,0:T(8,128)(2,1)S(1)}, u32[]{:S(2)}, u32[]{:S(2)}) %collective-permute-start.3) | collective-permute-done | bytes 221216 | tf_op jit(solution)/shard_map/ppermute | solution.py:687
  29.2 1.0 collective-permute-done.5.refs_9_
  30.2 1.4 %collective-permute-done.4.refs_8_ = bf16[96,1152]{1,0:T(8,128)(2,1)S(1)} collective-permute-done((bf16[96,1152]{1,0:T(8,128)(2,1)S(1)}, bf16[96,1152]{1,0:T(8,128)(2,1)S(1)}, u32[]{:S(2)}, u32[]{:S(2)}) %collective-permute-start.4) | collective-permute-done | bytes 221216 | tf_op jit(solution)/shard_map/ppermute | solution.py:687
  31.6 2.5 %shard_map.307 = (bf16[24,768]{1,0:T(8,128)(2,1)S(1)}, bf16[192,1024]{1,0:T(8,128)(2,1)S(1)}, bf16[1024,256]{1,0:T(8,128)(2,1)S(1)}, bf16[24,256]{1,0:T(8,128)(2...) custom-call(bf16[1024,768]{1,0:T(8,128)(2,1)S(1)} %get-tuple-element, ...), custom_call_target="tpu_custom_call" | custom-call | flops 805306368 | bytes 6517760 | tf_op jit(solution)/shard_map/pallas_call | solution.py:55
  34.2 1.6 %collective-permute-start.8 = (bf16[24,768]{1,0:T(8,128)(2,1)S(1)}, bf16[24,768]{1,0:T(8,128)(2,1)S(1)}, u32[]{:S(2)}, u32[]{:S(2)}) collective-permute-start(bf16[24,768]{1,0:T(8,128)(2,1)S(1)} %get-tuple-element.112.refs_0_), channel_id=1, source_target_pairs={{0,2},{1,3},{2,0},{3,1},{4,6},{5,7},{6,4},{7,5},{8,10},{9,11},{10,... | collective-permute-start | bytes 110600 | tf_op jit(solution)/shard_map/ppermute | solution.py:682
  35.8 0.3 collective-permute-start.7
  36.0 1.8 %collective-permute-done.9.refs_3_ = bf16[24,768]{1,0:T(8,128)(2,1)S(1)} collective-permute-done((bf16[24,768]{1,0:T(8,128)(2,1)S(1)}, bf16[24,768]{1,0:T(8,128)(2,1)S(1)}, u32[]{:S(2)}, u32[]{:S(2)}) %collective-permute-start.9) | collective-permute-done | bytes 36896 | tf_op jit(solution)/shard_map/ppermute | solution.py:682
  37.9 0.5 collective-permute-done.8.refs_2_
  38.4 0.6 shard_map.308
  39.0 1.1 collective-permute-start.12
  40.0 0.9 collective-permute-start.11
  40.9 1.5 %collective-permute-done.12.refs_3_ = bf16[24,768]{1,0:T(8,128)(2,1)S(1)} collective-permute-done((bf16[24,768]{1,0:T(8,128)(2,1)S(1)}, bf16[24,768]{1,0:T(8,128)(2,1)S(1)}, u32[]{:S(2)}, u32[]{:S(2)}) %collective-permute-start.12) | collective-permute-done | bytes 36896 | tf_op jit(solution)/shard_map/ppermute | solution.py:682
  42.4 1.6 %collective-permute-done.11.refs_2_ = bf16[24,768]{1,0:T(8,128)(2,1)S(1)} collective-permute-done((bf16[24,768]{1,0:T(8,128)(2,1)S(1)}, bf16[24,768]{1,0:T(8,128)(2,1)S(1)}, u32[]{:S(2)}, u32[]{:S(2)}) %collective-permute-start.11) | collective-permute-done | bytes 36896 | tf_op jit(solution)/shard_map/ppermute | solution.py:682
  44.0 1.6 %shard_map.309 = (bf16[24,768]{1,0:T(8,128)(2,1)S(1)}, bf16[24,1536]{1,0:T(8,128)(2,1)S(1)}, f32[24,768]{1,0:T(8,128)S(1)}, bf16[24,768]{1,0:T(8,128)(2,1)S(1)},...) custom-call(bf16[24,768]{1,0:T(8,128)(2,1)S(1)} %get-tuple-element.114.refs_0_, ...), custom_call_target="tpu_custom_call" | custom-call | flops 56623104 | bytes 3490912 | tf_op jit(solution)/shard_map/pallas_call | solution.py:55
  45.6 0.6 shard_map.311
  46.3 0.4 collective-permute-start.24
  46.6 0.4 collective-permute-start.15
  47.1 0.8 collective-permute-start.14
  47.9 0.6 collective-permute-start.13
  48.5 1.7 %collective-permute-done.15.refs_3_ = bf16[24,768]{1,0:T(8,128)(2,1)S(1)} collective-permute-done((bf16[24,768]{1,0:T(8,128)(2,1)S(1)}, bf16[24,768]{1,0:T(8,128)(2,1)S(1)}, u32[]{:S(2)}, u32[]{:S(2)}) %collective-permute-start.15) | collective-permute-done | bytes 36896 | tf_op jit(solution)/shard_map/ppermute | solution.py:682
  50.2 1.0 collective-permute-done.14.refs_2_
  51.2 2.3 %shard_map.310 = (bf16[4,96,384]{2,1,0:T(8,128)(2,1)S(1)}, bf16[4,96,384]{2,1,0:T(8,128)(2,1)S(1)}, f32[8,256]{1,0:T(8,128)S(1)}, f32[8,768]{1,0:T(8,128)S(1)}, ...) custom-call(bf16[24,768]{1,0:T(8,128)(2,1)S(1)} %get-tuple-element.117.refs_0_, ...), custom_call_target="tpu_custom_call" | custom-call | flops 805306368 | bytes 5280768 | tf_op jit(solution)/shard_map/pallas_call | solution.py:55
  53.5 1.8 %collective-permute-start.16 = (bf16[4,96,384]{2,1,0:T(8,128)(2,1)S(1)}, bf16[4,96,384]{2,1,0:T(8,128)(2,1)S(1)}, u32[]{:S(2)}, u32[]{:S(2)}) collective-permute-start(bf16[4,96,384]{2,1,0:T(8,128)(2,1)S(1)} %get-tuple-element.125), channel_id=1, source_target_pairs={{0,4},{4,0},{8,12},{12,8},{16,20},{20,16},{24,28},{28,24},{1,5},{5... | collective-permute-start | bytes 884744 | tf_op jit(solution)/shard_map/ppermute | solution.py:687
  55.3 1.1 shard_map.312
  56.4 0.1 collective-permute-start.17
  56.5 1.0 collective-permute-start.18
  57.5 0.8 collective-permute-start.19
  58.3 0.1 shard_map.315
  58.4 0.4 collective-permute-start.27
  58.8 3.3 %collective-permute-done.18.refs_2_ = bf16[64,768]{1,0:T(8,128)(2,1)S(1)} collective-permute-done((bf16[64,768]{1,0:T(8,128)(2,1)S(1)}, bf16[64,768]{1,0:T(8,128)(2,1)S(1)}, u32[]{:S(2)}, u32[]{:S(2)}) %collective-permute-start.18) | collective-permute-done | bytes 98336 | tf_op jit(solution)/shard_map/ppermute | solution.py:842
  62.1 1.2 %collective-permute-done.19.refs_3_ = bf16[64,768]{1,0:T(8,128)(2,1)S(1)} collective-permute-done((bf16[64,768]{1,0:T(8,128)(2,1)S(1)}, bf16[64,768]{1,0:T(8,128)(2,1)S(1)}, u32[]{:S(2)}, u32[]{:S(2)}) %collective-permute-start.19) | collective-permute-done | bytes 98336 | tf_op jit(solution)/shard_map/ppermute | solution.py:842
  63.3 0.1 shard_map.313
  63.4 0.3 collective-permute-start.20
  63.8 0.5 collective-permute-start.26
  64.3 4.5 %collective-permute-done.20.table_came = bf16[4,32,384]{2,1,0:T(8,128)(2,1)S(1)} collective-permute-done((bf16[4,32,384]{2,1,0:T(8,128)(2,1)S(1)}, bf16[4,32,384]{2,1,0:T(8,128)(2,1)S(1)}, u32[]{:S(2)}, u32[]{:S(2)}) %collective-permute-start.20) | collective-permute-done | bytes 98336 | tf_op jit(solution)/shard_map/ppermute | solution.py:687
  68.8 0.2 shard_map.314
  69.0 0.4 collective-permute-start.21
  69.4 2.3 %collective-permute-start.22 = (bf16[128,384]{1,0:T(8,128)(2,1)S(1)}, bf16[128,384]{1,0:T(8,128)(2,1)S(1)}, u32[]{:S(2)}, u32[]{:S(2)}) collective-permute-start(bf16[128,384]{1,0:T(8,128)(2,1)S(1)} %get-tuple-element.148), channel_id=1, source_target_pairs={{0,16},{4,20},{8,24},{12,28},{16,0},{20,4},{24,8},{28,12},{1,17},{... | collective-permute-start | bytes 294920 | tf_op jit(solution)/shard_map/ppermute | solution.py:687
  71.7 1.8 %collective-permute-start.23 = (bf16[128,384]{1,0:T(8,128)(2,1)S(1)}, bf16[128,384]{1,0:T(8,128)(2,1)S(1)}, u32[]{:S(2)}, u32[]{:S(2)}) collective-permute-start(bf16[128,384]{1,0:T(8,128)(2,1)S(1)} %get-tuple-element.149), channel_id=1, source_target_pairs={{0,24},{4,28},{8,16},{12,20},{16,8},{20,12},{24,0},{28,4},{1,25},{... | collective-permute-start | bytes 294920 | tf_op jit(solution)/shard_map/ppermute | solution.py:687
  73.5 2.7 %collective-permute-start.28 = (bf16[96,384]{1,0:T(8,128)(2,1)S(1)}, bf16[96,384]{1,0:T(8,128)(2,1)S(1)}, u32[]{:S(2)}, u32[]{:S(2)}) collective-permute-start(bf16[96,384]{1,0:T(8,128)(2,1)S(1)} %get-tuple-element.160), channel_id=1, source_target_pairs={{0,16},{4,20},{8,24},{12,28},{16,0},{20,4},{24,8},{28,12},{1,17},{... | collective-permute-start | bytes 221192 | tf_op jit(solution)/shard_map/ppermute | solution.py:687
  76.2 3.2 %collective-permute-done.25.refs_1_ = bf16[2,48,384]{2,1,0:T(8,128)(2,1)S(1)} collective-permute-done((bf16[2,48,384]{2,1,0:T(8,128)(2,1)S(1)}, bf16[2,48,384]{2,1,0:T(8,128)(2,1)S(1)}, u32[]{:S(2)}, u32[]{:S(2)}) %collective-permute-start.25) | collective-permute-done | bytes 73760 | tf_op jit(solution)/shard_map/ppermute | solution.py:687
  79.4 2.3 %collective-permute-done.22.refs_2_ = bf16[128,384]{1,0:T(8,128)(2,1)S(1)} collective-permute-done((bf16[128,384]{1,0:T(8,128)(2,1)S(1)}, bf16[128,384]{1,0:T(8,128)(2,1)S(1)}, u32[]{:S(2)}, u32[]{:S(2)}) %collective-permute-start.22) | collective-permute-done | bytes 98336 | tf_op jit(solution)/shard_map/ppermute | solution.py:687
  81.7 2.4 %collective-permute-done.28.refs_5_ = bf16[96,384]{1,0:T(8,128)(2,1)S(1)} collective-permute-done((bf16[96,384]{1,0:T(8,128)(2,1)S(1)}, bf16[96,384]{1,0:T(8,128)(2,1)S(1)}, u32[]{:S(2)}, u32[]{:S(2)}) %collective-permute-start.28) | collective-permute-done | bytes 73760 | tf_op jit(solution)/shard_map/ppermute | solution.py:687
  84.1 1.2 %shard_map.317 = (f32[6,96,192]{2,1,0:T(8,128)S(1)}, bf16[8,16,512]{2,1,0:T(8,128)(2,1)}, f32[8,128]{1,0:T(8,128)S(1)}) custom-call(bf16[128,384]{1,0:T(8,128)(2,1)S(1)} %get-tuple-element.153.refs_0_, bf16[128,384]{1,0:T(8,128)(2,1)S(1)} %collective-permute-done.21.refs_1_, bf16[128,384]{1,0:T(8,128)(2,1)S(1)} %collective-permute-done.22.refs_2_, ...), custom_call_target="tpu_custom_call" | custom-call | flops 50331648 | bytes 1160192 | tf_op jit(solution)/shard_map/pallas_call | solution.py:55
  85.2 3.6 %all-to-all-start = ((bf16[8,16,512]{2,1,0:T(8,128)(2,1)}), bf16[8,16,512]{2,1,0:T(8,128)(2,1)S(1)}, u32[]{:S(2)}, u32[]{:S(2)}) async-start(bf16[8,16,512]{2,1,0:T(8,128)(2,1)} %get-tuple-element.162), calls=%async_computation | async-start | bytes 262144 | tf_op jit(solution)/shard_map/all_to_all | solution.py:864
  88.8 1.8 %collective-permute-start.32 = (bf16[2,48,384]{2,1,0:T(8,128)(2,1)S(1)}, bf16[2,48,384]{2,1,0:T(8,128)(2,1)S(1)}, u32[]{:S(2)}, u32[]{:S(2)}) collective-permute-start(bf16[2,48,384]{2,1,0:T(8,128)(2,1)S(1)} %collective-permute-done.26.refs_2_), channel_id=1, source_target_pairs={{0,8},{4,12},{8,0},{12,4},{16,24},{20,28},{24,16},{28,20},{1,9},{5... | collective-permute-start | bytes 221192 | tf_op jit(solution)/shard_map/ppermute | solution.py:687
  90.6 2.9 %collective-permute-done.32.refs_3_ = bf16[2,48,384]{2,1,0:T(8,128)(2,1)S(1)} collective-permute-done((bf16[2,48,384]{2,1,0:T(8,128)(2,1)S(1)}, bf16[2,48,384]{2,1,0:T(8,128)(2,1)S(1)}, u32[]{:S(2)}, u32[]{:S(2)}) %collective-permute-start.32) | collective-permute-done | bytes 73760 | tf_op jit(solution)/shard_map/ppermute | solution.py:687
  93.5 2.4 %all-to-all-done.refs_0_ = bf16[8,16,512]{2,1,0:T(8,128)(2,1)S(1)} async-done(((bf16[8,16,512]{2,1,0:T(8,128)(2,1)}), bf16[8,16,512]{2,1,0:T(8,128)(2,1)S(1)}, u32[]{:S(2)}, u32[]{:S(2)}) %all-to-all-start) | async-done | bytes 131104 | tf_op jit(solution)/shard_map/all_to_all | solution.py:864
  96.0 1.1 collective-permute-start.31
  97.1 1.1 collective-permute-start.30
  98.2 4.9 %shard_map.320 = (f32[6,96,96]{2,1,0:T(8,128)S(1)}, f32[6,192,192]{2,1,0:T(8,128)S(1)}, f32[6,96,192]{2,1,0:T(8,128)S(1)}, f32[96,1152]{1,0:T(8,128)S(1)}, f32[6...) custom-call(f32[6,96,192]{2,1,0:T(8,128)S(1)} %get-tuple-element.167, ...), custom_call_target="tpu_custom_call" | custom-call | flops 764411904 | bytes 24680448 | tf_op jit(solution)/shard_map/pallas_call | solution.py:55
  103.1 0.7 shard_map.319
  103.8 0.9 collective-permute-done.30.refs_2_
  104.7 6.0 %shard_map.321 = (f32[1,1]{1,0:T(1,128)}, f32[1,1]{1,0:T(1,128)}, f32[1,1]{1,0:T(1,128)}, f32[96,1152]{1,0:T(8,128)}, f32[96,1152]{1,0:T(8,128)}, /*index=5*/f32...) custom-call(bf16[8,16,512]{2,1,0:T(8,128)(2,1)S(1)} %all-to-all-done, ...), custom_call_target="tpu_custom_call" | custom-call | flops 11796480 | bytes 26908684 | tf_op jit(solution)/shard_map/pallas_call | solution.py:55
  (31 shorter events, 0.3 us)
Async XLA Ops:
  0.6 30.9 %copy-start.1 = (f32[11,768]{1,0:T(8,128)S(1)}, f32[11,768]{1,0:T(8,128)}, u32[]{:S(2)}) copy-start(f32[11,768]{1,0:T(8,128)} %refs_9_.1) | copy-start | bytes 101380
  0.7 30.9 %copy-start.2 = (s32[1,1024]{1,0:T(1,128)S(1)}, s32[1,1024]{1,0:T(1,128)}, u32[]{:S(2)}) copy-start(s32[1,1024]{1,0:T(1,128)} %refs_7_.7) | copy-start | bytes 12292
  1.7 11.8 %collective-permute-start.2 = (bf16[96,1152]{1,0:T(8,128)(2,1)S(1)}, bf16[96,1152]{1,0:T(8,128)(2,1)S(1)}, u32[]{:S(2)}, u32[]{:S(2)}) collective-permute-start(bf16[96,1152]{1,0:T(8,128)(2,1)S(1)} %convert_element_type.3.refs_3_), channel_id=1, source_target_pairs={{0,8},{4,12},{8,0},{12,4},{16,24},{20,28},{24,16},{28,20},{1,9},{5... | collective-permute-start | bytes 663560 | tf_op jit(solution)/shard_map/ppermute | solution.py:687
  4.8 8.7 %collective-permute-start.1 = (bf16[96,1152]{1,0:T(8,128)(2,1)S(1)}, bf16[96,1152]{1,0:T(8,128)(2,1)S(1)}, u32[]{:S(2)}, u32[]{:S(2)}) collective-permute-start(bf16[96,1152]{1,0:T(8,128)(2,1)S(1)} %convert_element_type.3.refs_3_), channel_id=1, source_target_pairs={{0,4},{4,0},{8,12},{12,8},{16,20},{20,16},{24,28},{28,24},{1,5},{5... | collective-permute-start | bytes 663560 | tf_op jit(solution)/shard_map/ppermute | solution.py:687
  6.3 12.3 %collective-permute-start = (bf16[96,1152]{1,0:T(8,128)(2,1)S(1)}, bf16[96,1152]{1,0:T(8,128)(2,1)S(1)}, u32[]{:S(2)}, u32[]{:S(2)}) collective-permute-start(bf16[96,1152]{1,0:T(8,128)(2,1)S(1)} %convert_element_type.3.refs_3_), channel_id=1, source_target_pairs={{0,16},{4,20},{8,24},{12,28},{16,0},{20,4},{24,8},{28,12},{1,17},{... | collective-permute-start | bytes 663560 | tf_op jit(solution)/shard_map/ppermute | solution.py:687
  11.2 32.8 %copy-start = (f32[768,768]{1,0:T(8,128)S(1)}, f32[768,768]{1,0:T(8,128)}, u32[]{:S(2)}) copy-start(f32[768,768]{1,0:T(8,128)} %refs_6_.3) | copy-start | bytes 7077892
  11.2 32.8 %copy-start.3 = (f32[1,24]{1,0:T(1,128)S(1)}, f32[1,24]{1,0:T(1,128)}, u32[]{:S(2)}) copy-start(f32[1,24]{1,0:T(1,128)} %refs_7_.5) | copy-start | bytes 292
  18.6 9.3 %collective-permute-start.6 = (bf16[96,1152]{1,0:T(8,128)(2,1)S(1)}, bf16[96,1152]{1,0:T(8,128)(2,1)S(1)}, u32[]{:S(2)}, u32[]{:S(2)}) collective-permute-start(bf16[96,1152]{1,0:T(8,128)(2,1)S(1)} %collective-permute-done.1.refs_4_), channel_id=1, source_target_pairs={{0,24},{4,28},{8,16},{12,20},{16,8},{20,12},{24,0},{28,4},{1,25},{... | collective-permute-start | bytes 663560 | tf_op jit(solution)/shard_map/ppermute | solution.py:687
  21.9 7.3 %collective-permute-start.3 = (bf16[96,1152]{1,0:T(8,128)(2,1)S(1)}, bf16[96,1152]{1,0:T(8,128)(2,1)S(1)}, u32[]{:S(2)}, u32[]{:S(2)}) collective-permute-start(bf16[96,1152]{1,0:T(8,128)(2,1)S(1)} %collective-permute-done.2.refs_5_), channel_id=1, source_target_pairs={{0,4},{4,0},{8,12},{12,8},{16,20},{20,16},{24,28},{28,24},{1,5},{5... | collective-permute-start | bytes 663560 | tf_op jit(solution)/shard_map/ppermute | solution.py:687
  21.9 8.3 %collective-permute-start.5 = (bf16[96,1152]{1,0:T(8,128)(2,1)S(1)}, bf16[96,1152]{1,0:T(8,128)(2,1)S(1)}, u32[]{:S(2)}, u32[]{:S(2)}) collective-permute-start(bf16[96,1152]{1,0:T(8,128)(2,1)S(1)} %collective-permute-done.refs_7_), channel_id=1, source_target_pairs={{0,8},{4,12},{8,0},{12,4},{16,24},{20,28},{24,16},{28,20},{1,9},{5... | collective-permute-start | bytes 663560 | tf_op jit(solution)/shard_map/ppermute | solution.py:687
  21.9 9.7 %collective-permute-start.4 = (bf16[96,1152]{1,0:T(8,128)(2,1)S(1)}, bf16[96,1152]{1,0:T(8,128)(2,1)S(1)}, u32[]{:S(2)}, u32[]{:S(2)}) collective-permute-start(bf16[96,1152]{1,0:T(8,128)(2,1)S(1)} %collective-permute-done.refs_7_), channel_id=1, source_target_pairs={{0,4},{4,0},{8,12},{12,8},{16,20},{20,16},{24,28},{28,24},{1,5},{5... | collective-permute-start | bytes 663560 | tf_op jit(solution)/shard_map/ppermute | solution.py:687
  34.1 3.8 %collective-permute-start.9 = (bf16[24,768]{1,0:T(8,128)(2,1)S(1)}, bf16[24,768]{1,0:T(8,128)(2,1)S(1)}, u32[]{:S(2)}, u32[]{:S(2)}) collective-permute-start(bf16[24,768]{1,0:T(8,128)(2,1)S(1)} %get-tuple-element.112.refs_0_), channel_id=1, source_target_pairs={{0,3},{1,2},{2,1},{3,0},{4,7},{5,6},{6,5},{7,4},{8,11},{9,10},{10,... | collective-permute-start | bytes 110600 | tf_op jit(solution)/shard_map/ppermute | solution.py:682
  34.2 4.2 %collective-permute-start.8 = (bf16[24,768]{1,0:T(8,128)(2,1)S(1)}, bf16[24,768]{1,0:T(8,128)(2,1)S(1)}, u32[]{:S(2)}, u32[]{:S(2)}) collective-permute-start(bf16[24,768]{1,0:T(8,128)(2,1)S(1)} %get-tuple-element.112.refs_0_), channel_id=1, source_target_pairs={{0,2},{1,3},{2,0},{3,1},{4,6},{5,7},{6,4},{7,5},{8,10},{9,11},{10,... | collective-permute-start | bytes 110600 | tf_op jit(solution)/shard_map/ppermute | solution.py:682
  35.8 2.6 %collective-permute-start.7 = (bf16[24,768]{1,0:T(8,128)(2,1)S(1)}, bf16[24,768]{1,0:T(8,128)(2,1)S(1)}, u32[]{:S(2)}, u32[]{:S(2)}) collective-permute-start(bf16[24,768]{1,0:T(8,128)(2,1)S(1)} %get-tuple-element.112.refs_0_), channel_id=1, source_target_pairs={{0,1},{1,0},{2,3},{3,2},{4,5},{5,4},{6,7},{7,6},{8,9},{9,8},{10,11... | collective-permute-start | bytes 110600 | tf_op jit(solution)/shard_map/ppermute | solution.py:682
  39.0 3.4 %collective-permute-start.12 = (bf16[24,768]{1,0:T(8,128)(2,1)S(1)}, bf16[24,768]{1,0:T(8,128)(2,1)S(1)}, u32[]{:S(2)}, u32[]{:S(2)}) collective-permute-start(bf16[24,768]{1,0:T(8,128)(2,1)S(1)} %get-tuple-element.114.refs_0_), channel_id=1, source_target_pairs={{0,3},{1,2},{2,1},{3,0},{4,7},{5,6},{6,5},{7,4},{8,11},{9,10},{10,... | collective-permute-start | bytes 110600 | tf_op jit(solution)/shard_map/ppermute | solution.py:682
  40.0 4.0 %collective-permute-start.11 = (bf16[24,768]{1,0:T(8,128)(2,1)S(1)}, bf16[24,768]{1,0:T(8,128)(2,1)S(1)}, u32[]{:S(2)}, u32[]{:S(2)}) collective-permute-start(bf16[24,768]{1,0:T(8,128)(2,1)S(1)} %get-tuple-element.114.refs_0_), channel_id=1, source_target_pairs={{0,2},{1,3},{2,0},{3,1},{4,6},{5,7},{6,4},{7,5},{8,10},{9,11},{10,... | collective-permute-start | bytes 110600 | tf_op jit(solution)/shard_map/ppermute | solution.py:682
  40.9 3.1 %collective-permute-start.10 = (bf16[24,768]{1,0:T(8,128)(2,1)S(1)}, bf16[24,768]{1,0:T(8,128)(2,1)S(1)}, u32[]{:S(2)}, u32[]{:S(2)}) collective-permute-start(bf16[24,768]{1,0:T(8,128)(2,1)S(1)} %get-tuple-element.114.refs_0_), channel_id=1, source_target_pairs={{0,1},{1,0},{2,3},{3,2},{4,5},{5,4},{6,7},{7,6},{8,9},{9,8},{10,11... | collective-permute-start | bytes 110600 | tf_op jit(solution)/shard_map/ppermute | solution.py:682
  46.3 12.0 %collective-permute-start.24 = (bf16[9,48,384]{2,1,0:T(8,128)(2,1)S(1)}, bf16[9,48,384]{2,1,0:T(8,128)(2,1)S(1)}, u32[]{:S(2)}, u32[]{:S(2)}) collective-permute-start(bf16[9,48,384]{2,1,0:T(8,128)(2,1)S(1)} %get-tuple-element.151), channel_id=1, source_target_pairs={{0,4},{4,0},{8,12},{12,8},{16,20},{20,16},{24,28},{28,24},{1,5},{5... | collective-permute-start | bytes 995336 | tf_op jit(solution)/shard_map/ppermute | solution.py:687
  46.6 3.6 %collective-permute-start.15 = (bf16[24,768]{1,0:T(8,128)(2,1)S(1)}, bf16[24,768]{1,0:T(8,128)(2,1)S(1)}, u32[]{:S(2)}, u32[]{:S(2)}) collective-permute-start(bf16[24,768]{1,0:T(8,128)(2,1)S(1)} %get-tuple-element.117.refs_0_), channel_id=1, source_target_pairs={{0,3},{1,2},{2,1},{3,0},{4,7},{5,6},{6,5},{7,4},{8,11},{9,10},{10,... | collective-permute-start | bytes 110600 | tf_op jit(solution)/shard_map/ppermute | solution.py:682
  47.1 4.1 %collective-permute-start.14 = (bf16[24,768]{1,0:T(8,128)(2,1)S(1)}, bf16[24,768]{1,0:T(8,128)(2,1)S(1)}, u32[]{:S(2)}, u32[]{:S(2)}) collective-permute-start(bf16[24,768]{1,0:T(8,128)(2,1)S(1)} %get-tuple-element.117.refs_0_), channel_id=1, source_target_pairs={{0,2},{1,3},{2,0},{3,1},{4,6},{5,7},{6,4},{7,5},{8,10},{9,11},{10,... | collective-permute-start | bytes 110600 | tf_op jit(solution)/shard_map/ppermute | solution.py:682
  47.9 3.3 %collective-permute-start.13 = (bf16[24,768]{1,0:T(8,128)(2,1)S(1)}, bf16[24,768]{1,0:T(8,128)(2,1)S(1)}, u32[]{:S(2)}, u32[]{:S(2)}) collective-permute-start(bf16[24,768]{1,0:T(8,128)(2,1)S(1)} %get-tuple-element.117.refs_0_), channel_id=1, source_target_pairs={{0,1},{1,0},{2,3},{3,2},{4,5},{5,4},{6,7},{7,6},{8,9},{9,8},{10,11... | collective-permute-start | bytes 110600 | tf_op jit(solution)/shard_map/ppermute | solution.py:682
  53.5 15.3 %collective-permute-start.16 = (bf16[4,96,384]{2,1,0:T(8,128)(2,1)S(1)}, bf16[4,96,384]{2,1,0:T(8,128)(2,1)S(1)}, u32[]{:S(2)}, u32[]{:S(2)}) collective-permute-start(bf16[4,96,384]{2,1,0:T(8,128)(2,1)S(1)} %get-tuple-element.125), channel_id=1, source_target_pairs={{0,4},{4,0},{8,12},{12,8},{16,20},{20,16},{24,28},{28,24},{1,5},{5... | collective-permute-start | bytes 884744 | tf_op jit(solution)/shard_map/ppermute | solution.py:687
  56.4 2.4 %collective-permute-start.17 = (bf16[64,768]{1,0:T(8,128)(2,1)S(1)}, bf16[64,768]{1,0:T(8,128)(2,1)S(1)}, u32[]{:S(2)}, u32[]{:S(2)}) collective-permute-start(bf16[64,768]{1,0:T(8,128)(2,1)S(1)} %get-tuple-element.139), channel_id=1, source_target_pairs={{0,1},{1,0},{2,3},{3,2},{4,5},{5,4},{6,7},{7,6},{8,9},{9,8},{10,11... | collective-permute-start | bytes 294920 | tf_op jit(solution)/shard_map/ppermute | solution.py:842
  56.5 5.7 %collective-permute-start.18 = (bf16[64,768]{1,0:T(8,128)(2,1)S(1)}, bf16[64,768]{1,0:T(8,128)(2,1)S(1)}, u32[]{:S(2)}, u32[]{:S(2)}) collective-permute-start(bf16[64,768]{1,0:T(8,128)(2,1)S(1)} %get-tuple-element.140), channel_id=1, source_target_pairs={{0,2},{1,3},{2,0},{3,1},{4,6},{5,7},{6,4},{7,5},{8,10},{9,11},{10,... | collective-permute-start | bytes 294920 | tf_op jit(solution)/shard_map/ppermute | solution.py:842
  57.5 5.8 %collective-permute-start.19 = (bf16[64,768]{1,0:T(8,128)(2,1)S(1)}, bf16[64,768]{1,0:T(8,128)(2,1)S(1)}, u32[]{:S(2)}, u32[]{:S(2)}) collective-permute-start(bf16[64,768]{1,0:T(8,128)(2,1)S(1)} %get-tuple-element.141), channel_id=1, source_target_pairs={{0,3},{1,2},{2,1},{3,0},{4,7},{5,6},{6,5},{7,4},{8,11},{9,10},{10,... | collective-permute-start | bytes 294920 | tf_op jit(solution)/shard_map/ppermute | solution.py:842
  58.4 15.1 %collective-permute-start.27 = (bf16[2,96,384]{2,1,0:T(8,128)(2,1)S(1)}, bf16[2,96,384]{2,1,0:T(8,128)(2,1)S(1)}, u32[]{:S(2)}, u32[]{:S(2)}) collective-permute-start(bf16[2,96,384]{2,1,0:T(8,128)(2,1)S(1)} %get-tuple-element.158), channel_id=1, source_target_pairs={{0,8},{4,12},{8,0},{12,4},{16,24},{20,28},{24,16},{28,20},{1,9},{5... | collective-permute-start | bytes 442376 | tf_op jit(solution)/shard_map/ppermute | solution.py:687
  63.4 5.3 %collective-permute-start.20 = (bf16[4,32,384]{2,1,0:T(8,128)(2,1)S(1)}, bf16[4,32,384]{2,1,0:T(8,128)(2,1)S(1)}, u32[]{:S(2)}, u32[]{:S(2)}) collective-permute-start(bf16[4,32,384]{2,1,0:T(8,128)(2,1)S(1)} %get-tuple-element.145), channel_id=1, source_target_pairs={{0,4},{4,0},{8,12},{12,8},{16,20},{20,16},{24,28},{28,24},{1,5},{5... | collective-permute-start | bytes 294920 | tf_op jit(solution)/shard_map/ppermute | solution.py:687
  63.8 9.7 %collective-permute-start.26 = (bf16[2,48,384]{2,1,0:T(8,128)(2,1)S(1)}, bf16[2,48,384]{2,1,0:T(8,128)(2,1)S(1)}, u32[]{:S(2)}, u32[]{:S(2)}) collective-permute-start(bf16[2,48,384]{2,1,0:T(8,128)(2,1)S(1)} %get-tuple-element.152.refs_0_), channel_id=1, source_target_pairs={{0,16},{4,20},{8,24},{12,28},{16,0},{20,4},{24,8},{28,12},{1,17},{... | collective-permute-start | bytes 221192 | tf_op jit(solution)/shard_map/ppermute | solution.py:687
  69.0 10.4 %collective-permute-start.21 = (bf16[128,384]{1,0:T(8,128)(2,1)S(1)}, bf16[128,384]{1,0:T(8,128)(2,1)S(1)}, u32[]{:S(2)}, u32[]{:S(2)}) collective-permute-start(bf16[128,384]{1,0:T(8,128)(2,1)S(1)} %get-tuple-element.147), channel_id=1, source_target_pairs={{0,8},{4,12},{8,0},{12,4},{16,24},{20,28},{24,16},{28,20},{1,9},{5... | collective-permute-start | bytes 294920 | tf_op jit(solution)/shard_map/ppermute | solution.py:687
  69.4 12.2 %collective-permute-start.22 = (bf16[128,384]{1,0:T(8,128)(2,1)S(1)}, bf16[128,384]{1,0:T(8,128)(2,1)S(1)}, u32[]{:S(2)}, u32[]{:S(2)}) collective-permute-start(bf16[128,384]{1,0:T(8,128)(2,1)S(1)} %get-tuple-element.148), channel_id=1, source_target_pairs={{0,16},{4,20},{8,24},{12,28},{16,0},{20,4},{24,8},{28,12},{1,17},{... | collective-permute-start | bytes 294920 | tf_op jit(solution)/shard_map/ppermute | solution.py:687
  71.7 10.0 %collective-permute-start.23 = (bf16[128,384]{1,0:T(8,128)(2,1)S(1)}, bf16[128,384]{1,0:T(8,128)(2,1)S(1)}, u32[]{:S(2)}, u32[]{:S(2)}) collective-permute-start(bf16[128,384]{1,0:T(8,128)(2,1)S(1)} %get-tuple-element.149), channel_id=1, source_target_pairs={{0,24},{4,28},{8,16},{12,20},{16,8},{20,12},{24,0},{28,4},{1,25},{... | collective-permute-start | bytes 294920 | tf_op jit(solution)/shard_map/ppermute | solution.py:687
  73.5 5.9 %collective-permute-start.25 = (bf16[2,48,384]{2,1,0:T(8,128)(2,1)S(1)}, bf16[2,48,384]{2,1,0:T(8,128)(2,1)S(1)}, u32[]{:S(2)}, u32[]{:S(2)}) collective-permute-start(bf16[2,48,384]{2,1,0:T(8,128)(2,1)S(1)} %get-tuple-element.152.refs_0_), channel_id=1, source_target_pairs={{0,8},{4,12},{8,0},{12,4},{16,24},{20,28},{24,16},{28,20},{1,9},{5... | collective-permute-start | bytes 221192 | tf_op jit(solution)/shard_map/ppermute | solution.py:687
  73.5 10.5 %collective-permute-start.28 = (bf16[96,384]{1,0:T(8,128)(2,1)S(1)}, bf16[96,384]{1,0:T(8,128)(2,1)S(1)}, u32[]{:S(2)}, u32[]{:S(2)}) collective-permute-start(bf16[96,384]{1,0:T(8,128)(2,1)S(1)} %get-tuple-element.160), channel_id=1, source_target_pairs={{0,16},{4,20},{8,24},{12,28},{16,0},{20,4},{24,8},{28,12},{1,17},{... | collective-permute-start | bytes 221192 | tf_op jit(solution)/shard_map/ppermute | solution.py:687
  85.2 10.7 %all-to-all-start = ((bf16[8,16,512]{2,1,0:T(8,128)(2,1)}), bf16[8,16,512]{2,1,0:T(8,128)(2,1)S(1)}, u32[]{:S(2)}, u32[]{:S(2)}) async-start(bf16[8,16,512]{2,1,0:T(8,128)(2,1)} %get-tuple-element.162), calls=%async_computation | async-start | bytes 262144 | tf_op jit(solution)/shard_map/all_to_all | solution.py:864
  88.8 4.7 %collective-permute-start.32 = (bf16[2,48,384]{2,1,0:T(8,128)(2,1)S(1)}, bf16[2,48,384]{2,1,0:T(8,128)(2,1)S(1)}, u32[]{:S(2)}, u32[]{:S(2)}) collective-permute-start(bf16[2,48,384]{2,1,0:T(8,128)(2,1)S(1)} %collective-permute-done.26.refs_2_), channel_id=1, source_target_pairs={{0,8},{4,12},{8,0},{12,4},{16,24},{20,28},{24,16},{28,20},{1,9},{5... | collective-permute-start | bytes 221192 | tf_op jit(solution)/shard_map/ppermute | solution.py:687
  95.9 7.1 %collective-permute-start.33 = (bf16[256,768]{1,0:T(8,128)(2,1)S(1)}, bf16[256,768]{1,0:T(8,128)(2,1)S(1)}, u32[]{:S(2)}, u32[]{:S(2)}) collective-permute-start(bf16[256,768]{1,0:T(8,128)(2,1)S(1)} %shard_map.318.keep), channel_id=1, source_target_pairs={{0,1},{1,0},{2,3},{3,2},{4,5},{5,4},{6,7},{7,6},{8,9},{9,8},{10,11... | collective-permute-start | bytes 1179656 | tf_op jit(solution)/shard_map/ppermute | solution.py:870
  96.0 7.7 %collective-permute-start.31 = (bf16[8,16,512]{2,1,0:T(8,128)(2,1)S(1)}, bf16[8,16,512]{2,1,0:T(8,128)(2,1)S(1)}, u32[]{:S(2)}, u32[]{:S(2)}) collective-permute-start(bf16[8,16,512]{2,1,0:T(8,128)(2,1)S(1)} %all-to-all-done.refs_0_), channel_id=1, source_target_pairs={{0,3},{1,2},{2,1},{3,0},{4,7},{5,6},{6,5},{7,4},{8,11},{9,10},{10,... | collective-permute-start | bytes 393224 | tf_op jit(solution)/shard_map/ppermute | solution.py:682
  97.1 7.6 %collective-permute-start.30 = (bf16[8,16,512]{2,1,0:T(8,128)(2,1)S(1)}, bf16[8,16,512]{2,1,0:T(8,128)(2,1)S(1)}, u32[]{:S(2)}, u32[]{:S(2)}) collective-permute-start(bf16[8,16,512]{2,1,0:T(8,128)(2,1)S(1)} %all-to-all-done.refs_0_), channel_id=1, source_target_pairs={{0,2},{1,3},{2,0},{3,1},{4,6},{5,7},{6,4},{7,5},{8,10},{9,11},{10,... | collective-permute-start | bytes 393224 | tf_op jit(solution)/shard_map/ppermute | solution.py:682
  98.2 6.5 %collective-permute-start.29 = (bf16[8,16,512]{2,1,0:T(8,128)(2,1)S(1)}, bf16[8,16,512]{2,1,0:T(8,128)(2,1)S(1)}, u32[]{:S(2)}, u32[]{:S(2)}) collective-permute-start(bf16[8,16,512]{2,1,0:T(8,128)(2,1)S(1)} %all-to-all-done.refs_0_), channel_id=1, source_target_pairs={{0,1},{1,0},{2,3},{3,2},{4,5},{5,4},{6,7},{7,6},{8,9},{9,8},{10,11... | collective-permute-start | bytes 393224 | tf_op jit(solution)/shard_map/ppermute | solution.py:682

commit v4 on v3

--- a/solution.py
+++ b/solution.py
@@ -118,6 +118,10 @@
         second[here, :] = piece[:, split:]
 
 
+def spaced(t):
+    return t + ((t * 9363) >> 16)
+
+
 def embed_kernel(mols, *refs):
     sources, (at, normed, hats, invs), held, (high, low, prev, sems) = refs[:6], refs[6:10], refs[10:16], refs[16:]
     copies = [pltpu.make_async_copy(a, b, sems.at[i]) for i, (a, b) in enumerate(zip(sources, held))]
@@ -132,14 +136,18 @@
     rows = tables.shape[0]
     tab = tables[...]
     tab_high = tab.astype(BF)
-    high[0:rows, :] = tab_high
-    rest = jnp.where(iota(tab.shape, 0) < TYPES, tab - tab_high.astype(F32), 0.0)
-    low[0:rows, :] = rest.astype(BF)
-    r = iota((FEATS - rows, width), 0)
-    extra = jnp.where(r == 0, vectors[6:7, :], jnp.where(r == 1, vectors[7:8, :], jnp.where(r == 2, vectors[8:9, :], 0.0)))
+    rest = jnp.where(iota(tab.shape, 0) < TYPES, tab - tab_high.astype(F32), 0.0).astype(BF)
+    place = (iota((FEATS, rows), 0) == spaced(iota((FEATS, rows), 1))).astype(F32).astype(BF)
+    r = iota((32, width), 0)
+    extra = jnp.where(r == 7, vectors[6:7, :], jnp.where(r == 15, vectors[7:8, :], jnp.where(r == 23, vectors[8:9, :], 0.0)))
     extra_high = extra.astype(BF)
-    high[rows:FEATS, :] = extra_high
-    low[rows:FEATS, :] = (extra - extra_high.astype(F32)).astype(BF)
+    placed = dot(place, tab_high)
+    high[0:32, :] = (placed[0:32, :] + extra_high.astype(F32)).astype(BF)
+    high[32:, :] = placed[32:, :].astype(BF)
+    placed = dot(place, rest)
+    low[0:32, :] = (placed[0:32, :] + extra - extra_high.astype(F32)).astype(BF)
+    low[32:, :] = placed[32:, :].astype(BF)
+    place = place[:, TYPES:]
     seg_row = seg[...]
     before = pltpu.roll(jnp.broadcast_to(seg_row, (8, length)), 1, 1)
     before = jnp.where(iota((8, length), 1) == 0, -1, before)
@@ -161,14 +169,12 @@
         pair_two = dot(near, (source == two).astype(F32).astype(BF))
         seg_here = seg[0:1, here]
         begins = (seg_here != mols) & (seg_here != prev[0:1, here])
-        kind = jnp.where(begins, -1, kinds[0:1, here])
+        kind = jnp.where(begins, -1, spaced(kinds[0:1, here]))
         keep = jnp.where(begins, 0.0, 1.0)
-        at[0:TYPES, here] = (iota((TYPES, BLOCK), 0) == kind).astype(F32).astype(BF)
-        half = pair_one.shape[0]
-        at[TYPES : TYPES + half, here] = (pair_one * keep).astype(BF)
-        at[TYPES + half : rows, here] = (pair_two * keep).astype(BF)
-        which = jnp.where(begins, 2, jnp.where(one == two, 0, 1))
-        at[rows:FEATS, here] = (iota((FEATS - rows, BLOCK), 0) == which).astype(F32).astype(BF)
+        which = jnp.where(begins, 23, jnp.where(one == two, 7, 15))
+        pair = (jnp.concatenate([pair_one, pair_two], 0) * keep).astype(BF)
+        spot = iota((FEATS, BLOCK), 0)
+        at[:, here] = (((spot == kind) | (spot == which)).astype(F32) + dot(place, pair)).astype(BF)
         picks = at[:, here]
         resid = dot(picks, high[...], TN) + dot(picks, low[...], TN)
         hat, inverse = norm_parts(resid)
@@ -387,13 +393,13 @@
     first = jnp.where(group == 0, 1.0, 0.0)
     row_graph = norm_back(grad_row, hat_start, inverse_start, gain) + first * grad_start
     r = iota(extras.shape, 0)
-    extra = jnp.where(r == 2, row_graph, 0.0)
-    extra = jnp.where(r == 3, grad_row * hat_start, extra)
-    extra = jnp.where(r == 4, grad_row, extra)
-    extra = jnp.where(r == 5, first * grad_gain, extra)
-    extra = jnp.where(r == 6, first * grad_shift, extra)
-    for i in range(4):
-        extra = jnp.where(r == 7 + i, first * head_rows[i : i + 1, :], extra)
+    extra = jnp.where(r == 0, grad_row * hat_start, 0.0)
+    extra = jnp.where(r == 1, grad_row, extra)
+    extra = jnp.where(r == 2, first * grad_gain, extra)
+    extra = jnp.where(r == 3, first * grad_shift, extra)
+    extra = jnp.where(r == 8, row_graph, extra)
+    for i, o in enumerate((4, 5, 9, 10)):
+        extra = jnp.where(r == o, first * head_rows[i : i + 1, :], extra)
     extras[...] = extra
 
 
@@ -417,11 +423,16 @@
         return 0
 
     lax.fori_loop(0, (filled + BLOCK - 1) // BLOCK, one_block, 0)
-    base = FEATS - extras.shape[0]
     r = iota(extras.shape, 0)
-    extra = extras[...] + jnp.where(r == 3, jnp.sum(gains[0:8, :], 0, keepdims=True), 0.0)
-    extra += jnp.where(r == 4, jnp.sum(gains[8:16, :], 0, keepdims=True), 0.0)
-    total[base:FEATS, :] += extra
+    extra = extras[...] + jnp.where(r == 0, jnp.sum(gains[0:8, :], 0, keepdims=True), 0.0)
+    extra += jnp.where(r == 1, jnp.sum(gains[8:16, :], 0, keepdims=True), 0.0)
+    for i in range(3):
+        extra += jnp.where(r == 6 + i, total[8 * i + 7 : 8 * i + 8, :], 0.0)
+    half = width // 2
+    nothing = jnp.zeros((1, half), F32)
+    for d in range(FEATS // 8):
+        row = extra[d // 2 : d // 2 + 1, d % 2 * half : (d % 2 + 1) * half] if d < 22 else nothing
+        total[8 * d + 7 : 8 * d + 8, :] = jnp.concatenate([row, nothing], 1)
     group = lax.axis_index("mp")
     each = FEATS // nmp
     for k in range(nmp):
@@ -490,27 +501,39 @@
     pair[1 - odd] = came[last]
 
 
-def ffn_z_kernel(keep, came, far_keep, far_send):
+def ffn_z_kernel(keep, came, pair, far_keep, far_send):
     side = lax.axis_index("dp") >> 2
-    for out, h in ((far_keep, side), (far_send, 1 - side)):
-        out[...] = (keep[h].astype(F32) + came[h].astype(F32)).astype(BF)
+    each = far_send.shape[1]
+    for i in range(2):
+        rows = slice(i * each, (i + 1) * each)
+        far_keep[i] = (keep[side, rows].astype(F32) + came[side, rows].astype(F32)).astype(BF)
+        far_send[i] = (keep[1 - side, rows].astype(F32) + came[1 - side, rows].astype(F32)).astype(BF)
+        far_send[2 + i] = pair[i]
 
 
 def sum_squares(value):
     return jnp.sum(jnp.sum(value * value, 0, keepdims=True), 1, keepdims=True)
 
 
-def rows_kernel(*refs):
-    pieces, out = refs[:-1], refs[-1]
+def rows_kernel(npiece, nkept, *refs):
+    pieces, sources, out, kept = refs[:npiece], refs[npiece : npiece + nkept], refs[npiece + nkept], refs[npiece + nkept + 1 : -1]
+    sems = refs[-1]
+    copies = [pltpu.make_async_copy(a, b, sems.at[i]) for i, (a, b) in enumerate(zip(sources, kept))]
+    for copy in copies:
+        copy.start()
     mine = lax.axis_index("dp") >> 1
-    slot = out.shape[0] // (2 * len(pieces))
-    for k, piece in enumerate(pieces):
+    if npiece == 1:
+        out[...] = pieces[0][...]
+    for k in range(4 if npiece == 2 else 0):
         for x in range(2):
-            rows = piece[x].astype(F32)
+            rows = pieces[k & 1][(k & 2) + x].astype(F32)
             mols = rows.shape[0] // 2
             rows = jnp.concatenate([rows[0:mols, :], rows[mols:, :]], 1)
+            slot = out.shape[0] // 8
             rows = jnp.concatenate([rows, jnp.zeros((slot - mols, rows.shape[1]), F32)], 0).astype(BF)
             out[pl.ds(pl.multiple_of(((mine ^ k) * 2 + x) * slot, 16), slot), :] = rows
+    for copy in copies:
+        copy.wait()
 
 
 def outer_kernel(keep, came, head_grad, square):
@@ -524,10 +547,18 @@
 
 
 def owner_kernel(own, cols, scale, dp, *refs):
-    parts, ffn_parts, (query, vectors, layer, send, scalars) = refs[: dp // 2], refs[dp // 2 : -5], refs[-5:]
+    parts, ffn_parts, (query, vectors, layer, send, scalars, quad) = refs[: dp // 2], refs[dp // 2 : -6], refs[-6:]
     width = vectors.shape[1]
     summed = tree(parts)
-    ffn = tree(ffn_parts)
+    if len(ffn_parts) == 3:
+        near, far, pair = ffn_parts
+        ffn = jnp.concatenate([near[i].astype(F32) + far[i].astype(F32) for i in range(2)], 0)
+        for i in range(2):
+            quad[i] = pair[i]
+            quad[2 + i] = far[2 + i]
+    else:
+        ffn = tree(ffn_parts)
+        quad[...] = jnp.zeros(quad.shape, BF)
     deep = ffn.shape[0]
     acc, summed = summed[0:deep, :], summed[deep:, :]
     table, keys, side = summed[0:16, :], summed[16:24, 0:128], summed[24:32, :]
@@ -543,34 +574,13 @@
         layer[j] = grad
         square += sum_squares(grad)
     a, b, c = three(square)
-    lane = iota((16, 128), 1)
-    r = iota((16, 128), 0)
-    tail = jnp.where(r == 0, jnp.where(lane == 0, a, jnp.where(lane == 1, b, jnp.where(lane == 2, c, 0.0))), 0.0)
-    packet = jnp.concatenate([table, tail], 1).astype(BF)
-    for p in range(dp):
+    lane = iota((16, 384), 1)
+    tail = jnp.where(lane == 0, a, jnp.where(lane == 1, b, jnp.where(lane == 2, c, 0.0)))
+    packet = jnp.where(iota((16, 384), 0) == 15, tail, table).astype(BF)
+    for p in range(send.shape[0]):
         send[p] = packet
     loss = side[1:2, 0:1] + side[1:2, 1:2] + side[1:2, 2:3]
     scalars[...] = jnp.where(iota(scalars.shape, 1) == 0, loss, side[1:2, 3:4])
-
-
-def stats_kernel(nkept, layer, left_source, right_source, *refs):
-    sources, (left, right, shaped), kept = refs[:nkept], refs[nkept : nkept + 3], refs[nkept + 3 : 2 * nkept + 3]
-    left_roots, right_roots, sems = refs[2 * nkept + 3 :]
-    pairs = [(left_source, left_roots), (right_source, right_roots), *zip(sources, kept)]
-    copies = [pltpu.make_async_copy(a, b, sems.at[i]) for i, (a, b) in enumerate(pairs)]
-    for copy in copies:
-        copy.start()
-    for j in range(6):
-        low = layer[j].astype(BF)
-        left[j] = dot(low, low, NT)
-        right[j] = dot(low, low, TN)
-    copies[0].wait()
-    copies[1].wait()
-    for j in range(6):
-        near = dot(left_roots[j].astype(BF), layer[j].astype(BF))
-        shaped[j] = dot(near.astype(BF), right_roots[j].astype(BF))
-    for copy in copies[2:]:
-        copy.wait()
 
 
 def adam(weight, first, second, grad, rate):
@@ -582,16 +592,16 @@
     return first_new, second_new, weight - rate * (update + WEIGHT_DECAY * weight)
 
 
-def update_kernel(nmp, owners, cols, *refs):
-    packets = refs[:nmp]
+def update_kernel(nmp, cols, *refs):
+    arrived, refs = refs[:nmp], refs[nmp:]
     (
-        head_square, scalars, layer, left_add, right_add, shaped, weights, left, right,
+        head_square, scalars, layer, left_roots, right_roots, weights, left, right,
         tables, tables_m, tables_v, head, head_m, head_v, head_grad, vectors, vectors_m, vectors_v,
-    ) = refs[nmp : nmp + 19]
-    loss_out, count_out, norm_out = refs[nmp + 19 : nmp + 22]
-    outs = refs[nmp + 22 : nmp + 35]
-    held = refs[nmp + 35 : nmp + 48]
-    grads, sems = refs[nmp + 48 :]
+    ) = refs[:18]
+    loss_out, count_out, norm_out = refs[18:21]
+    outs = refs[21:34]
+    held = refs[34:47]
+    grads, vector_grads, packets, sems = refs[47:]
     layer_out, weights_out, left_out, right_out, tm_out, tv_out, t_out, hm_out, hv_out, h_out, vm_out, vv_out, v_out = held
     started = []
 
@@ -603,16 +613,14 @@
         copy.start()
         started.append(copy)
 
-    parts = []
-    for packet in packets:
-        s = jnp.zeros((1, 1), F32)
-        for p in range(packet.shape[0]):
-            tail = packet[p, :, 384:512].astype(F32)
-            s += tail[0:1, 0:1] + tail[0:1, 1:2] + tail[0:1, 2:3]
-        parts.append(s)
-    while len(parts) > 1:
-        parts = [parts[i] + parts[i + 1] for i in range(0, len(parts), 2)]
-    square = parts[0] + head_square[0:1, 0:1]
+    group = lax.axis_index("mp")
+    for k in range(nmp):
+        packets[group ^ k] = arrived[k][...]
+    tails = jnp.zeros((16, 128), F32)
+    for m in range(nmp):
+        for p in range(packets.shape[1]):
+            tails += packets[m, p, :, 0:128].astype(F32)
+    square = head_square[0:1, 0:1] + tails[15:16, 0:1] + tails[15:16, 1:2] + tails[15:16, 2:3]
     loss, count = scalars[0:1, 0:1], scalars[0:1, 1:2]
     norm = jnp.sqrt(square) / count
     factor = CLIP / jnp.maximum(norm, CLIP) / count
@@ -635,25 +643,29 @@
         for k in (7, 8, 9):
             send(k, pl.ds(i * each, each))
     scale = (1.0 - STATS_DECAY) * factor * factor
-    right_out[...] = STATS_DECAY * right[...] + scale[None] * right_add[...]
+    for j in range(6):
+        low = layer[j].astype(BF)
+        right_out[j] = STATS_DECAY * right[j] + scale * dot(low, low, TN)
+        left_out[j] = STATS_DECAY * left[j] + scale * dot(low, low, NT)
     send(3)
-    left_out[...] = STATS_DECAY * left[...] + scale[None] * left_add[...]
     send(2)
     for j in range(6):
         span = slice(j * cols, (j + 1) * cols)
+        low = layer[j].astype(BF)
+        shaped = dot(dot(left_roots[j].astype(BF), low).astype(BF), right_roots[j].astype(BF))
         layer_out[:, span] = layer[j] * factor
-        weights_out[:, span] = weights[:, span] - RATE_LAYER * (shaped[j] * factor + WEIGHT_DECAY * weights[:, span])
+        weights_out[:, span] = weights[:, span] - RATE_LAYER * (shaped * factor + WEIGHT_DECAY * weights[:, span])
     send(0)
     send(1)
-    group = lax.axis_index("mp")
-    share = FEATS // nmp
-    half = 384
-    for k in range(nmp):
-        start = pl.multiple_of((group ^ k) * share, 8)
-        for p in range(owners):
-            piece = packets[k][p, :, 0:half].astype(F32)
-            piece = jnp.concatenate([piece[0:8, :], piece[8:16, :]], 1) * factor
-            grads[pl.ds(pl.multiple_of(start + p * 8, 8), 8), :] = piece
+    half = grads.shape[1] // 2
+    high = FEATS // 8 // nmp
+    for m in range(nmp):
+        for p in range(high):
+            piece = packets[m, p].astype(F32) * factor
+            d = m * high + p
+            grads[7 * d : 7 * d + 7, :] = jnp.concatenate([piece[0:7, :], piece[8:15, :]], 1)
+            if d < 22:
+                vector_grads[d // 2 : d // 2 + 1, d % 2 * half : (d % 2 + 1) * half] = piece[7:8, :]
     rows = tables.shape[0]
 
     def table_rows(t, unused):
@@ -664,13 +676,8 @@
     lax.fori_loop(0, rows // 8, table_rows, 0, unroll=4)
     for k in (4, 5, 6):
         send(k)
-    order = (3, 4, 5, 6, 7, 8, 0, 1, 2, 9, 10)
-    r = iota((16, vectors.shape[1]), 0)
-    tail = jnp.zeros(r.shape, F32)
-    for i, o in enumerate(order):
-        tail = jnp.where(r == i, grads[rows + o : rows + o + 1, :], tail)
     nrows = vectors.shape[0]
-    vm_out[...], vv_out[...], v_out[...] = adam(vectors[...], vectors_m[...], vectors_v[...], tail[0:nrows, :], RATE_VECTORS)
+    vm_out[...], vv_out[...], v_out[...] = adam(vectors[...], vectors_m[...], vectors_v[...], vector_grads[0:nrows, :], RATE_VECTORS)
     for k in (10, 11, 12):
         send(k)
     for copy in started:
@@ -802,6 +809,7 @@
         return [sds((high * number + more, own // number, lanes), BF)] * 2 if nlayer == 2 else [sds((width, lanes), BF)]
 
     number = 2 if direct else 1
+    parts = exchange(part, "mp")
     *ffn_parts, comb = call(
         functools.partial(ffn_grad_kernel, nlayer, high),
         half_shapes(384, number, number - 1) + [sds((256, width), BF)],
@@ -811,22 +819,11 @@
     )
     ffn_keep, ffn_send = halves(ffn_parts)
     ffn_came = flip(ffn_send, 1)
-    if direct:
-        near_keep, near_send, pair = call(
-            ffn_x_kernel,
-            [sds((2, own, 384), BF)] * 2 + [sds((2, 2 * mols, width // 2), BF)],
-            [ffn_keep, ffn_came],
-        )
-        far_keep, far_send = call(ffn_z_kernel, [sds((own, 384), BF)] * 2, [near_keep, flip(near_send, 2)])
-        ffn_parts = [far_keep, flip(far_send, 4)]
-    else:
-        ffn_parts = call(ffn_all_kernel, [sds((deep, 384), BF)] * high, [ffn_keep, ffn_came])
-        ffn_parts = [ffn_parts[0]] + [flip(ffn_parts[k], 2 * k) for k in range(1, high)]
     *layer_halves, side, key_rows, sides, extras = call(
         functools.partial(attn_back_kernel, nmp, nlayer, high, mols, heads, scale),
         half_shapes(384)
-        + [sds((8, 256), F32), sds((8, width), F32), sds((256, length), BF), sds((FEATS - TYPES - 32, width), F32)],
-        [*exchange(part, "mp"), resid_one, grad_two, head_rows, vectors, probs, values, normed, w1, ctx],
+        + [sds((8, 256), F32), sds((8, width), F32), sds((256, length), BF), sds((16, width), F32)],
+        [*parts, resid_one, grad_two, head_rows, vectors, probs, values, normed, w1, ctx],
         [pltpu.VMEM((width, 384), BF)],
         flops=4 * length * 256 * width,
     )
@@ -846,54 +843,71 @@
         [*moved, side, key_rows],
         [pltpu.VMEM((FEATS // nmp, width), F32), pltpu.VMEM((dp, 8, 384), F32)],
     )
+    (ffn_came,) = after([ffn_came], shares[0])
+    if direct:
+        near_keep, near_send, pair = call(
+            ffn_x_kernel,
+            [sds((2, own, 384), BF)] * 2 + [sds((2, 2 * mols, width // 2), BF)],
+            [ffn_keep, ffn_came],
+        )
+        far_keep, far_send = call(
+            ffn_z_kernel,
+            [sds((2, own // 2, 384), BF), sds((4, own // 2, 384), BF)],
+            [near_keep, flip(near_send, 2), pair],
+        )
+        ffn_parts = [far_keep, flip(far_send, 4), pair]
+    else:
+        ffn_parts = call(ffn_all_kernel, [sds((deep, 384), BF)] * high, [ffn_keep, ffn_came])
+        ffn_parts = [ffn_parts[0]] + [flip(ffn_parts[k], 2 * k) for k in range(1, high)]
     merged = call(
         merge_kernel,
         [sds((deep + 32, 384), BF)] * high,
         [layer_keep, layer_came, table_keep, flip(table_send, 1)],
     )
     merged = [merged[0]] + [flip(merged[k], 2 * k) for k in range(1, high)]
-    if direct:
-        two, four = flip(pair, 2), flip(pair, 4)
-        merged = after(merged, two, four)
-    layer, send, scalars = call(
+    layer, send, scalars, quad = call(
         functools.partial(owner_kernel, own, cols, scale, dp),
-        [sds((6, own, cols), F32), sds((dp, 16, 512), BF), sds((8, 128), F32)],
+        [sds((6, own, cols), F32), sds((dp, 16, 384), BF), sds((8, 128), F32), sds((4, 2 * mols, 384), BF)],
         [*merged, *ffn_parts, query, vectors],
         flops=2 * own * 256 * 1024,
     )
+    swap = [(i, i ^ 1) for i in range(nmp)]
+    kept = [
+        jnp.swapaxes(left_roots, 0, 1), right_roots[0], layer_weights, jnp.swapaxes(left_stats, 0, 1), right_stats[0],
+        tables, tables_m, tables_v, head_weight, head_m, head_v, vectors, vectors_m, vectors_v,
+    ]
     sums = lax.all_to_all(send, "dp", 0, 0, tiled=True)
-    swap = [(i, i ^ 1) for i in range(nmp)]
     if direct:
-        (later,) = after([four], scalars)
-        (six,) = after([flip(later, 2)], sums)
-        (mine,) = call(rows_kernel, [sds((dp * 32, width), BF)], [pair, two, four, six])
-        other = lax.ppermute(mine, "mp", swap)
+        (came,) = after([flip(quad, 2)], sums)
+        pieces = [quad, came]
     else:
         packs = lax.all_gather(pack, "dp", axis=0)
         packs = jnp.pad(packs, ((0, 0), (0, 32 - mols), (0, 0))).reshape(dp * 32, -1)
         first = (lax.axis_index("mp") & 1) == 0
-        mine = jnp.where(first, packs[:, :width], packs[:, width:])
-        other = jnp.where(first, packs[:, width:], packs[:, :width])
+        pieces = [jnp.where(first, packs[:, :width], packs[:, width:])]
+    (mine,) = call(
+        functools.partial(rows_kernel, len(pieces), 0),
+        [sds((dp * 32, width), BF)],
+        [*pieces],
+        [pltpu.SemaphoreType.DMA((1,))],
+        vmem=8,
+    )
     sums = exchange(sums, "mp")
+    token, *kept = call(
+        functools.partial(rows_kernel, 1, len(kept)),
+        [sds(scalars.shape, F32)] + [pltpu.VMEM(x.shape, F32) for x in kept],
+        [scalars, *[in_hbm(x) for x in kept]],
+        [pltpu.SemaphoreType.DMA((len(kept),))],
+        in_specs=[IN_VMEM] + [IN_PLACE] * len(kept),
+        vmem=2,
+    )
+    other = lax.ppermute(mine, "mp", swap)
     head_grad, head_square = call(
         outer_kernel,
         [sds((width, width), F32), sds((8, 128), F32)],
         [mine, other],
         flops=2 * dp * mols * width * width,
         vmem=16 + dp // 4,
-    )
-    left_roots, right_roots = jnp.swapaxes(left_roots, 0, 1), right_roots[0]
-    kept = [
-        layer_weights, jnp.swapaxes(left_stats, 0, 1), right_stats[0],
-        tables, tables_m, tables_v, head_weight, head_m, head_v, vectors, vectors_m, vectors_v,
-    ]
-    left_add, right_add, shaped, *kept = call(
-        functools.partial(stats_kernel, len(kept)),
-        [sds((6, own, own), F32), sds((6, cols, cols), F32), sds((6, own, cols), F32)] + [pltpu.VMEM(x.shape, F32) for x in kept],
-        [layer, *[in_hbm(x) for x in (left_roots, right_roots, *kept)]],
-        [pltpu.VMEM(left_roots.shape, F32), pltpu.VMEM(right_roots.shape, F32), pltpu.SemaphoreType.DMA((14,))],
-        flops=12 * 6 * own * cols * (2 * own + 2 * cols),
-        in_specs=[IN_VMEM] + [IN_PLACE] * 14,
     )
     kept = [in_vmem(x) for x in kept]
     results = [
@@ -906,12 +920,12 @@
         *[sds(vectors.shape, F32)] * 3,
     ]
     outs = call(
-        functools.partial(update_kernel, nmp, owners, cols),
+        functools.partial(update_kernel, nmp, cols),
         [sds((1, 1), F32)] * 3 + results,
         [
-            *sums, head_square, scalars, layer, left_add, right_add, shaped, *kept[:9], head_grad, *kept[9:],
+            *sums, head_square, token, layer, *kept[:11], head_grad, *kept[11:],
         ],
-        [pltpu.VMEM(x.shape, x.dtype) for x in results] + [pltpu.VMEM((FEATS, width), F32), pltpu.SemaphoreType.DMA((34,))],
+        [pltpu.VMEM(x.shape, x.dtype) for x in results] + [pltpu.VMEM((FEATS, width), F32), pltpu.VMEM((16, width), F32), pltpu.VMEM((nmp, dp, 16, 384), BF), pltpu.SemaphoreType.DMA((34,))],
         flops=20 * width * width,
         vmem=24,
         out_specs=[IN_VMEM] * 3 + [IN_PLACE] * 13,

time: 111 us -> 109 us (0.982)
  waiting for transfers between devices: 46.3 us -> 44 us
    ppermute x18 -> x16, starting transfers between devices: 24.8 us -> 22.8 us  [flip(): return lax.ppermute(x, 'dp', [(i, i ^ k) for i in range(n)])]
    all_to_all x1, waiting for transfers between devices: 2.39 us -> 0.51 us  [per_device(): sums = lax.all_to_all(send, 'dp', 0, 0, tiled=True)]
    all_to_all x1, starting transfers between devices: 3.55 us -> 4.99 us  [per_device(): sums = lax.all_to_all(send, 'dp', 0, 0, tiled=True)]
    ppermute x18 -> x16, waiting for transfers between devices: 30.3 us -> 30.8 us  [flip(): return lax.ppermute(x, 'dp', [(i, i ^ k) for i in range(n)])]
  transfers between devices with their start and end apart: 35 -> 33, of which waited for: 21 -> 20; matrix products, arithmetic and copies ran while one was open for 0% -> 0% of each run, Pallas kernels for 11% -> 11%
where the time goes in v4:
time: 109 us
  waiting for transfers between devices  44 us (40%)
  starting transfers between devices  37.7 us (35%)
  Pallas kernels  24.8 us (23%)
    ppermute x16, waiting for transfers between devices, flip(): return lax.ppermute(x, 'dp', [(i, i ^ k) for i in range(n)])  30.8 us
    pallas_call x16, Pallas kernels, call(): pl.pallas_call(kernel, out_shape=tuple(outs), in_specs=in_specs or [IN_VM...  24.8 us
    ppermute x16, starting transfers between devices, flip(): return lax.ppermute(x, 'dp', [(i, i ^ k) for i in range(n)])  22.8 us
    ppermute x12, waiting for transfers between devices, exchange(): lax.ppermute(x, axis, [(i, i ^ k) for i in range(n)])  8.14 us
    ppermute x12, starting transfers between devices, exchange(): lax.ppermute(x, axis, [(i, i ^ k) for i in range(n)])  7.85 us
    all_to_all x1, starting transfers between devices, per_device(): sums = lax.all_to_all(send, 'dp', 0, 0, tiled=True)  4.99 us
    ppermute x3, waiting for transfers between devices, per_device(): lax.ppermute(shares[k], 'mp', [(i, i ^ k) for i in range(nmp)])  4.51 us
  transfers between devices with their start and end apart: 33, of which 20 were waited for; matrix products, arithmetic and copies ran while one was open for 0% of the time, Pallas kernels for 11%

profile of v4, /device:TPU:0, one launch (start us, length us, event | category | flops | bytes accessed | tf_op | source)
XLA Modules:
  0.0 108.5 jit_solution(1468794462176446838)
XLA Ops:
  0.7 1.1 convert_element_type.3.refs_3_
  1.7 3.1 %collective-permute-start.2 = (bf16[96,1152]{1,0:T(8,128)(2,1)S(1)}, bf16[96,1152]{1,0:T(8,128)(2,1)S(1)}, u32[]{:S(2)}, u32[]{:S(2)}) collective-permute-start(bf16[96,1152]{1,0:T(8,128)(2,1)S(1)} %convert_element_type.3.refs_3_), channel_id=1, source_target_pairs={{0,8},{4,12},{8,0},{12,4},{16,24},{20,28},{24,16},{28,20},{1,9},{5... | collective-permute-start | bytes 663560 | tf_op jit(solution)/shard_map/ppermute | solution.py:694
  4.8 1.5 %collective-permute-start.1 = (bf16[96,1152]{1,0:T(8,128)(2,1)S(1)}, bf16[96,1152]{1,0:T(8,128)(2,1)S(1)}, u32[]{:S(2)}, u32[]{:S(2)}) collective-permute-start(bf16[96,1152]{1,0:T(8,128)(2,1)S(1)} %convert_element_type.3.refs_3_), channel_id=1, source_target_pairs={{0,4},{4,0},{8,12},{12,8},{16,20},{20,16},{24,28},{28,24},{1,5},{5... | collective-permute-start | bytes 663560 | tf_op jit(solution)/shard_map/ppermute | solution.py:694
  6.3 2.6 %collective-permute-start = (bf16[96,1152]{1,0:T(8,128)(2,1)S(1)}, bf16[96,1152]{1,0:T(8,128)(2,1)S(1)}, u32[]{:S(2)}, u32[]{:S(2)}) collective-permute-start(bf16[96,1152]{1,0:T(8,128)(2,1)S(1)} %convert_element_type.3.refs_3_), channel_id=1, source_target_pairs={{0,16},{4,20},{8,24},{12,28},{16,0},{20,4},{24,8},{28,12},{1,17},{... | collective-permute-start | bytes 663560 | tf_op jit(solution)/shard_map/ppermute | solution.py:694
  8.9 2.6 %shard_map.306 = (bf16[256,1024]{1,0:T(8,128)(2,1)S(1)}, bf16[1024,768]{1,0:T(8,128)(2,1)S(1)}, bf16[1024,768]{1,0:T(8,128)(2,1)S(1)}, f32[1024,128]{1,0:T(8,128)S(1)}) custom-call(f32[16,1024]{1,0:T(8,128)} %bitcast.21, s32[2,1024]{1,0:T(2,128)} %bitcast.22, s32[1,1024]{1,0:T(1,128)} %refs_2_.2, s32[1,1024]{1,0:T(1,128)} %refs_7_.6, f32[224,768]{1,0:T(8,128)} %refs_6_.3, ...), custom_call_target="tpu_custom_call" | custom-call | flops 805306368 | bytes 4998144 | tf_op jit(solution)/shard_map/pallas_call | solution.py:55
  11.5 2.0 %collective-permute-done.2.refs_5_ = bf16[96,1152]{1,0:T(8,128)(2,1)S(1)} collective-permute-done((bf16[96,1152]{1,0:T(8,128)(2,1)S(1)}, bf16[96,1152]{1,0:T(8,128)(2,1)S(1)}, u32[]{:S(2)}, u32[]{:S(2)}) %collective-permute-start.2) | collective-permute-done | bytes 221216 | tf_op jit(solution)/shard_map/ppermute | solution.py:694
  13.5 5.1 %collective-permute-done.refs_7_ = bf16[96,1152]{1,0:T(8,128)(2,1)S(1)} collective-permute-done((bf16[96,1152]{1,0:T(8,128)(2,1)S(1)}, bf16[96,1152]{1,0:T(8,128)(2,1)S(1)}, u32[]{:S(2)}, u32[]{:S(2)}) %collective-permute-start) | collective-permute-done | bytes 221216 | tf_op jit(solution)/shard_map/ppermute | solution.py:694
  18.6 3.3 %collective-permute-start.6 = (bf16[96,1152]{1,0:T(8,128)(2,1)S(1)}, bf16[96,1152]{1,0:T(8,128)(2,1)S(1)}, u32[]{:S(2)}, u32[]{:S(2)}) collective-permute-start(bf16[96,1152]{1,0:T(8,128)(2,1)S(1)} %collective-permute-done.1.refs_4_), channel_id=1, source_target_pairs={{0,24},{4,28},{8,16},{12,20},{16,8},{20,12},{24,0},{28,4},{1,25},{... | collective-permute-start | bytes 663560 | tf_op jit(solution)/shard_map/ppermute | solution.py:694
  21.9 2.0 %collective-permute-start.4 = (bf16[96,1152]{1,0:T(8,128)(2,1)S(1)}, bf16[96,1152]{1,0:T(8,128)(2,1)S(1)}, u32[]{:S(2)}, u32[]{:S(2)}) collective-permute-start(bf16[96,1152]{1,0:T(8,128)(2,1)S(1)} %collective-permute-done.refs_7_), channel_id=1, source_target_pairs={{0,4},{4,0},{8,12},{12,8},{16,20},{20,16},{24,28},{28,24},{1,5},{5... | collective-permute-start | bytes 663560 | tf_op jit(solution)/shard_map/ppermute | solution.py:694
  23.9 4.0 %collective-permute-done.6.refs_10_ = bf16[96,1152]{1,0:T(8,128)(2,1)S(1)} collective-permute-done((bf16[96,1152]{1,0:T(8,128)(2,1)S(1)}, bf16[96,1152]{1,0:T(8,128)(2,1)S(1)}, u32[]{:S(2)}, u32[]{:S(2)}) %collective-permute-start.6) | collective-permute-done | bytes 221216 | tf_op jit(solution)/shard_map/ppermute | solution.py:694
  27.9 1.3 %collective-permute-done.3.refs_6_ = bf16[96,1152]{1,0:T(8,128)(2,1)S(1)} collective-permute-done((bf16[96,1152]{1,0:T(8,128)(2,1)S(1)}, bf16[96,1152]{1,0:T(8,128)(2,1)S(1)}, u32[]{:S(2)}, u32[]{:S(2)}) %collective-permute-start.3) | collective-permute-done | bytes 221216 | tf_op jit(solution)/shard_map/ppermute | solution.py:694
  29.2 1.0 collective-permute-done.5.refs_9_
  30.2 1.4 %collective-permute-done.4.refs_8_ = bf16[96,1152]{1,0:T(8,128)(2,1)S(1)} collective-permute-done((bf16[96,1152]{1,0:T(8,128)(2,1)S(1)}, bf16[96,1152]{1,0:T(8,128)(2,1)S(1)}, u32[]{:S(2)}, u32[]{:S(2)}) %collective-permute-start.4) | collective-permute-done | bytes 221216 | tf_op jit(solution)/shard_map/ppermute | solution.py:694
  31.6 2.5 %shard_map.307 = (bf16[24,768]{1,0:T(8,128)(2,1)S(1)}, bf16[192,1024]{1,0:T(8,128)(2,1)S(1)}, bf16[1024,256]{1,0:T(8,128)(2,1)S(1)}, bf16[24,256]{1,0:T(8,128)(2...) custom-call(bf16[1024,768]{1,0:T(8,128)(2,1)S(1)} %get-tuple-element, ...), custom_call_target="tpu_custom_call" | custom-call | flops 805306368 | bytes 6517760 | tf_op jit(solution)/shard_map/pallas_call | solution.py:55
  34.1 0.1 collective-permute-start.9
  34.2 1.6 %collective-permute-start.8 = (bf16[24,768]{1,0:T(8,128)(2,1)S(1)}, bf16[24,768]{1,0:T(8,128)(2,1)S(1)}, u32[]{:S(2)}, u32[]{:S(2)}) collective-permute-start(bf16[24,768]{1,0:T(8,128)(2,1)S(1)} %get-tuple-element.109.refs_0_), channel_id=1, source_target_pairs={{0,2},{1,3},{2,0},{3,1},{4,6},{5,7},{6,4},{7,5},{8,10},{9,11},{10,... | collective-permute-start | bytes 110600 | tf_op jit(solution)/shard_map/ppermute | solution.py:689
  35.8 0.3 collective-permute-start.7
  36.0 1.8 %collective-permute-done.9.refs_3_ = bf16[24,768]{1,0:T(8,128)(2,1)S(1)} collective-permute-done((bf16[24,768]{1,0:T(8,128)(2,1)S(1)}, bf16[24,768]{1,0:T(8,128)(2,1)S(1)}, u32[]{:S(2)}, u32[]{:S(2)}) %collective-permute-start.9) | collective-permute-done | bytes 36896 | tf_op jit(solution)/shard_map/ppermute | solution.py:689
  37.9 0.5 collective-permute-done.8.refs_2_
  38.4 0.6 shard_map.308
  39.0 1.1 collective-permute-start.12
  40.0 0.9 collective-permute-start.11
  40.9 1.5 %collective-permute-done.12.refs_3_ = bf16[24,768]{1,0:T(8,128)(2,1)S(1)} collective-permute-done((bf16[24,768]{1,0:T(8,128)(2,1)S(1)}, bf16[24,768]{1,0:T(8,128)(2,1)S(1)}, u32[]{:S(2)}, u32[]{:S(2)}) %collective-permute-start.12) | collective-permute-done | bytes 36896 | tf_op jit(solution)/shard_map/ppermute | solution.py:689
  42.4 1.6 %collective-permute-done.11.refs_2_ = bf16[24,768]{1,0:T(8,128)(2,1)S(1)} collective-permute-done((bf16[24,768]{1,0:T(8,128)(2,1)S(1)}, bf16[24,768]{1,0:T(8,128)(2,1)S(1)}, u32[]{:S(2)}, u32[]{:S(2)}) %collective-permute-start.11) | collective-permute-done | bytes 36896 | tf_op jit(solution)/shard_map/ppermute | solution.py:689
  44.0 1.6 %shard_map.309 = (bf16[24,768]{1,0:T(8,128)(2,1)S(1)}, bf16[24,1536]{1,0:T(8,128)(2,1)S(1)}, f32[24,768]{1,0:T(8,128)S(1)}, bf16[24,768]{1,0:T(8,128)(2,1)S(1)},...) custom-call(bf16[24,768]{1,0:T(8,128)(2,1)S(1)} %get-tuple-element.111.refs_0_, ...), custom_call_target="tpu_custom_call" | custom-call | flops 56623104 | bytes 3490912 | tf_op jit(solution)/shard_map/pallas_call | solution.py:55
  45.6 0.6 shard_map.311
  46.3 0.4 collective-permute-start.24
  46.6 0.4 collective-permute-start.15
  47.1 0.8 collective-permute-start.14
  47.9 0.6 collective-permute-start.13
  48.5 1.7 %collective-permute-done.15.refs_3_ = bf16[24,768]{1,0:T(8,128)(2,1)S(1)} collective-permute-done((bf16[24,768]{1,0:T(8,128)(2,1)S(1)}, bf16[24,768]{1,0:T(8,128)(2,1)S(1)}, u32[]{:S(2)}, u32[]{:S(2)}) %collective-permute-start.15) | collective-permute-done | bytes 36896 | tf_op jit(solution)/shard_map/ppermute | solution.py:689
  50.2 1.0 collective-permute-done.14.refs_2_
  51.2 2.3 %shard_map.310 = (bf16[4,96,384]{2,1,0:T(8,128)(2,1)S(1)}, bf16[4,96,384]{2,1,0:T(8,128)(2,1)S(1)}, f32[8,256]{1,0:T(8,128)S(1)}, f32[8,768]{1,0:T(8,128)S(1)}, ...) custom-call(bf16[24,768]{1,0:T(8,128)(2,1)S(1)} %get-tuple-element.114.refs_0_, ...), custom_call_target="tpu_custom_call" | custom-call | flops 805306368 | bytes 5231616 | tf_op jit(solution)/shard_map/pallas_call | solution.py:55
  53.5 1.8 %collective-permute-start.16 = (bf16[4,96,384]{2,1,0:T(8,128)(2,1)S(1)}, bf16[4,96,384]{2,1,0:T(8,128)(2,1)S(1)}, u32[]{:S(2)}, u32[]{:S(2)}) collective-permute-start(bf16[4,96,384]{2,1,0:T(8,128)(2,1)S(1)} %get-tuple-element.122), channel_id=1, source_target_pairs={{0,4},{4,0},{8,12},{12,8},{16,20},{20,16},{24,28},{28,24},{1,5},{5... | collective-permute-start | bytes 884744 | tf_op jit(solution)/shard_map/ppermute | solution.py:694
  55.3 1.1 %shard_map.312 = (bf16[64,768]{1,0:T(8,128)(2,1)S(1)}, bf16[64,768]{1,0:T(8,128)(2,1)S(1)}, bf16[64,768]{1,0:T(8,128)(2,1)S(1)}, bf16[64,768]{1,0:T(8,128)(2,1)S(1)}) custom-call(bf16[256,1024]{1,0:T(8,128)(2,1)S(1)} %get-tuple-element.123.refs_0_, bf16[256,768]{1,0:T(8,128)(2,1)S(1)} %get-tuple-element.130.refs_1_, ...), custom_call_target="tpu_custom_call" | custom-call | flops 805306368 | bytes 4019200 | tf_op jit(solution)/shard_map/pallas_call | solution.py:55
  56.4 0.1 collective-permute-start.17
  56.5 1.0 collective-permute-start.18
  57.5 0.8 collective-permute-start.19
  58.4 0.1 shard_map.315
  58.4 0.4 collective-permute-start.25
  58.8 3.3 %collective-permute-done.18.refs_2_ = bf16[64,768]{1,0:T(8,128)(2,1)S(1)} collective-permute-done((bf16[64,768]{1,0:T(8,128)(2,1)S(1)}, bf16[64,768]{1,0:T(8,128)(2,1)S(1)}, u32[]{:S(2)}, u32[]{:S(2)}) %collective-permute-start.18) | collective-permute-done | bytes 98336 | tf_op jit(solution)/shard_map/ppermute | solution.py:839
  62.1 1.2 %collective-permute-done.19.refs_3_ = bf16[64,768]{1,0:T(8,128)(2,1)S(1)} collective-permute-done((bf16[64,768]{1,0:T(8,128)(2,1)S(1)}, bf16[64,768]{1,0:T(8,128)(2,1)S(1)}, u32[]{:S(2)}, u32[]{:S(2)}) %collective-permute-start.19) | collective-permute-done | bytes 98336 | tf_op jit(solution)/shard_map/ppermute | solution.py:839
  63.4 0.1 shard_map.313
  63.5 0.3 collective-permute-start.20
  63.8 0.8 collective-permute-done.25.came
  64.7 0.9 collective-permute-start.26
  65.6 3.2 %collective-permute-done.20.table_came = bf16[4,32,384]{2,1,0:T(8,128)(2,1)S(1)} collective-permute-done((bf16[4,32,384]{2,1,0:T(8,128)(2,1)S(1)}, bf16[4,32,384]{2,1,0:T(8,128)(2,1)S(1)}, u32[]{:S(2)}, u32[]{:S(2)}) %collective-permute-start.20) | collective-permute-done | bytes 98336 | tf_op jit(solution)/shard_map/ppermute | solution.py:694
  68.8 0.2 shard_map.314
  69.0 0.4 collective-permute-start.21
  69.5 2.3 %collective-permute-start.22 = (bf16[128,384]{1,0:T(8,128)(2,1)S(1)}, bf16[128,384]{1,0:T(8,128)(2,1)S(1)}, u32[]{:S(2)}, u32[]{:S(2)}) collective-permute-start(bf16[128,384]{1,0:T(8,128)(2,1)S(1)} %get-tuple-element.145), channel_id=1, source_target_pairs={{0,16},{4,20},{8,24},{12,28},{16,0},{20,4},{24,8},{28,12},{1,17},{... | collective-permute-start | bytes 294920 | tf_op jit(solution)/shard_map/ppermute | solution.py:694
  71.7 1.8 %collective-permute-start.23 = (bf16[128,384]{1,0:T(8,128)(2,1)S(1)}, bf16[128,384]{1,0:T(8,128)(2,1)S(1)}, u32[]{:S(2)}, u32[]{:S(2)}) collective-permute-start(bf16[128,384]{1,0:T(8,128)(2,1)S(1)} %get-tuple-element.146), channel_id=1, source_target_pairs={{0,24},{4,28},{8,16},{12,20},{16,8},{20,12},{24,0},{28,4},{1,25},{... | collective-permute-start | bytes 294920 | tf_op jit(solution)/shard_map/ppermute | solution.py:694
  73.5 3.3 %collective-permute-done.21.refs_1_ = bf16[128,384]{1,0:T(8,128)(2,1)S(1)} collective-permute-done((bf16[128,384]{1,0:T(8,128)(2,1)S(1)}, bf16[128,384]{1,0:T(8,128)(2,1)S(1)}, u32[]{:S(2)}, u32[]{:S(2)}) %collective-permute-start.21) | collective-permute-done | bytes 98336 | tf_op jit(solution)/shard_map/ppermute | solution.py:694
  76.8 3.6 %collective-permute-done.22.refs_2_ = bf16[128,384]{1,0:T(8,128)(2,1)S(1)} collective-permute-done((bf16[128,384]{1,0:T(8,128)(2,1)S(1)}, bf16[128,384]{1,0:T(8,128)(2,1)S(1)}, u32[]{:S(2)}, u32[]{:S(2)}) %collective-permute-start.22) | collective-permute-done | bytes 98336 | tf_op jit(solution)/shard_map/ppermute | solution.py:694
  80.3 1.2 %shard_map.317 = (f32[6,96,192]{2,1,0:T(8,128)S(1)}, bf16[8,16,384]{2,1,0:T(8,128)(2,1)}, f32[8,128]{1,0:T(8,128)S(1)}, bf16[4,48,384]{2,1,0:T(8,128)(2,1)S(1)}) custom-call(bf16[128,384]{1,0:T(8,128)(2,1)S(1)} %get-tuple-element.143.refs_0_, bf16[128,384]{1,0:T(8,128)(2,1)S(1)} %collective-permute-done.21.refs_1_, ...), custom_call_target="tpu_custom_call" | custom-call | flops 50331648 | bytes 1422336 | tf_op jit(solution)/shard_map/pallas_call | solution.py:55
  81.5 5.0 %all-to-all-start = ((bf16[8,16,384]{2,1,0:T(8,128)(2,1)}), bf16[8,16,384]{2,1,0:T(8,128)(2,1)S(1)}, u32[]{:S(2)}, u32[]{:S(2)}) async-start(bf16[8,16,384]{2,1,0:T(8,128)(2,1)} %get-tuple-element.156), calls=%async_computation | async-start | bytes 196608 | tf_op jit(solution)/shard_map/all_to_all | solution.py:879
  86.5 2.0 %collective-permute-start.30 = (bf16[4,48,384]{2,1,0:T(8,128)(2,1)S(1)}, bf16[4,48,384]{2,1,0:T(8,128)(2,1)S(1)}, u32[]{:S(2)}, u32[]{:S(2)}) collective-permute-start(bf16[4,48,384]{2,1,0:T(8,128)(2,1)S(1)} %get-tuple-element.157.refs_0_), channel_id=1, source_target_pairs={{0,8},{4,12},{8,0},{12,4},{16,24},{20,28},{24,16},{28,20},{1,9},{5... | collective-permute-start | bytes 442376 | tf_op jit(solution)/shard_map/ppermute | solution.py:694
  88.5 5.3 %collective-permute-done.30.refs_1_ = bf16[4,48,384]{2,1,0:T(8,128)(2,1)S(1)} collective-permute-done((bf16[4,48,384]{2,1,0:T(8,128)(2,1)S(1)}, bf16[4,48,384]{2,1,0:T(8,128)(2,1)S(1)}, u32[]{:S(2)}, u32[]{:S(2)}) %collective-permute-start.30) | collective-permute-done | bytes 147488 | tf_op jit(solution)/shard_map/ppermute | solution.py:694
  93.8 0.5 all-to-all-done.refs_0_
  94.4 0.1 collective-permute-start.31
  94.4 1.1 collective-permute-start.29
  95.5 1.1 collective-permute-start.28
  96.6 4.9 %shard_map.320 = (f32[8,128]{1,0:T(8,128)S(1)}, f32[6,96,96]{2,1,0:T(8,128)S(1)}, f32[6,192,192]{2,1,0:T(8,128)S(1)}, f32[96,1152]{1,0:T(8,128)S(1)}, f32[6,96,9...) custom-call(f32[8,128]{1,0:T(8,128)S(1)} %get-tuple-element.160.refs, ...), custom_call_target="tpu_custom_call" | custom-call | bytes 23803904 | tf_op jit(solution)/shard_map/pallas_call | solution.py:55
  101.5 0.7 shard_map.319
  102.2 6.2 %shard_map.321 = (f32[1,1]{1,0:T(1,128)}, f32[1,1]{1,0:T(1,128)}, f32[1,1]{1,0:T(1,128)}, f32[96,1152]{1,0:T(8,128)}, f32[96,1152]{1,0:T(8,128)}, /*index=5*/f32...) custom-call(bf16[8,16,384]{2,1,0:T(8,128)(2,1)S(1)} %all-to-all-done, ...), custom_call_target="tpu_custom_call" | custom-call | flops 11796480 | bytes 26335244 | tf_op jit(solution)/shard_map/pallas_call | solution.py:55
  (27 shorter events, 0.2 us)
Async XLA Ops:
  0.6 30.9 %copy-start.1 = (f32[11,768]{1,0:T(8,128)S(1)}, f32[11,768]{1,0:T(8,128)}, u32[]{:S(2)}) copy-start(f32[11,768]{1,0:T(8,128)} %refs_12_.1) | copy-start | bytes 101380
  0.7 30.9 %copy-start.2 = (s32[1,1024]{1,0:T(1,128)S(1)}, s32[1,1024]{1,0:T(1,128)}, u32[]{:S(2)}) copy-start(s32[1,1024]{1,0:T(1,128)} %refs_7_.6) | copy-start | bytes 12292
  1.7 11.8 %collective-permute-start.2 = (bf16[96,1152]{1,0:T(8,128)(2,1)S(1)}, bf16[96,1152]{1,0:T(8,128)(2,1)S(1)}, u32[]{:S(2)}, u32[]{:S(2)}) collective-permute-start(bf16[96,1152]{1,0:T(8,128)(2,1)S(1)} %convert_element_type.3.refs_3_), channel_id=1, source_target_pairs={{0,8},{4,12},{8,0},{12,4},{16,24},{20,28},{24,16},{28,20},{1,9},{5... | collective-permute-start | bytes 663560 | tf_op jit(solution)/shard_map/ppermute | solution.py:694
  4.8 8.7 %collective-permute-start.1 = (bf16[96,1152]{1,0:T(8,128)(2,1)S(1)}, bf16[96,1152]{1,0:T(8,128)(2,1)S(1)}, u32[]{:S(2)}, u32[]{:S(2)}) collective-permute-start(bf16[96,1152]{1,0:T(8,128)(2,1)S(1)} %convert_element_type.3.refs_3_), channel_id=1, source_target_pairs={{0,4},{4,0},{8,12},{12,8},{16,20},{20,16},{24,28},{28,24},{1,5},{5... | collective-permute-start | bytes 663560 | tf_op jit(solution)/shard_map/ppermute | solution.py:694
  6.3 12.3 %collective-permute-start = (bf16[96,1152]{1,0:T(8,128)(2,1)S(1)}, bf16[96,1152]{1,0:T(8,128)(2,1)S(1)}, u32[]{:S(2)}, u32[]{:S(2)}) collective-permute-start(bf16[96,1152]{1,0:T(8,128)(2,1)S(1)} %convert_element_type.3.refs_3_), channel_id=1, source_target_pairs={{0,16},{4,20},{8,24},{12,28},{16,0},{20,4},{24,8},{28,12},{1,17},{... | collective-permute-start | bytes 663560 | tf_op jit(solution)/shard_map/ppermute | solution.py:694
  11.5 32.5 %copy-start = (f32[768,768]{1,0:T(8,128)S(1)}, f32[768,768]{1,0:T(8,128)}, u32[]{:S(2)}) copy-start(f32[768,768]{1,0:T(8,128)} %refs_9_.1) | copy-start | bytes 7077892
  11.5 32.5 %copy-start.3 = (f32[1,24]{1,0:T(1,128)S(1)}, f32[1,24]{1,0:T(1,128)}, u32[]{:S(2)}) copy-start(f32[1,24]{1,0:T(1,128)} %refs_7_.4) | copy-start | bytes 292
  18.6 9.3 %collective-permute-start.6 = (bf16[96,1152]{1,0:T(8,128)(2,1)S(1)}, bf16[96,1152]{1,0:T(8,128)(2,1)S(1)}, u32[]{:S(2)}, u32[]{:S(2)}) collective-permute-start(bf16[96,1152]{1,0:T(8,128)(2,1)S(1)} %collective-permute-done.1.refs_4_), channel_id=1, source_target_pairs={{0,24},{4,28},{8,16},{12,20},{16,8},{20,12},{24,0},{28,4},{1,25},{... | collective-permute-start | bytes 663560 | tf_op jit(solution)/shard_map/ppermute | solution.py:694
  21.9 7.3 %collective-permute-start.3 = (bf16[96,1152]{1,0:T(8,128)(2,1)S(1)}, bf16[96,1152]{1,0:T(8,128)(2,1)S(1)}, u32[]{:S(2)}, u32[]{:S(2)}) collective-permute-start(bf16[96,1152]{1,0:T(8,128)(2,1)S(1)} %collective-permute-done.2.refs_5_), channel_id=1, source_target_pairs={{0,4},{4,0},{8,12},{12,8},{16,20},{20,16},{24,28},{28,24},{1,5},{5... | collective-permute-start | bytes 663560 | tf_op jit(solution)/shard_map/ppermute | solution.py:694
  21.9 8.3 %collective-permute-start.5 = (bf16[96,1152]{1,0:T(8,128)(2,1)S(1)}, bf16[96,1152]{1,0:T(8,128)(2,1)S(1)}, u32[]{:S(2)}, u32[]{:S(2)}) collective-permute-start(bf16[96,1152]{1,0:T(8,128)(2,1)S(1)} %collective-permute-done.refs_7_), channel_id=1, source_target_pairs={{0,8},{4,12},{8,0},{12,4},{16,24},{20,28},{24,16},{28,20},{1,9},{5... | collective-permute-start | bytes 663560 | tf_op jit(solution)/shard_map/ppermute | solution.py:694
  21.9 9.7 %collective-permute-start.4 = (bf16[96,1152]{1,0:T(8,128)(2,1)S(1)}, bf16[96,1152]{1,0:T(8,128)(2,1)S(1)}, u32[]{:S(2)}, u32[]{:S(2)}) collective-permute-start(bf16[96,1152]{1,0:T(8,128)(2,1)S(1)} %collective-permute-done.refs_7_), channel_id=1, source_target_pairs={{0,4},{4,0},{8,12},{12,8},{16,20},{20,16},{24,28},{28,24},{1,5},{5... | collective-permute-start | bytes 663560 | tf_op jit(solution)/shard_map/ppermute | solution.py:694
  34.1 3.8 %collective-permute-start.9 = (bf16[24,768]{1,0:T(8,128)(2,1)S(1)}, bf16[24,768]{1,0:T(8,128)(2,1)S(1)}, u32[]{:S(2)}, u32[]{:S(2)}) collective-permute-start(bf16[24,768]{1,0:T(8,128)(2,1)S(1)} %get-tuple-element.109.refs_0_), channel_id=1, source_target_pairs={{0,3},{1,2},{2,1},{3,0},{4,7},{5,6},{6,5},{7,4},{8,11},{9,10},{10,... | collective-permute-start | bytes 110600 | tf_op jit(solution)/shard_map/ppermute | solution.py:689
  34.2 4.2 %collective-permute-start.8 = (bf16[24,768]{1,0:T(8,128)(2,1)S(1)}, bf16[24,768]{1,0:T(8,128)(2,1)S(1)}, u32[]{:S(2)}, u32[]{:S(2)}) collective-permute-start(bf16[24,768]{1,0:T(8,128)(2,1)S(1)} %get-tuple-element.109.refs_0_), channel_id=1, source_target_pairs={{0,2},{1,3},{2,0},{3,1},{4,6},{5,7},{6,4},{7,5},{8,10},{9,11},{10,... | collective-permute-start | bytes 110600 | tf_op jit(solution)/shard_map/ppermute | solution.py:689
  35.8 2.6 %collective-permute-start.7 = (bf16[24,768]{1,0:T(8,128)(2,1)S(1)}, bf16[24,768]{1,0:T(8,128)(2,1)S(1)}, u32[]{:S(2)}, u32[]{:S(2)}) collective-permute-start(bf16[24,768]{1,0:T(8,128)(2,1)S(1)} %get-tuple-element.109.refs_0_), channel_id=1, source_target_pairs={{0,1},{1,0},{2,3},{3,2},{4,5},{5,4},{6,7},{7,6},{8,9},{9,8},{10,11... | collective-permute-start | bytes 110600 | tf_op jit(solution)/shard_map/ppermute | solution.py:689
  39.0 3.4 %collective-permute-start.12 = (bf16[24,768]{1,0:T(8,128)(2,1)S(1)}, bf16[24,768]{1,0:T(8,128)(2,1)S(1)}, u32[]{:S(2)}, u32[]{:S(2)}) collective-permute-start(bf16[24,768]{1,0:T(8,128)(2,1)S(1)} %get-tuple-element.111.refs_0_), channel_id=1, source_target_pairs={{0,3},{1,2},{2,1},{3,0},{4,7},{5,6},{6,5},{7,4},{8,11},{9,10},{10,... | collective-permute-start | bytes 110600 | tf_op jit(solution)/shard_map/ppermute | solution.py:689
  40.0 4.0 %collective-permute-start.11 = (bf16[24,768]{1,0:T(8,128)(2,1)S(1)}, bf16[24,768]{1,0:T(8,128)(2,1)S(1)}, u32[]{:S(2)}, u32[]{:S(2)}) collective-permute-start(bf16[24,768]{1,0:T(8,128)(2,1)S(1)} %get-tuple-element.111.refs_0_), channel_id=1, source_target_pairs={{0,2},{1,3},{2,0},{3,1},{4,6},{5,7},{6,4},{7,5},{8,10},{9,11},{10,... | collective-permute-start | bytes 110600 | tf_op jit(solution)/shard_map/ppermute | solution.py:689
  40.9 3.1 %collective-permute-start.10 = (bf16[24,768]{1,0:T(8,128)(2,1)S(1)}, bf16[24,768]{1,0:T(8,128)(2,1)S(1)}, u32[]{:S(2)}, u32[]{:S(2)}) collective-permute-start(bf16[24,768]{1,0:T(8,128)(2,1)S(1)} %get-tuple-element.111.refs_0_), channel_id=1, source_target_pairs={{0,1},{1,0},{2,3},{3,2},{4,5},{5,4},{6,7},{7,6},{8,9},{9,8},{10,11... | collective-permute-start | bytes 110600 | tf_op jit(solution)/shard_map/ppermute | solution.py:689
  46.3 12.1 %collective-permute-start.24 = (bf16[9,48,384]{2,1,0:T(8,128)(2,1)S(1)}, bf16[9,48,384]{2,1,0:T(8,128)(2,1)S(1)}, u32[]{:S(2)}, u32[]{:S(2)}) collective-permute-start(bf16[9,48,384]{2,1,0:T(8,128)(2,1)S(1)} %get-tuple-element.148), channel_id=1, source_target_pairs={{0,4},{4,0},{8,12},{12,8},{16,20},{20,16},{24,28},{28,24},{1,5},{5... | collective-permute-start | bytes 995336 | tf_op jit(solution)/shard_map/ppermute | solution.py:694
  46.6 3.6 %collective-permute-start.15 = (bf16[24,768]{1,0:T(8,128)(2,1)S(1)}, bf16[24,768]{1,0:T(8,128)(2,1)S(1)}, u32[]{:S(2)}, u32[]{:S(2)}) collective-permute-start(bf16[24,768]{1,0:T(8,128)(2,1)S(1)} %get-tuple-element.114.refs_0_), channel_id=1, source_target_pairs={{0,3},{1,2},{2,1},{3,0},{4,7},{5,6},{6,5},{7,4},{8,11},{9,10},{10,... | collective-permute-start | bytes 110600 | tf_op jit(solution)/shard_map/ppermute | solution.py:689
  47.1 4.1 %collective-permute-start.14 = (bf16[24,768]{1,0:T(8,128)(2,1)S(1)}, bf16[24,768]{1,0:T(8,128)(2,1)S(1)}, u32[]{:S(2)}, u32[]{:S(2)}) collective-permute-start(bf16[24,768]{1,0:T(8,128)(2,1)S(1)} %get-tuple-element.114.refs_0_), channel_id=1, source_target_pairs={{0,2},{1,3},{2,0},{3,1},{4,6},{5,7},{6,4},{7,5},{8,10},{9,11},{10,... | collective-permute-start | bytes 110600 | tf_op jit(solution)/shard_map/ppermute | solution.py:689
  47.9 3.3 %collective-permute-start.13 = (bf16[24,768]{1,0:T(8,128)(2,1)S(1)}, bf16[24,768]{1,0:T(8,128)(2,1)S(1)}, u32[]{:S(2)}, u32[]{:S(2)}) collective-permute-start(bf16[24,768]{1,0:T(8,128)(2,1)S(1)} %get-tuple-element.114.refs_0_), channel_id=1, source_target_pairs={{0,1},{1,0},{2,3},{3,2},{4,5},{5,4},{6,7},{7,6},{8,9},{9,8},{10,11... | collective-permute-start | bytes 110600 | tf_op jit(solution)/shard_map/ppermute | solution.py:689
  53.5 15.3 %collective-permute-start.16 = (bf16[4,96,384]{2,1,0:T(8,128)(2,1)S(1)}, bf16[4,96,384]{2,1,0:T(8,128)(2,1)S(1)}, u32[]{:S(2)}, u32[]{:S(2)}) collective-permute-start(bf16[4,96,384]{2,1,0:T(8,128)(2,1)S(1)} %get-tuple-element.122), channel_id=1, source_target_pairs={{0,4},{4,0},{8,12},{12,8},{16,20},{20,16},{24,28},{28,24},{1,5},{5... | collective-permute-start | bytes 884744 | tf_op jit(solution)/shard_map/ppermute | solution.py:694
  56.4 2.4 %collective-permute-start.17 = (bf16[64,768]{1,0:T(8,128)(2,1)S(1)}, bf16[64,768]{1,0:T(8,128)(2,1)S(1)}, u32[]{:S(2)}, u32[]{:S(2)}) collective-permute-start(bf16[64,768]{1,0:T(8,128)(2,1)S(1)} %get-tuple-element.136), channel_id=1, source_target_pairs={{0,1},{1,0},{2,3},{3,2},{4,5},{5,4},{6,7},{7,6},{8,9},{9,8},{10,11... | collective-permute-start | bytes 294920 | tf_op jit(solution)/shard_map/ppermute | solution.py:839
  56.5 5.7 %collective-permute-start.18 = (bf16[64,768]{1,0:T(8,128)(2,1)S(1)}, bf16[64,768]{1,0:T(8,128)(2,1)S(1)}, u32[]{:S(2)}, u32[]{:S(2)}) collective-permute-start(bf16[64,768]{1,0:T(8,128)(2,1)S(1)} %get-tuple-element.137), channel_id=1, source_target_pairs={{0,2},{1,3},{2,0},{3,1},{4,6},{5,7},{6,4},{7,5},{8,10},{9,11},{10,... | collective-permute-start | bytes 294920 | tf_op jit(solution)/shard_map/ppermute | solution.py:839
  57.5 5.8 %collective-permute-start.19 = (bf16[64,768]{1,0:T(8,128)(2,1)S(1)}, bf16[64,768]{1,0:T(8,128)(2,1)S(1)}, u32[]{:S(2)}, u32[]{:S(2)}) collective-permute-start(bf16[64,768]{1,0:T(8,128)(2,1)S(1)} %get-tuple-element.138), channel_id=1, source_target_pairs={{0,3},{1,2},{2,1},{3,0},{4,7},{5,6},{6,5},{7,4},{8,11},{9,10},{10,... | collective-permute-start | bytes 294920 | tf_op jit(solution)/shard_map/ppermute | solution.py:839
  58.4 6.2 %collective-permute-start.25 = (bf16[2,96,384]{2,1,0:T(8,128)(2,1)S(1)}, bf16[2,96,384]{2,1,0:T(8,128)(2,1)S(1)}, u32[]{:S(2)}, u32[]{:S(2)}) collective-permute-start(bf16[2,96,384]{2,1,0:T(8,128)(2,1)S(1)} %get-tuple-element.151), channel_id=1, source_target_pairs={{0,8},{4,12},{8,0},{12,4},{16,24},{20,28},{24,16},{28,20},{1,9},{5... | collective-permute-start | bytes 442376 | tf_op jit(solution)/shard_map/ppermute | solution.py:694
  63.5 5.3 %collective-permute-start.20 = (bf16[4,32,384]{2,1,0:T(8,128)(2,1)S(1)}, bf16[4,32,384]{2,1,0:T(8,128)(2,1)S(1)}, u32[]{:S(2)}, u32[]{:S(2)}) collective-permute-start(bf16[4,32,384]{2,1,0:T(8,128)(2,1)S(1)} %get-tuple-element.142), channel_id=1, source_target_pairs={{0,4},{4,0},{8,12},{12,8},{16,20},{20,16},{24,28},{28,24},{1,5},{5... | collective-permute-start | bytes 294920 | tf_op jit(solution)/shard_map/ppermute | solution.py:694
  64.7 15.7 %collective-permute-start.26 = (bf16[4,48,384]{2,1,0:T(8,128)(2,1)S(1)}, bf16[4,48,384]{2,1,0:T(8,128)(2,1)S(1)}, u32[]{:S(2)}, u32[]{:S(2)}) collective-permute-start(bf16[4,48,384]{2,1,0:T(8,128)(2,1)S(1)} %get-tuple-element.154), channel_id=1, source_target_pairs={{0,16},{4,20},{8,24},{12,28},{16,0},{20,4},{24,8},{28,12},{1,17},{... | collective-permute-start | bytes 442376 | tf_op jit(solution)/shard_map/ppermute | solution.py:694
  69.0 7.7 %collective-permute-start.21 = (bf16[128,384]{1,0:T(8,128)(2,1)S(1)}, bf16[128,384]{1,0:T(8,128)(2,1)S(1)}, u32[]{:S(2)}, u32[]{:S(2)}) collective-permute-start(bf16[128,384]{1,0:T(8,128)(2,1)S(1)} %get-tuple-element.144), channel_id=1, source_target_pairs={{0,8},{4,12},{8,0},{12,4},{16,24},{20,28},{24,16},{28,20},{1,9},{5... | collective-permute-start | bytes 294920 | tf_op jit(solution)/shard_map/ppermute | solution.py:694
  69.5 10.9 %collective-permute-start.22 = (bf16[128,384]{1,0:T(8,128)(2,1)S(1)}, bf16[128,384]{1,0:T(8,128)(2,1)S(1)}, u32[]{:S(2)}, u32[]{:S(2)}) collective-permute-start(bf16[128,384]{1,0:T(8,128)(2,1)S(1)} %get-tuple-element.145), channel_id=1, source_target_pairs={{0,16},{4,20},{8,24},{12,28},{16,0},{20,4},{24,8},{28,12},{1,17},{... | collective-permute-start | bytes 294920 | tf_op jit(solution)/shard_map/ppermute | solution.py:694
  71.7 8.6 %collective-permute-start.23 = (bf16[128,384]{1,0:T(8,128)(2,1)S(1)}, bf16[128,384]{1,0:T(8,128)(2,1)S(1)}, u32[]{:S(2)}, u32[]{:S(2)}) collective-permute-start(bf16[128,384]{1,0:T(8,128)(2,1)S(1)} %get-tuple-element.146), channel_id=1, source_target_pairs={{0,24},{4,28},{8,16},{12,20},{16,8},{20,12},{24,0},{28,4},{1,25},{... | collective-permute-start | bytes 294920 | tf_op jit(solution)/shard_map/ppermute | solution.py:694
  81.5 12.8 %all-to-all-start = ((bf16[8,16,384]{2,1,0:T(8,128)(2,1)}), bf16[8,16,384]{2,1,0:T(8,128)(2,1)S(1)}, u32[]{:S(2)}, u32[]{:S(2)}) async-start(bf16[8,16,384]{2,1,0:T(8,128)(2,1)} %get-tuple-element.156), calls=%async_computation | async-start | bytes 196608 | tf_op jit(solution)/shard_map/all_to_all | solution.py:879
  86.5 7.3 %collective-permute-start.30 = (bf16[4,48,384]{2,1,0:T(8,128)(2,1)S(1)}, bf16[4,48,384]{2,1,0:T(8,128)(2,1)S(1)}, u32[]{:S(2)}, u32[]{:S(2)}) collective-permute-start(bf16[4,48,384]{2,1,0:T(8,128)(2,1)S(1)} %get-tuple-element.157.refs_0_), channel_id=1, source_target_pairs={{0,8},{4,12},{8,0},{12,4},{16,24},{20,28},{24,16},{28,20},{1,9},{5... | collective-permute-start | bytes 442376 | tf_op jit(solution)/shard_map/ppermute | solution.py:694
  94.4 7.1 %collective-permute-start.31 = (bf16[256,768]{1,0:T(8,128)(2,1)S(1)}, bf16[256,768]{1,0:T(8,128)(2,1)S(1)}, u32[]{:S(2)}, u32[]{:S(2)}) collective-permute-start(bf16[256,768]{1,0:T(8,128)(2,1)S(1)} %shard_map.318.keep), channel_id=1, source_target_pairs={{0,1},{1,0},{2,3},{3,2},{4,5},{5,4},{6,7},{7,6},{8,9},{9,8},{10,11... | collective-permute-start | bytes 1179656 | tf_op jit(solution)/shard_map/ppermute | solution.py:904
  94.4 7.7 %collective-permute-start.29 = (bf16[8,16,384]{2,1,0:T(8,128)(2,1)S(1)}, bf16[8,16,384]{2,1,0:T(8,128)(2,1)S(1)}, u32[]{:S(2)}, u32[]{:S(2)}) collective-permute-start(bf16[8,16,384]{2,1,0:T(8,128)(2,1)S(1)} %all-to-all-done.refs_0_), channel_id=1, source_target_pairs={{0,3},{1,2},{2,1},{3,0},{4,7},{5,6},{6,5},{7,4},{8,11},{9,10},{10,... | collective-permute-start | bytes 294920 | tf_op jit(solution)/shard_map/ppermute | solution.py:689
  95.5 6.7 %collective-permute-start.28 = (bf16[8,16,384]{2,1,0:T(8,128)(2,1)S(1)}, bf16[8,16,384]{2,1,0:T(8,128)(2,1)S(1)}, u32[]{:S(2)}, u32[]{:S(2)}) collective-permute-start(bf16[8,16,384]{2,1,0:T(8,128)(2,1)S(1)} %all-to-all-done.refs_0_), channel_id=1, source_target_pairs={{0,2},{1,3},{2,0},{3,1},{4,6},{5,7},{6,4},{7,5},{8,10},{9,11},{10,... | collective-permute-start | bytes 294920 | tf_op jit(solution)/shard_map/ppermute | solution.py:689
  96.6 5.6 %collective-permute-start.27 = (bf16[8,16,384]{2,1,0:T(8,128)(2,1)S(1)}, bf16[8,16,384]{2,1,0:T(8,128)(2,1)S(1)}, u32[]{:S(2)}, u32[]{:S(2)}) collective-permute-start(bf16[8,16,384]{2,1,0:T(8,128)(2,1)S(1)} %all-to-all-done.refs_0_), channel_id=1, source_target_pairs={{0,1},{1,0},{2,3},{3,2},{4,5},{5,4},{6,7},{7,6},{8,9},{9,8},{10,11... | collective-permute-start | bytes 294920 | tf_op jit(solution)/shard_map/ppermute | solution.py:689

commit v5 on v4

--- a/solution.py
+++ b/solution.py
@@ -225,10 +225,9 @@
     mine = iota((mols, 1, length), 0) == seg_row[None]
     masked = jnp.where(mine, scores[None], MASKED)
     peak = jnp.max(masked, -1, keepdims=True)
-    grown = jnp.where(mine, jnp.exp(masked - peak), 0.0)
+    grown = jnp.exp(masked - peak)
     total = jnp.sum(grown, -1, keepdims=True)
-    total = jnp.where(total > 0.0, total, 1.0)
-    prob = (grown / total).reshape(mols * heads, length).astype(BF)
+    prob = (grown * (1.0 / total)).reshape(mols * heads, length).astype(BF)
     probs[...] = prob
     wide = dot(prob, values[...])
     r = iota(wide.shape, 0) & (heads - 1)
@@ -259,7 +258,7 @@
 def head_kernel(nmp, cols, *refs):
     terms = refs[:nmp]
     resid_one, vectors, head, targets, seg, hidden, w2 = refs[nmp : nmp + 7]
-    part, pack, grad_out, low_out, hidden_out, rows_out, head_low = refs[nmp + 7 :]
+    part, pack, pred_out, grad_out, low_out, hidden_out, rows_out, head_low = refs[nmp + 7 :]
     width = vectors.shape[1]
     mols = targets.shape[1]
     head_low[...] = head[...].astype(BF)
@@ -296,8 +295,8 @@
     _, slope_hidden = gelu_pair(hidden[...])
     grad_hidden = jnp.where(iota(grad_act.shape, 1) < cols, grad_act * slope_hidden, 0.0).astype(BF)
     part[...] = dot(grad_hidden, w2[:, 0:256], NT).astype(BF)
-    pack[:, 0:width] = low
-    pack[:, width : 2 * width] = grad_mid
+    pack[...] = low
+    pred_out[...] = jnp.broadcast_to(grad_pred, pred_out.shape)
     low_out[...] = grad_low
     hidden_out[...] = grad_hidden
     r = iota((8, width), 0)
@@ -331,9 +330,7 @@
         half = outs[0].shape[1]
         parts_for(rows, *outs, half, lax.axis_index("dp") & 1, high, 2)
         if outs[0].shape[0] > 2 * high:
-            width = pack.shape[1] // 2
             lanes = pack[...].astype(F32)
-            lanes = jnp.where((lax.axis_index("mp") & 1) == 0, lanes[:, 0:width], lanes[:, width:])
             lanes = jnp.concatenate([lanes[:, 0:384], lanes[:, 384:768]], 0).astype(BF)
             outs[0][2 * high] = lanes
             outs[1][2 * high] = lanes
@@ -448,14 +445,17 @@
 
 def merge_table_kernel(nmp, owners, own, high, *refs):
     terms = refs[:nmp]
-    side, key_rows, table_keep, table_send, table_sum, key_sum = refs[nmp:]
+    side, key_rows, preds, table_keep, table_send, table_sum, key_sum = refs[nmp:]
     odd = lax.axis_index("dp") & 1
     table_sum[...] = tree(terms)
     half = table_sum.shape[1] // 2
     query = jnp.concatenate([side[0:1, :], jnp.zeros((1, 128), F32)], 1)
     scal = loss_row(side[1:2, 0:1], side[1:2, 1:2], 384)
     r = iota((8, 384), 0)
-    scal = jnp.where(r == 0, query, jnp.where(r == 1, scal, 0.0))
+    mols = preds.shape[0]
+    spot = iota((mols, 384), 1) == iota((mols, 384), 0) + lax.axis_index("dp") * mols
+    pred_high, pred_mid, _ = three(jnp.sum(jnp.where(spot, preds[:, 0:1], 0.0), 0, keepdims=True))
+    scal = jnp.where(r == 0, query, jnp.where(r == 1, scal, jnp.where(r == 2, pred_high, jnp.where(r == 3, pred_mid, 0.0))))
     fill = jnp.zeros((8, 384 - own), F32)
     for p in range(2 * high):
         key_sum[p] = jnp.concatenate([key_rows[:, p * own : (p + 1) * own], fill], 1)
@@ -501,6 +501,12 @@
     pair[1 - odd] = came[last]
 
 
+def quad_kernel(pair, far, quad):
+    for i in range(2):
+        quad[i] = pair[i]
+        quad[2 + i] = far[2 + i]
+
+
 def ffn_z_kernel(keep, came, pair, far_keep, far_send):
     side = lax.axis_index("dp") >> 2
     each = far_send.shape[1]
@@ -515,53 +521,57 @@
     return jnp.sum(jnp.sum(value * value, 0, keepdims=True), 1, keepdims=True)
 
 
-def rows_kernel(npiece, nkept, *refs):
-    pieces, sources, out, kept = refs[:npiece], refs[npiece : npiece + nkept], refs[npiece + nkept], refs[npiece + nkept + 1 : -1]
-    sems = refs[-1]
-    copies = [pltpu.make_async_copy(a, b, sems.at[i]) for i, (a, b) in enumerate(zip(sources, kept))]
-    for copy in copies:
-        copy.start()
-    mine = lax.axis_index("dp") >> 1
+def outer_kernel(npiece, nkept, head_at, *refs):
+    pieces, (preds, vectors), sources = refs[:npiece], refs[npiece : npiece + 2], refs[npiece + 2 : npiece + 2 + nkept]
+    head_grad, square = refs[npiece + 2 + nkept : npiece + 4 + nkept]
+    kept, (rows, low, sems) = refs[npiece + 4 + nkept : -3], refs[-3:]
+    copies = [pltpu.make_async_copy(sources[i], kept[i], sems.at[i]) for i in range(nkept)]
+    copies[head_at].start()
+    for i, copy in enumerate(copies):
+        if i != head_at:
+            copy.start()
+    slots = rows.shape[0]
     if npiece == 1:
-        out[...] = pieces[0][...]
-    for k in range(4 if npiece == 2 else 0):
-        for x in range(2):
-            rows = pieces[k & 1][(k & 2) + x].astype(F32)
-            mols = rows.shape[0] // 2
-            rows = jnp.concatenate([rows[0:mols, :], rows[mols:, :]], 1)
-            slot = out.shape[0] // 8
-            rows = jnp.concatenate([rows, jnp.zeros((slot - mols, rows.shape[1]), F32)], 0).astype(BF)
-            out[pl.ds(pl.multiple_of(((mine ^ k) * 2 + x) * slot, 16), slot), :] = rows
-    for copy in copies:
-        copy.wait()
-
-
-def outer_kernel(keep, came, head_grad, square):
-    first = (lax.axis_index("mp") & 1) == 0
-    mine, other = keep[...].astype(F32), came[...].astype(F32)
-    head_in = jnp.where(first, mine, other).astype(BF)
-    grad_mid = jnp.where(first, other, mine).astype(BF)
-    grad = dot(head_in, grad_mid, TN)
+        rows[...] = pieces[0][...]
+        column = preds[:, 0:1]
+    else:
+        mine = lax.axis_index("dp") >> 1
+        for k in range(4):
+            for x in range(2):
+                part = pieces[k & 1][(k & 2) + x].astype(F32)
+                mols = part.shape[0] // 2
+                part = jnp.concatenate([part[0:mols, :], part[mols:, :]], 1)
+                part = jnp.concatenate([part, jnp.zeros((32 - mols, part.shape[1]), F32)], 0).astype(BF)
+                rows[pl.ds(pl.multiple_of(((mine ^ k) * 2 + x) * 32, 16), 32), :] = part
+        r = iota((slots, 384), 0)
+        spot = (iota((slots, 384), 1) == r - (r >> 5) * (32 - mols)) & ((r & 31) < mols)
+        column = jnp.sum(jnp.where(spot, preds[2:3, :] + preds[3:4, :], 0.0), -1, keepdims=True)
+    copies[head_at].wait()
+    low[...] = kept[head_at][...].astype(BF)
+    mid = dot(rows[...], low[...]) + vectors[9:10, :]
+    _, slope = gelu_pair(mid)
+    readout = vectors[10:11, :].astype(BF).astype(F32)
+    grad = dot(rows[...], (column * readout * slope).astype(BF), TN)
     head_grad[...] = grad
     square[...] = jnp.broadcast_to(sum_squares(grad), square.shape)
+    for i, copy in enumerate(copies):
+        if i != head_at:
+            copy.wait()
 
 
 def owner_kernel(own, cols, scale, dp, *refs):
-    parts, ffn_parts, (query, vectors, layer, send, scalars, quad) = refs[: dp // 2], refs[dp // 2 : -6], refs[-6:]
+    parts, ffn_parts, (query, vectors, layer, send, scalars, preds) = refs[: dp // 2], refs[dp // 2 : -6], refs[-6:]
     width = vectors.shape[1]
     summed = tree(parts)
-    if len(ffn_parts) == 3:
-        near, far, pair = ffn_parts
+    if ffn_parts[0].shape[0] == 2:
+        near, far = ffn_parts
         ffn = jnp.concatenate([near[i].astype(F32) + far[i].astype(F32) for i in range(2)], 0)
-        for i in range(2):
-            quad[i] = pair[i]
-            quad[2 + i] = far[2 + i]
     else:
         ffn = tree(ffn_parts)
-        quad[...] = jnp.zeros(quad.shape, BF)
     deep = ffn.shape[0]
     acc, summed = summed[0:deep, :], summed[deep:, :]
     table, keys, side = summed[0:16, :], summed[16:24, 0:128], summed[24:32, :]
+    preds[...] = side
     key_grad = dot(keys, query[...], TN, HIGHEST) * scale
     hat, _ = norm_parts(vectors[8:9, :])
     start_row = (hat * vectors[0:1, :] + vectors[1:2, :]).astype(BF).astype(F32)
@@ -588,7 +598,9 @@
     second_new = BETA_TWO * second + (1.0 - BETA_TWO) * grad * grad
     fixed_one = 1.0 - BETA_ONE**STEP
     fixed_two = 1.0 - BETA_TWO**STEP
-    update = first_new * (1.0 / fixed_one) / (jnp.sqrt(second_new * (1.0 / fixed_two)) + ADAM_EPS)
+    scaled = second_new * (1.0 / fixed_two)
+    root = scaled * lax.rsqrt(jnp.maximum(scaled, 1e-36))
+    update = first_new * (1.0 / fixed_one) / (root + ADAM_EPS)
     return first_new, second_new, weight - rate * (update + WEIGHT_DECAY * weight)
 
 
@@ -627,6 +639,9 @@
     loss_out[...] = loss
     count_out[...] = count
     norm_out[...] = norm
+    for j in range(6):
+        layer_out[:, j * cols : (j + 1) * cols] = layer[j] * factor
+    send(0)
     width = head.shape[0]
     parts = 8
     each = width // parts
@@ -653,9 +668,7 @@
         span = slice(j * cols, (j + 1) * cols)
         low = layer[j].astype(BF)
         shaped = dot(dot(left_roots[j].astype(BF), low).astype(BF), right_roots[j].astype(BF))
-        layer_out[:, span] = layer[j] * factor
         weights_out[:, span] = weights[:, span] - RATE_LAYER * (shaped * factor + WEIGHT_DECAY * weights[:, span])
-    send(0)
     send(1)
     half = grads.shape[1] // 2
     high = FEATS // 8 // nmp
@@ -779,11 +792,12 @@
         [*exchange(part, "mp"), vectors, w2],
         flops=4 * mols * width * 256,
     )
-    part, pack, grad_two, grad_low, grad_hidden, head_rows = call(
+    part, pack, grad_pred, grad_two, grad_low, grad_hidden, head_rows = call(
         functools.partial(head_kernel, nmp, cols),
         [
             sds((mols, width), BF),
-            sds((mols, 2 * width), BF),
+            sds((mols, width), BF),
+            sds((mols, 128), F32),
             sds((mols, width), F32),
             sds((mols, width), BF),
             sds((mols, 256), BF),
@@ -818,6 +832,7 @@
         flops=4 * mols * width * 256,
     )
     ffn_keep, ffn_send = halves(ffn_parts)
+    (ffn_send,) = after([ffn_send], *parts[1:])
     ffn_came = flip(ffn_send, 1)
     *layer_halves, side, key_rows, sides, extras = call(
         functools.partial(attn_back_kernel, nmp, nlayer, high, mols, heads, scale),
@@ -840,7 +855,7 @@
     table_keep, table_send = call(
         functools.partial(merge_table_kernel, nmp, owners, own, high),
         [sds((high, 32, 384), BF)] * 2,
-        [*moved, side, key_rows],
+        [*moved, side, key_rows, grad_pred],
         [pltpu.VMEM((FEATS // nmp, width), F32), pltpu.VMEM((dp, 8, 384), F32)],
     )
     (ffn_came,) = after([ffn_came], shares[0])
@@ -855,7 +870,7 @@
             [sds((2, own // 2, 384), BF), sds((4, own // 2, 384), BF)],
             [near_keep, flip(near_send, 2), pair],
         )
-        ffn_parts = [far_keep, flip(far_send, 4), pair]
+        ffn_parts = [far_keep, flip(far_send, 4)]
     else:
         ffn_parts = call(ffn_all_kernel, [sds((deep, 384), BF)] * high, [ffn_keep, ffn_came])
         ffn_parts = [ffn_parts[0]] + [flip(ffn_parts[k], 2 * k) for k in range(1, high)]
@@ -865,48 +880,33 @@
         [layer_keep, layer_came, table_keep, flip(table_send, 1)],
     )
     merged = [merged[0]] + [flip(merged[k], 2 * k) for k in range(1, high)]
-    layer, send, scalars, quad = call(
+    layer, send, scalars, preds = call(
         functools.partial(owner_kernel, own, cols, scale, dp),
-        [sds((6, own, cols), F32), sds((dp, 16, 384), BF), sds((8, 128), F32), sds((4, 2 * mols, 384), BF)],
+        [sds((6, own, cols), F32), sds((dp, 16, 384), BF), sds((8, 128), F32), sds((8, 384), F32)],
         [*merged, *ffn_parts, query, vectors],
         flops=2 * own * 256 * 1024,
     )
-    swap = [(i, i ^ 1) for i in range(nmp)]
     kept = [
         jnp.swapaxes(left_roots, 0, 1), right_roots[0], layer_weights, jnp.swapaxes(left_stats, 0, 1), right_stats[0],
         tables, tables_m, tables_v, head_weight, head_m, head_v, vectors, vectors_m, vectors_v,
     ]
     sums = lax.all_to_all(send, "dp", 0, 0, tiled=True)
     if direct:
+        (far,) = after([ffn_parts[1]], scalars)
+        (quad,) = call(quad_kernel, [sds((4, 2 * mols, 384), BF)], [pair, far])
         (came,) = after([flip(quad, 2)], sums)
         pieces = [quad, came]
     else:
-        packs = lax.all_gather(pack, "dp", axis=0)
-        packs = jnp.pad(packs, ((0, 0), (0, 32 - mols), (0, 0))).reshape(dp * 32, -1)
-        first = (lax.axis_index("mp") & 1) == 0
-        pieces = [jnp.where(first, packs[:, :width], packs[:, width:])]
-    (mine,) = call(
-        functools.partial(rows_kernel, len(pieces), 0),
-        [sds((dp * 32, width), BF)],
-        [*pieces],
-        [pltpu.SemaphoreType.DMA((1,))],
-        vmem=8,
-    )
+        pieces = [jnp.pad(lax.all_gather(pack, "dp", axis=0), ((0, 0), (0, 32 - mols), (0, 0))).reshape(dp * 32, -1)]
+        preds = jnp.pad(lax.all_gather(grad_pred, "dp", axis=0), ((0, 0), (0, 32 - mols), (0, 0))).reshape(dp * 32, -1)
     sums = exchange(sums, "mp")
-    token, *kept = call(
-        functools.partial(rows_kernel, 1, len(kept)),
-        [sds(scalars.shape, F32)] + [pltpu.VMEM(x.shape, F32) for x in kept],
-        [scalars, *[in_hbm(x) for x in kept]],
-        [pltpu.SemaphoreType.DMA((len(kept),))],
-        in_specs=[IN_VMEM] + [IN_PLACE] * len(kept),
-        vmem=2,
-    )
-    other = lax.ppermute(mine, "mp", swap)
-    head_grad, head_square = call(
-        outer_kernel,
-        [sds((width, width), F32), sds((8, 128), F32)],
-        [mine, other],
-        flops=2 * dp * mols * width * width,
+    head_grad, head_square, *kept = call(
+        functools.partial(outer_kernel, len(pieces), len(kept), 8),
+        [sds((width, width), F32), sds((8, 128), F32)] + [pltpu.VMEM(x.shape, F32) for x in kept],
+        [*pieces, preds, vectors, *[in_hbm(x) for x in kept]],
+        [pltpu.VMEM((dp * 32, width), BF), pltpu.VMEM((width, width), BF), pltpu.SemaphoreType.DMA((len(kept),))],
+        flops=4 * dp * mols * width * width,
+        in_specs=[IN_VMEM] * (len(pieces) + 2) + [IN_PLACE] * len(kept),
         vmem=16 + dp // 4,
     )
     kept = [in_vmem(x) for x in kept]
@@ -923,7 +923,7 @@
         functools.partial(update_kernel, nmp, cols),
         [sds((1, 1), F32)] * 3 + results,
         [
-            *sums, head_square, token, layer, *kept[:11], head_grad, *kept[11:],
+            *sums, head_square, scalars, layer, *kept[:11], head_grad, *kept[11:],
         ],
         [pltpu.VMEM(x.shape, x.dtype) for x in results] + [pltpu.VMEM((FEATS, width), F32), pltpu.VMEM((16, width), F32), pltpu.VMEM((nmp, dp, 16, 384), BF), pltpu.SemaphoreType.DMA((34,))],
         flops=20 * width * width,

time: 109 us -> 107 us (0.982)
  starting transfers between devices: 37.7 us -> 34.9 us
  waiting for transfers between devices: 44 us -> 45.7 us
    all_to_all x1, waiting for transfers between devices: 0.51 us -> 5.71 us  [per_device(): sums = lax.all_to_all(send, 'dp', 0, 0, tiled=True)]
    ppermute x3, waiting for transfers between devices: 4.51 us -> 1.21 us  [per_device(): lax.ppermute(shares[k], 'mp', [(i, i ^ k) for i in range(nmp)])]
    all_to_all x1, starting transfers between devices: 4.99 us -> 3.54 us  [per_device(): sums = lax.all_to_all(send, 'dp', 0, 0, tiled=True)]
    pallas_call x16 -> x15, Pallas kernels: 24.8 us -> 24.4 us  [call(): pl.pallas_call(kernel, out_shape=tuple(outs), in_specs=in_specs or [IN_VM...]
  transfers between devices with their start and end apart: 33 -> 32, of which waited for: 20 -> 19; matrix products, arithmetic and copies ran while one was open for 0% -> 0% of each run, Pallas kernels for 11% -> 12%
where the time goes in v5:
time: 107 us
  waiting for transfers between devices  45.7 us (43%)
  starting transfers between devices  34.9 us (33%)
  Pallas kernels  24.4 us (23%)
    ppermute x16, waiting for transfers between devices, flip(): return lax.ppermute(x, 'dp', [(i, i ^ k) for i in range(n)])  31.2 us
    pallas_call x15, Pallas kernels, call(): pl.pallas_call(kernel, out_shape=tuple(outs), in_specs=in_specs or [IN_VM...  24.4 us
    ppermute x16, starting transfers between devices, flip(): return lax.ppermute(x, 'dp', [(i, i ^ k) for i in range(n)])  21.8 us
    ppermute x12, starting transfers between devices, exchange(): lax.ppermute(x, axis, [(i, i ^ k) for i in range(n)])  7.61 us
    ppermute x12, waiting for transfers between devices, exchange(): lax.ppermute(x, axis, [(i, i ^ k) for i in range(n)])  7.57 us
    all_to_all x1, waiting for transfers between devices, per_device(): sums = lax.all_to_all(send, 'dp', 0, 0, tiled=True)  5.71 us
    all_to_all x1, starting transfers between devices, per_device(): sums = lax.all_to_all(send, 'dp', 0, 0, tiled=True)  3.54 us
  transfers between devices with their start and end apart: 32, of which 19 were waited for; matrix products, arithmetic and copies ran while one was open for 0% of the time, Pallas kernels for 12%

profile of v5, /device:TPU:0, one launch (start us, length us, event | category | flops | bytes accessed | tf_op | source)
XLA Modules:
  0.0 107.0 jit_solution(13522914638978163688)
XLA Ops:
  0.6 0.0 copy-start.1
  0.7 0.0 copy-start.2
  0.7 1.1 convert_element_type.3.refs_3_
  1.7 3.1 %collective-permute-start.2 = (bf16[96,1152]{1,0:T(8,128)(2,1)S(1)}, bf16[96,1152]{1,0:T(8,128)(2,1)S(1)}, u32[]{:S(2)}, u32[]{:S(2)}) collective-permute-start(bf16[96,1152]{1,0:T(8,128)(2,1)S(1)} %convert_element_type.3.refs_3_), channel_id=1, source_target_pairs={{0,8},{4,12},{8,0},{12,4},{16,24},{20,28},{24,16},{28,20},{1,9},{5... | collective-permute-start | bytes 663560 | tf_op jit(solution)/shard_map/ppermute | solution.py:707
  4.8 1.5 %collective-permute-start.1 = (bf16[96,1152]{1,0:T(8,128)(2,1)S(1)}, bf16[96,1152]{1,0:T(8,128)(2,1)S(1)}, u32[]{:S(2)}, u32[]{:S(2)}) collective-permute-start(bf16[96,1152]{1,0:T(8,128)(2,1)S(1)} %convert_element_type.3.refs_3_), channel_id=1, source_target_pairs={{0,4},{4,0},{8,12},{12,8},{16,20},{20,16},{24,28},{28,24},{1,5},{5... | collective-permute-start | bytes 663560 | tf_op jit(solution)/shard_map/ppermute | solution.py:707
  6.3 2.6 %collective-permute-start = (bf16[96,1152]{1,0:T(8,128)(2,1)S(1)}, bf16[96,1152]{1,0:T(8,128)(2,1)S(1)}, u32[]{:S(2)}, u32[]{:S(2)}) collective-permute-start(bf16[96,1152]{1,0:T(8,128)(2,1)S(1)} %convert_element_type.3.refs_3_), channel_id=1, source_target_pairs={{0,16},{4,20},{8,24},{12,28},{16,0},{20,4},{24,8},{28,12},{1,17},{... | collective-permute-start | bytes 663560 | tf_op jit(solution)/shard_map/ppermute | solution.py:707
  8.9 2.6 %shard_map.306 = (bf16[256,1024]{1,0:T(8,128)(2,1)S(1)}, bf16[1024,768]{1,0:T(8,128)(2,1)S(1)}, bf16[1024,768]{1,0:T(8,128)(2,1)S(1)}, f32[1024,128]{1,0:T(8,128)S(1)}) custom-call(f32[16,1024]{1,0:T(8,128)} %bitcast.21, s32[2,1024]{1,0:T(2,128)} %bitcast.22, s32[1,1024]{1,0:T(1,128)} %refs_2_.2, s32[1,1024]{1,0:T(1,128)} %refs_7_.6, f32[224,768]{1,0:T(8,128)} %refs_9_.1, ...), custom_call_target="tpu_custom_call" | custom-call | flops 805306368 | bytes 4998144 | tf_op jit(solution)/shard_map/pallas_call | solution.py:55
  11.5 0.0 copy-start.3
  11.5 2.0 %collective-permute-done.2.refs_5_ = bf16[96,1152]{1,0:T(8,128)(2,1)S(1)} collective-permute-done((bf16[96,1152]{1,0:T(8,128)(2,1)S(1)}, bf16[96,1152]{1,0:T(8,128)(2,1)S(1)}, u32[]{:S(2)}, u32[]{:S(2)}) %collective-permute-start.2) | collective-permute-done | bytes 221216 | tf_op jit(solution)/shard_map/ppermute | solution.py:707
  13.5 5.1 %collective-permute-done.refs_7_ = bf16[96,1152]{1,0:T(8,128)(2,1)S(1)} collective-permute-done((bf16[96,1152]{1,0:T(8,128)(2,1)S(1)}, bf16[96,1152]{1,0:T(8,128)(2,1)S(1)}, u32[]{:S(2)}, u32[]{:S(2)}) %collective-permute-start) | collective-permute-done | bytes 221216 | tf_op jit(solution)/shard_map/ppermute | solution.py:707
  18.6 3.3 %collective-permute-start.6 = (bf16[96,1152]{1,0:T(8,128)(2,1)S(1)}, bf16[96,1152]{1,0:T(8,128)(2,1)S(1)}, u32[]{:S(2)}, u32[]{:S(2)}) collective-permute-start(bf16[96,1152]{1,0:T(8,128)(2,1)S(1)} %collective-permute-done.1.refs_4_), channel_id=1, source_target_pairs={{0,24},{4,28},{8,16},{12,20},{16,8},{20,12},{24,0},{28,4},{1,25},{... | collective-permute-start | bytes 663560 | tf_op jit(solution)/shard_map/ppermute | solution.py:707
  21.9 2.0 %collective-permute-start.4 = (bf16[96,1152]{1,0:T(8,128)(2,1)S(1)}, bf16[96,1152]{1,0:T(8,128)(2,1)S(1)}, u32[]{:S(2)}, u32[]{:S(2)}) collective-permute-start(bf16[96,1152]{1,0:T(8,128)(2,1)S(1)} %collective-permute-done.refs_7_), channel_id=1, source_target_pairs={{0,4},{4,0},{8,12},{12,8},{16,20},{20,16},{24,28},{28,24},{1,5},{5... | collective-permute-start | bytes 663560 | tf_op jit(solution)/shard_map/ppermute | solution.py:707
  23.9 4.0 %collective-permute-done.6.refs_10_ = bf16[96,1152]{1,0:T(8,128)(2,1)S(1)} collective-permute-done((bf16[96,1152]{1,0:T(8,128)(2,1)S(1)}, bf16[96,1152]{1,0:T(8,128)(2,1)S(1)}, u32[]{:S(2)}, u32[]{:S(2)}) %collective-permute-start.6) | collective-permute-done | bytes 221216 | tf_op jit(solution)/shard_map/ppermute | solution.py:707
  27.9 1.3 %collective-permute-done.3.refs_6_ = bf16[96,1152]{1,0:T(8,128)(2,1)S(1)} collective-permute-done((bf16[96,1152]{1,0:T(8,128)(2,1)S(1)}, bf16[96,1152]{1,0:T(8,128)(2,1)S(1)}, u32[]{:S(2)}, u32[]{:S(2)}) %collective-permute-start.3) | collective-permute-done | bytes 221216 | tf_op jit(solution)/shard_map/ppermute | solution.py:707
  29.2 1.0 collective-permute-done.5.refs_9_
  30.2 1.4 %collective-permute-done.4.refs_8_ = bf16[96,1152]{1,0:T(8,128)(2,1)S(1)} collective-permute-done((bf16[96,1152]{1,0:T(8,128)(2,1)S(1)}, bf16[96,1152]{1,0:T(8,128)(2,1)S(1)}, u32[]{:S(2)}, u32[]{:S(2)}) %collective-permute-start.4) | collective-permute-done | bytes 221216 | tf_op jit(solution)/shard_map/ppermute | solution.py:707
  31.6 2.5 %shard_map.307 = (bf16[24,768]{1,0:T(8,128)(2,1)S(1)}, bf16[192,1024]{1,0:T(8,128)(2,1)S(1)}, bf16[1024,256]{1,0:T(8,128)(2,1)S(1)}, bf16[24,256]{1,0:T(8,128)(2...) custom-call(bf16[1024,768]{1,0:T(8,128)(2,1)S(1)} %get-tuple-element, ...), custom_call_target="tpu_custom_call" | custom-call | flops 805306368 | bytes 6517760 | tf_op jit(solution)/shard_map/pallas_call | solution.py:55
  34.1 0.1 collective-permute-start.9
  34.1 1.6 %collective-permute-start.8 = (bf16[24,768]{1,0:T(8,128)(2,1)S(1)}, bf16[24,768]{1,0:T(8,128)(2,1)S(1)}, u32[]{:S(2)}, u32[]{:S(2)}) collective-permute-start(bf16[24,768]{1,0:T(8,128)(2,1)S(1)} %get-tuple-element.111.refs_0_), channel_id=1, source_target_pairs={{0,2},{1,3},{2,0},{3,1},{4,6},{5,7},{6,4},{7,5},{8,10},{9,11},{10,... | collective-permute-start | bytes 110600 | tf_op jit(solution)/shard_map/ppermute | solution.py:702
  35.7 0.3 collective-permute-start.7
  36.0 1.8 %collective-permute-done.9.refs_3_ = bf16[24,768]{1,0:T(8,128)(2,1)S(1)} collective-permute-done((bf16[24,768]{1,0:T(8,128)(2,1)S(1)}, bf16[24,768]{1,0:T(8,128)(2,1)S(1)}, u32[]{:S(2)}, u32[]{:S(2)}) %collective-permute-start.9) | collective-permute-done | bytes 36896 | tf_op jit(solution)/shard_map/ppermute | solution.py:702
  37.8 0.5 collective-permute-done.8.refs_2_
  38.3 0.6 shard_map.308
  38.9 1.1 collective-permute-start.12
  40.0 0.9 collective-permute-start.11
  40.8 1.5 %collective-permute-done.12.refs_3_ = bf16[24,768]{1,0:T(8,128)(2,1)S(1)} collective-permute-done((bf16[24,768]{1,0:T(8,128)(2,1)S(1)}, bf16[24,768]{1,0:T(8,128)(2,1)S(1)}, u32[]{:S(2)}, u32[]{:S(2)}) %collective-permute-start.12) | collective-permute-done | bytes 36896 | tf_op jit(solution)/shard_map/ppermute | solution.py:702
  42.3 1.6 %collective-permute-done.11.refs_2_ = bf16[24,768]{1,0:T(8,128)(2,1)S(1)} collective-permute-done((bf16[24,768]{1,0:T(8,128)(2,1)S(1)}, bf16[24,768]{1,0:T(8,128)(2,1)S(1)}, u32[]{:S(2)}, u32[]{:S(2)}) %collective-permute-start.11) | collective-permute-done | bytes 36896 | tf_op jit(solution)/shard_map/ppermute | solution.py:702
  44.0 1.6 %shard_map.309 = (bf16[24,768]{1,0:T(8,128)(2,1)S(1)}, bf16[24,768]{1,0:T(8,128)(2,1)S(1)}, f32[24,128]{1,0:T(8,128)S(1)}, f32[24,768]{1,0:T(8,128)S(1)}, bf16[2...) custom-call(bf16[24,768]{1,0:T(8,128)(2,1)S(1)} %get-tuple-element.113.refs_0_, ...), custom_call_target="tpu_custom_call" | custom-call | flops 56623104 | bytes 3466336 | tf_op jit(solution)/shard_map/pallas_call | solution.py:55
  45.6 0.7 collective-permute-start.15
  46.2 0.8 collective-permute-start.14
  47.1 0.4 collective-permute-start.13
  47.5 0.6 shard_map.311
  48.1 1.3 %collective-permute-done.15.refs_3_ = bf16[24,768]{1,0:T(8,128)(2,1)S(1)} collective-permute-done((bf16[24,768]{1,0:T(8,128)(2,1)S(1)}, bf16[24,768]{1,0:T(8,128)(2,1)S(1)}, u32[]{:S(2)}, u32[]{:S(2)}) %collective-permute-start.15) | collective-permute-done | bytes 36896 | tf_op jit(solution)/shard_map/ppermute | solution.py:702
  49.4 0.8 collective-permute-done.14.refs_2_
  50.2 0.3 collective-permute-start.24
  50.5 2.3 %shard_map.310 = (bf16[4,96,384]{2,1,0:T(8,128)(2,1)S(1)}, bf16[4,96,384]{2,1,0:T(8,128)(2,1)S(1)}, f32[8,256]{1,0:T(8,128)S(1)}, f32[8,768]{1,0:T(8,128)S(1)}, ...) custom-call(bf16[24,768]{1,0:T(8,128)(2,1)S(1)} %get-tuple-element.116.refs_0_, ...), custom_call_target="tpu_custom_call" | custom-call | flops 805306368 | bytes 5231616 | tf_op jit(solution)/shard_map/pallas_call | solution.py:55
  52.8 1.8 %collective-permute-start.16 = (bf16[4,96,384]{2,1,0:T(8,128)(2,1)S(1)}, bf16[4,96,384]{2,1,0:T(8,128)(2,1)S(1)}, u32[]{:S(2)}, u32[]{:S(2)}) collective-permute-start(bf16[4,96,384]{2,1,0:T(8,128)(2,1)S(1)} %get-tuple-element.124), channel_id=1, source_target_pairs={{0,4},{4,0},{8,12},{12,8},{16,20},{20,16},{24,28},{28,24},{1,5},{5... | collective-permute-start | bytes 884744 | tf_op jit(solution)/shard_map/ppermute | solution.py:707
  54.6 1.1 %shard_map.312 = (bf16[64,768]{1,0:T(8,128)(2,1)S(1)}, bf16[64,768]{1,0:T(8,128)(2,1)S(1)}, bf16[64,768]{1,0:T(8,128)(2,1)S(1)}, bf16[64,768]{1,0:T(8,128)(2,1)S(1)}) custom-call(bf16[256,1024]{1,0:T(8,128)(2,1)S(1)} %get-tuple-element.125.refs_0_, bf16[256,768]{1,0:T(8,128)(2,1)S(1)} %get-tuple-element.132.refs_1_, ...), custom_call_target="tpu_custom_call" | custom-call | flops 805306368 | bytes 4019200 | tf_op jit(solution)/shard_map/pallas_call | solution.py:55
  55.7 0.1 collective-permute-start.17
  55.8 1.1 %collective-permute-start.18 = (bf16[64,768]{1,0:T(8,128)(2,1)S(1)}, bf16[64,768]{1,0:T(8,128)(2,1)S(1)}, u32[]{:S(2)}, u32[]{:S(2)}) collective-permute-start(bf16[64,768]{1,0:T(8,128)(2,1)S(1)} %get-tuple-element.139), channel_id=1, source_target_pairs={{0,2},{1,3},{2,0},{3,1},{4,6},{5,7},{6,4},{7,5},{8,10},{9,11},{10,... | collective-permute-start | bytes 294920 | tf_op jit(solution)/shard_map/ppermute | solution.py:854
  56.9 0.7 collective-permute-start.19
  57.6 3.3 %collective-permute-done.24.came = bf16[9,48,384]{2,1,0:T(8,128)(2,1)S(1)} collective-permute-done((bf16[9,48,384]{2,1,0:T(8,128)(2,1)S(1)}, bf16[9,48,384]{2,1,0:T(8,128)(2,1)S(1)}, u32[]{:S(2)}, u32[]{:S(2)}) %collective-permute-start.24) | collective-permute-done | bytes 331808 | tf_op jit(solution)/shard_map/ppermute | solution.py:707
  60.9 0.1 shard_map.315
  61.0 0.4 collective-permute-start.25
  61.4 1.2 %collective-permute-done.19.refs_3_ = bf16[64,768]{1,0:T(8,128)(2,1)S(1)} collective-permute-done((bf16[64,768]{1,0:T(8,128)(2,1)S(1)}, bf16[64,768]{1,0:T(8,128)(2,1)S(1)}, u32[]{:S(2)}, u32[]{:S(2)}) %collective-permute-start.19) | collective-permute-done | bytes 98336 | tf_op jit(solution)/shard_map/ppermute | solution.py:854
  62.6 0.1 shard_map.313
  62.8 0.4 collective-permute-start.20
  63.1 3.1 %collective-permute-done.25.came = bf16[2,96,384]{2,1,0:T(8,128)(2,1)S(1)} collective-permute-done((bf16[2,96,384]{2,1,0:T(8,128)(2,1)S(1)}, bf16[2,96,384]{2,1,0:T(8,128)(2,1)S(1)}, u32[]{:S(2)}, u32[]{:S(2)}) %collective-permute-start.25) | collective-permute-done | bytes 147488 | tf_op jit(solution)/shard_map/ppermute | solution.py:707
  66.3 0.1 collective-permute-start.26
  66.4 1.7 %collective-permute-done.20.table_came = bf16[4,32,384]{2,1,0:T(8,128)(2,1)S(1)} collective-permute-done((bf16[4,32,384]{2,1,0:T(8,128)(2,1)S(1)}, bf16[4,32,384]{2,1,0:T(8,128)(2,1)S(1)}, u32[]{:S(2)}, u32[]{:S(2)}) %collective-permute-start.20) | collective-permute-done | bytes 98336 | tf_op jit(solution)/shard_map/ppermute | solution.py:707
  68.1 0.2 shard_map.314
  68.3 0.4 collective-permute-start.21
  68.8 2.2 %collective-permute-start.22 = (bf16[128,384]{1,0:T(8,128)(2,1)S(1)}, bf16[128,384]{1,0:T(8,128)(2,1)S(1)}, u32[]{:S(2)}, u32[]{:S(2)}) collective-permute-start(bf16[128,384]{1,0:T(8,128)(2,1)S(1)} %get-tuple-element.148), channel_id=1, source_target_pairs={{0,16},{4,20},{8,24},{12,28},{16,0},{20,4},{24,8},{28,12},{1,17},{... | collective-permute-start | bytes 294920 | tf_op jit(solution)/shard_map/ppermute | solution.py:707
  71.0 1.8 %collective-permute-start.23 = (bf16[128,384]{1,0:T(8,128)(2,1)S(1)}, bf16[128,384]{1,0:T(8,128)(2,1)S(1)}, u32[]{:S(2)}, u32[]{:S(2)}) collective-permute-start(bf16[128,384]{1,0:T(8,128)(2,1)S(1)} %get-tuple-element.149), channel_id=1, source_target_pairs={{0,24},{4,28},{8,16},{12,20},{16,8},{20,12},{24,0},{28,4},{1,25},{... | collective-permute-start | bytes 294920 | tf_op jit(solution)/shard_map/ppermute | solution.py:707
  72.8 1.8 %collective-permute-done.21.refs_1_ = bf16[128,384]{1,0:T(8,128)(2,1)S(1)} collective-permute-done((bf16[128,384]{1,0:T(8,128)(2,1)S(1)}, bf16[128,384]{1,0:T(8,128)(2,1)S(1)}, u32[]{:S(2)}, u32[]{:S(2)}) %collective-permute-start.21) | collective-permute-done | bytes 98336 | tf_op jit(solution)/shard_map/ppermute | solution.py:707
  74.6 6.5 %collective-permute-done.22.refs_2_ = bf16[128,384]{1,0:T(8,128)(2,1)S(1)} collective-permute-done((bf16[128,384]{1,0:T(8,128)(2,1)S(1)}, bf16[128,384]{1,0:T(8,128)(2,1)S(1)}, u32[]{:S(2)}, u32[]{:S(2)}) %collective-permute-start.22) | collective-permute-done | bytes 98336 | tf_op jit(solution)/shard_map/ppermute | solution.py:707
  81.1 1.1 %shard_map.317 = (f32[6,96,192]{2,1,0:T(8,128)S(1)}, bf16[8,16,384]{2,1,0:T(8,128)(2,1)}, f32[8,128]{1,0:T(8,128)S(1)}, f32[8,384]{1,0:T(8,128)S(1)}) custom-call(bf16[128,384]{1,0:T(8,128)(2,1)S(1)} %get-tuple-element.146.refs_0_, bf16[128,384]{1,0:T(8,128)(2,1)S(1)} %collective-permute-done.21.refs_1_, ...), custom_call_target="tpu_custom_call" | custom-call | flops 50331648 | bytes 1213440 | tf_op jit(solution)/shard_map/pallas_call | solution.py:55
  82.3 3.5 %all-to-all-start = ((bf16[8,16,384]{2,1,0:T(8,128)(2,1)}), bf16[8,16,384]{2,1,0:T(8,128)(2,1)S(1)}, u32[]{:S(2)}, u32[]{:S(2)}) async-start(bf16[8,16,384]{2,1,0:T(8,128)(2,1)} %get-tuple-element.160), calls=%async_computation | async-start | bytes 196608 | tf_op jit(solution)/shard_map/all_to_all | solution.py:893
  85.8 2.0 %collective-permute-start.30 = (bf16[4,48,384]{2,1,0:T(8,128)(2,1)S(1)}, bf16[4,48,384]{2,1,0:T(8,128)(2,1)S(1)}, u32[]{:S(2)}, u32[]{:S(2)}) collective-permute-start(bf16[4,48,384]{2,1,0:T(8,128)(2,1)S(1)} %shard_map.318.refs_0_), channel_id=1, source_target_pairs={{0,8},{4,12},{8,0},{12,4},{16,24},{20,28},{24,16},{28,20},{1,9},{5... | collective-permute-start | bytes 442376 | tf_op jit(solution)/shard_map/ppermute | solution.py:707
  87.8 5.7 %all-to-all-done.refs_0_ = bf16[8,16,384]{2,1,0:T(8,128)(2,1)S(1)} async-done(((bf16[8,16,384]{2,1,0:T(8,128)(2,1)}), bf16[8,16,384]{2,1,0:T(8,128)(2,1)S(1)}, u32[]{:S(2)}, u32[]{:S(2)}) %all-to-all-start) | async-done | bytes 98336 | tf_op jit(solution)/shard_map/all_to_all | solution.py:893
  93.5 1.1 collective-permute-start.28
  94.6 0.8 collective-permute-start.27
  95.4 5.7 %shard_map.319 = (f32[768,768]{1,0:T(8,128)S(1)}, f32[8,128]{1,0:T(8,128)S(1)}, f32[6,96,96]{2,1,0:T(8,128)S(1)}, f32[6,192,192]{2,1,0:T(8,128)S(1)}, f32[96,115...) custom-call(bf16[4,48,384]{2,1,0:T(8,128)(2,1)S(1)} %shard_map.318.r, ...), custom_call_target="tpu_custom_call" | custom-call | flops 452984832 | bytes 26500096 | tf_op jit(solution)/shard_map/pallas_call | solution.py:55
  101.2 5.7 %shard_map.320 = (f32[1,1]{1,0:T(1,128)}, f32[1,1]{1,0:T(1,128)}, f32[1,1]{1,0:T(1,128)}, f32[96,1152]{1,0:T(8,128)}, f32[96,1152]{1,0:T(8,128)}, /*index=5*/f32...) custom-call(bf16[8,16,384]{2,1,0:T(8,128)(2,1)S(1)} %all-to-all-done, ...), custom_call_target="tpu_custom_call" | custom-call | flops 11796480 | bytes 26335244 | tf_op jit(solution)/shard_map/pallas_call | solution.py:55
  (24 shorter events, 0.1 us)
Async XLA Ops:
  0.6 30.9 %copy-start.1 = (f32[11,768]{1,0:T(8,128)S(1)}, f32[11,768]{1,0:T(8,128)}, u32[]{:S(2)}) copy-start(f32[11,768]{1,0:T(8,128)} %refs_15_.1) | copy-start | bytes 101380
  0.7 30.9 %copy-start.2 = (s32[1,1024]{1,0:T(1,128)S(1)}, s32[1,1024]{1,0:T(1,128)}, u32[]{:S(2)}) copy-start(s32[1,1024]{1,0:T(1,128)} %refs_7_.6) | copy-start | bytes 12292
  1.7 11.8 %collective-permute-start.2 = (bf16[96,1152]{1,0:T(8,128)(2,1)S(1)}, bf16[96,1152]{1,0:T(8,128)(2,1)S(1)}, u32[]{:S(2)}, u32[]{:S(2)}) collective-permute-start(bf16[96,1152]{1,0:T(8,128)(2,1)S(1)} %convert_element_type.3.refs_3_), channel_id=1, source_target_pairs={{0,8},{4,12},{8,0},{12,4},{16,24},{20,28},{24,16},{28,20},{1,9},{5... | collective-permute-start | bytes 663560 | tf_op jit(solution)/shard_map/ppermute | solution.py:707
  4.8 8.7 %collective-permute-start.1 = (bf16[96,1152]{1,0:T(8,128)(2,1)S(1)}, bf16[96,1152]{1,0:T(8,128)(2,1)S(1)}, u32[]{:S(2)}, u32[]{:S(2)}) collective-permute-start(bf16[96,1152]{1,0:T(8,128)(2,1)S(1)} %convert_element_type.3.refs_3_), channel_id=1, source_target_pairs={{0,4},{4,0},{8,12},{12,8},{16,20},{20,16},{24,28},{28,24},{1,5},{5... | collective-permute-start | bytes 663560 | tf_op jit(solution)/shard_map/ppermute | solution.py:707
  6.3 12.3 %collective-permute-start = (bf16[96,1152]{1,0:T(8,128)(2,1)S(1)}, bf16[96,1152]{1,0:T(8,128)(2,1)S(1)}, u32[]{:S(2)}, u32[]{:S(2)}) collective-permute-start(bf16[96,1152]{1,0:T(8,128)(2,1)S(1)} %convert_element_type.3.refs_3_), channel_id=1, source_target_pairs={{0,16},{4,20},{8,24},{12,28},{16,0},{20,4},{24,8},{28,12},{1,17},{... | collective-permute-start | bytes 663560 | tf_op jit(solution)/shard_map/ppermute | solution.py:707
  11.5 32.5 %copy-start = (f32[768,768]{1,0:T(8,128)S(1)}, f32[768,768]{1,0:T(8,128)}, u32[]{:S(2)}) copy-start(f32[768,768]{1,0:T(8,128)} %refs_12_.1) | copy-start | bytes 7077892
  11.5 32.4 %copy-start.3 = (f32[1,24]{1,0:T(1,128)S(1)}, f32[1,24]{1,0:T(1,128)}, u32[]{:S(2)}) copy-start(f32[1,24]{1,0:T(1,128)} %refs_7_.4) | copy-start | bytes 292
  18.6 9.3 %collective-permute-start.6 = (bf16[96,1152]{1,0:T(8,128)(2,1)S(1)}, bf16[96,1152]{1,0:T(8,128)(2,1)S(1)}, u32[]{:S(2)}, u32[]{:S(2)}) collective-permute-start(bf16[96,1152]{1,0:T(8,128)(2,1)S(1)} %collective-permute-done.1.refs_4_), channel_id=1, source_target_pairs={{0,24},{4,28},{8,16},{12,20},{16,8},{20,12},{24,0},{28,4},{1,25},{... | collective-permute-start | bytes 663560 | tf_op jit(solution)/shard_map/ppermute | solution.py:707
  21.9 7.3 %collective-permute-start.3 = (bf16[96,1152]{1,0:T(8,128)(2,1)S(1)}, bf16[96,1152]{1,0:T(8,128)(2,1)S(1)}, u32[]{:S(2)}, u32[]{:S(2)}) collective-permute-start(bf16[96,1152]{1,0:T(8,128)(2,1)S(1)} %collective-permute-done.2.refs_5_), channel_id=1, source_target_pairs={{0,4},{4,0},{8,12},{12,8},{16,20},{20,16},{24,28},{28,24},{1,5},{5... | collective-permute-start | bytes 663560 | tf_op jit(solution)/shard_map/ppermute | solution.py:707
  21.9 8.3 %collective-permute-start.5 = (bf16[96,1152]{1,0:T(8,128)(2,1)S(1)}, bf16[96,1152]{1,0:T(8,128)(2,1)S(1)}, u32[]{:S(2)}, u32[]{:S(2)}) collective-permute-start(bf16[96,1152]{1,0:T(8,128)(2,1)S(1)} %collective-permute-done.refs_7_), channel_id=1, source_target_pairs={{0,8},{4,12},{8,0},{12,4},{16,24},{20,28},{24,16},{28,20},{1,9},{5... | collective-permute-start | bytes 663560 | tf_op jit(solution)/shard_map/ppermute | solution.py:707
  21.9 9.7 %collective-permute-start.4 = (bf16[96,1152]{1,0:T(8,128)(2,1)S(1)}, bf16[96,1152]{1,0:T(8,128)(2,1)S(1)}, u32[]{:S(2)}, u32[]{:S(2)}) collective-permute-start(bf16[96,1152]{1,0:T(8,128)(2,1)S(1)} %collective-permute-done.refs_7_), channel_id=1, source_target_pairs={{0,4},{4,0},{8,12},{12,8},{16,20},{20,16},{24,28},{28,24},{1,5},{5... | collective-permute-start | bytes 663560 | tf_op jit(solution)/shard_map/ppermute | solution.py:707
  34.1 3.8 %collective-permute-start.9 = (bf16[24,768]{1,0:T(8,128)(2,1)S(1)}, bf16[24,768]{1,0:T(8,128)(2,1)S(1)}, u32[]{:S(2)}, u32[]{:S(2)}) collective-permute-start(bf16[24,768]{1,0:T(8,128)(2,1)S(1)} %get-tuple-element.111.refs_0_), channel_id=1, source_target_pairs={{0,3},{1,2},{2,1},{3,0},{4,7},{5,6},{6,5},{7,4},{8,11},{9,10},{10,... | collective-permute-start | bytes 110600 | tf_op jit(solution)/shard_map/ppermute | solution.py:702
  34.1 4.2 %collective-permute-start.8 = (bf16[24,768]{1,0:T(8,128)(2,1)S(1)}, bf16[24,768]{1,0:T(8,128)(2,1)S(1)}, u32[]{:S(2)}, u32[]{:S(2)}) collective-permute-start(bf16[24,768]{1,0:T(8,128)(2,1)S(1)} %get-tuple-element.111.refs_0_), channel_id=1, source_target_pairs={{0,2},{1,3},{2,0},{3,1},{4,6},{5,7},{6,4},{7,5},{8,10},{9,11},{10,... | collective-permute-start | bytes 110600 | tf_op jit(solution)/shard_map/ppermute | solution.py:702
  35.7 2.6 %collective-permute-start.7 = (bf16[24,768]{1,0:T(8,128)(2,1)S(1)}, bf16[24,768]{1,0:T(8,128)(2,1)S(1)}, u32[]{:S(2)}, u32[]{:S(2)}) collective-permute-start(bf16[24,768]{1,0:T(8,128)(2,1)S(1)} %get-tuple-element.111.refs_0_), channel_id=1, source_target_pairs={{0,1},{1,0},{2,3},{3,2},{4,5},{5,4},{6,7},{7,6},{8,9},{9,8},{10,11... | collective-permute-start | bytes 110600 | tf_op jit(solution)/shard_map/ppermute | solution.py:702
  38.9 3.4 %collective-permute-start.12 = (bf16[24,768]{1,0:T(8,128)(2,1)S(1)}, bf16[24,768]{1,0:T(8,128)(2,1)S(1)}, u32[]{:S(2)}, u32[]{:S(2)}) collective-permute-start(bf16[24,768]{1,0:T(8,128)(2,1)S(1)} %get-tuple-element.113.refs_0_), channel_id=1, source_target_pairs={{0,3},{1,2},{2,1},{3,0},{4,7},{5,6},{6,5},{7,4},{8,11},{9,10},{10,... | collective-permute-start | bytes 110600 | tf_op jit(solution)/shard_map/ppermute | solution.py:702
  40.0 4.0 %collective-permute-start.11 = (bf16[24,768]{1,0:T(8,128)(2,1)S(1)}, bf16[24,768]{1,0:T(8,128)(2,1)S(1)}, u32[]{:S(2)}, u32[]{:S(2)}) collective-permute-start(bf16[24,768]{1,0:T(8,128)(2,1)S(1)} %get-tuple-element.113.refs_0_), channel_id=1, source_target_pairs={{0,2},{1,3},{2,0},{3,1},{4,6},{5,7},{6,4},{7,5},{8,10},{9,11},{10,... | collective-permute-start | bytes 110600 | tf_op jit(solution)/shard_map/ppermute | solution.py:702
  40.8 3.1 %collective-permute-start.10 = (bf16[24,768]{1,0:T(8,128)(2,1)S(1)}, bf16[24,768]{1,0:T(8,128)(2,1)S(1)}, u32[]{:S(2)}, u32[]{:S(2)}) collective-permute-start(bf16[24,768]{1,0:T(8,128)(2,1)S(1)} %get-tuple-element.113.refs_0_), channel_id=1, source_target_pairs={{0,1},{1,0},{2,3},{3,2},{4,5},{5,4},{6,7},{7,6},{8,9},{9,8},{10,11... | collective-permute-start | bytes 110600 | tf_op jit(solution)/shard_map/ppermute | solution.py:702
  45.6 3.8 %collective-permute-start.15 = (bf16[24,768]{1,0:T(8,128)(2,1)S(1)}, bf16[24,768]{1,0:T(8,128)(2,1)S(1)}, u32[]{:S(2)}, u32[]{:S(2)}) collective-permute-start(bf16[24,768]{1,0:T(8,128)(2,1)S(1)} %get-tuple-element.116.refs_0_), channel_id=1, source_target_pairs={{0,3},{1,2},{2,1},{3,0},{4,7},{5,6},{6,5},{7,4},{8,11},{9,10},{10,... | collective-permute-start | bytes 110600 | tf_op jit(solution)/shard_map/ppermute | solution.py:702
  46.2 4.0 %collective-permute-start.14 = (bf16[24,768]{1,0:T(8,128)(2,1)S(1)}, bf16[24,768]{1,0:T(8,128)(2,1)S(1)}, u32[]{:S(2)}, u32[]{:S(2)}) collective-permute-start(bf16[24,768]{1,0:T(8,128)(2,1)S(1)} %get-tuple-element.116.refs_0_), channel_id=1, source_target_pairs={{0,2},{1,3},{2,0},{3,1},{4,6},{5,7},{6,4},{7,5},{8,10},{9,11},{10,... | collective-permute-start | bytes 110600 | tf_op jit(solution)/shard_map/ppermute | solution.py:702
  47.1 3.1 %collective-permute-start.13 = (bf16[24,768]{1,0:T(8,128)(2,1)S(1)}, bf16[24,768]{1,0:T(8,128)(2,1)S(1)}, u32[]{:S(2)}, u32[]{:S(2)}) collective-permute-start(bf16[24,768]{1,0:T(8,128)(2,1)S(1)} %get-tuple-element.116.refs_0_), channel_id=1, source_target_pairs={{0,1},{1,0},{2,3},{3,2},{4,5},{5,4},{6,7},{7,6},{8,9},{9,8},{10,11... | collective-permute-start | bytes 110600 | tf_op jit(solution)/shard_map/ppermute | solution.py:702
  50.2 10.7 %collective-permute-start.24 = (bf16[9,48,384]{2,1,0:T(8,128)(2,1)S(1)}, bf16[9,48,384]{2,1,0:T(8,128)(2,1)S(1)}, u32[]{:S(2)}, u32[]{:S(2)}) collective-permute-start(bf16[9,48,384]{2,1,0:T(8,128)(2,1)S(1)} %get-tuple-element.152), channel_id=1, source_target_pairs={{0,4},{4,0},{8,12},{12,8},{16,20},{20,16},{24,28},{28,24},{1,5},{5... | collective-permute-start | bytes 995336 | tf_op jit(solution)/shard_map/ppermute | solution.py:707
  52.8 15.3 %collective-permute-start.16 = (bf16[4,96,384]{2,1,0:T(8,128)(2,1)S(1)}, bf16[4,96,384]{2,1,0:T(8,128)(2,1)S(1)}, u32[]{:S(2)}, u32[]{:S(2)}) collective-permute-start(bf16[4,96,384]{2,1,0:T(8,128)(2,1)S(1)} %get-tuple-element.124), channel_id=1, source_target_pairs={{0,4},{4,0},{8,12},{12,8},{16,20},{20,16},{24,28},{28,24},{1,5},{5... | collective-permute-start | bytes 884744 | tf_op jit(solution)/shard_map/ppermute | solution.py:707
  55.7 5.7 %collective-permute-start.17 = (bf16[64,768]{1,0:T(8,128)(2,1)S(1)}, bf16[64,768]{1,0:T(8,128)(2,1)S(1)}, u32[]{:S(2)}, u32[]{:S(2)}) collective-permute-start(bf16[64,768]{1,0:T(8,128)(2,1)S(1)} %get-tuple-element.138), channel_id=1, source_target_pairs={{0,1},{1,0},{2,3},{3,2},{4,5},{5,4},{6,7},{7,6},{8,9},{9,8},{10,11... | collective-permute-start | bytes 294920 | tf_op jit(solution)/shard_map/ppermute | solution.py:854
  55.8 5.7 %collective-permute-start.18 = (bf16[64,768]{1,0:T(8,128)(2,1)S(1)}, bf16[64,768]{1,0:T(8,128)(2,1)S(1)}, u32[]{:S(2)}, u32[]{:S(2)}) collective-permute-start(bf16[64,768]{1,0:T(8,128)(2,1)S(1)} %get-tuple-element.139), channel_id=1, source_target_pairs={{0,2},{1,3},{2,0},{3,1},{4,6},{5,7},{6,4},{7,5},{8,10},{9,11},{10,... | collective-permute-start | bytes 294920 | tf_op jit(solution)/shard_map/ppermute | solution.py:854
  56.9 5.7 %collective-permute-start.19 = (bf16[64,768]{1,0:T(8,128)(2,1)S(1)}, bf16[64,768]{1,0:T(8,128)(2,1)S(1)}, u32[]{:S(2)}, u32[]{:S(2)}) collective-permute-start(bf16[64,768]{1,0:T(8,128)(2,1)S(1)} %get-tuple-element.140), channel_id=1, source_target_pairs={{0,3},{1,2},{2,1},{3,0},{4,7},{5,6},{6,5},{7,4},{8,11},{9,10},{10,... | collective-permute-start | bytes 294920 | tf_op jit(solution)/shard_map/ppermute | solution.py:854
  61.0 5.2 %collective-permute-start.25 = (bf16[2,96,384]{2,1,0:T(8,128)(2,1)S(1)}, bf16[2,96,384]{2,1,0:T(8,128)(2,1)S(1)}, u32[]{:S(2)}, u32[]{:S(2)}) collective-permute-start(bf16[2,96,384]{2,1,0:T(8,128)(2,1)S(1)} %get-tuple-element.155), channel_id=1, source_target_pairs={{0,8},{4,12},{8,0},{12,4},{16,24},{20,28},{24,16},{28,20},{1,9},{5... | collective-permute-start | bytes 442376 | tf_op jit(solution)/shard_map/ppermute | solution.py:707
  62.8 5.3 %collective-permute-start.20 = (bf16[4,32,384]{2,1,0:T(8,128)(2,1)S(1)}, bf16[4,32,384]{2,1,0:T(8,128)(2,1)S(1)}, u32[]{:S(2)}, u32[]{:S(2)}) collective-permute-start(bf16[4,32,384]{2,1,0:T(8,128)(2,1)S(1)} %get-tuple-element.145), channel_id=1, source_target_pairs={{0,4},{4,0},{8,12},{12,8},{16,20},{20,16},{24,28},{28,24},{1,5},{5... | collective-permute-start | bytes 294920 | tf_op jit(solution)/shard_map/ppermute | solution.py:707
  66.3 14.8 %collective-permute-start.26 = (bf16[4,48,384]{2,1,0:T(8,128)(2,1)S(1)}, bf16[4,48,384]{2,1,0:T(8,128)(2,1)S(1)}, u32[]{:S(2)}, u32[]{:S(2)}) collective-permute-start(bf16[4,48,384]{2,1,0:T(8,128)(2,1)S(1)} %get-tuple-element.158), channel_id=1, source_target_pairs={{0,16},{4,20},{8,24},{12,28},{16,0},{20,4},{24,8},{28,12},{1,17},{... | collective-permute-start | bytes 442376 | tf_op jit(solution)/shard_map/ppermute | solution.py:707
  68.3 6.3 %collective-permute-start.21 = (bf16[128,384]{1,0:T(8,128)(2,1)S(1)}, bf16[128,384]{1,0:T(8,128)(2,1)S(1)}, u32[]{:S(2)}, u32[]{:S(2)}) collective-permute-start(bf16[128,384]{1,0:T(8,128)(2,1)S(1)} %get-tuple-element.147), channel_id=1, source_target_pairs={{0,8},{4,12},{8,0},{12,4},{16,24},{20,28},{24,16},{28,20},{1,9},{5... | collective-permute-start | bytes 294920 | tf_op jit(solution)/shard_map/ppermute | solution.py:707
  68.8 12.4 %collective-permute-start.22 = (bf16[128,384]{1,0:T(8,128)(2,1)S(1)}, bf16[128,384]{1,0:T(8,128)(2,1)S(1)}, u32[]{:S(2)}, u32[]{:S(2)}) collective-permute-start(bf16[128,384]{1,0:T(8,128)(2,1)S(1)} %get-tuple-element.148), channel_id=1, source_target_pairs={{0,16},{4,20},{8,24},{12,28},{16,0},{20,4},{24,8},{28,12},{1,17},{... | collective-permute-start | bytes 294920 | tf_op jit(solution)/shard_map/ppermute | solution.py:707
  71.0 10.1 %collective-permute-start.23 = (bf16[128,384]{1,0:T(8,128)(2,1)S(1)}, bf16[128,384]{1,0:T(8,128)(2,1)S(1)}, u32[]{:S(2)}, u32[]{:S(2)}) collective-permute-start(bf16[128,384]{1,0:T(8,128)(2,1)S(1)} %get-tuple-element.149), channel_id=1, source_target_pairs={{0,24},{4,28},{8,16},{12,20},{16,8},{20,12},{24,0},{28,4},{1,25},{... | collective-permute-start | bytes 294920 | tf_op jit(solution)/shard_map/ppermute | solution.py:707
  82.3 11.3 %all-to-all-start = ((bf16[8,16,384]{2,1,0:T(8,128)(2,1)}), bf16[8,16,384]{2,1,0:T(8,128)(2,1)S(1)}, u32[]{:S(2)}, u32[]{:S(2)}) async-start(bf16[8,16,384]{2,1,0:T(8,128)(2,1)} %get-tuple-element.160), calls=%async_computation | async-start | bytes 196608 | tf_op jit(solution)/shard_map/all_to_all | solution.py:893
  85.8 9.5 %collective-permute-start.30 = (bf16[4,48,384]{2,1,0:T(8,128)(2,1)S(1)}, bf16[4,48,384]{2,1,0:T(8,128)(2,1)S(1)}, u32[]{:S(2)}, u32[]{:S(2)}) collective-permute-start(bf16[4,48,384]{2,1,0:T(8,128)(2,1)S(1)} %shard_map.318.refs_0_), channel_id=1, source_target_pairs={{0,8},{4,12},{8,0},{12,4},{16,24},{20,28},{24,16},{28,20},{1,9},{5... | collective-permute-start | bytes 442376 | tf_op jit(solution)/shard_map/ppermute | solution.py:707
  93.5 7.6 %collective-permute-start.29 = (bf16[8,16,384]{2,1,0:T(8,128)(2,1)S(1)}, bf16[8,16,384]{2,1,0:T(8,128)(2,1)S(1)}, u32[]{:S(2)}, u32[]{:S(2)}) collective-permute-start(bf16[8,16,384]{2,1,0:T(8,128)(2,1)S(1)} %all-to-all-done.refs_0_), channel_id=1, source_target_pairs={{0,3},{1,2},{2,1},{3,0},{4,7},{5,6},{6,5},{7,4},{8,11},{9,10},{10,... | collective-permute-start | bytes 294920 | tf_op jit(solution)/shard_map/ppermute | solution.py:702
  93.5 7.6 %collective-permute-start.28 = (bf16[8,16,384]{2,1,0:T(8,128)(2,1)S(1)}, bf16[8,16,384]{2,1,0:T(8,128)(2,1)S(1)}, u32[]{:S(2)}, u32[]{:S(2)}) collective-permute-start(bf16[8,16,384]{2,1,0:T(8,128)(2,1)S(1)} %all-to-all-done.refs_0_), channel_id=1, source_target_pairs={{0,2},{1,3},{2,0},{3,1},{4,6},{5,7},{6,4},{7,5},{8,10},{9,11},{10,... | collective-permute-start | bytes 294920 | tf_op jit(solution)/shard_map/ppermute | solution.py:702
  94.6 6.6 %collective-permute-start.27 = (bf16[8,16,384]{2,1,0:T(8,128)(2,1)S(1)}, bf16[8,16,384]{2,1,0:T(8,128)(2,1)S(1)}, u32[]{:S(2)}, u32[]{:S(2)}) collective-permute-start(bf16[8,16,384]{2,1,0:T(8,128)(2,1)S(1)} %all-to-all-done.refs_0_), channel_id=1, source_target_pairs={{0,1},{1,0},{2,3},{3,2},{4,5},{5,4},{6,7},{7,6},{8,9},{9,8},{10,11... | collective-permute-start | bytes 294920 | tf_op jit(solution)/shard_map/ppermute | solution.py:702

commit v6 on v5

--- a/solution.py
+++ b/solution.py
@@ -712,7 +712,10 @@
 
 
 def spread(x, second=()):
-    four, one, two = after([flip(x, 4), flip(x, 1), flip(x, 2)], *second)
+    four, one, two = flip(x, 4), flip(x, 1), flip(x, 2)
+    (one,) = after([one], *second)
+    (two,) = after([two], *second)
+    (four,) = after([four], *second)
     return [x, one, two, flip(two, 1), four, flip(four, 1), flip(four, 2), flip(one, 6)]
 
 

time: 107 us -> 107 us (level)
  transfers between devices with their start and end apart: 32 -> 32, of which waited for: 19 -> 20; matrix products, arithmetic and copies ran while one was open for 0% -> 0% of each run, Pallas kernels for 12% -> 12%
where the time goes in v6:
time: 107 us
  waiting for transfers between devices  44.7 us (42%)
  starting transfers between devices  35.9 us (34%)
  Pallas kernels  24.4 us (23%)
    ppermute x16, waiting for transfers between devices, flip(): return lax.ppermute(x, 'dp', [(i, i ^ k) for i in range(n)])  30.4 us
    pallas_call x15, Pallas kernels, call(): pl.pallas_call(kernel, out_shape=tuple(outs), in_specs=in_specs or [IN_VM...  24.4 us
    ppermute x16, starting transfers between devices, flip(): return lax.ppermute(x, 'dp', [(i, i ^ k) for i in range(n)])  22.9 us
    ppermute x12, starting transfers between devices, exchange(): lax.ppermute(x, axis, [(i, i ^ k) for i in range(n)])  7.61 us
    ppermute x12, waiting for transfers between devices, exchange(): lax.ppermute(x, axis, [(i, i ^ k) for i in range(n)])  7.57 us
    all_to_all x1, waiting for transfers between devices, per_device(): sums = lax.all_to_all(send, 'dp', 0, 0, tiled=True)  5.46 us
    all_to_all x1, starting transfers between devices, per_device(): sums = lax.all_to_all(send, 'dp', 0, 0, tiled=True)  3.54 us
  transfers between devices with their start and end apart: 32, of which 20 were waited for; matrix products, arithmetic and copies ran while one was open for 0% of the time, Pallas kernels for 12%

profile of v6, /device:TPU:0, one launch (start us, length us, event | category | flops | bytes accessed | tf_op | source)
XLA Modules:
  0.0 107.1 jit_solution(492419598191089258)
XLA Ops:
  0.7 0.0 copy-start.2
  0.7 1.1 convert_element_type.3.refs_3_
  1.7 4.1 %collective-permute-start.3 = (bf16[96,1152]{1,0:T(8,128)(2,1)S(1)}, bf16[96,1152]{1,0:T(8,128)(2,1)S(1)}, u32[]{:S(2)}, u32[]{:S(2)}) collective-permute-start(bf16[96,1152]{1,0:T(8,128)(2,1)S(1)} %convert_element_type.3.refs_3_), channel_id=1, source_target_pairs={{0,16},{4,20},{8,24},{12,28},{16,0},{20,4},{24,8},{28,12},{1,17},{... | collective-permute-start | bytes 663560 | tf_op jit(solution)/shard_map/ppermute | solution.py:707
  5.8 1.6 %collective-permute-start.1 = (bf16[96,1152]{1,0:T(8,128)(2,1)S(1)}, bf16[96,1152]{1,0:T(8,128)(2,1)S(1)}, u32[]{:S(2)}, u32[]{:S(2)}) collective-permute-start(bf16[96,1152]{1,0:T(8,128)(2,1)S(1)} %convert_element_type.3.refs_3_), channel_id=1, source_target_pairs={{0,8},{4,12},{8,0},{12,4},{16,24},{20,28},{24,16},{28,20},{1,9},{5... | collective-permute-start | bytes 663560 | tf_op jit(solution)/shard_map/ppermute | solution.py:707
  7.4 1.5 %collective-permute-start = (bf16[96,1152]{1,0:T(8,128)(2,1)S(1)}, bf16[96,1152]{1,0:T(8,128)(2,1)S(1)}, u32[]{:S(2)}, u32[]{:S(2)}) collective-permute-start(bf16[96,1152]{1,0:T(8,128)(2,1)S(1)} %convert_element_type.3.refs_3_), channel_id=1, source_target_pairs={{0,4},{4,0},{8,12},{12,8},{16,20},{20,16},{24,28},{28,24},{1,5},{5... | collective-permute-start | bytes 663560 | tf_op jit(solution)/shard_map/ppermute | solution.py:707
  8.9 2.6 %shard_map.306 = (bf16[256,1024]{1,0:T(8,128)(2,1)S(1)}, bf16[1024,768]{1,0:T(8,128)(2,1)S(1)}, bf16[1024,768]{1,0:T(8,128)(2,1)S(1)}, f32[1024,128]{1,0:T(8,128)S(1)}) custom-call(f32[16,1024]{1,0:T(8,128)} %bitcast.21, s32[2,1024]{1,0:T(2,128)} %bitcast.22, s32[1,1024]{1,0:T(1,128)} %refs_2_.2, s32[1,1024]{1,0:T(1,128)} %refs_7_.6, f32[224,768]{1,0:T(8,128)} %refs_9_.1, ...), custom_call_target="tpu_custom_call" | custom-call | flops 805306368 | bytes 4998144 | tf_op jit(solution)/shard_map/pallas_call | solution.py:55
  11.5 4.6 %collective-permute-done.3.refs_7_ = bf16[96,1152]{1,0:T(8,128)(2,1)S(1)} collective-permute-done((bf16[96,1152]{1,0:T(8,128)(2,1)S(1)}, bf16[96,1152]{1,0:T(8,128)(2,1)S(1)}, u32[]{:S(2)}, u32[]{:S(2)}) %collective-permute-start.3) | collective-permute-done | bytes 221216 | tf_op jit(solution)/shard_map/ppermute | solution.py:707
  16.1 0.2 collective-permute-done.1.refs_5_
  16.3 3.2 %collective-permute-start.6 = (bf16[96,1152]{1,0:T(8,128)(2,1)S(1)}, bf16[96,1152]{1,0:T(8,128)(2,1)S(1)}, u32[]{:S(2)}, u32[]{:S(2)}) collective-permute-start(bf16[96,1152]{1,0:T(8,128)(2,1)S(1)} %collective-permute-done.refs_4_), channel_id=1, source_target_pairs={{0,24},{4,28},{8,16},{12,20},{16,8},{20,12},{24,0},{28,4},{1,25},{... | collective-permute-start | bytes 663560 | tf_op jit(solution)/shard_map/ppermute | solution.py:707
  19.5 1.5 %collective-permute-start.2 = (bf16[96,1152]{1,0:T(8,128)(2,1)S(1)}, bf16[96,1152]{1,0:T(8,128)(2,1)S(1)}, u32[]{:S(2)}, u32[]{:S(2)}) collective-permute-start(bf16[96,1152]{1,0:T(8,128)(2,1)S(1)} %collective-permute-done.1.refs_5_), channel_id=1, source_target_pairs={{0,4},{4,0},{8,12},{12,8},{16,20},{20,16},{24,28},{28,24},{1,5},{5... | collective-permute-start | bytes 663560 | tf_op jit(solution)/shard_map/ppermute | solution.py:707
  21.0 0.5 collective-permute-start.4
  21.6 4.9 %collective-permute-done.6.refs_10_ = bf16[96,1152]{1,0:T(8,128)(2,1)S(1)} collective-permute-done((bf16[96,1152]{1,0:T(8,128)(2,1)S(1)}, bf16[96,1152]{1,0:T(8,128)(2,1)S(1)}, u32[]{:S(2)}, u32[]{:S(2)}) %collective-permute-start.6) | collective-permute-done | bytes 221216 | tf_op jit(solution)/shard_map/ppermute | solution.py:707
  26.4 1.4 %collective-permute-done.2.refs_6_ = bf16[96,1152]{1,0:T(8,128)(2,1)S(1)} collective-permute-done((bf16[96,1152]{1,0:T(8,128)(2,1)S(1)}, bf16[96,1152]{1,0:T(8,128)(2,1)S(1)}, u32[]{:S(2)}, u32[]{:S(2)}) %collective-permute-start.2) | collective-permute-done | bytes 221216 | tf_op jit(solution)/shard_map/ppermute | solution.py:707
  27.9 2.1 %collective-permute-done.5.refs_9_ = bf16[96,1152]{1,0:T(8,128)(2,1)S(1)} collective-permute-done((bf16[96,1152]{1,0:T(8,128)(2,1)S(1)}, bf16[96,1152]{1,0:T(8,128)(2,1)S(1)}, u32[]{:S(2)}, u32[]{:S(2)}) %collective-permute-start.5) | collective-permute-done | bytes 221216 | tf_op jit(solution)/shard_map/ppermute | solution.py:707
  30.0 1.4 %collective-permute-done.4.refs_8_ = bf16[96,1152]{1,0:T(8,128)(2,1)S(1)} collective-permute-done((bf16[96,1152]{1,0:T(8,128)(2,1)S(1)}, bf16[96,1152]{1,0:T(8,128)(2,1)S(1)}, u32[]{:S(2)}, u32[]{:S(2)}) %collective-permute-start.4) | collective-permute-done | bytes 221216 | tf_op jit(solution)/shard_map/ppermute | solution.py:707
  31.4 2.5 %shard_map.307 = (bf16[24,768]{1,0:T(8,128)(2,1)S(1)}, bf16[192,1024]{1,0:T(8,128)(2,1)S(1)}, bf16[1024,256]{1,0:T(8,128)(2,1)S(1)}, bf16[24,256]{1,0:T(8,128)(2...) custom-call(bf16[1024,768]{1,0:T(8,128)(2,1)S(1)} %get-tuple-element, ...), custom_call_target="tpu_custom_call" | custom-call | flops 805306368 | bytes 6517760 | tf_op jit(solution)/shard_map/pallas_call | solution.py:55
  33.8 0.1 collective-permute-start.9
  33.9 1.6 %collective-permute-start.8 = (bf16[24,768]{1,0:T(8,128)(2,1)S(1)}, bf16[24,768]{1,0:T(8,128)(2,1)S(1)}, u32[]{:S(2)}, u32[]{:S(2)}) collective-permute-start(bf16[24,768]{1,0:T(8,128)(2,1)S(1)} %get-tuple-element.111.refs_0_), channel_id=1, source_target_pairs={{0,2},{1,3},{2,0},{3,1},{4,6},{5,7},{6,4},{7,5},{8,10},{9,11},{10,... | collective-permute-start | bytes 110600 | tf_op jit(solution)/shard_map/ppermute | solution.py:702
  35.5 0.3 collective-permute-start.7
  35.7 1.8 %collective-permute-done.9.refs_3_ = bf16[24,768]{1,0:T(8,128)(2,1)S(1)} collective-permute-done((bf16[24,768]{1,0:T(8,128)(2,1)S(1)}, bf16[24,768]{1,0:T(8,128)(2,1)S(1)}, u32[]{:S(2)}, u32[]{:S(2)}) %collective-permute-start.9) | collective-permute-done | bytes 36896 | tf_op jit(solution)/shard_map/ppermute | solution.py:702
  37.6 0.5 collective-permute-done.8.refs_2_
  38.1 0.6 shard_map.308
  38.7 1.1 collective-permute-start.12
  39.7 0.9 collective-permute-start.11
  40.6 1.5 %collective-permute-done.12.refs_3_ = bf16[24,768]{1,0:T(8,128)(2,1)S(1)} collective-permute-done((bf16[24,768]{1,0:T(8,128)(2,1)S(1)}, bf16[24,768]{1,0:T(8,128)(2,1)S(1)}, u32[]{:S(2)}, u32[]{:S(2)}) %collective-permute-start.12) | collective-permute-done | bytes 36896 | tf_op jit(solution)/shard_map/ppermute | solution.py:702
  42.1 1.6 %collective-permute-done.11.refs_2_ = bf16[24,768]{1,0:T(8,128)(2,1)S(1)} collective-permute-done((bf16[24,768]{1,0:T(8,128)(2,1)S(1)}, bf16[24,768]{1,0:T(8,128)(2,1)S(1)}, u32[]{:S(2)}, u32[]{:S(2)}) %collective-permute-start.11) | collective-permute-done | bytes 36896 | tf_op jit(solution)/shard_map/ppermute | solution.py:702
  43.8 1.6 %shard_map.309 = (bf16[24,768]{1,0:T(8,128)(2,1)S(1)}, bf16[24,768]{1,0:T(8,128)(2,1)S(1)}, f32[24,128]{1,0:T(8,128)S(1)}, f32[24,768]{1,0:T(8,128)S(1)}, bf16[2...) custom-call(bf16[24,768]{1,0:T(8,128)(2,1)S(1)} %get-tuple-element.113.refs_0_, ...), custom_call_target="tpu_custom_call" | custom-call | flops 56623104 | bytes 3466336 | tf_op jit(solution)/shard_map/pallas_call | solution.py:55
  45.3 0.7 collective-permute-start.15
  46.0 0.8 collective-permute-start.14
  46.9 0.4 collective-permute-start.13
  47.2 0.6 shard_map.311
  47.8 1.3 %collective-permute-done.15.refs_3_ = bf16[24,768]{1,0:T(8,128)(2,1)S(1)} collective-permute-done((bf16[24,768]{1,0:T(8,128)(2,1)S(1)}, bf16[24,768]{1,0:T(8,128)(2,1)S(1)}, u32[]{:S(2)}, u32[]{:S(2)}) %collective-permute-start.15) | collective-permute-done | bytes 36896 | tf_op jit(solution)/shard_map/ppermute | solution.py:702
  49.1 0.8 collective-permute-done.14.refs_2_
  50.0 1.5 %collective-permute-start.24 = (bf16[9,48,384]{2,1,0:T(8,128)(2,1)S(1)}, bf16[9,48,384]{2,1,0:T(8,128)(2,1)S(1)}, u32[]{:S(2)}, u32[]{:S(2)}) collective-permute-start(bf16[9,48,384]{2,1,0:T(8,128)(2,1)S(1)} %get-tuple-element.152), channel_id=1, source_target_pairs={{0,4},{4,0},{8,12},{12,8},{16,20},{20,16},{24,28},{28,24},{1,5},{5... | collective-permute-start | bytes 995336 | tf_op jit(solution)/shard_map/ppermute | solution.py:707
  51.5 2.3 %shard_map.310 = (bf16[4,96,384]{2,1,0:T(8,128)(2,1)S(1)}, bf16[4,96,384]{2,1,0:T(8,128)(2,1)S(1)}, f32[8,256]{1,0:T(8,128)S(1)}, f32[8,768]{1,0:T(8,128)S(1)}, ...) custom-call(bf16[24,768]{1,0:T(8,128)(2,1)S(1)} %get-tuple-element.116.refs_0_, ...), custom_call_target="tpu_custom_call" | custom-call | flops 805306368 | bytes 5231616 | tf_op jit(solution)/shard_map/pallas_call | solution.py:55
  53.8 0.6 collective-permute-start.16
  54.4 1.1 %shard_map.312 = (bf16[64,768]{1,0:T(8,128)(2,1)S(1)}, bf16[64,768]{1,0:T(8,128)(2,1)S(1)}, bf16[64,768]{1,0:T(8,128)(2,1)S(1)}, bf16[64,768]{1,0:T(8,128)(2,1)S(1)}) custom-call(bf16[256,1024]{1,0:T(8,128)(2,1)S(1)} %get-tuple-element.125.refs_0_, bf16[256,768]{1,0:T(8,128)(2,1)S(1)} %get-tuple-element.132.refs_1_, ...), custom_call_target="tpu_custom_call" | custom-call | flops 805306368 | bytes 4019200 | tf_op jit(solution)/shard_map/pallas_call | solution.py:55
  55.5 0.1 collective-permute-start.17
  55.6 1.1 %collective-permute-start.18 = (bf16[64,768]{1,0:T(8,128)(2,1)S(1)}, bf16[64,768]{1,0:T(8,128)(2,1)S(1)}, u32[]{:S(2)}, u32[]{:S(2)}) collective-permute-start(bf16[64,768]{1,0:T(8,128)(2,1)S(1)} %get-tuple-element.139), channel_id=1, source_target_pairs={{0,2},{1,3},{2,0},{3,1},{4,6},{5,7},{6,4},{7,5},{8,10},{9,11},{10,... | collective-permute-start | bytes 294920 | tf_op jit(solution)/shard_map/ppermute | solution.py:857
  56.7 0.7 collective-permute-start.19
  57.4 3.3 %collective-permute-done.24.came = bf16[9,48,384]{2,1,0:T(8,128)(2,1)S(1)} collective-permute-done((bf16[9,48,384]{2,1,0:T(8,128)(2,1)S(1)}, bf16[9,48,384]{2,1,0:T(8,128)(2,1)S(1)}, u32[]{:S(2)}, u32[]{:S(2)}) %collective-permute-start.24) | collective-permute-done | bytes 331808 | tf_op jit(solution)/shard_map/ppermute | solution.py:707
  60.7 0.1 shard_map.315
  60.8 0.3 collective-permute-start.25
  61.1 0.1 collective-permute-done.18.refs_2_
  61.2 1.2 %collective-permute-done.19.refs_3_ = bf16[64,768]{1,0:T(8,128)(2,1)S(1)} collective-permute-done((bf16[64,768]{1,0:T(8,128)(2,1)S(1)}, bf16[64,768]{1,0:T(8,128)(2,1)S(1)}, u32[]{:S(2)}, u32[]{:S(2)}) %collective-permute-start.19) | collective-permute-done | bytes 98336 | tf_op jit(solution)/shard_map/ppermute | solution.py:857
  62.4 0.1 shard_map.313
  62.5 1.6 %collective-permute-start.20 = (bf16[4,32,384]{2,1,0:T(8,128)(2,1)S(1)}, bf16[4,32,384]{2,1,0:T(8,128)(2,1)S(1)}, u32[]{:S(2)}, u32[]{:S(2)}) collective-permute-start(bf16[4,32,384]{2,1,0:T(8,128)(2,1)S(1)} %get-tuple-element.145), channel_id=1, source_target_pairs={{0,4},{4,0},{8,12},{12,8},{16,20},{20,16},{24,28},{28,24},{1,5},{5... | collective-permute-start | bytes 294920 | tf_op jit(solution)/shard_map/ppermute | solution.py:707
  64.1 1.9 %collective-permute-done.25.came = bf16[2,96,384]{2,1,0:T(8,128)(2,1)S(1)} collective-permute-done((bf16[2,96,384]{2,1,0:T(8,128)(2,1)S(1)}, bf16[2,96,384]{2,1,0:T(8,128)(2,1)S(1)}, u32[]{:S(2)}, u32[]{:S(2)}) %collective-permute-start.25) | collective-permute-done | bytes 147488 | tf_op jit(solution)/shard_map/ppermute | solution.py:707
  66.1 0.1 collective-permute-start.26
  66.1 1.7 %collective-permute-done.20.table_came = bf16[4,32,384]{2,1,0:T(8,128)(2,1)S(1)} collective-permute-done((bf16[4,32,384]{2,1,0:T(8,128)(2,1)S(1)}, bf16[4,32,384]{2,1,0:T(8,128)(2,1)S(1)}, u32[]{:S(2)}, u32[]{:S(2)}) %collective-permute-start.20) | collective-permute-done | bytes 98336 | tf_op jit(solution)/shard_map/ppermute | solution.py:707
  67.9 0.2 shard_map.314
  68.1 0.5 collective-permute-start.21
  68.6 3.5 %collective-permute-start.22 = (bf16[128,384]{1,0:T(8,128)(2,1)S(1)}, bf16[128,384]{1,0:T(8,128)(2,1)S(1)}, u32[]{:S(2)}, u32[]{:S(2)}) collective-permute-start(bf16[128,384]{1,0:T(8,128)(2,1)S(1)} %get-tuple-element.148), channel_id=1, source_target_pairs={{0,16},{4,20},{8,24},{12,28},{16,0},{20,4},{24,8},{28,12},{1,17},{... | collective-permute-start | bytes 294920 | tf_op jit(solution)/shard_map/ppermute | solution.py:707
  72.0 0.5 collective-permute-start.23
  72.6 2.4 %collective-permute-done.21.refs_1_ = bf16[128,384]{1,0:T(8,128)(2,1)S(1)} collective-permute-done((bf16[128,384]{1,0:T(8,128)(2,1)S(1)}, bf16[128,384]{1,0:T(8,128)(2,1)S(1)}, u32[]{:S(2)}, u32[]{:S(2)}) %collective-permute-start.21) | collective-permute-done | bytes 98336 | tf_op jit(solution)/shard_map/ppermute | solution.py:707
  74.9 6.6 %collective-permute-done.22.refs_2_ = bf16[128,384]{1,0:T(8,128)(2,1)S(1)} collective-permute-done((bf16[128,384]{1,0:T(8,128)(2,1)S(1)}, bf16[128,384]{1,0:T(8,128)(2,1)S(1)}, u32[]{:S(2)}, u32[]{:S(2)}) %collective-permute-start.22) | collective-permute-done | bytes 98336 | tf_op jit(solution)/shard_map/ppermute | solution.py:707
  81.5 1.1 %shard_map.317 = (f32[6,96,192]{2,1,0:T(8,128)S(1)}, bf16[8,16,384]{2,1,0:T(8,128)(2,1)}, f32[8,128]{1,0:T(8,128)S(1)}, f32[8,384]{1,0:T(8,128)S(1)}) custom-call(bf16[128,384]{1,0:T(8,128)(2,1)S(1)} %get-tuple-element.146.refs_0_, bf16[128,384]{1,0:T(8,128)(2,1)S(1)} %collective-permute-done.21.refs_1_, ...), custom_call_target="tpu_custom_call" | custom-call | flops 50331648 | bytes 1213440 | tf_op jit(solution)/shard_map/pallas_call | solution.py:55
  82.6 3.5 %all-to-all-start = ((bf16[8,16,384]{2,1,0:T(8,128)(2,1)}), bf16[8,16,384]{2,1,0:T(8,128)(2,1)S(1)}, u32[]{:S(2)}, u32[]{:S(2)}) async-start(bf16[8,16,384]{2,1,0:T(8,128)(2,1)} %get-tuple-element.160), calls=%async_computation | async-start | bytes 196608 | tf_op jit(solution)/shard_map/all_to_all | solution.py:896
  86.2 1.9 %collective-permute-start.30 = (bf16[4,48,384]{2,1,0:T(8,128)(2,1)S(1)}, bf16[4,48,384]{2,1,0:T(8,128)(2,1)S(1)}, u32[]{:S(2)}, u32[]{:S(2)}) collective-permute-start(bf16[4,48,384]{2,1,0:T(8,128)(2,1)S(1)} %shard_map.318.refs_0_), channel_id=1, source_target_pairs={{0,8},{4,12},{8,0},{12,4},{16,24},{20,28},{24,16},{28,20},{1,9},{5... | collective-permute-start | bytes 442376 | tf_op jit(solution)/shard_map/ppermute | solution.py:707
  88.1 5.5 %all-to-all-done.refs_0_ = bf16[8,16,384]{2,1,0:T(8,128)(2,1)S(1)} async-done(((bf16[8,16,384]{2,1,0:T(8,128)(2,1)}), bf16[8,16,384]{2,1,0:T(8,128)(2,1)S(1)}, u32[]{:S(2)}, u32[]{:S(2)}) %all-to-all-start) | async-done | bytes 98336 | tf_op jit(solution)/shard_map/all_to_all | solution.py:896
  93.6 1.0 collective-permute-start.28
  94.6 0.8 collective-permute-start.27
  95.4 5.7 %shard_map.319 = (f32[768,768]{1,0:T(8,128)S(1)}, f32[8,128]{1,0:T(8,128)S(1)}, f32[6,96,96]{2,1,0:T(8,128)S(1)}, f32[6,192,192]{2,1,0:T(8,128)S(1)}, f32[96,115...) custom-call(bf16[4,48,384]{2,1,0:T(8,128)(2,1)S(1)} %shard_map.318.r, ...), custom_call_target="tpu_custom_call" | custom-call | flops 452984832 | bytes 26500096 | tf_op jit(solution)/shard_map/pallas_call | solution.py:55
  101.2 5.7 %shard_map.320 = (f32[1,1]{1,0:T(1,128)}, f32[1,1]{1,0:T(1,128)}, f32[1,1]{1,0:T(1,128)}, f32[96,1152]{1,0:T(8,128)}, f32[96,1152]{1,0:T(8,128)}, /*index=5*/f32...) custom-call(bf16[8,16,384]{2,1,0:T(8,128)(2,1)S(1)} %all-to-all-done, ...), custom_call_target="tpu_custom_call" | custom-call | flops 11796480 | bytes 26335244 | tf_op jit(solution)/shard_map/pallas_call | solution.py:55
  (24 shorter events, 0.1 us)
Async XLA Ops:
  0.6 30.7 %copy-start.1 = (f32[11,768]{1,0:T(8,128)S(1)}, f32[11,768]{1,0:T(8,128)}, u32[]{:S(2)}) copy-start(f32[11,768]{1,0:T(8,128)} %refs_15_.1) | copy-start | bytes 101380
  0.7 30.7 %copy-start.2 = (s32[1,1024]{1,0:T(1,128)S(1)}, s32[1,1024]{1,0:T(1,128)}, u32[]{:S(2)}) copy-start(s32[1,1024]{1,0:T(1,128)} %refs_7_.6) | copy-start | bytes 12292
  1.7 14.4 %collective-permute-start.3 = (bf16[96,1152]{1,0:T(8,128)(2,1)S(1)}, bf16[96,1152]{1,0:T(8,128)(2,1)S(1)}, u32[]{:S(2)}, u32[]{:S(2)}) collective-permute-start(bf16[96,1152]{1,0:T(8,128)(2,1)S(1)} %convert_element_type.3.refs_3_), channel_id=1, source_target_pairs={{0,16},{4,20},{8,24},{12,28},{16,0},{20,4},{24,8},{28,12},{1,17},{... | collective-permute-start | bytes 663560 | tf_op jit(solution)/shard_map/ppermute | solution.py:707
  5.8 10.5 %collective-permute-start.1 = (bf16[96,1152]{1,0:T(8,128)(2,1)S(1)}, bf16[96,1152]{1,0:T(8,128)(2,1)S(1)}, u32[]{:S(2)}, u32[]{:S(2)}) collective-permute-start(bf16[96,1152]{1,0:T(8,128)(2,1)S(1)} %convert_element_type.3.refs_3_), channel_id=1, source_target_pairs={{0,8},{4,12},{8,0},{12,4},{16,24},{20,28},{24,16},{28,20},{1,9},{5... | collective-permute-start | bytes 663560 | tf_op jit(solution)/shard_map/ppermute | solution.py:707
  7.4 8.9 %collective-permute-start = (bf16[96,1152]{1,0:T(8,128)(2,1)S(1)}, bf16[96,1152]{1,0:T(8,128)(2,1)S(1)}, u32[]{:S(2)}, u32[]{:S(2)}) collective-permute-start(bf16[96,1152]{1,0:T(8,128)(2,1)S(1)} %convert_element_type.3.refs_3_), channel_id=1, source_target_pairs={{0,4},{4,0},{8,12},{12,8},{16,20},{20,16},{24,28},{28,24},{1,5},{5... | collective-permute-start | bytes 663560 | tf_op jit(solution)/shard_map/ppermute | solution.py:707
  11.5 32.2 %copy-start = (f32[768,768]{1,0:T(8,128)S(1)}, f32[768,768]{1,0:T(8,128)}, u32[]{:S(2)}) copy-start(f32[768,768]{1,0:T(8,128)} %refs_12_.1) | copy-start | bytes 7077892
  11.5 32.2 %copy-start.3 = (f32[1,24]{1,0:T(1,128)S(1)}, f32[1,24]{1,0:T(1,128)}, u32[]{:S(2)}) copy-start(f32[1,24]{1,0:T(1,128)} %refs_7_.4) | copy-start | bytes 292
  16.3 10.1 %collective-permute-start.6 = (bf16[96,1152]{1,0:T(8,128)(2,1)S(1)}, bf16[96,1152]{1,0:T(8,128)(2,1)S(1)}, u32[]{:S(2)}, u32[]{:S(2)}) collective-permute-start(bf16[96,1152]{1,0:T(8,128)(2,1)S(1)} %collective-permute-done.refs_4_), channel_id=1, source_target_pairs={{0,24},{4,28},{8,16},{12,20},{16,8},{20,12},{24,0},{28,4},{1,25},{... | collective-permute-start | bytes 663560 | tf_op jit(solution)/shard_map/ppermute | solution.py:707
  19.5 8.3 %collective-permute-start.2 = (bf16[96,1152]{1,0:T(8,128)(2,1)S(1)}, bf16[96,1152]{1,0:T(8,128)(2,1)S(1)}, u32[]{:S(2)}, u32[]{:S(2)}) collective-permute-start(bf16[96,1152]{1,0:T(8,128)(2,1)S(1)} %collective-permute-done.1.refs_5_), channel_id=1, source_target_pairs={{0,4},{4,0},{8,12},{12,8},{16,20},{20,16},{24,28},{28,24},{1,5},{5... | collective-permute-start | bytes 663560 | tf_op jit(solution)/shard_map/ppermute | solution.py:707
  21.0 9.0 %collective-permute-start.5 = (bf16[96,1152]{1,0:T(8,128)(2,1)S(1)}, bf16[96,1152]{1,0:T(8,128)(2,1)S(1)}, u32[]{:S(2)}, u32[]{:S(2)}) collective-permute-start(bf16[96,1152]{1,0:T(8,128)(2,1)S(1)} %collective-permute-done.3.refs_7_), channel_id=1, source_target_pairs={{0,8},{4,12},{8,0},{12,4},{16,24},{20,28},{24,16},{28,20},{1,9},{5... | collective-permute-start | bytes 663560 | tf_op jit(solution)/shard_map/ppermute | solution.py:707
  21.0 10.3 %collective-permute-start.4 = (bf16[96,1152]{1,0:T(8,128)(2,1)S(1)}, bf16[96,1152]{1,0:T(8,128)(2,1)S(1)}, u32[]{:S(2)}, u32[]{:S(2)}) collective-permute-start(bf16[96,1152]{1,0:T(8,128)(2,1)S(1)} %collective-permute-done.3.refs_7_), channel_id=1, source_target_pairs={{0,4},{4,0},{8,12},{12,8},{16,20},{20,16},{24,28},{28,24},{1,5},{5... | collective-permute-start | bytes 663560 | tf_op jit(solution)/shard_map/ppermute | solution.py:707
  33.8 3.8 %collective-permute-start.9 = (bf16[24,768]{1,0:T(8,128)(2,1)S(1)}, bf16[24,768]{1,0:T(8,128)(2,1)S(1)}, u32[]{:S(2)}, u32[]{:S(2)}) collective-permute-start(bf16[24,768]{1,0:T(8,128)(2,1)S(1)} %get-tuple-element.111.refs_0_), channel_id=1, source_target_pairs={{0,3},{1,2},{2,1},{3,0},{4,7},{5,6},{6,5},{7,4},{8,11},{9,10},{10,... | collective-permute-start | bytes 110600 | tf_op jit(solution)/shard_map/ppermute | solution.py:702
  33.9 4.2 %collective-permute-start.8 = (bf16[24,768]{1,0:T(8,128)(2,1)S(1)}, bf16[24,768]{1,0:T(8,128)(2,1)S(1)}, u32[]{:S(2)}, u32[]{:S(2)}) collective-permute-start(bf16[24,768]{1,0:T(8,128)(2,1)S(1)} %get-tuple-element.111.refs_0_), channel_id=1, source_target_pairs={{0,2},{1,3},{2,0},{3,1},{4,6},{5,7},{6,4},{7,5},{8,10},{9,11},{10,... | collective-permute-start | bytes 110600 | tf_op jit(solution)/shard_map/ppermute | solution.py:702
  35.5 2.6 %collective-permute-start.7 = (bf16[24,768]{1,0:T(8,128)(2,1)S(1)}, bf16[24,768]{1,0:T(8,128)(2,1)S(1)}, u32[]{:S(2)}, u32[]{:S(2)}) collective-permute-start(bf16[24,768]{1,0:T(8,128)(2,1)S(1)} %get-tuple-element.111.refs_0_), channel_id=1, source_target_pairs={{0,1},{1,0},{2,3},{3,2},{4,5},{5,4},{6,7},{7,6},{8,9},{9,8},{10,11... | collective-permute-start | bytes 110600 | tf_op jit(solution)/shard_map/ppermute | solution.py:702
  38.7 3.4 %collective-permute-start.12 = (bf16[24,768]{1,0:T(8,128)(2,1)S(1)}, bf16[24,768]{1,0:T(8,128)(2,1)S(1)}, u32[]{:S(2)}, u32[]{:S(2)}) collective-permute-start(bf16[24,768]{1,0:T(8,128)(2,1)S(1)} %get-tuple-element.113.refs_0_), channel_id=1, source_target_pairs={{0,3},{1,2},{2,1},{3,0},{4,7},{5,6},{6,5},{7,4},{8,11},{9,10},{10,... | collective-permute-start | bytes 110600 | tf_op jit(solution)/shard_map/ppermute | solution.py:702
  39.7 4.0 %collective-permute-start.11 = (bf16[24,768]{1,0:T(8,128)(2,1)S(1)}, bf16[24,768]{1,0:T(8,128)(2,1)S(1)}, u32[]{:S(2)}, u32[]{:S(2)}) collective-permute-start(bf16[24,768]{1,0:T(8,128)(2,1)S(1)} %get-tuple-element.113.refs_0_), channel_id=1, source_target_pairs={{0,2},{1,3},{2,0},{3,1},{4,6},{5,7},{6,4},{7,5},{8,10},{9,11},{10,... | collective-permute-start | bytes 110600 | tf_op jit(solution)/shard_map/ppermute | solution.py:702
  40.6 3.1 %collective-permute-start.10 = (bf16[24,768]{1,0:T(8,128)(2,1)S(1)}, bf16[24,768]{1,0:T(8,128)(2,1)S(1)}, u32[]{:S(2)}, u32[]{:S(2)}) collective-permute-start(bf16[24,768]{1,0:T(8,128)(2,1)S(1)} %get-tuple-element.113.refs_0_), channel_id=1, source_target_pairs={{0,1},{1,0},{2,3},{3,2},{4,5},{5,4},{6,7},{7,6},{8,9},{9,8},{10,11... | collective-permute-start | bytes 110600 | tf_op jit(solution)/shard_map/ppermute | solution.py:702
  45.3 3.8 %collective-permute-start.15 = (bf16[24,768]{1,0:T(8,128)(2,1)S(1)}, bf16[24,768]{1,0:T(8,128)(2,1)S(1)}, u32[]{:S(2)}, u32[]{:S(2)}) collective-permute-start(bf16[24,768]{1,0:T(8,128)(2,1)S(1)} %get-tuple-element.116.refs_0_), channel_id=1, source_target_pairs={{0,3},{1,2},{2,1},{3,0},{4,7},{5,6},{6,5},{7,4},{8,11},{9,10},{10,... | collective-permute-start | bytes 110600 | tf_op jit(solution)/shard_map/ppermute | solution.py:702
  46.0 4.0 %collective-permute-start.14 = (bf16[24,768]{1,0:T(8,128)(2,1)S(1)}, bf16[24,768]{1,0:T(8,128)(2,1)S(1)}, u32[]{:S(2)}, u32[]{:S(2)}) collective-permute-start(bf16[24,768]{1,0:T(8,128)(2,1)S(1)} %get-tuple-element.116.refs_0_), channel_id=1, source_target_pairs={{0,2},{1,3},{2,0},{3,1},{4,6},{5,7},{6,4},{7,5},{8,10},{9,11},{10,... | collective-permute-start | bytes 110600 | tf_op jit(solution)/shard_map/ppermute | solution.py:702
  46.9 3.1 %collective-permute-start.13 = (bf16[24,768]{1,0:T(8,128)(2,1)S(1)}, bf16[24,768]{1,0:T(8,128)(2,1)S(1)}, u32[]{:S(2)}, u32[]{:S(2)}) collective-permute-start(bf16[24,768]{1,0:T(8,128)(2,1)S(1)} %get-tuple-element.116.refs_0_), channel_id=1, source_target_pairs={{0,1},{1,0},{2,3},{3,2},{4,5},{5,4},{6,7},{7,6},{8,9},{9,8},{10,11... | collective-permute-start | bytes 110600 | tf_op jit(solution)/shard_map/ppermute | solution.py:702
  50.0 10.7 %collective-permute-start.24 = (bf16[9,48,384]{2,1,0:T(8,128)(2,1)S(1)}, bf16[9,48,384]{2,1,0:T(8,128)(2,1)S(1)}, u32[]{:S(2)}, u32[]{:S(2)}) collective-permute-start(bf16[9,48,384]{2,1,0:T(8,128)(2,1)S(1)} %get-tuple-element.152), channel_id=1, source_target_pairs={{0,4},{4,0},{8,12},{12,8},{16,20},{20,16},{24,28},{28,24},{1,5},{5... | collective-permute-start | bytes 995336 | tf_op jit(solution)/shard_map/ppermute | solution.py:707
  53.8 14.1 %collective-permute-start.16 = (bf16[4,96,384]{2,1,0:T(8,128)(2,1)S(1)}, bf16[4,96,384]{2,1,0:T(8,128)(2,1)S(1)}, u32[]{:S(2)}, u32[]{:S(2)}) collective-permute-start(bf16[4,96,384]{2,1,0:T(8,128)(2,1)S(1)} %get-tuple-element.124), channel_id=1, source_target_pairs={{0,4},{4,0},{8,12},{12,8},{16,20},{20,16},{24,28},{28,24},{1,5},{5... | collective-permute-start | bytes 884744 | tf_op jit(solution)/shard_map/ppermute | solution.py:707
  55.5 5.7 %collective-permute-start.17 = (bf16[64,768]{1,0:T(8,128)(2,1)S(1)}, bf16[64,768]{1,0:T(8,128)(2,1)S(1)}, u32[]{:S(2)}, u32[]{:S(2)}) collective-permute-start(bf16[64,768]{1,0:T(8,128)(2,1)S(1)} %get-tuple-element.138), channel_id=1, source_target_pairs={{0,1},{1,0},{2,3},{3,2},{4,5},{5,4},{6,7},{7,6},{8,9},{9,8},{10,11... | collective-permute-start | bytes 294920 | tf_op jit(solution)/shard_map/ppermute | solution.py:857
  55.6 5.7 %collective-permute-start.18 = (bf16[64,768]{1,0:T(8,128)(2,1)S(1)}, bf16[64,768]{1,0:T(8,128)(2,1)S(1)}, u32[]{:S(2)}, u32[]{:S(2)}) collective-permute-start(bf16[64,768]{1,0:T(8,128)(2,1)S(1)} %get-tuple-element.139), channel_id=1, source_target_pairs={{0,2},{1,3},{2,0},{3,1},{4,6},{5,7},{6,4},{7,5},{8,10},{9,11},{10,... | collective-permute-start | bytes 294920 | tf_op jit(solution)/shard_map/ppermute | solution.py:857
  56.7 5.7 %collective-permute-start.19 = (bf16[64,768]{1,0:T(8,128)(2,1)S(1)}, bf16[64,768]{1,0:T(8,128)(2,1)S(1)}, u32[]{:S(2)}, u32[]{:S(2)}) collective-permute-start(bf16[64,768]{1,0:T(8,128)(2,1)S(1)} %get-tuple-element.140), channel_id=1, source_target_pairs={{0,3},{1,2},{2,1},{3,0},{4,7},{5,6},{6,5},{7,4},{8,11},{9,10},{10,... | collective-permute-start | bytes 294920 | tf_op jit(solution)/shard_map/ppermute | solution.py:857
  60.8 5.2 %collective-permute-start.25 = (bf16[2,96,384]{2,1,0:T(8,128)(2,1)S(1)}, bf16[2,96,384]{2,1,0:T(8,128)(2,1)S(1)}, u32[]{:S(2)}, u32[]{:S(2)}) collective-permute-start(bf16[2,96,384]{2,1,0:T(8,128)(2,1)S(1)} %get-tuple-element.155), channel_id=1, source_target_pairs={{0,8},{4,12},{8,0},{12,4},{16,24},{20,28},{24,16},{28,20},{1,9},{5... | collective-permute-start | bytes 442376 | tf_op jit(solution)/shard_map/ppermute | solution.py:707
  62.5 5.3 %collective-permute-start.20 = (bf16[4,32,384]{2,1,0:T(8,128)(2,1)S(1)}, bf16[4,32,384]{2,1,0:T(8,128)(2,1)S(1)}, u32[]{:S(2)}, u32[]{:S(2)}) collective-permute-start(bf16[4,32,384]{2,1,0:T(8,128)(2,1)S(1)} %get-tuple-element.145), channel_id=1, source_target_pairs={{0,4},{4,0},{8,12},{12,8},{16,20},{20,16},{24,28},{28,24},{1,5},{5... | collective-permute-start | bytes 294920 | tf_op jit(solution)/shard_map/ppermute | solution.py:707
  66.1 15.4 %collective-permute-start.26 = (bf16[4,48,384]{2,1,0:T(8,128)(2,1)S(1)}, bf16[4,48,384]{2,1,0:T(8,128)(2,1)S(1)}, u32[]{:S(2)}, u32[]{:S(2)}) collective-permute-start(bf16[4,48,384]{2,1,0:T(8,128)(2,1)S(1)} %get-tuple-element.158), channel_id=1, source_target_pairs={{0,16},{4,20},{8,24},{12,28},{16,0},{20,4},{24,8},{28,12},{1,17},{... | collective-permute-start | bytes 442376 | tf_op jit(solution)/shard_map/ppermute | solution.py:707
  68.1 6.8 %collective-permute-start.21 = (bf16[128,384]{1,0:T(8,128)(2,1)S(1)}, bf16[128,384]{1,0:T(8,128)(2,1)S(1)}, u32[]{:S(2)}, u32[]{:S(2)}) collective-permute-start(bf16[128,384]{1,0:T(8,128)(2,1)S(1)} %get-tuple-element.147), channel_id=1, source_target_pairs={{0,8},{4,12},{8,0},{12,4},{16,24},{20,28},{24,16},{28,20},{1,9},{5... | collective-permute-start | bytes 294920 | tf_op jit(solution)/shard_map/ppermute | solution.py:707
  68.6 12.9 %collective-permute-start.22 = (bf16[128,384]{1,0:T(8,128)(2,1)S(1)}, bf16[128,384]{1,0:T(8,128)(2,1)S(1)}, u32[]{:S(2)}, u32[]{:S(2)}) collective-permute-start(bf16[128,384]{1,0:T(8,128)(2,1)S(1)} %get-tuple-element.148), channel_id=1, source_target_pairs={{0,16},{4,20},{8,24},{12,28},{16,0},{20,4},{24,8},{28,12},{1,17},{... | collective-permute-start | bytes 294920 | tf_op jit(solution)/shard_map/ppermute | solution.py:707
  72.0 9.4 %collective-permute-start.23 = (bf16[128,384]{1,0:T(8,128)(2,1)S(1)}, bf16[128,384]{1,0:T(8,128)(2,1)S(1)}, u32[]{:S(2)}, u32[]{:S(2)}) collective-permute-start(bf16[128,384]{1,0:T(8,128)(2,1)S(1)} %get-tuple-element.149), channel_id=1, source_target_pairs={{0,24},{4,28},{8,16},{12,20},{16,8},{20,12},{24,0},{28,4},{1,25},{... | collective-permute-start | bytes 294920 | tf_op jit(solution)/shard_map/ppermute | solution.py:707
  82.6 10.9 %all-to-all-start = ((bf16[8,16,384]{2,1,0:T(8,128)(2,1)}), bf16[8,16,384]{2,1,0:T(8,128)(2,1)S(1)}, u32[]{:S(2)}, u32[]{:S(2)}) async-start(bf16[8,16,384]{2,1,0:T(8,128)(2,1)} %get-tuple-element.160), calls=%async_computation | async-start | bytes 196608 | tf_op jit(solution)/shard_map/all_to_all | solution.py:896
  86.2 9.2 %collective-permute-start.30 = (bf16[4,48,384]{2,1,0:T(8,128)(2,1)S(1)}, bf16[4,48,384]{2,1,0:T(8,128)(2,1)S(1)}, u32[]{:S(2)}, u32[]{:S(2)}) collective-permute-start(bf16[4,48,384]{2,1,0:T(8,128)(2,1)S(1)} %shard_map.318.refs_0_), channel_id=1, source_target_pairs={{0,8},{4,12},{8,0},{12,4},{16,24},{20,28},{24,16},{28,20},{1,9},{5... | collective-permute-start | bytes 442376 | tf_op jit(solution)/shard_map/ppermute | solution.py:707
  93.6 7.6 %collective-permute-start.29 = (bf16[8,16,384]{2,1,0:T(8,128)(2,1)S(1)}, bf16[8,16,384]{2,1,0:T(8,128)(2,1)S(1)}, u32[]{:S(2)}, u32[]{:S(2)}) collective-permute-start(bf16[8,16,384]{2,1,0:T(8,128)(2,1)S(1)} %all-to-all-done.refs_0_), channel_id=1, source_target_pairs={{0,3},{1,2},{2,1},{3,0},{4,7},{5,6},{6,5},{7,4},{8,11},{9,10},{10,... | collective-permute-start | bytes 294920 | tf_op jit(solution)/shard_map/ppermute | solution.py:702
  93.6 7.6 %collective-permute-start.28 = (bf16[8,16,384]{2,1,0:T(8,128)(2,1)S(1)}, bf16[8,16,384]{2,1,0:T(8,128)(2,1)S(1)}, u32[]{:S(2)}, u32[]{:S(2)}) collective-permute-start(bf16[8,16,384]{2,1,0:T(8,128)(2,1)S(1)} %all-to-all-done.refs_0_), channel_id=1, source_target_pairs={{0,2},{1,3},{2,0},{3,1},{4,6},{5,7},{6,4},{7,5},{8,10},{9,11},{10,... | collective-permute-start | bytes 294920 | tf_op jit(solution)/shard_map/ppermute | solution.py:702
  94.6 6.6 %collective-permute-start.27 = (bf16[8,16,384]{2,1,0:T(8,128)(2,1)S(1)}, bf16[8,16,384]{2,1,0:T(8,128)(2,1)S(1)}, u32[]{:S(2)}, u32[]{:S(2)}) collective-permute-start(bf16[8,16,384]{2,1,0:T(8,128)(2,1)S(1)} %all-to-all-done.refs_0_), channel_id=1, source_target_pairs={{0,1},{1,0},{2,3},{3,2},{4,5},{5,4},{6,7},{7,6},{8,9},{9,8},{10,11... | collective-permute-start | bytes 294920 | tf_op jit(solution)/shard_map/ppermute | solution.py:702

commit v7 on v6

--- a/solution.py
+++ b/solution.py
@@ -654,7 +654,7 @@
             )
             return 0
 
-        lax.fori_loop(0, each // 8, some_rows, 0, unroll=4)
+        lax.fori_loop(0, each // 8, some_rows, 0, unroll=12)
         for k in (7, 8, 9):
             send(k, pl.ds(i * each, each))
     scale = (1.0 - STATS_DECAY) * factor * factor
@@ -686,7 +686,7 @@
         tm_out[r, :], tv_out[r, :], t_out[r, :] = adam(tables[r, :], tables_m[r, :], tables_v[r, :], grads[r, :], RATE_TABLES)
         return 0
 
-    lax.fori_loop(0, rows // 8, table_rows, 0, unroll=4)
+    lax.fori_loop(0, rows // 8, table_rows, 0, unroll=7)
     for k in (4, 5, 6):
         send(k)
     nrows = vectors.shape[0]

time: 107 us -> 107 us (level)
  no operation moved by 1% of the time
where the time goes in v7:
time: 107 us
  waiting for transfers between devices  44.5 us (42%)
  starting transfers between devices  35.8 us (33%)
  Pallas kernels  24.5 us (23%)
    ppermute x16, waiting for transfers between devices, flip(): return lax.ppermute(x, 'dp', [(i, i ^ k) for i in range(n)])  30.4 us
    pallas_call x15, Pallas kernels, call(): pl.pallas_call(kernel, out_shape=tuple(outs), in_specs=in_specs or [IN_VM...  24.5 us
    ppermute x16, starting transfers between devices, flip(): return lax.ppermute(x, 'dp', [(i, i ^ k) for i in range(n)])  22.8 us
    ppermute x12, starting transfers between devices, exchange(): lax.ppermute(x, axis, [(i, i ^ k) for i in range(n)])  7.61 us
    ppermute x12, waiting for transfers between devices, exchange(): lax.ppermute(x, axis, [(i, i ^ k) for i in range(n)])  7.57 us
    all_to_all x1, waiting for transfers between devices, per_device(): sums = lax.all_to_all(send, 'dp', 0, 0, tiled=True)  5.24 us
    all_to_all x1, starting transfers between devices, per_device(): sums = lax.all_to_all(send, 'dp', 0, 0, tiled=True)  3.54 us
  transfers between devices with their start and end apart: 32, of which 20 were waited for; matrix products, arithmetic and copies ran while one was open for 0% of the time, Pallas kernels for 12%

profile of v7, /device:TPU:0, one launch (start us, length us, event | category | flops | bytes accessed | tf_op | source)
XLA Modules:
  0.0 106.9 jit_solution(13952102796608884030)
XLA Ops:
  0.7 1.1 convert_element_type.3.refs_3_
  1.7 4.1 %collective-permute-start.3 = (bf16[96,1152]{1,0:T(8,128)(2,1)S(1)}, bf16[96,1152]{1,0:T(8,128)(2,1)S(1)}, u32[]{:S(2)}, u32[]{:S(2)}) collective-permute-start(bf16[96,1152]{1,0:T(8,128)(2,1)S(1)} %convert_element_type.3.refs_3_), channel_id=1, source_target_pairs={{0,16},{4,20},{8,24},{12,28},{16,0},{20,4},{24,8},{28,12},{1,17},{... | collective-permute-start | bytes 663560 | tf_op jit(solution)/shard_map/ppermute | solution.py:707
  5.8 1.6 %collective-permute-start.1 = (bf16[96,1152]{1,0:T(8,128)(2,1)S(1)}, bf16[96,1152]{1,0:T(8,128)(2,1)S(1)}, u32[]{:S(2)}, u32[]{:S(2)}) collective-permute-start(bf16[96,1152]{1,0:T(8,128)(2,1)S(1)} %convert_element_type.3.refs_3_), channel_id=1, source_target_pairs={{0,8},{4,12},{8,0},{12,4},{16,24},{20,28},{24,16},{28,20},{1,9},{5... | collective-permute-start | bytes 663560 | tf_op jit(solution)/shard_map/ppermute | solution.py:707
  7.4 1.5 %collective-permute-start = (bf16[96,1152]{1,0:T(8,128)(2,1)S(1)}, bf16[96,1152]{1,0:T(8,128)(2,1)S(1)}, u32[]{:S(2)}, u32[]{:S(2)}) collective-permute-start(bf16[96,1152]{1,0:T(8,128)(2,1)S(1)} %convert_element_type.3.refs_3_), channel_id=1, source_target_pairs={{0,4},{4,0},{8,12},{12,8},{16,20},{20,16},{24,28},{28,24},{1,5},{5... | collective-permute-start | bytes 663560 | tf_op jit(solution)/shard_map/ppermute | solution.py:707
  8.9 2.6 %shard_map.306 = (bf16[256,1024]{1,0:T(8,128)(2,1)S(1)}, bf16[1024,768]{1,0:T(8,128)(2,1)S(1)}, bf16[1024,768]{1,0:T(8,128)(2,1)S(1)}, f32[1024,128]{1,0:T(8,128)S(1)}) custom-call(f32[16,1024]{1,0:T(8,128)} %bitcast.21, s32[2,1024]{1,0:T(2,128)} %bitcast.22, s32[1,1024]{1,0:T(1,128)} %refs_2_.2, s32[1,1024]{1,0:T(1,128)} %refs_7_.6, f32[224,768]{1,0:T(8,128)} %refs_9_.1, ...), custom_call_target="tpu_custom_call" | custom-call | flops 805306368 | bytes 4998144 | tf_op jit(solution)/shard_map/pallas_call | solution.py:55
  11.5 0.0 copy-start.3
  11.5 4.6 %collective-permute-done.3.refs_7_ = bf16[96,1152]{1,0:T(8,128)(2,1)S(1)} collective-permute-done((bf16[96,1152]{1,0:T(8,128)(2,1)S(1)}, bf16[96,1152]{1,0:T(8,128)(2,1)S(1)}, u32[]{:S(2)}, u32[]{:S(2)}) %collective-permute-start.3) | collective-permute-done | bytes 221216 | tf_op jit(solution)/shard_map/ppermute | solution.py:707
  16.1 0.2 collective-permute-done.1.refs_5_
  16.3 3.2 %collective-permute-start.6 = (bf16[96,1152]{1,0:T(8,128)(2,1)S(1)}, bf16[96,1152]{1,0:T(8,128)(2,1)S(1)}, u32[]{:S(2)}, u32[]{:S(2)}) collective-permute-start(bf16[96,1152]{1,0:T(8,128)(2,1)S(1)} %collective-permute-done.refs_4_), channel_id=1, source_target_pairs={{0,24},{4,28},{8,16},{12,20},{16,8},{20,12},{24,0},{28,4},{1,25},{... | collective-permute-start | bytes 663560 | tf_op jit(solution)/shard_map/ppermute | solution.py:707
  19.5 1.5 %collective-permute-start.2 = (bf16[96,1152]{1,0:T(8,128)(2,1)S(1)}, bf16[96,1152]{1,0:T(8,128)(2,1)S(1)}, u32[]{:S(2)}, u32[]{:S(2)}) collective-permute-start(bf16[96,1152]{1,0:T(8,128)(2,1)S(1)} %collective-permute-done.1.refs_5_), channel_id=1, source_target_pairs={{0,4},{4,0},{8,12},{12,8},{16,20},{20,16},{24,28},{28,24},{1,5},{5... | collective-permute-start | bytes 663560 | tf_op jit(solution)/shard_map/ppermute | solution.py:707
  21.0 0.5 collective-permute-start.4
  21.6 4.9 %collective-permute-done.6.refs_10_ = bf16[96,1152]{1,0:T(8,128)(2,1)S(1)} collective-permute-done((bf16[96,1152]{1,0:T(8,128)(2,1)S(1)}, bf16[96,1152]{1,0:T(8,128)(2,1)S(1)}, u32[]{:S(2)}, u32[]{:S(2)}) %collective-permute-start.6) | collective-permute-done | bytes 221216 | tf_op jit(solution)/shard_map/ppermute | solution.py:707
  26.4 1.4 %collective-permute-done.2.refs_6_ = bf16[96,1152]{1,0:T(8,128)(2,1)S(1)} collective-permute-done((bf16[96,1152]{1,0:T(8,128)(2,1)S(1)}, bf16[96,1152]{1,0:T(8,128)(2,1)S(1)}, u32[]{:S(2)}, u32[]{:S(2)}) %collective-permute-start.2) | collective-permute-done | bytes 221216 | tf_op jit(solution)/shard_map/ppermute | solution.py:707
  27.9 2.1 %collective-permute-done.5.refs_9_ = bf16[96,1152]{1,0:T(8,128)(2,1)S(1)} collective-permute-done((bf16[96,1152]{1,0:T(8,128)(2,1)S(1)}, bf16[96,1152]{1,0:T(8,128)(2,1)S(1)}, u32[]{:S(2)}, u32[]{:S(2)}) %collective-permute-start.5) | collective-permute-done | bytes 221216 | tf_op jit(solution)/shard_map/ppermute | solution.py:707
  30.0 1.4 %collective-permute-done.4.refs_8_ = bf16[96,1152]{1,0:T(8,128)(2,1)S(1)} collective-permute-done((bf16[96,1152]{1,0:T(8,128)(2,1)S(1)}, bf16[96,1152]{1,0:T(8,128)(2,1)S(1)}, u32[]{:S(2)}, u32[]{:S(2)}) %collective-permute-start.4) | collective-permute-done | bytes 221216 | tf_op jit(solution)/shard_map/ppermute | solution.py:707
  31.4 2.5 %shard_map.307 = (bf16[24,768]{1,0:T(8,128)(2,1)S(1)}, bf16[192,1024]{1,0:T(8,128)(2,1)S(1)}, bf16[1024,256]{1,0:T(8,128)(2,1)S(1)}, bf16[24,256]{1,0:T(8,128)(2...) custom-call(bf16[1024,768]{1,0:T(8,128)(2,1)S(1)} %get-tuple-element, ...), custom_call_target="tpu_custom_call" | custom-call | flops 805306368 | bytes 6517760 | tf_op jit(solution)/shard_map/pallas_call | solution.py:55
  33.8 0.1 collective-permute-start.9
  33.9 1.6 %collective-permute-start.8 = (bf16[24,768]{1,0:T(8,128)(2,1)S(1)}, bf16[24,768]{1,0:T(8,128)(2,1)S(1)}, u32[]{:S(2)}, u32[]{:S(2)}) collective-permute-start(bf16[24,768]{1,0:T(8,128)(2,1)S(1)} %get-tuple-element.111.refs_0_), channel_id=1, source_target_pairs={{0,2},{1,3},{2,0},{3,1},{4,6},{5,7},{6,4},{7,5},{8,10},{9,11},{10,... | collective-permute-start | bytes 110600 | tf_op jit(solution)/shard_map/ppermute | solution.py:702
  35.5 0.3 collective-permute-start.7
  35.7 1.8 %collective-permute-done.9.refs_3_ = bf16[24,768]{1,0:T(8,128)(2,1)S(1)} collective-permute-done((bf16[24,768]{1,0:T(8,128)(2,1)S(1)}, bf16[24,768]{1,0:T(8,128)(2,1)S(1)}, u32[]{:S(2)}, u32[]{:S(2)}) %collective-permute-start.9) | collective-permute-done | bytes 36896 | tf_op jit(solution)/shard_map/ppermute | solution.py:702
  37.6 0.5 collective-permute-done.8.refs_2_
  38.1 0.6 shard_map.308
  38.7 1.1 collective-permute-start.12
  39.7 0.9 collective-permute-start.11
  40.6 1.5 %collective-permute-done.12.refs_3_ = bf16[24,768]{1,0:T(8,128)(2,1)S(1)} collective-permute-done((bf16[24,768]{1,0:T(8,128)(2,1)S(1)}, bf16[24,768]{1,0:T(8,128)(2,1)S(1)}, u32[]{:S(2)}, u32[]{:S(2)}) %collective-permute-start.12) | collective-permute-done | bytes 36896 | tf_op jit(solution)/shard_map/ppermute | solution.py:702
  42.1 1.6 %collective-permute-done.11.refs_2_ = bf16[24,768]{1,0:T(8,128)(2,1)S(1)} collective-permute-done((bf16[24,768]{1,0:T(8,128)(2,1)S(1)}, bf16[24,768]{1,0:T(8,128)(2,1)S(1)}, u32[]{:S(2)}, u32[]{:S(2)}) %collective-permute-start.11) | collective-permute-done | bytes 36896 | tf_op jit(solution)/shard_map/ppermute | solution.py:702
  43.8 1.6 %shard_map.309 = (bf16[24,768]{1,0:T(8,128)(2,1)S(1)}, bf16[24,768]{1,0:T(8,128)(2,1)S(1)}, f32[24,128]{1,0:T(8,128)S(1)}, f32[24,768]{1,0:T(8,128)S(1)}, bf16[2...) custom-call(bf16[24,768]{1,0:T(8,128)(2,1)S(1)} %get-tuple-element.113.refs_0_, ...), custom_call_target="tpu_custom_call" | custom-call | flops 56623104 | bytes 3466336 | tf_op jit(solution)/shard_map/pallas_call | solution.py:55
  45.3 0.7 collective-permute-start.15
  46.0 0.8 collective-permute-start.14
  46.9 0.4 collective-permute-start.13
  47.2 0.6 shard_map.311
  47.8 1.3 %collective-permute-done.15.refs_3_ = bf16[24,768]{1,0:T(8,128)(2,1)S(1)} collective-permute-done((bf16[24,768]{1,0:T(8,128)(2,1)S(1)}, bf16[24,768]{1,0:T(8,128)(2,1)S(1)}, u32[]{:S(2)}, u32[]{:S(2)}) %collective-permute-start.15) | collective-permute-done | bytes 36896 | tf_op jit(solution)/shard_map/ppermute | solution.py:702
  49.1 0.8 collective-permute-done.14.refs_2_
  50.0 1.5 %collective-permute-start.24 = (bf16[9,48,384]{2,1,0:T(8,128)(2,1)S(1)}, bf16[9,48,384]{2,1,0:T(8,128)(2,1)S(1)}, u32[]{:S(2)}, u32[]{:S(2)}) collective-permute-start(bf16[9,48,384]{2,1,0:T(8,128)(2,1)S(1)} %get-tuple-element.152), channel_id=1, source_target_pairs={{0,4},{4,0},{8,12},{12,8},{16,20},{20,16},{24,28},{28,24},{1,5},{5... | collective-permute-start | bytes 995336 | tf_op jit(solution)/shard_map/ppermute | solution.py:707
  51.5 2.3 %shard_map.310 = (bf16[4,96,384]{2,1,0:T(8,128)(2,1)S(1)}, bf16[4,96,384]{2,1,0:T(8,128)(2,1)S(1)}, f32[8,256]{1,0:T(8,128)S(1)}, f32[8,768]{1,0:T(8,128)S(1)}, ...) custom-call(bf16[24,768]{1,0:T(8,128)(2,1)S(1)} %get-tuple-element.116.refs_0_, ...), custom_call_target="tpu_custom_call" | custom-call | flops 805306368 | bytes 5231616 | tf_op jit(solution)/shard_map/pallas_call | solution.py:55
  53.8 0.6 collective-permute-start.16
  54.4 1.1 %shard_map.312 = (bf16[64,768]{1,0:T(8,128)(2,1)S(1)}, bf16[64,768]{1,0:T(8,128)(2,1)S(1)}, bf16[64,768]{1,0:T(8,128)(2,1)S(1)}, bf16[64,768]{1,0:T(8,128)(2,1)S(1)}) custom-call(bf16[256,1024]{1,0:T(8,128)(2,1)S(1)} %get-tuple-element.125.refs_0_, bf16[256,768]{1,0:T(8,128)(2,1)S(1)} %get-tuple-element.132.refs_1_, ...), custom_call_target="tpu_custom_call" | custom-call | flops 805306368 | bytes 4019200 | tf_op jit(solution)/shard_map/pallas_call | solution.py:55
  55.5 0.1 collective-permute-start.17
  55.6 1.1 %collective-permute-start.18 = (bf16[64,768]{1,0:T(8,128)(2,1)S(1)}, bf16[64,768]{1,0:T(8,128)(2,1)S(1)}, u32[]{:S(2)}, u32[]{:S(2)}) collective-permute-start(bf16[64,768]{1,0:T(8,128)(2,1)S(1)} %get-tuple-element.139), channel_id=1, source_target_pairs={{0,2},{1,3},{2,0},{3,1},{4,6},{5,7},{6,4},{7,5},{8,10},{9,11},{10,... | collective-permute-start | bytes 294920 | tf_op jit(solution)/shard_map/ppermute | solution.py:857
  56.7 0.7 collective-permute-start.19
  57.4 3.3 %collective-permute-done.24.came = bf16[9,48,384]{2,1,0:T(8,128)(2,1)S(1)} collective-permute-done((bf16[9,48,384]{2,1,0:T(8,128)(2,1)S(1)}, bf16[9,48,384]{2,1,0:T(8,128)(2,1)S(1)}, u32[]{:S(2)}, u32[]{:S(2)}) %collective-permute-start.24) | collective-permute-done | bytes 331808 | tf_op jit(solution)/shard_map/ppermute | solution.py:707
  60.7 0.1 shard_map.315
  60.8 0.3 collective-permute-start.25
  61.1 0.1 collective-permute-done.18.refs_2_
  61.2 1.2 %collective-permute-done.19.refs_3_ = bf16[64,768]{1,0:T(8,128)(2,1)S(1)} collective-permute-done((bf16[64,768]{1,0:T(8,128)(2,1)S(1)}, bf16[64,768]{1,0:T(8,128)(2,1)S(1)}, u32[]{:S(2)}, u32[]{:S(2)}) %collective-permute-start.19) | collective-permute-done | bytes 98336 | tf_op jit(solution)/shard_map/ppermute | solution.py:857
  62.4 0.1 shard_map.313
  62.5 1.6 %collective-permute-start.20 = (bf16[4,32,384]{2,1,0:T(8,128)(2,1)S(1)}, bf16[4,32,384]{2,1,0:T(8,128)(2,1)S(1)}, u32[]{:S(2)}, u32[]{:S(2)}) collective-permute-start(bf16[4,32,384]{2,1,0:T(8,128)(2,1)S(1)} %get-tuple-element.145), channel_id=1, source_target_pairs={{0,4},{4,0},{8,12},{12,8},{16,20},{20,16},{24,28},{28,24},{1,5},{5... | collective-permute-start | bytes 294920 | tf_op jit(solution)/shard_map/ppermute | solution.py:707
  64.1 1.9 %collective-permute-done.25.came = bf16[2,96,384]{2,1,0:T(8,128)(2,1)S(1)} collective-permute-done((bf16[2,96,384]{2,1,0:T(8,128)(2,1)S(1)}, bf16[2,96,384]{2,1,0:T(8,128)(2,1)S(1)}, u32[]{:S(2)}, u32[]{:S(2)}) %collective-permute-start.25) | collective-permute-done | bytes 147488 | tf_op jit(solution)/shard_map/ppermute | solution.py:707
  66.1 0.1 collective-permute-start.26
  66.1 1.7 %collective-permute-done.20.table_came = bf16[4,32,384]{2,1,0:T(8,128)(2,1)S(1)} collective-permute-done((bf16[4,32,384]{2,1,0:T(8,128)(2,1)S(1)}, bf16[4,32,384]{2,1,0:T(8,128)(2,1)S(1)}, u32[]{:S(2)}, u32[]{:S(2)}) %collective-permute-start.20) | collective-permute-done | bytes 98336 | tf_op jit(solution)/shard_map/ppermute | solution.py:707
  67.9 0.2 shard_map.314
  68.1 0.5 collective-permute-start.21
  68.6 2.6 %collective-permute-start.22 = (bf16[128,384]{1,0:T(8,128)(2,1)S(1)}, bf16[128,384]{1,0:T(8,128)(2,1)S(1)}, u32[]{:S(2)}, u32[]{:S(2)}) collective-permute-start(bf16[128,384]{1,0:T(8,128)(2,1)S(1)} %get-tuple-element.148), channel_id=1, source_target_pairs={{0,16},{4,20},{8,24},{12,28},{16,0},{20,4},{24,8},{28,12},{1,17},{... | collective-permute-start | bytes 294920 | tf_op jit(solution)/shard_map/ppermute | solution.py:707
  71.2 1.4 %collective-permute-start.23 = (bf16[128,384]{1,0:T(8,128)(2,1)S(1)}, bf16[128,384]{1,0:T(8,128)(2,1)S(1)}, u32[]{:S(2)}, u32[]{:S(2)}) collective-permute-start(bf16[128,384]{1,0:T(8,128)(2,1)S(1)} %get-tuple-element.149), channel_id=1, source_target_pairs={{0,24},{4,28},{8,16},{12,20},{16,8},{20,12},{24,0},{28,4},{1,25},{... | collective-permute-start | bytes 294920 | tf_op jit(solution)/shard_map/ppermute | solution.py:707
  72.6 2.3 %collective-permute-done.21.refs_1_ = bf16[128,384]{1,0:T(8,128)(2,1)S(1)} collective-permute-done((bf16[128,384]{1,0:T(8,128)(2,1)S(1)}, bf16[128,384]{1,0:T(8,128)(2,1)S(1)}, u32[]{:S(2)}, u32[]{:S(2)}) %collective-permute-start.21) | collective-permute-done | bytes 98336 | tf_op jit(solution)/shard_map/ppermute | solution.py:707
  74.8 6.6 %collective-permute-done.22.refs_2_ = bf16[128,384]{1,0:T(8,128)(2,1)S(1)} collective-permute-done((bf16[128,384]{1,0:T(8,128)(2,1)S(1)}, bf16[128,384]{1,0:T(8,128)(2,1)S(1)}, u32[]{:S(2)}, u32[]{:S(2)}) %collective-permute-start.22) | collective-permute-done | bytes 98336 | tf_op jit(solution)/shard_map/ppermute | solution.py:707
  81.5 1.1 %shard_map.317 = (f32[6,96,192]{2,1,0:T(8,128)S(1)}, bf16[8,16,384]{2,1,0:T(8,128)(2,1)}, f32[8,128]{1,0:T(8,128)S(1)}, f32[8,384]{1,0:T(8,128)S(1)}) custom-call(bf16[128,384]{1,0:T(8,128)(2,1)S(1)} %get-tuple-element.146.refs_0_, bf16[128,384]{1,0:T(8,128)(2,1)S(1)} %collective-permute-done.21.refs_1_, ...), custom_call_target="tpu_custom_call" | custom-call | flops 50331648 | bytes 1213440 | tf_op jit(solution)/shard_map/pallas_call | solution.py:55
  82.6 3.5 %all-to-all-start = ((bf16[8,16,384]{2,1,0:T(8,128)(2,1)}), bf16[8,16,384]{2,1,0:T(8,128)(2,1)S(1)}, u32[]{:S(2)}, u32[]{:S(2)}) async-start(bf16[8,16,384]{2,1,0:T(8,128)(2,1)} %get-tuple-element.160), calls=%async_computation | async-start | bytes 196608 | tf_op jit(solution)/shard_map/all_to_all | solution.py:896
  86.2 1.8 %collective-permute-start.30 = (bf16[4,48,384]{2,1,0:T(8,128)(2,1)S(1)}, bf16[4,48,384]{2,1,0:T(8,128)(2,1)S(1)}, u32[]{:S(2)}, u32[]{:S(2)}) collective-permute-start(bf16[4,48,384]{2,1,0:T(8,128)(2,1)S(1)} %shard_map.318.refs_0_), channel_id=1, source_target_pairs={{0,8},{4,12},{8,0},{12,4},{16,24},{20,28},{24,16},{28,20},{1,9},{5... | collective-permute-start | bytes 442376 | tf_op jit(solution)/shard_map/ppermute | solution.py:707
  88.0 5.2 %all-to-all-done.refs_0_ = bf16[8,16,384]{2,1,0:T(8,128)(2,1)S(1)} async-done(((bf16[8,16,384]{2,1,0:T(8,128)(2,1)}), bf16[8,16,384]{2,1,0:T(8,128)(2,1)S(1)}, u32[]{:S(2)}, u32[]{:S(2)}) %all-to-all-start) | async-done | bytes 98336 | tf_op jit(solution)/shard_map/all_to_all | solution.py:896
  93.2 1.1 %collective-permute-start.28 = (bf16[8,16,384]{2,1,0:T(8,128)(2,1)S(1)}, bf16[8,16,384]{2,1,0:T(8,128)(2,1)S(1)}, u32[]{:S(2)}, u32[]{:S(2)}) collective-permute-start(bf16[8,16,384]{2,1,0:T(8,128)(2,1)S(1)} %all-to-all-done.refs_0_), channel_id=1, source_target_pairs={{0,2},{1,3},{2,0},{3,1},{4,6},{5,7},{6,4},{7,5},{8,10},{9,11},{10,... | collective-permute-start | bytes 294920 | tf_op jit(solution)/shard_map/ppermute | solution.py:702
  94.3 0.7 collective-permute-start.27
  95.1 5.7 %shard_map.319 = (f32[768,768]{1,0:T(8,128)S(1)}, f32[8,128]{1,0:T(8,128)S(1)}, f32[6,96,96]{2,1,0:T(8,128)S(1)}, f32[6,192,192]{2,1,0:T(8,128)S(1)}, f32[96,115...) custom-call(bf16[4,48,384]{2,1,0:T(8,128)(2,1)S(1)} %shard_map.318.r, ...), custom_call_target="tpu_custom_call" | custom-call | flops 452984832 | bytes 26500096 | tf_op jit(solution)/shard_map/pallas_call | solution.py:55
  100.8 5.9 %shard_map.320 = (f32[1,1]{1,0:T(1,128)}, f32[1,1]{1,0:T(1,128)}, f32[1,1]{1,0:T(1,128)}, f32[96,1152]{1,0:T(8,128)}, f32[96,1152]{1,0:T(8,128)}, /*index=5*/f32...) custom-call(bf16[8,16,384]{2,1,0:T(8,128)(2,1)S(1)} %all-to-all-done, ...), custom_call_target="tpu_custom_call" | custom-call | flops 11796480 | bytes 26335244 | tf_op jit(solution)/shard_map/pallas_call | solution.py:55
  (24 shorter events, 0.1 us)
Async XLA Ops:
  0.6 30.7 %copy-start.1 = (f32[11,768]{1,0:T(8,128)S(1)}, f32[11,768]{1,0:T(8,128)}, u32[]{:S(2)}) copy-start(f32[11,768]{1,0:T(8,128)} %refs_15_.1) | copy-start | bytes 101380
  0.7 30.7 %copy-start.2 = (s32[1,1024]{1,0:T(1,128)S(1)}, s32[1,1024]{1,0:T(1,128)}, u32[]{:S(2)}) copy-start(s32[1,1024]{1,0:T(1,128)} %refs_7_.6) | copy-start | bytes 12292
  1.7 14.4 %collective-permute-start.3 = (bf16[96,1152]{1,0:T(8,128)(2,1)S(1)}, bf16[96,1152]{1,0:T(8,128)(2,1)S(1)}, u32[]{:S(2)}, u32[]{:S(2)}) collective-permute-start(bf16[96,1152]{1,0:T(8,128)(2,1)S(1)} %convert_element_type.3.refs_3_), channel_id=1, source_target_pairs={{0,16},{4,20},{8,24},{12,28},{16,0},{20,4},{24,8},{28,12},{1,17},{... | collective-permute-start | bytes 663560 | tf_op jit(solution)/shard_map/ppermute | solution.py:707
  5.8 10.5 %collective-permute-start.1 = (bf16[96,1152]{1,0:T(8,128)(2,1)S(1)}, bf16[96,1152]{1,0:T(8,128)(2,1)S(1)}, u32[]{:S(2)}, u32[]{:S(2)}) collective-permute-start(bf16[96,1152]{1,0:T(8,128)(2,1)S(1)} %convert_element_type.3.refs_3_), channel_id=1, source_target_pairs={{0,8},{4,12},{8,0},{12,4},{16,24},{20,28},{24,16},{28,20},{1,9},{5... | collective-permute-start | bytes 663560 | tf_op jit(solution)/shard_map/ppermute | solution.py:707
  7.4 8.9 %collective-permute-start = (bf16[96,1152]{1,0:T(8,128)(2,1)S(1)}, bf16[96,1152]{1,0:T(8,128)(2,1)S(1)}, u32[]{:S(2)}, u32[]{:S(2)}) collective-permute-start(bf16[96,1152]{1,0:T(8,128)(2,1)S(1)} %convert_element_type.3.refs_3_), channel_id=1, source_target_pairs={{0,4},{4,0},{8,12},{12,8},{16,20},{20,16},{24,28},{28,24},{1,5},{5... | collective-permute-start | bytes 663560 | tf_op jit(solution)/shard_map/ppermute | solution.py:707
  11.5 32.2 %copy-start = (f32[768,768]{1,0:T(8,128)S(1)}, f32[768,768]{1,0:T(8,128)}, u32[]{:S(2)}) copy-start(f32[768,768]{1,0:T(8,128)} %refs_12_.1) | copy-start | bytes 7077892
  11.5 32.2 %copy-start.3 = (f32[1,24]{1,0:T(1,128)S(1)}, f32[1,24]{1,0:T(1,128)}, u32[]{:S(2)}) copy-start(f32[1,24]{1,0:T(1,128)} %refs_7_.4) | copy-start | bytes 292
  16.3 10.1 %collective-permute-start.6 = (bf16[96,1152]{1,0:T(8,128)(2,1)S(1)}, bf16[96,1152]{1,0:T(8,128)(2,1)S(1)}, u32[]{:S(2)}, u32[]{:S(2)}) collective-permute-start(bf16[96,1152]{1,0:T(8,128)(2,1)S(1)} %collective-permute-done.refs_4_), channel_id=1, source_target_pairs={{0,24},{4,28},{8,16},{12,20},{16,8},{20,12},{24,0},{28,4},{1,25},{... | collective-permute-start | bytes 663560 | tf_op jit(solution)/shard_map/ppermute | solution.py:707
  19.5 8.3 %collective-permute-start.2 = (bf16[96,1152]{1,0:T(8,128)(2,1)S(1)}, bf16[96,1152]{1,0:T(8,128)(2,1)S(1)}, u32[]{:S(2)}, u32[]{:S(2)}) collective-permute-start(bf16[96,1152]{1,0:T(8,128)(2,1)S(1)} %collective-permute-done.1.refs_5_), channel_id=1, source_target_pairs={{0,4},{4,0},{8,12},{12,8},{16,20},{20,16},{24,28},{28,24},{1,5},{5... | collective-permute-start | bytes 663560 | tf_op jit(solution)/shard_map/ppermute | solution.py:707
  21.0 9.0 %collective-permute-start.5 = (bf16[96,1152]{1,0:T(8,128)(2,1)S(1)}, bf16[96,1152]{1,0:T(8,128)(2,1)S(1)}, u32[]{:S(2)}, u32[]{:S(2)}) collective-permute-start(bf16[96,1152]{1,0:T(8,128)(2,1)S(1)} %collective-permute-done.3.refs_7_), channel_id=1, source_target_pairs={{0,8},{4,12},{8,0},{12,4},{16,24},{20,28},{24,16},{28,20},{1,9},{5... | collective-permute-start | bytes 663560 | tf_op jit(solution)/shard_map/ppermute | solution.py:707
  21.0 10.3 %collective-permute-start.4 = (bf16[96,1152]{1,0:T(8,128)(2,1)S(1)}, bf16[96,1152]{1,0:T(8,128)(2,1)S(1)}, u32[]{:S(2)}, u32[]{:S(2)}) collective-permute-start(bf16[96,1152]{1,0:T(8,128)(2,1)S(1)} %collective-permute-done.3.refs_7_), channel_id=1, source_target_pairs={{0,4},{4,0},{8,12},{12,8},{16,20},{20,16},{24,28},{28,24},{1,5},{5... | collective-permute-start | bytes 663560 | tf_op jit(solution)/shard_map/ppermute | solution.py:707
  33.8 3.8 %collective-permute-start.9 = (bf16[24,768]{1,0:T(8,128)(2,1)S(1)}, bf16[24,768]{1,0:T(8,128)(2,1)S(1)}, u32[]{:S(2)}, u32[]{:S(2)}) collective-permute-start(bf16[24,768]{1,0:T(8,128)(2,1)S(1)} %get-tuple-element.111.refs_0_), channel_id=1, source_target_pairs={{0,3},{1,2},{2,1},{3,0},{4,7},{5,6},{6,5},{7,4},{8,11},{9,10},{10,... | collective-permute-start | bytes 110600 | tf_op jit(solution)/shard_map/ppermute | solution.py:702
  33.9 4.2 %collective-permute-start.8 = (bf16[24,768]{1,0:T(8,128)(2,1)S(1)}, bf16[24,768]{1,0:T(8,128)(2,1)S(1)}, u32[]{:S(2)}, u32[]{:S(2)}) collective-permute-start(bf16[24,768]{1,0:T(8,128)(2,1)S(1)} %get-tuple-element.111.refs_0_), channel_id=1, source_target_pairs={{0,2},{1,3},{2,0},{3,1},{4,6},{5,7},{6,4},{7,5},{8,10},{9,11},{10,... | collective-permute-start | bytes 110600 | tf_op jit(solution)/shard_map/ppermute | solution.py:702
  35.5 2.6 %collective-permute-start.7 = (bf16[24,768]{1,0:T(8,128)(2,1)S(1)}, bf16[24,768]{1,0:T(8,128)(2,1)S(1)}, u32[]{:S(2)}, u32[]{:S(2)}) collective-permute-start(bf16[24,768]{1,0:T(8,128)(2,1)S(1)} %get-tuple-element.111.refs_0_), channel_id=1, source_target_pairs={{0,1},{1,0},{2,3},{3,2},{4,5},{5,4},{6,7},{7,6},{8,9},{9,8},{10,11... | collective-permute-start | bytes 110600 | tf_op jit(solution)/shard_map/ppermute | solution.py:702
  38.7 3.4 %collective-permute-start.12 = (bf16[24,768]{1,0:T(8,128)(2,1)S(1)}, bf16[24,768]{1,0:T(8,128)(2,1)S(1)}, u32[]{:S(2)}, u32[]{:S(2)}) collective-permute-start(bf16[24,768]{1,0:T(8,128)(2,1)S(1)} %get-tuple-element.113.refs_0_), channel_id=1, source_target_pairs={{0,3},{1,2},{2,1},{3,0},{4,7},{5,6},{6,5},{7,4},{8,11},{9,10},{10,... | collective-permute-start | bytes 110600 | tf_op jit(solution)/shard_map/ppermute | solution.py:702
  39.7 4.0 %collective-permute-start.11 = (bf16[24,768]{1,0:T(8,128)(2,1)S(1)}, bf16[24,768]{1,0:T(8,128)(2,1)S(1)}, u32[]{:S(2)}, u32[]{:S(2)}) collective-permute-start(bf16[24,768]{1,0:T(8,128)(2,1)S(1)} %get-tuple-element.113.refs_0_), channel_id=1, source_target_pairs={{0,2},{1,3},{2,0},{3,1},{4,6},{5,7},{6,4},{7,5},{8,10},{9,11},{10,... | collective-permute-start | bytes 110600 | tf_op jit(solution)/shard_map/ppermute | solution.py:702
  40.6 3.1 %collective-permute-start.10 = (bf16[24,768]{1,0:T(8,128)(2,1)S(1)}, bf16[24,768]{1,0:T(8,128)(2,1)S(1)}, u32[]{:S(2)}, u32[]{:S(2)}) collective-permute-start(bf16[24,768]{1,0:T(8,128)(2,1)S(1)} %get-tuple-element.113.refs_0_), channel_id=1, source_target_pairs={{0,1},{1,0},{2,3},{3,2},{4,5},{5,4},{6,7},{7,6},{8,9},{9,8},{10,11... | collective-permute-start | bytes 110600 | tf_op jit(solution)/shard_map/ppermute | solution.py:702
  45.3 3.8 %collective-permute-start.15 = (bf16[24,768]{1,0:T(8,128)(2,1)S(1)}, bf16[24,768]{1,0:T(8,128)(2,1)S(1)}, u32[]{:S(2)}, u32[]{:S(2)}) collective-permute-start(bf16[24,768]{1,0:T(8,128)(2,1)S(1)} %get-tuple-element.116.refs_0_), channel_id=1, source_target_pairs={{0,3},{1,2},{2,1},{3,0},{4,7},{5,6},{6,5},{7,4},{8,11},{9,10},{10,... | collective-permute-start | bytes 110600 | tf_op jit(solution)/shard_map/ppermute | solution.py:702
  46.0 4.0 %collective-permute-start.14 = (bf16[24,768]{1,0:T(8,128)(2,1)S(1)}, bf16[24,768]{1,0:T(8,128)(2,1)S(1)}, u32[]{:S(2)}, u32[]{:S(2)}) collective-permute-start(bf16[24,768]{1,0:T(8,128)(2,1)S(1)} %get-tuple-element.116.refs_0_), channel_id=1, source_target_pairs={{0,2},{1,3},{2,0},{3,1},{4,6},{5,7},{6,4},{7,5},{8,10},{9,11},{10,... | collective-permute-start | bytes 110600 | tf_op jit(solution)/shard_map/ppermute | solution.py:702
  46.9 3.1 %collective-permute-start.13 = (bf16[24,768]{1,0:T(8,128)(2,1)S(1)}, bf16[24,768]{1,0:T(8,128)(2,1)S(1)}, u32[]{:S(2)}, u32[]{:S(2)}) collective-permute-start(bf16[24,768]{1,0:T(8,128)(2,1)S(1)} %get-tuple-element.116.refs_0_), channel_id=1, source_target_pairs={{0,1},{1,0},{2,3},{3,2},{4,5},{5,4},{6,7},{7,6},{8,9},{9,8},{10,11... | collective-permute-start | bytes 110600 | tf_op jit(solution)/shard_map/ppermute | solution.py:702
  50.0 10.7 %collective-permute-start.24 = (bf16[9,48,384]{2,1,0:T(8,128)(2,1)S(1)}, bf16[9,48,384]{2,1,0:T(8,128)(2,1)S(1)}, u32[]{:S(2)}, u32[]{:S(2)}) collective-permute-start(bf16[9,48,384]{2,1,0:T(8,128)(2,1)S(1)} %get-tuple-element.152), channel_id=1, source_target_pairs={{0,4},{4,0},{8,12},{12,8},{16,20},{20,16},{24,28},{28,24},{1,5},{5... | collective-permute-start | bytes 995336 | tf_op jit(solution)/shard_map/ppermute | solution.py:707
  53.8 14.1 %collective-permute-start.16 = (bf16[4,96,384]{2,1,0:T(8,128)(2,1)S(1)}, bf16[4,96,384]{2,1,0:T(8,128)(2,1)S(1)}, u32[]{:S(2)}, u32[]{:S(2)}) collective-permute-start(bf16[4,96,384]{2,1,0:T(8,128)(2,1)S(1)} %get-tuple-element.124), channel_id=1, source_target_pairs={{0,4},{4,0},{8,12},{12,8},{16,20},{20,16},{24,28},{28,24},{1,5},{5... | collective-permute-start | bytes 884744 | tf_op jit(solution)/shard_map/ppermute | solution.py:707
  55.5 5.7 %collective-permute-start.17 = (bf16[64,768]{1,0:T(8,128)(2,1)S(1)}, bf16[64,768]{1,0:T(8,128)(2,1)S(1)}, u32[]{:S(2)}, u32[]{:S(2)}) collective-permute-start(bf16[64,768]{1,0:T(8,128)(2,1)S(1)} %get-tuple-element.138), channel_id=1, source_target_pairs={{0,1},{1,0},{2,3},{3,2},{4,5},{5,4},{6,7},{7,6},{8,9},{9,8},{10,11... | collective-permute-start | bytes 294920 | tf_op jit(solution)/shard_map/ppermute | solution.py:857
  55.6 5.7 %collective-permute-start.18 = (bf16[64,768]{1,0:T(8,128)(2,1)S(1)}, bf16[64,768]{1,0:T(8,128)(2,1)S(1)}, u32[]{:S(2)}, u32[]{:S(2)}) collective-permute-start(bf16[64,768]{1,0:T(8,128)(2,1)S(1)} %get-tuple-element.139), channel_id=1, source_target_pairs={{0,2},{1,3},{2,0},{3,1},{4,6},{5,7},{6,4},{7,5},{8,10},{9,11},{10,... | collective-permute-start | bytes 294920 | tf_op jit(solution)/shard_map/ppermute | solution.py:857
  56.7 5.7 %collective-permute-start.19 = (bf16[64,768]{1,0:T(8,128)(2,1)S(1)}, bf16[64,768]{1,0:T(8,128)(2,1)S(1)}, u32[]{:S(2)}, u32[]{:S(2)}) collective-permute-start(bf16[64,768]{1,0:T(8,128)(2,1)S(1)} %get-tuple-element.140), channel_id=1, source_target_pairs={{0,3},{1,2},{2,1},{3,0},{4,7},{5,6},{6,5},{7,4},{8,11},{9,10},{10,... | collective-permute-start | bytes 294920 | tf_op jit(solution)/shard_map/ppermute | solution.py:857
  60.8 5.2 %collective-permute-start.25 = (bf16[2,96,384]{2,1,0:T(8,128)(2,1)S(1)}, bf16[2,96,384]{2,1,0:T(8,128)(2,1)S(1)}, u32[]{:S(2)}, u32[]{:S(2)}) collective-permute-start(bf16[2,96,384]{2,1,0:T(8,128)(2,1)S(1)} %get-tuple-element.155), channel_id=1, source_target_pairs={{0,8},{4,12},{8,0},{12,4},{16,24},{20,28},{24,16},{28,20},{1,9},{5... | collective-permute-start | bytes 442376 | tf_op jit(solution)/shard_map/ppermute | solution.py:707
  62.5 5.3 %collective-permute-start.20 = (bf16[4,32,384]{2,1,0:T(8,128)(2,1)S(1)}, bf16[4,32,384]{2,1,0:T(8,128)(2,1)S(1)}, u32[]{:S(2)}, u32[]{:S(2)}) collective-permute-start(bf16[4,32,384]{2,1,0:T(8,128)(2,1)S(1)} %get-tuple-element.145), channel_id=1, source_target_pairs={{0,4},{4,0},{8,12},{12,8},{16,20},{20,16},{24,28},{28,24},{1,5},{5... | collective-permute-start | bytes 294920 | tf_op jit(solution)/shard_map/ppermute | solution.py:707
  66.1 15.4 %collective-permute-start.26 = (bf16[4,48,384]{2,1,0:T(8,128)(2,1)S(1)}, bf16[4,48,384]{2,1,0:T(8,128)(2,1)S(1)}, u32[]{:S(2)}, u32[]{:S(2)}) collective-permute-start(bf16[4,48,384]{2,1,0:T(8,128)(2,1)S(1)} %get-tuple-element.158), channel_id=1, source_target_pairs={{0,16},{4,20},{8,24},{12,28},{16,0},{20,4},{24,8},{28,12},{1,17},{... | collective-permute-start | bytes 442376 | tf_op jit(solution)/shard_map/ppermute | solution.py:707
  68.1 6.7 %collective-permute-start.21 = (bf16[128,384]{1,0:T(8,128)(2,1)S(1)}, bf16[128,384]{1,0:T(8,128)(2,1)S(1)}, u32[]{:S(2)}, u32[]{:S(2)}) collective-permute-start(bf16[128,384]{1,0:T(8,128)(2,1)S(1)} %get-tuple-element.147), channel_id=1, source_target_pairs={{0,8},{4,12},{8,0},{12,4},{16,24},{20,28},{24,16},{28,20},{1,9},{5... | collective-permute-start | bytes 294920 | tf_op jit(solution)/shard_map/ppermute | solution.py:707
  68.6 12.9 %collective-permute-start.22 = (bf16[128,384]{1,0:T(8,128)(2,1)S(1)}, bf16[128,384]{1,0:T(8,128)(2,1)S(1)}, u32[]{:S(2)}, u32[]{:S(2)}) collective-permute-start(bf16[128,384]{1,0:T(8,128)(2,1)S(1)} %get-tuple-element.148), channel_id=1, source_target_pairs={{0,16},{4,20},{8,24},{12,28},{16,0},{20,4},{24,8},{28,12},{1,17},{... | collective-permute-start | bytes 294920 | tf_op jit(solution)/shard_map/ppermute | solution.py:707
  71.2 10.3 %collective-permute-start.23 = (bf16[128,384]{1,0:T(8,128)(2,1)S(1)}, bf16[128,384]{1,0:T(8,128)(2,1)S(1)}, u32[]{:S(2)}, u32[]{:S(2)}) collective-permute-start(bf16[128,384]{1,0:T(8,128)(2,1)S(1)} %get-tuple-element.149), channel_id=1, source_target_pairs={{0,24},{4,28},{8,16},{12,20},{16,8},{20,12},{24,0},{28,4},{1,25},{... | collective-permute-start | bytes 294920 | tf_op jit(solution)/shard_map/ppermute | solution.py:707
  82.6 10.6 %all-to-all-start = ((bf16[8,16,384]{2,1,0:T(8,128)(2,1)}), bf16[8,16,384]{2,1,0:T(8,128)(2,1)S(1)}, u32[]{:S(2)}, u32[]{:S(2)}) async-start(bf16[8,16,384]{2,1,0:T(8,128)(2,1)} %get-tuple-element.160), calls=%async_computation | async-start | bytes 196608 | tf_op jit(solution)/shard_map/all_to_all | solution.py:896
  86.2 8.9 %collective-permute-start.30 = (bf16[4,48,384]{2,1,0:T(8,128)(2,1)S(1)}, bf16[4,48,384]{2,1,0:T(8,128)(2,1)S(1)}, u32[]{:S(2)}, u32[]{:S(2)}) collective-permute-start(bf16[4,48,384]{2,1,0:T(8,128)(2,1)S(1)} %shard_map.318.refs_0_), channel_id=1, source_target_pairs={{0,8},{4,12},{8,0},{12,4},{16,24},{20,28},{24,16},{28,20},{1,9},{5... | collective-permute-start | bytes 442376 | tf_op jit(solution)/shard_map/ppermute | solution.py:707
  93.2 7.6 %collective-permute-start.29 = (bf16[8,16,384]{2,1,0:T(8,128)(2,1)S(1)}, bf16[8,16,384]{2,1,0:T(8,128)(2,1)S(1)}, u32[]{:S(2)}, u32[]{:S(2)}) collective-permute-start(bf16[8,16,384]{2,1,0:T(8,128)(2,1)S(1)} %all-to-all-done.refs_0_), channel_id=1, source_target_pairs={{0,3},{1,2},{2,1},{3,0},{4,7},{5,6},{6,5},{7,4},{8,11},{9,10},{10,... | collective-permute-start | bytes 294920 | tf_op jit(solution)/shard_map/ppermute | solution.py:702
  93.2 7.6 %collective-permute-start.28 = (bf16[8,16,384]{2,1,0:T(8,128)(2,1)S(1)}, bf16[8,16,384]{2,1,0:T(8,128)(2,1)S(1)}, u32[]{:S(2)}, u32[]{:S(2)}) collective-permute-start(bf16[8,16,384]{2,1,0:T(8,128)(2,1)S(1)} %all-to-all-done.refs_0_), channel_id=1, source_target_pairs={{0,2},{1,3},{2,0},{3,1},{4,6},{5,7},{6,4},{7,5},{8,10},{9,11},{10,... | collective-permute-start | bytes 294920 | tf_op jit(solution)/shard_map/ppermute | solution.py:702
  94.3 6.5 %collective-permute-start.27 = (bf16[8,16,384]{2,1,0:T(8,128)(2,1)S(1)}, bf16[8,16,384]{2,1,0:T(8,128)(2,1)S(1)}, u32[]{:S(2)}, u32[]{:S(2)}) collective-permute-start(bf16[8,16,384]{2,1,0:T(8,128)(2,1)S(1)} %all-to-all-done.refs_0_), channel_id=1, source_target_pairs={{0,1},{1,0},{2,3},{3,2},{4,5},{5,4},{6,7},{7,6},{8,9},{9,8},{10,11... | collective-permute-start | bytes 294920 | tf_op jit(solution)/shard_map/ppermute | solution.py:702
